TPU v7x, 32 devices: a whole 2x2x4 slice. The times are simulated.
32 devices in a mesh: rep: 4 (over x, core), fsdp: 8 (over z, y).
Axes of the slice: x: 2, y: 2, z: 4, core: 2. Of those that a mesh axis runs over, the one named last changes fastest.
Arguments:
- block_input: bfloat16 [8192, 1024], P(('rep', 'fsdp')), may hold values from -6 to 6
- segments: int32 [32, 256], P(('rep', 'fsdp')), may hold values from 0 to 7, never falling along the last dimension, each value on 1 to 128 neighbouring positions
- cotangent: bfloat16 [8192, 1024], P(('rep', 'fsdp')), may hold values from -6 to 6
- first_gain: bfloat16 [1024], P('fsdp'), may hold values from 0.5 to 1.5
- first_shift: bfloat16 [1024], P('fsdp'), may hold values from -3 to 3
- mix_weight: bfloat16 [1024, 3072], P('fsdp'), may hold values from -0.1875 to 0.1875
- mix_bias: bfloat16 [3072], P('fsdp'), may hold values from -3 to 3
- dense_weight: bfloat16 [1024, 1024], P('fsdp'), may hold values from -0.75 to 0.75
- dense_bias: bfloat16 [1024], P('fsdp'), may hold values from -3 to 3
- second_gain: bfloat16 [1024], P('fsdp'), may hold values from 0.5 to 1.5
- second_shift: bfloat16 [1024], P('fsdp'), may hold values from -3 to 3
- expand_weight: bfloat16 [1024, 4096], P('fsdp'), may hold values from -0.1875 to 0.1875
- expand_bias: bfloat16 [4096], P('fsdp'), may hold values from -3 to 3
- shrink_weight: bfloat16 [4096, 1024], P('fsdp'), may hold values from -0.09375 to 0.09375
- shrink_bias: bfloat16 [1024], P('fsdp'), may hold values from -3 to 3
Outputs:
- block_out: bfloat16 [8192, 1024], P(('rep', 'fsdp'))
- input_grad: float32 [8192, 1024], P(('rep', 'fsdp'))
- first_gain_grad: float32 [1024], P('fsdp')
- first_shift_grad: float32 [1024], P('fsdp')
- mix_weight_grad: float32 [1024, 3072], P('fsdp')
- mix_bias_grad: float32 [3072], P('fsdp')
- dense_weight_grad: float32 [1024, 1024], P('fsdp')
- dense_bias_grad: float32 [1024], P('fsdp')
- second_gain_grad: float32 [1024], P('fsdp')
- second_shift_grad: float32 [1024], P('fsdp')
- expand_weight_grad: float32 [1024, 4096], P('fsdp')
- expand_bias_grad: float32 [4096], P('fsdp')
- shrink_weight_grad: float32 [4096, 1024], P('fsdp')
- shrink_bias_grad: float32 [1024], P('fsdp')
Inputs may be any that keep to these rules, and one draw needn't show every extreme that they name: `segments`: within each row of 256 tokens the document numbers never fall; each document holds 1 to 128 tokens.
All inputs are finite; a program needn't handle non-finite values.
Results may differ from a plain program's by a relative error of at most 0.0099.
Values may be sent and summed in bfloat16 or wider, within the bound.
No kernel may reach another device: no remote copies, remote signals or barrier semaphores. Data moves between devices by JAX's collectives and lax.ppermute only.
A program may use at most 192 MiB of HBM per device.

v0:
```python
import jax
import jax.numpy as jnp
from jax import lax
from jax.sharding import PartitionSpec as P

HEADS = 16
HEAD = 64
ROT = 16


EPSILON = 1e-05


def layer_norm(inputs, gain_row, shift_row):
    average = jnp.mean(inputs, axis=-1, keepdims=True)
    centred = inputs - average
    variance = jnp.mean(centred * centred, axis=-1, keepdims=True)
    return centred * lax.rsqrt(variance + EPSILON) * gain_row + shift_row


def rotate(heads_in, cos_table, sin_table):
    half_rot = ROT // 2
    first_half = heads_in[..., :half_rot]
    second_half = heads_in[..., half_rot:ROT]
    return jnp.concatenate(
        [
            first_half * cos_table - second_half * sin_table,
            second_half * cos_table + first_half * sin_table,
            heads_in[..., ROT:],
        ],
        axis=-1,
    )


def rotary_tables(segment_row):
    length = segment_row.shape[0]
    same_doc = segment_row[:, None] == segment_row[None, :]
    row_index = lax.broadcasted_iota(jnp.int32, (length, length), 0)
    col_index = lax.broadcasted_iota(jnp.int32, (length, length), 1)
    earlier = jnp.where(same_doc & (col_index < row_index), 1.0, 0.0)
    position = jnp.sum(earlier, axis=-1).astype(jnp.float32)
    allowed = same_doc & (col_index <= row_index)
    frequency = jnp.power(10000.0, -2.0 * jnp.arange(ROT // 2).astype(jnp.float32) / ROT)
    phases = position[:, None] * frequency
    return (jnp.cos(phases)[:, None, :], jnp.sin(phases)[:, None, :], allowed)


def product_left(left, right):
    return lax.dot_general(
        left, right, (((0,), (0,)), ((), ())), preferred_element_type=jnp.float32
    )


def product_right(left, right):
    return lax.dot_general(
        left, right, (((1,), (1,)), ((), ())), preferred_element_type=jnp.float32
    )


def norm_backward(inputs, gain_row, shift_row, upstream):
    _, pullback = jax.vjp(layer_norm, inputs, gain_row, shift_row)
    return pullback(upstream)


def local(
    block_input,
    segments,
    cotangent,
    first_gain,
    first_shift,
    mix_weight,
    mix_bias,
    dense_weight,
    dense_bias,
    second_gain,
    second_shift,
    expand_weight,
    expand_bias,
    shrink_weight,
    shrink_bias,
):
    attention_parts = (
        lax.all_gather(first_gain, "fsdp", axis=0, tiled=True),
        lax.all_gather(first_shift, "fsdp", axis=0, tiled=True),
        lax.all_gather(mix_weight, "fsdp", axis=0, tiled=True),
        lax.all_gather(mix_bias, "fsdp", axis=0, tiled=True),
        lax.all_gather(dense_weight, "fsdp", axis=0, tiled=True),
        lax.all_gather(dense_bias, "fsdp", axis=0, tiled=True),
    )
    feed_parts = (
        lax.all_gather(second_gain, "fsdp", axis=0, tiled=True),
        lax.all_gather(second_shift, "fsdp", axis=0, tiled=True),
        lax.all_gather(expand_weight, "fsdp", axis=0, tiled=True),
        lax.all_gather(expand_bias, "fsdp", axis=0, tiled=True),
        lax.all_gather(shrink_weight, "fsdp", axis=0, tiled=True),
        lax.all_gather(shrink_bias, "fsdp", axis=0, tiled=True),
    )
    token_count = block_input.shape[0]
    feature_count = block_input.shape[1]
    score_scale = HEAD ** (-0.5)
    block_float = block_input.astype(jnp.float32)
    cot_float = cotangent.astype(jnp.float32)
    cos_table, sin_table, allowed = rotary_tables(segments[0])
    normed_one = layer_norm(
        block_float, attention_parts[0].astype(jnp.float32), attention_parts[1].astype(jnp.float32)
    ).astype(jnp.bfloat16)
    mixed_rows = jnp.dot(normed_one, attention_parts[2], preferred_element_type=jnp.float32)
    mixed_rows = mixed_rows + attention_parts[3].astype(jnp.float32)
    triple = mixed_rows.reshape(token_count, 3, HEADS, HEAD)
    queries = rotate(triple[:, 0], cos_table, sin_table).astype(jnp.bfloat16)
    keys_all = rotate(triple[:, 1], cos_table, sin_table).astype(jnp.bfloat16)
    values_all = triple[:, 2].astype(jnp.bfloat16)

    def masked_scores():
        raw_scores = (
            jnp.einsum("qhd,khd->hqk", queries, keys_all, preferred_element_type=jnp.float32)
            * score_scale
        )
        return jnp.where(allowed[None], raw_scores, -1e30)

    forward_scores = masked_scores()
    row_peak = jnp.max(forward_scores, axis=-1, keepdims=True)
    weights_raw = jnp.exp(forward_scores - row_peak)
    row_total = jnp.sum(weights_raw, axis=-1, keepdims=True)
    log_total = row_peak + jnp.log(row_total)
    probs_low = (weights_raw / row_total).astype(jnp.bfloat16)
    context = jnp.einsum("hqk,khd->qhd", probs_low, values_all, preferred_element_type=jnp.float32)
    context = context.reshape(token_count, feature_count).astype(jnp.bfloat16)
    attention_branch = jnp.dot(context, attention_parts[4], preferred_element_type=jnp.float32)
    attention_branch = attention_branch + attention_parts[5].astype(jnp.float32)
    normed_two = layer_norm(
        block_float, feed_parts[0].astype(jnp.float32), feed_parts[1].astype(jnp.float32)
    ).astype(jnp.bfloat16)
    hidden_pre = jnp.dot(normed_two, feed_parts[2], preferred_element_type=jnp.float32)
    hidden_pre = hidden_pre + feed_parts[3].astype(jnp.float32)
    hidden_act = jax.nn.gelu(hidden_pre, approximate=False).astype(jnp.bfloat16)
    feedforward_branch = jnp.dot(hidden_act, feed_parts[4], preferred_element_type=jnp.float32)
    feedforward_branch = feedforward_branch + feed_parts[5].astype(jnp.float32)
    block_out = (block_float + attention_branch + feedforward_branch).astype(jnp.bfloat16)
    feed_back = (
        lax.all_gather(second_gain, "fsdp", axis=0, tiled=True),
        lax.all_gather(second_shift, "fsdp", axis=0, tiled=True),
        lax.all_gather(expand_weight, "fsdp", axis=0, tiled=True),
        lax.all_gather(expand_bias, "fsdp", axis=0, tiled=True),
        lax.all_gather(shrink_weight, "fsdp", axis=0, tiled=True),
        lax.all_gather(shrink_bias, "fsdp", axis=0, tiled=True),
    )
    bias_sum = jnp.sum(cot_float, axis=0)
    shrink_grad = product_left(hidden_act, cotangent)
    grad_act = product_right(cotangent, feed_back[4])
    _, gelu_pull = jax.vjp(lambda pre_value: jax.nn.gelu(pre_value, approximate=False), hidden_pre)
    grad_pre = gelu_pull(grad_act)[0].astype(jnp.bfloat16)
    expand_grad = product_left(normed_two, grad_pre)
    expand_bias_grad = jnp.sum(grad_pre.astype(jnp.float32), axis=0)
    grad_normed_two = product_right(grad_pre, feed_back[2])
    part_two, second_gain_grad, second_shift_grad = norm_backward(
        block_float,
        feed_back[0].astype(jnp.float32),
        feed_back[1].astype(jnp.float32),
        grad_normed_two,
    )
    feed_grads = (
        lax.psum_scatter(second_gain_grad, "fsdp", scatter_dimension=0, tiled=True),
        lax.psum_scatter(second_shift_grad, "fsdp", scatter_dimension=0, tiled=True),
        lax.psum_scatter(expand_grad, "fsdp", scatter_dimension=0, tiled=True),
        lax.psum_scatter(expand_bias_grad, "fsdp", scatter_dimension=0, tiled=True),
        lax.psum_scatter(shrink_grad, "fsdp", scatter_dimension=0, tiled=True),
        lax.psum_scatter(bias_sum, "fsdp", scatter_dimension=0, tiled=True),
    )
    gain_two_sum, shift_two_sum, expand_sum, expand_bias_sum, shrink_sum, shrink_bias_sum = (
        feed_grads
    )
    attention_back = (
        lax.all_gather(first_gain, "fsdp", axis=0, tiled=True),
        lax.all_gather(first_shift, "fsdp", axis=0, tiled=True),
        lax.all_gather(mix_weight, "fsdp", axis=0, tiled=True),
        lax.all_gather(mix_bias, "fsdp", axis=0, tiled=True),
        lax.all_gather(dense_weight, "fsdp", axis=0, tiled=True),
        lax.all_gather(dense_bias, "fsdp", axis=0, tiled=True),
    )
    dense_grad = product_left(context, cotangent)
    grad_context = product_right(cotangent, attention_back[4]).astype(jnp.bfloat16)
    grad_context = grad_context.reshape(token_count, HEADS, HEAD)
    grad_values = jnp.einsum(
        "hqk,qhd->khd", probs_low, grad_context, preferred_element_type=jnp.float32
    )
    grad_probs = jnp.einsum(
        "qhd,khd->hqk", grad_context, values_all, preferred_element_type=jnp.float32
    )
    probs_exact = jnp.exp(masked_scores() - log_total)
    grad_scores = probs_exact * (
        grad_probs - jnp.sum(probs_exact * grad_probs, axis=-1, keepdims=True)
    )
    grad_scores = grad_scores.astype(jnp.bfloat16)
    grad_queries = (
        jnp.einsum("hqk,khd->qhd", grad_scores, keys_all, preferred_element_type=jnp.float32)
        * score_scale
    )
    grad_keys = (
        jnp.einsum("hqk,qhd->khd", grad_scores, queries, preferred_element_type=jnp.float32)
        * score_scale
    )
    _, rotate_pull = jax.vjp(lambda heads_in: rotate(heads_in, cos_table, sin_table), grad_queries)
    grad_mixed = jnp.stack(
        [rotate_pull(grad_queries)[0], rotate_pull(grad_keys)[0], grad_values], axis=1
    )
    grad_mixed = grad_mixed.reshape(token_count, 3 * feature_count).astype(jnp.bfloat16)
    mix_grad = product_left(normed_one, grad_mixed)
    mix_bias_grad = jnp.sum(grad_mixed.astype(jnp.float32), axis=0)
    grad_normed_one = product_right(grad_mixed, attention_back[2])
    part_one, first_gain_grad, first_shift_grad = norm_backward(
        block_float,
        attention_back[0].astype(jnp.float32),
        attention_back[1].astype(jnp.float32),
        grad_normed_one,
    )
    attention_grads = (
        lax.psum_scatter(first_gain_grad, "fsdp", scatter_dimension=0, tiled=True),
        lax.psum_scatter(first_shift_grad, "fsdp", scatter_dimension=0, tiled=True),
        lax.psum_scatter(mix_grad, "fsdp", scatter_dimension=0, tiled=True),
        lax.psum_scatter(mix_bias_grad, "fsdp", scatter_dimension=0, tiled=True),
        lax.psum_scatter(dense_grad, "fsdp", scatter_dimension=0, tiled=True),
        lax.psum_scatter(bias_sum, "fsdp", scatter_dimension=0, tiled=True),
    )
    gain_one_sum, shift_one_sum, mix_sum, mix_bias_sum, dense_sum, dense_bias_sum = attention_grads
    (
        gain_one_sum,
        shift_one_sum,
        mix_sum,
        mix_bias_sum,
        dense_sum,
        dense_bias_sum,
        gain_two_sum,
        shift_two_sum,
        expand_sum,
        expand_bias_sum,
        shrink_sum,
        shrink_bias_sum,
    ) = lax.psum(
        (
            gain_one_sum,
            shift_one_sum,
            mix_sum,
            mix_bias_sum,
            dense_sum,
            dense_bias_sum,
            gain_two_sum,
            shift_two_sum,
            expand_sum,
            expand_bias_sum,
            shrink_sum,
            shrink_bias_sum,
        ),
        "rep",
    )
    input_grad = cot_float + part_one + part_two
    return (
        block_out,
        input_grad,
        gain_one_sum,
        shift_one_sum,
        mix_sum,
        mix_bias_sum,
        dense_sum,
        dense_bias_sum,
        gain_two_sum,
        shift_two_sum,
        expand_sum,
        expand_bias_sum,
        shrink_sum,
        shrink_bias_sum,
    )


def solution(mesh):
    return jax.shard_map(
        local,
        mesh=mesh,
        in_specs=(
            P(("rep", "fsdp"), None),
            P(("rep", "fsdp"), None),
            P(("rep", "fsdp"), None),
            P("fsdp"),
            P("fsdp"),
            P("fsdp", None),
            P("fsdp"),
            P("fsdp", None),
            P("fsdp"),
            P("fsdp"),
            P("fsdp"),
            P("fsdp", None),
            P("fsdp"),
            P("fsdp", None),
            P("fsdp"),
        ),
        out_specs=(
            P(("rep", "fsdp"), None),
            P(("rep", "fsdp"), None),
            P("fsdp"),
            P("fsdp"),
            P("fsdp", None),
            P("fsdp"),
            P("fsdp", None),
            P("fsdp"),
            P("fsdp"),
            P("fsdp"),
            P("fsdp", None),
            P("fsdp"),
            P("fsdp", None),
            P("fsdp"),
        ),
        check_vma=False,
    )
```

profile of v0, /device:TPU:6, one launch (start us, length us, event | category | flops | bytes accessed | tf_op | source)
XLA Modules:
  0.0 1419.1 jit_solution(10603109605819763451)
XLA Ops:
  10.7 26.3 %all-gather.2 = bf16[8,1,384]{2,1,0:T(2,128)(2,1)S(1)} all-gather(bf16[1,1,384]{2,1,0:T(2,128)(2,1)S(1)} %reshape.200), channel_id=1, replica_groups=mesh['rep'=4,'fsdp'=8] {'fsdp'}, dimensions={0}, use_global_device_ids=true | all-gather | bytes 6912 | tf_op jit(solution)/shard_map/all_gather | solution.py:86
  37.1 16.9 %all-gather.1 = bf16[8,1,128]{2,1,0:T(2,128)(2,1)S(1)} all-gather(bf16[1,1,128]{2,1,0:T(2,128)(2,1)} %bitcast.99), channel_id=1, replica_groups=mesh['rep'=4,'fsdp'=8] {'fsdp'}, dimensions={0}, use_global_device_ids=true | all-gather | bytes 2304 | tf_op jit(solution)/shard_map/all_gather | solution.py:84
  54.0 19.1 %all-gather = bf16[8,1,128]{2,1,0:T(2,128)(2,1)S(1)} all-gather(bf16[1,1,128]{2,1,0:T(2,128)(2,1)} %bitcast.100), channel_id=1, replica_groups=mesh['rep'=4,'fsdp'=8] {'fsdp'}, dimensions={0}, use_global_device_ids=true | all-gather | bytes 2304 | tf_op jit(solution)/shard_map/all_gather | solution.py:83
  73.1 0.9 select_reduce_fusion
  74.0 1.2 convert_reduce_fusion.2
  75.2 1.3 fusion.29
  77.1 2.4 convolution_convert_fusion
  79.7 80.0 %all-gather.13.cloned.1.call-done = bf16[1024,3072]{1,0:T(8,128)(2,1)} async-done(((bf16[128,3072]{1,0:T(8,128)(2,1)}), bf16[1024,3072]{1,0:T(8,128)(2,1)}) %all-gather.13.cloned.1.call-update) | async-done | bytes 6291472 | tf_op jit(solution)/shard_map/all_gather | solution.py:85
  159.8 6.4 convolution_add_fusion.1
  166.1 3.5 copy.44
  169.7 1.8 slice_bitcast_fusion.1
  173.2 0.9 fusion.6
  174.2 1.3 multiply_reduce_fusion
  175.6 3.8 multiply_convert_fusion
  179.9 2.8 fusion.53
  183.0 2.7 fusion.18
  188.2 1.1 copy-done.3
  189.3 6.5 fusion.44
  196.5 24.8 %all-gather.6 = bf16[8,1,512]{2,1,0:T(2,128)(2,1)S(1)} all-gather(bf16[1,1,512]{2,1,0:T(2,128)(2,1)S(1)} %reshape.208), channel_id=1, replica_groups=mesh['rep'=4,'fsdp'=8] {'fsdp'}, dimensions={0}, use_global_device_ids=true | all-gather | bytes 9216 | tf_op jit(solution)/shard_map/all_gather | solution.py:94
  221.3 19.6 %all-gather.5 = bf16[8,1,128]{2,1,0:T(2,128)(2,1)S(1)} all-gather(bf16[1,1,128]{2,1,0:T(2,128)(2,1)S(1)} %bitcast.101), channel_id=1, replica_groups=mesh['rep'=4,'fsdp'=8] {'fsdp'}, dimensions={0}, use_global_device_ids=true | all-gather | bytes 2304 | tf_op jit(solution)/shard_map/all_gather | solution.py:92
  240.9 16.6 %all-gather.4 = bf16[8,1,128]{2,1,0:T(2,128)(2,1)S(1)} all-gather(bf16[1,1,128]{2,1,0:T(2,128)(2,1)S(1)} %bitcast.102), channel_id=1, replica_groups=mesh['rep'=4,'fsdp'=8] {'fsdp'}, dimensions={0}, use_global_device_ids=true | all-gather | bytes 2304 | tf_op jit(solution)/shard_map/all_gather | solution.py:91
  257.5 27.9 %all-gather.17.cloned.1.call-done = bf16[1024,4096]{1,0:T(8,128)(2,1)} async-done(((bf16[128,4096]{1,0:T(8,128)(2,1)}), bf16[1024,4096]{1,0:T(8,128)(2,1)}) %all-gather.17.cloned.1.call-update) | async-done | bytes 8388624 | tf_op jit(solution)/shard_map/all_gather | solution.py:93
  285.4 7.8 convolution_add_fusion
  293.2 117.3 %all-gather.19.cloned.1.call-done = bf16[4096,1024]{1,0:T(8,128)(2,1)} async-done(((bf16[512,1024]{1,0:T(8,128)(2,1)}), bf16[4096,1024]{1,0:T(8,128)(2,1)}) %all-gather.19.cloned.1.call-update) | async-done | bytes 8388624 | tf_op jit(solution)/shard_map/all_gather | solution.py:95
  410.5 15.8 %convert_reduce_fusion = (f32[4096]{0:T(1024)S(1)}, bf16[256,4096]{1,0:T(8,128)(2,1)S(1)}, f32[256,4096]{1,0:T(8,128)}) fusion(f32[256,4096]{1,0:T(8,128)} %convolution_add_fusion, bf16[256,1024]{1,0:T(8,128)(2,1)S(1)} %copy-done.8, bf16[4096,1024]{1,0:T(8,128)(2,1)} %all-gather.19.cloned.1.call-done), kind=kOutput, calls=%fused_computation.3 | convolution fusion | flops 2225074176 | bytes 19415040 | tf_op jit(solution)/shard_map/dot_general | solution.py:55
  426.3 1.3 copy-done.15
  427.7 8.3 fusion.41
  436.0 4.5 multiply_convert_fusion.1
  440.5 8.1 fusion.54
  448.7 7.5 all-reduce.18.cloned.1.call-start
  456.2 17.7 %all-gather.7 = bf16[8,1,128]{2,1,0:T(2,128)(2,1)S(1)} all-gather(bf16[1,1,128]{2,1,0:T(2,128)(2,1)S(1)} %bitcast.103), channel_id=1, replica_groups=mesh['rep'=4,'fsdp'=8] {'fsdp'}, dimensions={0}, use_global_device_ids=true | all-gather | bytes 2304 | tf_op jit(solution)/shard_map/all_gather | solution.py:96
  473.9 17.5 %all-gather.3 = bf16[8,1,128]{2,1,0:T(2,128)(2,1)S(1)} all-gather(bf16[1,1,128]{2,1,0:T(2,128)(2,1)S(1)} %bitcast.104), channel_id=1, replica_groups=mesh['rep'=4,'fsdp'=8] {'fsdp'}, dimensions={0}, use_global_device_ids=true | all-gather | bytes 2304 | tf_op jit(solution)/shard_map/all_gather | solution.py:88
  494.0 7.5 fusion.52
  501.4 210.7 %reduce-scatter.5.cloned.1.call-done = f32[128,3072]{1,0:T(8,128)} async-done(((f32[1024,3072]{1,0:T(8,128)}), f32[128,3072]{1,0:T(8,128)}) %reduce-scatter.5.cloned.1.call-update) | async-done | bytes 1572880 | tf_op jit(solution)/shard_map/reduce_scatter | solution.py:220
  712.1 285.6 %reduce-scatter.9.cloned.1.call-done = f32[128,4096]{1,0:T(8,128)} async-done(((f32[1024,4096]{1,0:T(8,128)}), f32[128,4096]{1,0:T(8,128)}) %reduce-scatter.9.cloned.1.call-update) | async-done | bytes 2097168 | tf_op jit(solution)/shard_map/reduce_scatter | solution.py:165
  997.7 285.2 %reduce-scatter.11.cloned.1.call-done = f32[512,1024]{1,0:T(8,128)} async-done(((f32[4096,1024]{1,0:T(8,128)}), f32[512,1024]{1,0:T(8,128)}) %reduce-scatter.11.cloned.1.call-update) | async-done | bytes 2097168 | tf_op jit(solution)/shard_map/reduce_scatter | solution.py:167
  1283.0 5.7 fusion.50
  1288.8 0.9 fusion.28
  1289.7 1.7 convert_reduce_fusion.3
  1291.4 31.3 %all-reduce.13 = (f32[1024]{0:T(1024)S(1)}, f32[1024]{0:T(1024)S(1)}, f32[3072]{0:T(1024)S(1)}, f32[1024]{0:T(1024)S(1)}, f32[1024]{0:T(1024)S(1)}, /*index=5*/f32[1024]{0:T(1024)S(1)}, f32[4096]{0:T(1024)S(1)}) all-reduce(f32[1024]{0:T(1024)S(1)} %get-tuple-element.23, ...), channel_id=2, replica_groups=mesh['rep'=4,'fsdp'=8] {'fsdp'}, use_global_device_ids=true, to_apply=%region_11.12.clone | all-reduce | flops 12288 | bytes 98304
  1323.2 7.4 all-reduce.14
  1330.7 5.9 convolution_add_fusion.3
  1336.6 1.6 fusion.21
  1338.2 66.3 %all-reduce.18.cloned.1.call-done = (f32[128,3072]{1,0:T(8,128)}, f32[128,1024]{1,0:T(8,128)}, f32[128,4096]{1,0:T(8,128)}, f32[512,1024]{1,0:T(8,128)}) async-done(((f32[128,3072]{1,0:T(8,128)}, f32[128,1024]{1,0:T(8,128)}, f32[128,4096]{1,0:T(8,128)}, f32[512,1024]{1,0:T(8,128)}), (f32[128,3072]{1,0:T(8,128)}, f32[128,1024]{1,0:T(8,128)}, f32[128,4096]{1,0:T(8,128)}, ...) | async-done | bytes 6291472 | tf_op jit(solution)/shard_map/psum | solution.py:239
  1405.0 2.9 copy.60
  1407.8 1.9 copy.61
  1409.7 1.3 copy.62
  1411.0 1.3 copy.63
  (136 shorter events, 11.7 us)
Async XLA Ops:
  7.2 69.5 %copy-start.28 = (s32[1,256]{1,0:T(1,128)S(1)}, s32[1,256]{1,0:T(1,128)}, u32[]{:S(2)}) copy-start(s32[1,256]{1,0:T(1,128)} %param.16) | copy-start | bytes 3076
  7.2 69.9 %copy-start.6 = (bf16[256,1024]{1,0:T(8,128)(2,1)S(1)}, bf16[256,1024]{1,0:T(8,128)(2,1)}, u32[]{:S(2)}) copy-start(bf16[256,1024]{1,0:T(8,128)(2,1)} %param.17) | copy-start | bytes 1572868
  7.2 69.9 %all-gather.15.cloned.1.call-start = ((), (), s32[]{:S(2)}) async-start(), calls=%async_computation.5 | async-start | bytes 2359296 | tf_op jit(solution)/shard_map/all_gather | solution.py:87
  7.9 151.8 %copy-start = (bf16[256,1024]{1,0:T(8,128)(2,1)S(1)}, bf16[256,1024]{1,0:T(8,128)(2,1)}, u32[]{:S(2)}) copy-start(bf16[256,1024]{1,0:T(8,128)(2,1)} %param.15) | copy-start | bytes 1572868
  7.9 151.8 %all-gather.13.cloned.1.call-start = ((), (), s32[]{:S(2)}) async-start(), calls=%async_computation.4 | async-start | bytes 7077888 | tf_op jit(solution)/shard_map/all_gather | solution.py:85
  8.7 276.7 %all-gather.17.cloned.1.call-start = ((), (), s32[]{:S(2)}) async-start(), calls=%async_computation.6 | async-start | bytes 9437184 | tf_op jit(solution)/shard_map/all_gather | solution.py:93
  9.4 401.1 %all-gather.19.cloned.1.call-start = ((), (), s32[]{:S(2)}) async-start(), calls=%async_computation.7 | async-start | bytes 9437184 | tf_op jit(solution)/shard_map/all_gather | solution.py:95
  10.0 491.4 %reduce-scatter.7.cloned.1.call-start = ((), (), s32[]{:S(2)}) async-start(), calls=%async_computation.9 | async-start | bytes 4718592 | tf_op jit(solution)/shard_map/reduce_scatter | solution.py:222
  76.5 0.6 copy-start.29
  76.7 94.9 %copy-start.24 = (f32[256,8]{0,1:T(8,128)}, f32[256,8]{0,1:T(8,128)S(1)}, u32[]{:S(2)}) copy-start(f32[256,8]{0,1:T(8,128)S(1)} %get-tuple-element.69) | copy-start | bytes 24580
  76.7 94.9 %copy-start.26 = (f32[256,8]{0,1:T(8,128)}, f32[256,8]{0,1:T(8,128)S(1)}, u32[]{:S(2)}) copy-start(f32[256,8]{0,1:T(8,128)S(1)} %get-tuple-element.70) | copy-start | bytes 24580
  77.1 97.0 %copy-start.17 = (pred[256,256]{0,1:T(8,128)(4,1)}, pred[256,256]{0,1:T(8,128)(4,1)S(1)}, u32[]{:S(2)}) copy-start(pred[256,256]{0,1:T(8,128)(4,1)S(1)} %compare_and_fusion.1) | copy-start | bytes 196612
  79.7 94.4 %copy-start.4 = (bf16[256,1024]{0,1:T(8,128)(2,1)}, bf16[256,1024]{0,1:T(8,128)(2,1)S(1)}, u32[]{:S(2)}) copy-start(bf16[256,1024]{0,1:T(8,128)(2,1)S(1)} %copy.46) | copy-start | bytes 1572868
  171.6 0.7 copy-start.16
  171.7 2.4 copy-start.18
  171.7 2.4 copy-start.20
  171.7 2.4 copy-start.22
  171.7 2.4 copy-start.23
  172.3 1.9 copy-start.2
  175.6 4.3 copy-start.7
  182.7 529.4 %reduce-scatter.5.cloned.1.call-start = ((), (), s32[]{:S(2)}) async-start(), calls=%async_computation.8 | async-start | bytes 14155776 | tf_op jit(solution)/shard_map/reduce_scatter | solution.py:220
  183.0 2.8 copy-start.1
  183.0 2.8 copy-start.19
  183.0 2.8 copy-start.21
  185.7 0.7 copy-start.25
  185.7 0.7 copy-start.27
  185.8 1.0 copy-start.5
  188.1 1.1 copy-start.3
  195.8 0.7 copy-start.31
  195.8 25.5 %copy-start.32 = (bf16[128]{0:T(256)(128)(2,1)S(1)}, bf16[128]{0:T(256)(128)(2,1)}, u32[]{:S(2)}) copy-start(bf16[128]{0:T(256)(128)(2,1)} %param.25) | copy-start | bytes 772
  195.8 45.1 %copy-start.33 = (bf16[128]{0:T(256)(128)(2,1)S(1)}, bf16[128]{0:T(256)(128)(2,1)}, u32[]{:S(2)}) copy-start(bf16[128]{0:T(256)(128)(2,1)} %param.24) | copy-start | bytes 772
  195.8 801.9 %reduce-scatter.9.cloned.1.call-start = ((), (), s32[]{:S(2)}) async-start(), calls=%async_computation.10 | async-start | bytes 18874368 | tf_op jit(solution)/shard_map/reduce_scatter | solution.py:165
  285.4 125.1 %copy-start.8 = (bf16[256,1024]{1,0:T(8,128)(2,1)S(1)}, bf16[256,1024]{1,0:T(8,128)(2,1)}, u32[]{:S(2)}) copy-start(bf16[256,1024]{1,0:T(8,128)(2,1)} %param.17) | copy-start | bytes 1572868
  426.3 1.3 copy-start.15
  436.0 847.0 %reduce-scatter.11.cloned.1.call-start = ((), (), s32[]{:S(2)}) async-start(), calls=%async_computation.11 | async-start | bytes 18874368 | tf_op jit(solution)/shard_map/reduce_scatter | solution.py:167
  436.0 4.5 copy-start.9
  448.6 7.5 copy-start.34
  448.7 25.2 %copy-start.35 = (bf16[128]{0:T(256)(128)(2,1)S(1)}, bf16[128]{0:T(256)(128)(2,1)}, u32[]{:S(2)}) copy-start(bf16[128]{0:T(256)(128)(2,1)} %param.23) | copy-start | bytes 772
  448.7 42.7 %copy-start.37 = (u32[32]{0:T(128)S(1)}, u32[32]{0:T(128)}, u32[]{:S(2)}) copy-start(u32[32]{0:T(128)} %constant.105) | copy-start | bytes 388
  448.7 955.8 %all-reduce.18.cloned.1.call-start = ((), (), s32[]{:S(2)}) async-start(), calls=%async_computation.12 | async-start | bytes 12582912 | tf_op jit(solution)/shard_map/psum | solution.py:239
  1283.0 5.8 copy-start.30
  1283.0 5.8 copy-start.11
  1283.0 6.7 copy-start.10
  1330.7 73.8 %copy-start.36 = (f32[128]{0:T(128)}, f32[128]{0:T(128)S(1)}, u32[]{:S(2)}) copy-start(f32[128]{0:T(128)S(1)} %get-tuple-element.113) | copy-start | bytes 1540
  1330.7 5.9 copy-start.12
  1404.5 5.3 copy-start.14
  1405.0 6.1 copy-start.13
Sparse Core Ops, SparseCore 0:
  10.2 49.8 all-gather.14
  62.2 97.5 all-gather.12
  161.9 123.4 all-gather.16
  287.4 123.1 all-gather.18
  414.0 87.1 reduce-scatter.6
  505.1 206.9 reduce-scatter.4
  716.4 281.3 reduce-scatter.8
  1001.5 281.3 reduce-scatter.10
  1285.7 118.6 all-reduce.17
where the time goes:
time: 1430 us; the launch traced here: 1420 us
  waiting for transfers between devices  1080 us (76%)
  blocking collectives  197 us (14%)
  matrix products  85.3 us (6%)
  local copies, waits for them, and re-layouts  20 us (1%)
  between operations  16.6 us (1%)
  other arithmetic  16.3 us (1%)
    reduce_scatter x1, waiting for transfers between devices, local(): lax.psum_scatter(expand_grad, 'fsdp', scatter_dimension=0, tiled=True)  286 us
    reduce_scatter x1, waiting for transfers between devices, local(): lax.psum_scatter(shrink_grad, 'fsdp', scatter_dimension=0, tiled=True)  285 us
    reduce_scatter x1, waiting for transfers between devices, local(): lax.psum_scatter(mix_grad, 'fsdp', scatter_dimension=0, tiled=True)  211 us
    all_gather x1, waiting for transfers between devices, local(): lax.all_gather(shrink_weight, 'fsdp', axis=0, tiled=True)  117 us
    all_gather x1, waiting for transfers between devices, local(): lax.all_gather(mix_weight, 'fsdp', axis=0, tiled=True)  80 us
    psum x1, waiting for transfers between devices, local(): lax.psum((gain_one_sum, shift_one_sum, mix_sum, mix_bias_sum, dense_sum,...  66.3 us
    dot_general x4, matrix products, product_right(): lax.dot_general(left, right, (((1,), (1,)), ((), ())), preferred_element_...  31.4 us
    unnamed x1, blocking collectives  31.3 us
  transfers between devices with their start and end apart: 9, of which 7 were waited for; matrix products, arithmetic and copies ran while one was open for 8% of the time, Pallas kernels for 0%

commit v1 on v0

--- a/solution.py
+++ b/solution.py
@@ -62,7 +62,7 @@
     return pullback(upstream)
 
 
-def local(
+def local_general(
     block_input,
     segments,
     cotangent,
@@ -272,9 +272,323 @@
     )
 
 
+TP_REP = 4
+TP_FSDP = 8
+
+
+def coordinates():
+    rep = lax.axis_index("rep")
+    shard = lax.axis_index("fsdp")
+    return rep // 2, rep % 2, shard // 4, (shard // 2) % 2, shard % 2
+
+
+def permute(value, target):
+    pairs = []
+    for rep in range(TP_REP):
+        for shard in range(TP_FSDP):
+            place = (rep // 2, rep % 2, shard // 4, (shard // 2) % 2, shard % 2)
+            goal = target(*place)
+            if goal is not None:
+                x, core, high, low, y = goal
+                pairs.append((rep * TP_FSDP + shard, (2 * x + core) * TP_FSDP + 4 * high + 2 * low + y))
+    return lax.ppermute(value, ("rep", "fsdp"), pairs)
+
+
+def swap_x(value):
+    return permute(value, lambda x, c, h, l, y: (1 - x, c, h, l, y))
+
+
+def swap_core(value):
+    return permute(value, lambda x, c, h, l, y: (x, 1 - c, h, l, y))
+
+
+def swap_high(value):
+    return permute(value, lambda x, c, h, l, y: (x, c, 1 - h, l, y))
+
+
+def swap_low(value):
+    return permute(value, lambda x, c, h, l, y: (x, c, h, 1 - l, y))
+
+
+def swap_y(value):
+    return permute(value, lambda x, c, h, l, y: (x, c, h, l, 1 - y))
+
+
+def swap_x_low(value):
+    return permute(value, lambda x, c, h, l, y: (1 - x, c, h, 1 - l, y))
+
+
+def shift_z(value, step):
+    def target(x, c, h, l, y):
+        moved = (2 * h + l + step) % 4
+        return (x, c, moved // 2, moved % 2, y)
+
+    return permute(value, target)
+
+
+def gather_sequences(own):
+    near = jnp.stack([own, swap_low(own), swap_x(own), swap_x_low(own)])
+    return jnp.concatenate([near, swap_core(near)])
+
+
+def scatter_sequences(blocks):
+    four = blocks[:4].astype(jnp.float32) + swap_core(blocks[4:]).astype(jnp.float32)
+    half = four[2:].astype(jnp.bfloat16)
+    two = four[:2] + swap_x(half).astype(jnp.float32)
+    return two[0] + swap_low(two[1].astype(jnp.bfloat16)).astype(jnp.float32)
+
+
+def pick(array, index, axis=0):
+    return lax.dynamic_index_in_dim(array, index, axis, keepdims=False)
+
+
+def gather_pieces(mine, other, place):
+    _, _, high, low, y = place
+    z = 2 * high + low
+    along = [mine, shift_z(other, 1), shift_z(mine, 2), shift_z(other, 3)]
+    across = [swap_y(along[0])] + list(swap_y(jnp.stack(along[1:])))
+    pieces = jnp.zeros((4, 2) + mine.shape, mine.dtype)
+    zeros = (0,) * mine.ndim
+    for step in range(4):
+        source = (z + 4 - step) % 4
+        pieces = lax.dynamic_update_slice(pieces, along[step][None, None], (source, y) + zeros)
+        pieces = lax.dynamic_update_slice(pieces, across[step][None, None], (source, 1 - y) + zeros)
+    return pieces.reshape((8,) + mine.shape)
+
+
+def reduce_pieces(partial, place):
+    _, _, high, _, y = place
+    cut = partial.reshape((2, 2, 2) + partial.shape[1:])
+    sent = swap_y(pick(cut, 1 - y, 2).astype(jnp.bfloat16))
+    total = pick(cut, y, 2).astype(jnp.float32) + sent.astype(jnp.float32)
+    sent = swap_high(pick(total, 1 - high).astype(jnp.bfloat16))
+    return pick(total, high) + sent.astype(jnp.float32)
+
+
+def ordered(first, second, bit):
+    return jnp.stack([jnp.where(bit == 0, first, second), jnp.where(bit == 0, second, first)])
+
+
+def share_slices(total, vectors, place):
+    x, core, _, low, _ = place
+    shape = total.shape[1:]
+    total = total.astype(jnp.bfloat16)
+    mine = pick(total, low)
+    got = swap_low(pick(total, 1 - low))
+    pair = ordered(mine, got, low)
+    got = swap_x(pair)
+    four = ordered(pair, got, x)
+    got = swap_core(four)
+    return ordered(four, got, core)
+
+
+def reduce_vectors(total, place):
+    _, _, _, low, _ = place
+    total = total.astype(jnp.bfloat16)
+    total = pick(total, low).astype(jnp.float32) + swap_low(pick(total, 1 - low)).astype(jnp.float32)
+    total = total.astype(jnp.bfloat16)
+    total = (total.astype(jnp.float32) + swap_x(total).astype(jnp.float32)).astype(jnp.bfloat16)
+    return total.astype(jnp.float32) + swap_core(total).astype(jnp.float32)
+
+
+def fetch_dense(dense_weight, place):
+    x, core, high, _, y = place
+    got = permute(dense_weight, lambda x, c, h, l, y: (x, c, h, l, 1 - y) if y == c else None)
+    held = jnp.where(y == core, dense_weight, got)
+    got = permute(held, lambda x, c, h, l, y: (x, c, 1 - h, l, y) if h == x else None)
+    return jnp.where(high == x, held, got)
+
+
+def return_dense(partial, place):
+    x, core, high, _, y = place
+    got = permute(partial.astype(jnp.bfloat16), lambda x, c, h, l, y: (x, c, h, l, 1 - y) if y != c else None)
+    total = partial + got.astype(jnp.float32)
+    got = permute(total.astype(jnp.bfloat16), lambda x, c, h, l, y: (x, c, 1 - h, l, y) if h != x else None)
+    total = (total + got.astype(jnp.float32)).astype(jnp.bfloat16)
+    got = permute(total, lambda x, c, h, l, y: (1 - x, c, h, l, y) if h == x else None)
+    total = jnp.where(high == x, total, got)
+    got = permute(total, lambda x, c, h, l, y: (x, 1 - c, h, l, y) if y == c else None)
+    return jnp.where(y == core, total, got)
+
+
+def local(
+    block_input,
+    segments,
+    cotangent,
+    first_gain,
+    first_shift,
+    mix_weight,
+    mix_bias,
+    dense_weight,
+    dense_bias,
+    second_gain,
+    second_shift,
+    expand_weight,
+    expand_bias,
+    shrink_weight,
+    shrink_bias,
+):
+    f32, bf16 = jnp.float32, jnp.bfloat16
+    place = coordinates()
+    x, core, high, low, y = place
+    rank = 4 * x + 2 * low + core
+    mate = rank ^ 2
+    tokens, width = block_input.shape
+    rows = mix_weight.shape[0]
+    group = 8
+
+    marks = jnp.pad(segments.astype(bf16), ((0, 15), (0, width - tokens)))
+    near_all = gather_sequences(jnp.concatenate([block_input, marks]))
+    cot_all = gather_sequences(cotangent)
+
+    small = jnp.concatenate(
+        [first_gain, first_shift, second_gain, second_shift, dense_bias, shrink_bias, mix_bias, expand_bias]
+    )
+    small = jnp.pad(small, (0, 16 * 384 - small.shape[0])).reshape(16, 384)
+    mix_cut = mix_weight.reshape(rows, 3, group, 128)
+
+    def mix_slice(which):
+        return jnp.concatenate([pick(mix_cut, which, 2).reshape(rows, 384), small])
+
+    mix_pieces = gather_pieces(mix_slice(rank), mix_slice(mate), place)
+    expand_cut = expand_weight.reshape(rows, group, group, 64)
+    expand_pieces = gather_pieces(
+        pick(expand_cut, rank, 2).reshape(rows, 512), pick(expand_cut, mate, 2).reshape(rows, 512), place
+    )
+    shrink_cut = shrink_weight.reshape(group, 64, width)
+    shrink_pieces = gather_pieces(pick(shrink_cut, rank), pick(shrink_cut, mate), place)
+    dense = fetch_dense(dense_weight, place)
+
+    mix = mix_pieces[:, :rows].reshape(width, 384)
+    smalls = mix_pieces[:, rows:].reshape(8, 16 * 384).astype(f32)
+    parts, start = [], 0
+    for size in (rows,) * 6 + (mix_bias.shape[0], expand_bias.shape[0]):
+        parts.append(smalls[:, start : start + size].reshape(-1))
+        start += size
+    gain_one, shift_one, gain_two, shift_two, dense_bias_all, shrink_bias_all, mix_bias_all, expand_bias_all = parts
+    mix_bias_own = pick(mix_bias_all.reshape(3, group, 128), rank, 1)
+    expand_bias_own = pick(expand_bias_all.reshape(group, group, 64), rank, 1).reshape(512)
+    expand = expand_pieces.reshape(width, 512)
+    shrink = shrink_pieces.reshape(512, width)
+
+    inputs = near_all[:, :tokens].astype(f32)
+    segs = near_all[:, tokens, :tokens].astype(jnp.int32)
+    average = jnp.mean(inputs, axis=-1, keepdims=True)
+    centred = inputs - average
+    scale = lax.rsqrt(jnp.mean(centred * centred, axis=-1, keepdims=True) + EPSILON)
+    normed = (centred * scale).reshape(group * tokens, width)
+    normed_one = (normed * gain_one + shift_one).astype(bf16)
+    normed_two = (normed * gain_two + shift_two).astype(bf16)
+
+    score_scale = HEAD ** (-0.5)
+    cos_table, sin_table, allowed = jax.vmap(rotary_tables)(segs)
+    mixed = jnp.dot(normed_one, mix, preferred_element_type=f32) + mix_bias_own.reshape(384)
+    triple = mixed.reshape(group, tokens, 3, 2, HEAD)
+    queries = rotate(triple[:, :, 0], cos_table, sin_table).astype(bf16)
+    keys_all = rotate(triple[:, :, 1], cos_table, sin_table).astype(bf16)
+    values_all = triple[:, :, 2].astype(bf16)
+    scores = jnp.einsum("sqhd,skhd->shqk", queries, keys_all, preferred_element_type=f32) * score_scale
+    scores = jnp.where(allowed[:, None], scores, -1e30)
+    weights_raw = jnp.exp(scores - jnp.max(scores, axis=-1, keepdims=True))
+    probs = weights_raw / jnp.sum(weights_raw, axis=-1, keepdims=True)
+    probs_low = probs.astype(bf16)
+    context = jnp.einsum("shqk,skhd->sqhd", probs_low, values_all, preferred_element_type=f32)
+    context = context.reshape(group * tokens, 128).astype(bf16)
+
+    hidden_pre = jnp.dot(normed_two, expand, preferred_element_type=f32) + expand_bias_own
+    hidden_act = jax.nn.gelu(hidden_pre, approximate=False).astype(bf16)
+    branch = jnp.dot(context, dense, preferred_element_type=f32)
+    branch = branch + jnp.dot(hidden_act, shrink, preferred_element_type=f32)
+    branch = scatter_sequences(branch.astype(bf16).reshape(group, tokens, width))
+    block_out = block_input.astype(f32) + branch + (dense_bias_all + shrink_bias_all)
+    block_out = block_out.astype(bf16)
+
+    cots = cot_all.reshape(group * tokens, width)
+    shrink_grad = product_left(hidden_act, cots)
+    shrink_total = reduce_pieces(shrink_grad.reshape(8, 64, width), place)
+    grad_act = product_right(cots, shrink)
+    _, gelu_pull = jax.vjp(lambda pre_value: jax.nn.gelu(pre_value, approximate=False), hidden_pre)
+    grad_pre = gelu_pull(grad_act)[0].astype(bf16)
+    expand_grad = product_left(normed_two, grad_pre)
+    expand_total = reduce_pieces(expand_grad.reshape(8, rows, 512), place)
+    expand_bias_grad = jnp.sum(grad_pre.astype(f32), axis=0)
+    error_two = product_right(grad_pre, expand)
+
+    dense_grad = return_dense(product_left(context, cots), place)
+    grad_context = product_right(cots, dense).astype(bf16).reshape(group, tokens, 2, HEAD)
+    grad_values = jnp.einsum("shqk,sqhd->skhd", probs_low, grad_context, preferred_element_type=f32)
+    grad_probs = jnp.einsum("sqhd,skhd->shqk", grad_context, values_all, preferred_element_type=f32)
+    grad_scores = probs * (grad_probs - jnp.sum(probs * grad_probs, axis=-1, keepdims=True))
+    grad_scores = grad_scores.astype(bf16)
+    grad_queries = jnp.einsum("shqk,skhd->sqhd", grad_scores, keys_all, preferred_element_type=f32) * score_scale
+    grad_keys = jnp.einsum("shqk,sqhd->skhd", grad_scores, queries, preferred_element_type=f32) * score_scale
+    grad_mixed = jnp.stack(
+        [rotate(grad_queries, cos_table, -sin_table), rotate(grad_keys, cos_table, -sin_table), grad_values], axis=2
+    )
+    grad_mixed = grad_mixed.reshape(group * tokens, 384).astype(bf16)
+    mix_grad = product_left(normed_one, grad_mixed)
+    mix_bias_grad = jnp.sum(grad_mixed.astype(f32), axis=0)
+    error_one = product_right(grad_mixed, mix)
+
+    upstream = (error_one * gain_one + error_two * gain_two).astype(bf16)
+    upstream = scatter_sequences(upstream.reshape(group, tokens, width))
+    own = normed[:tokens]
+    pulled = upstream - jnp.mean(upstream, axis=-1, keepdims=True)
+    pulled = pulled - own * jnp.mean(upstream * own, axis=-1, keepdims=True)
+    input_grad = cotangent.astype(f32) + scale[0] * pulled
+
+    spread_mix = jnp.zeros((3, group, 128), f32)
+    spread_mix = lax.dynamic_update_slice(spread_mix, mix_bias_grad.reshape(3, 1, 128), (0, rank, 0))
+    spread_expand = jnp.zeros((group, group, 64), f32)
+    spread_expand = lax.dynamic_update_slice(spread_expand, expand_bias_grad.reshape(group, 1, 64), (0, rank, 0))
+    vectors = jnp.concatenate(
+        [
+            jnp.sum(error_one * normed, axis=0).reshape(8, -1),
+            jnp.sum(error_one, axis=0).reshape(8, -1),
+            jnp.sum(error_two * normed, axis=0).reshape(8, -1),
+            jnp.sum(error_two, axis=0).reshape(8, -1),
+            jnp.sum(cotangent.astype(f32), axis=0).reshape(8, -1),
+            spread_mix.reshape(8, -1),
+            spread_expand.reshape(8, -1),
+        ],
+        axis=1,
+    )
+    vectors = vectors.reshape(8, -1, 128)
+    mix_total = reduce_pieces(mix_grad.reshape(8, rows, 384), place)
+    vector_total = reduce_vectors(reduce_pieces(vectors, place), place).reshape(-1)
+    shards, start = [], 0
+    for size in (rows,) * 5 + (mix_bias.shape[0], expand_bias.shape[0]):
+        shards.append(vector_total[start : start + size])
+        start += size
+    gain_one_grad, shift_one_grad, gain_two_grad, shift_two_grad, cot_sum, mix_bias_sum, expand_bias_sum = shards
+
+    shrink_out = share_slices(shrink_total, None, place).transpose(1, 2, 0, 3, 4).reshape(512, width)
+    expand_out = share_slices(expand_total, None, place).reshape(2, 2, 2, rows, group, 64)
+    expand_out = expand_out.transpose(3, 4, 1, 2, 0, 5).reshape(rows, 4096)
+    mix_out = share_slices(mix_total, None, place).reshape(2, 2, 2, rows, 3, 128)
+    mix_out = mix_out.transpose(3, 4, 1, 2, 0, 5).reshape(rows, 3072)
+    return (
+        block_out,
+        input_grad,
+        gain_one_grad,
+        shift_one_grad,
+        mix_out.astype(f32),
+        mix_bias_sum,
+        dense_grad.astype(f32),
+        cot_sum,
+        gain_two_grad,
+        shift_two_grad,
+        expand_out.astype(f32),
+        expand_bias_sum,
+        shrink_out.astype(f32),
+        cot_sum,
+    )
+
+
 def solution(mesh):
+    tensor_parallel = mesh.shape["rep"] == TP_REP and mesh.shape["fsdp"] == TP_FSDP
     return jax.shard_map(
-        local,
+        local if tensor_parallel else local_general,
         mesh=mesh,
         in_specs=(
             P(("rep", "fsdp"), None),

time: 1430 us -> 454 us (0.32)
  waiting for transfers between devices: 1080 us -> 76.5 us
  blocking collectives: 197 us -> 0 us
  local copies, waits for them, and re-layouts: 20 us -> 138 us
  starting transfers between devices: 8.04 us -> 80.8 us
  other arithmetic: 16.3 us -> 69.5 us
    reduce_scatter x4 -> x0, waiting for transfers between devices: 782 us -> none  [the longest x1 286 us: local(): lax.psum_scatter(expand_grad, 'fsdp', scatter_dimension=0, tiled=True)]
    all_gather x4 -> x0, waiting for transfers between devices: 225 us -> none  [the longest x1 117 us: local(): lax.all_gather(shrink_weight, 'fsdp', axis=0, tiled=True)]
    all_gather x8 -> x0, blocking collectives: 159 us -> none  [the longest x1 26.3 us: local(): lax.all_gather(mix_bias, 'fsdp', axis=0, tiled=True)]
    ppermute x0 -> x55, starting transfers between devices: none -> 80.8 us  [permute(): return lax.ppermute(value, ('rep', 'fsdp'), pairs)]
    ppermute x0 -> x55, waiting for transfers between devices: none -> 76.5 us  [permute(): return lax.ppermute(value, ('rep', 'fsdp'), pairs)]
    psum x1 -> x0, waiting for transfers between devices: 66.3 us -> none  [local(): lax.psum((gain_one_sum, shift_one_sum, mix_sum, mix_bias_sum, dense_sum,...]
    unnamed x1 -> x0, blocking collectives: 31.3 us -> none
    unnamed x91 -> x150, local copies, waits for them, and re-layouts: 14.1 us -> 41.4 us
  transfers between devices with their start and end apart: 9 -> 55, of which waited for: 7 -> 20; matrix products, arithmetic and copies ran while one was open for 8% -> 45% of each run, Pallas kernels for 0% -> 0%
where the time goes in v1:
time: 454 us; the launch traced here: 446 us
  local copies, waits for them, and re-layouts  138 us (30%)
  starting transfers between devices  80.8 us (18%)
  matrix products  78.7 us (17%)
  waiting for transfers between devices  76.5 us (17%)
  other arithmetic  69.5 us (15%)
    ppermute x55, starting transfers between devices, permute(): return lax.ppermute(value, ('rep', 'fsdp'), pairs)  80.8 us
    ppermute x55, waiting for transfers between devices, permute(): return lax.ppermute(value, ('rep', 'fsdp'), pairs)  76.5 us
    unnamed x150, local copies, waits for them, and re-layouts  41.4 us
    dot_general x4, matrix products, product_right(): lax.dot_general(left, right, (((1,), (1,)), ((), ())), preferred_element_...  33.6 us
    dot_general x4, matrix products, product_left(): lax.dot_general(left, right, (((0,), (0,)), ((), ())), preferred_element_...  14.2 us
    dot_general x1, matrix products, local(): jnp.dot(normed_two, expand, preferred_element_type=f32) + expand_bias_own  13 us
    dot_general x2, local copies, waits for them, and re-layouts, product_left(): lax.dot_general(left, right, (((0,), (0,)), ((), ())), preferred_element_...  13 us
    dynamic_update_slice x13, local copies, waits for them, and re-layouts, gather_pieces(): lax.dynamic_update_slice(pieces, across[step][None, None], (source, 1 - y...  12.8 us
  transfers between devices with their start and end apart: 55, of which 20 were waited for; matrix products, arithmetic and copies ran while one was open for 45% of the time, Pallas kernels for 0%

profile of v1, /device:TPU:6, one launch (start us, length us, event | category | flops | bytes accessed | tf_op | source)
XLA Modules:
  0.0 446.2 jit_solution(13868603256047669033)
XLA Ops:
  2.5 3.6 collective-permute-start.19
  15.4 3.8 collective-permute-start.7
  32.2 2.4 collective-permute-start.18
  47.5 2.7 collective-permute-start.13
  61.9 3.0 collective-permute-start.26
  76.4 4.6 %collective-permute-done.8 = bf16[3,144,384]{2,1,0:T(8,128)(2,1)} collective-permute-done((bf16[3,144,384]{2,1,0:T(8,128)(2,1)}, bf16[3,144,384]{2,1,0:T(8,128)(2,1)}, u32[]{:S(2)}, u32[]{:S(2)}) %collective-permute-start.8) | collective-permute-done | bytes 331808 | tf_op jit(solution)/shard_map/ppermute | solution.py:294
  105.9 2.9 pad_maximum_fusion.1
  113.8 4.8 %collective-permute-done = bf16[272,1024]{1,0:T(8,128)(2,1)S(1)} collective-permute-done((bf16[272,1024]{1,0:T(8,128)(2,1)}, bf16[272,1024]{1,0:T(8,128)(2,1)S(1)}, u32[]{:S(2)}, u32[]{:S(2)}) %collective-permute-start) | collective-permute-done | bytes 557088 | tf_op jit(solution)/shard_map/ppermute | solution.py:294
  119.6 2.9 pad_maximum_fusion
  139.9 3.2 constant_dynamic-update-slice_fusion
  143.9 2.8 convert_reduce_fusion
  146.7 3.0 fusion.3
  149.8 7.6 %fusion.1 = (f32[8,256,1024]{2,1,0:T(8,128)}, bf16[8,256,1024]{2,1,0:T(8,128)(2,1)S(1)}, bf16[8,256,1024]{2,1,0:T(8,128)(2,1)}) fusion(f32[8,256]{1,0:T(8,128)S(1)} %add_rsqrt_fusion, f32[8,256]{1,0:T(8,128)S(1)} %broadcast_multiply_fusion, bf16[8,272,1024]{2,1,0:T(8,128)(2,1)} %constant_dynamic-update-slice_fusion, f32[1024]{0:T(1024)S(1)} %get-tuple-element.121, ...), kind=kLoop, calls=%fused_computation.3 | loop fusion | flops 18874368 | bytes 21004288 | tf_op jit(solution)/shard_map/mul | solution.py:479
  157.4 2.4 convolution_add_fusion
  159.8 5.4 %reshape.327 = f32[8,256,3,2,64]{4,3,2,1,0:T(2,128)} reshape(f32[2048,384]{1,0:T(8,128)S(1)} %convolution_add_fusion) | data formatting | bytes 6291456 | tf_op jit(solution)/shard_map/reshape | solution.py:486
  165.2 2.3 slice.250
  167.5 3.9 fusion.104
  175.1 2.7 copy.175
  184.0 4.7 %fusion.107 = (f32[8,2,256]{2,1,0:T(2,128)S(1)}, f32[8,2,256,256]{2,3,1,0:T(8,128)}) fusion(pred[8,256,256]{1,2,0:T(8,128)(4,1)} %compare_and_fusion.1, bf16[8,256,2,48]{1,3,2,0:T(8,128)(2,1)S(1)} %slice.373, bf16[8,256,2,8]{1,3,2,0:T(8,128)(2,1)S(1)} %get-tuple-element.125, bf16[8,256,2,8]{1,3,2,0:T(8,128)(2,1)S(1)} %get-tuple-element.126, ...), kind=kOutput, calls=%fused_computation.321 | convolution fusion | flops 141558016 | bytes 5783552 | tf_op jit(solution)/shard_map/sub | solution.py:492
  188.7 3.1 fusion.47
  196.8 13.0 %fusion.13 = (bf16[512,2048]{1,0:T(8,128)(2,1)S(1)}, f32[2048,512]{0,1:T(8,128)S(1)}) fusion(f32[512]{0:T(512)S(1)} %add.396, bf16[2048,1024]{1,0:T(8,128)(2,1)S(1)} %bitcast.451, bf16[1024,512]{1,0:T(8,128)(2,1)} %bitcast.44), kind=kOutput, calls=%fused_computation.25 | convolution fusion | flops 2216689664 | bytes 11536384 | tf_op jit(solution)/shard_map/dot_general | solution.py:498
  209.8 2.3 fusion.110
  216.4 3.2 collective-permute-start.41
  219.6 12.2 %convert_reduce_fusion.1 = (f32[512]{0:T(512)S(1)}, bf16[2048,512]{0,1:T(8,128)(2,1)S(1)}, f32[2048,512]{0,1:T(8,128)S(1)}) fusion(f32[2048,512]{0,1:T(8,128)S(1)} %get-tuple-element.144, f32[512]{0:T(512)S(1)} %add.396, bf16[2048,1024]{1,0:T(8,128)(2,1)S(1)} %bitcast.447, bf16[512,1024]{1,0:T(8,128)(2,1)S(1)} %bitcast.453), kind=kOutput, calls=%fused_computation.45 | convolution fusion | flops 2226126336 | bytes 15732736 | tf_op jit(solution)/shard_map/dot_general | solution.py:55
  231.8 2.9 fusion.34
  241.1 7.6 %fusion.109 = f32[2048,1024]{1,0:T(8,128)} fusion(bf16[2048,512]{0,1:T(8,128)(2,1)S(1)} %get-tuple-element.63, bf16[1024,512]{1,0:T(8,128)(2,1)} %bitcast.44), kind=kOutput, calls=%fused_computation.323 | convolution fusion | flops 2147483648 | bytes 11534336 | tf_op jit(solution)/shard_map/dot_general | solution.py:55
  248.7 11.6 %fusion.102 = (f32[1024]{0:T(1024)S(1)}, f32[1024]{0:T(1024)S(1)}, f32[1024]{0:T(1024)S(1)}, f32[1024]{0:T(1024)S(1)}, bf16[2048,1024]{1,0:T(8,128)(2,1)}, /*ind...) fusion(f32[2048,1024]{1,0:T(8,128)} %fusion.109, f32[8,256,1024]{2,1,0:T(8,128)S(1)} %bitcast.438, ...), kind=kOutput, calls=%fused_computation.317 | convolution fusion | flops 1644163072 | bytes 31752192 | tf_op jit(solution)/shard_map/dot_general | solution.py:55
  260.9 6.5 %copy.167 = bf16[1024,2048]{1,0:T(8,128)(2,1)} copy(bf16[1024,2048]{0,1:T(8,128)(2,1)} %bitcast.456) | data formatting | bytes 8388608 | tf_op jit(solution)/shard_map/dot_general | solution.py:49
  267.4 5.2 %fusion.35 = f32[2,2,2,128,512]{4,3,2,1,0:T(8,128)S(1)} fusion(bf16[2,2,2,128,2048]{4,3,2,1,0:T(8,128)(2,1)} %bitcast.457, bf16[2048,512]{0,1:T(8,128)(2,1)} %copy-done.56), kind=kOutput, calls=%fused_computation.80 | convolution fusion | flops 2147483648 | bytes 8388608 | tf_op jit(solution)/shard_map/dot_general | solution.py:49
  275.8 6.5 %copy.165 = bf16[1024,2048]{1,0:T(8,128)(2,1)} copy(bf16[1024,2048]{0,1:T(8,128)(2,1)} %bitcast.455) | data formatting | bytes 8388608 | tf_op jit(solution)/shard_map/dot_general | solution.py:49
  282.3 5.2 %fusion.42 = f32[2,2,2,128,384]{4,3,2,1,0:T(8,128)S(1)} fusion(bf16[2,2,2,128,2048]{4,3,2,1,0:T(8,128)(2,1)} %bitcast.458, bf16[2048,384]{0,1:T(8,128)(2,1)} %bitcast.473), kind=kOutput, calls=%fused_computation.91 | convolution fusion | flops 1610612736 | bytes 7340032 | tf_op jit(solution)/shard_map/dot_general | solution.py:49
  290.4 2.4 fusion.105
  295.6 4.9 %collective-permute-done.36 = bf16[2,2,128,384]{3,2,1,0:T(8,128)(2,1)} collective-permute-done((bf16[2,2,128,384]{3,2,1,0:T(8,128)(2,1)}, bf16[2,2,128,384]{3,2,1,0:T(8,128)(2,1)}, u32[]{:S(2)}, u32[]{:S(2)}) %collective-permute-start.36) | collective-permute-done | bytes 393248 | tf_op jit(solution)/shard_map/ppermute | solution.py:294
  304.8 3.7 collective-permute-done.42
  308.6 3.4 collective-permute-start.51
  314.9 14.9 %collective-permute-start.38 = (bf16[128,384]{1,0:T(8,128)(2,1)S(1)}, bf16[128,384]{1,0:T(8,128)(2,1)S(1)}, u32[]{:S(2)}, u32[]{:S(2)}) collective-permute-start(bf16[128,384]{1,0:T(8,128)(2,1)S(1)} %dynamic-slice_bitcast_fusion.4), channel_id=1, source_target_pairs={{0,2},{1,3},{2,0},{3,1},{4,6},{5,7},{6,4},{7,5},{8,10},{9,11},{10,... | collective-permute-start | bytes 294920 | tf_op jit(solution)/shard_map/ppermute | solution.py:294
  329.8 2.6 collective-permute-done.38
  332.4 4.0 collective-permute-start.46
  339.2 9.3 %collective-permute-done.46 = bf16[2,128,512]{2,1,0:T(8,128)(2,1)S(1)} collective-permute-done((bf16[2,128,512]{2,1,0:T(8,128)(2,1)S(1)}, bf16[2,128,512]{2,1,0:T(8,128)(2,1)S(1)}, u32[]{:S(2)}, u32[]{:S(2)}) %collective-permute-start.46) | collective-permute-done | bytes 262176 | tf_op jit(solution)/shard_map/ppermute | solution.py:294
  352.0 4.4 collective-permute-done.47
  359.7 6.1 %collective-permute-done.53 = bf16[2,64,1024]{2,1,0:T(8,128)(2,1)S(1)} collective-permute-done((bf16[2,64,1024]{2,1,0:T(8,128)(2,1)S(1)}, bf16[2,64,1024]{2,1,0:T(8,128)(2,1)S(1)}, u32[]{:S(2)}, u32[]{:S(2)}) %collective-permute-start.53) | collective-permute-done | bytes 262176 | tf_op jit(solution)/shard_map/ppermute | solution.py:294
  380.8 3.0 copy.155
  385.9 8.6 %collective-permute-done.29 = bf16[2,256,1024]{2,1,0:T(8,128)(2,1)} collective-permute-done((bf16[2,256,1024]{2,1,0:T(8,128)(2,1)}, bf16[2,256,1024]{2,1,0:T(8,128)(2,1)}, u32[]{:S(2)}, u32[]{:S(2)}) %collective-permute-start.29) | collective-permute-done | bytes 1048608 | tf_op jit(solution)/shard_map/ppermute | solution.py:294
  398.7 2.5 convert_add_fusion.1
  403.8 4.9 %collective-permute-done.30 = bf16[256,1024]{1,0:T(8,128)(2,1)S(1)} collective-permute-done((bf16[256,1024]{1,0:T(8,128)(2,1)S(1)}, bf16[256,1024]{1,0:T(8,128)(2,1)S(1)}, u32[]{:S(2)}, u32[]{:S(2)}) %collective-permute-start.30) | collective-permute-done | bytes 524320 | tf_op jit(solution)/shard_map/ppermute | solution.py:294
  410.2 2.6 convert_reduce_fusion.3
  417.7 8.2 %collective-permute-done.22 = bf16[2,256,1024]{2,1,0:T(8,128)(2,1)} collective-permute-done((bf16[2,256,1024]{2,1,0:T(8,128)(2,1)}, bf16[2,256,1024]{2,1,0:T(8,128)(2,1)}, u32[]{:S(2)}, u32[]{:S(2)}) %collective-permute-start.22) | collective-permute-done | bytes 1048608 | tf_op jit(solution)/shard_map/ppermute | solution.py:294
  435.5 6.0 %collective-permute-done.23 = bf16[256,1024]{1,0:T(8,128)(2,1)S(1)} collective-permute-done((bf16[256,1024]{1,0:T(8,128)(2,1)}, bf16[256,1024]{1,0:T(8,128)(2,1)S(1)}, u32[]{:S(2)}, u32[]{:S(2)}) %collective-permute-start.23) | collective-permute-done | bytes 524320 | tf_op jit(solution)/shard_map/ppermute | solution.py:294
  (414 shorter events, 204.2 us)
Async XLA Ops:
  2.5 51.0 %collective-permute-start.19 = (bf16[64,1024]{1,0:T(8,128)(2,1)}, bf16[64,1024]{1,0:T(8,128)(2,1)}, u32[]{:S(2)}, u32[]{:S(2)}) collective-permute-start(bf16[64,1024]{1,0:T(8,128)(2,1)} %get-tuple-element.93), channel_id=1, source_target_pairs={{0,6},{1,7},{2,0},{3,1},{4,2},{5,3},{6,4},{7,5},{8,14},{9,15},{10,... | collective-permute-start | bytes 393224 | tf_op jit(solution)/shard_map/ppermute | solution.py:294
  6.1 45.0 %collective-permute-start.17 = (bf16[64,1024]{1,0:T(8,128)(2,1)}, bf16[64,1024]{1,0:T(8,128)(2,1)}, u32[]{:S(2)}, u32[]{:S(2)}) collective-permute-start(bf16[64,1024]{1,0:T(8,128)(2,1)} %get-tuple-element.93), channel_id=1, source_target_pairs={{0,2},{1,3},{2,4},{3,5},{4,6},{5,7},{6,0},{7,1},{8,10},{9,11},{10,... | collective-permute-start | bytes 393224 | tf_op jit(solution)/shard_map/ppermute | solution.py:294
  15.4 16.8 %collective-permute-start.7 = (bf16[144,384]{0,1:T(8,128)(2,1)}, bf16[144,384]{0,1:T(8,128)(2,1)}, u32[]{:S(2)}, u32[]{:S(2)}) collective-permute-start(bf16[144,384]{0,1:T(8,128)(2,1)} %get-tuple-element.127), channel_id=1, source_target_pairs={{0,6},{1,7},{2,0},{3,1},{4,2},{5,3},{6,4},{7,5},{8,14},{9,15},{10,... | collective-permute-start | bytes 331784 | tf_op jit(solution)/shard_map/ppermute | solution.py:294
  19.2 19.2 %collective-permute-start.5 = (bf16[144,384]{0,1:T(8,128)(2,1)}, bf16[144,384]{0,1:T(8,128)(2,1)S(1)}, u32[]{:S(2)}, u32[]{:S(2)}) collective-permute-start(bf16[144,384]{0,1:T(8,128)(2,1)} %get-tuple-element.127), channel_id=1, source_target_pairs={{0,2},{1,3},{2,4},{3,5},{4,6},{5,7},{6,0},{7,1},{8,10},{9,11},{10,... | collective-permute-start | bytes 331784 | tf_op jit(solution)/shard_map/ppermute | solution.py:294
  19.2 17.0 %collective-permute-start.6 = (bf16[144,384]{0,1:T(8,128)(2,1)}, bf16[144,384]{0,1:T(8,128)(2,1)}, u32[]{:S(2)}, u32[]{:S(2)}) collective-permute-start(bf16[144,384]{0,1:T(8,128)(2,1)} %get-tuple-element.128), channel_id=1, source_target_pairs={{0,4},{1,5},{2,6},{3,7},{4,0},{5,1},{6,2},{7,3},{8,12},{9,13},{10,... | collective-permute-start | bytes 331784 | tf_op jit(solution)/shard_map/ppermute | solution.py:294
  32.2 21.5 %collective-permute-start.18 = (bf16[64,1024]{1,0:T(8,128)(2,1)}, bf16[64,1024]{1,0:T(8,128)(2,1)S(1)}, u32[]{:S(2)}, u32[]{:S(2)}) collective-permute-start(bf16[64,1024]{1,0:T(8,128)(2,1)} %get-tuple-element.94), channel_id=1, source_target_pairs={{0,4},{1,5},{2,6},{3,7},{4,0},{5,1},{6,2},{7,3},{8,12},{9,13},{10,... | collective-permute-start | bytes 393224 | tf_op jit(solution)/shard_map/ppermute | solution.py:294
  36.2 11.3 %collective-permute-start.16 = (bf16[64,1024]{1,0:T(8,128)(2,1)}, bf16[64,1024]{1,0:T(8,128)(2,1)}, u32[]{:S(2)}, u32[]{:S(2)}) collective-permute-start(bf16[64,1024]{1,0:T(8,128)(2,1)} %get-tuple-element.94), channel_id=1, source_target_pairs={{0,1},{1,0},{2,3},{3,2},{4,5},{5,4},{6,7},{7,6},{8,9},{9,8},{10,11... | collective-permute-start | bytes 393224 | tf_op jit(solution)/shard_map/ppermute | solution.py:294
  45.1 57.6 %collective-permute-start.24 = (bf16[256,1024]{1,0:T(8,128)(2,1)S(1)}, bf16[256,1024]{1,0:T(8,128)(2,1)}, u32[]{:S(2)}, u32[]{:S(2)}) collective-permute-start(bf16[256,1024]{1,0:T(8,128)(2,1)S(1)} %copy-done.9), channel_id=1, source_target_pairs={{0,2},{1,3},{2,0},{3,1},{4,6},{5,7},{6,4},{7,5},{8,10},{9,11},{10,... | collective-permute-start | bytes 1572872 | tf_op jit(solution)/shard_map/ppermute | solution.py:294
  47.5 14.3 %collective-permute-start.13 = (bf16[128,512]{0,1:T(8,128)(2,1)}, bf16[128,512]{0,1:T(8,128)(2,1)S(1)}, u32[]{:S(2)}, u32[]{:S(2)}) collective-permute-start(bf16[128,512]{0,1:T(8,128)(2,1)} %bitcast.484), channel_id=1, source_target_pairs={{0,4},{1,5},{2,6},{3,7},{4,0},{5,1},{6,2},{7,3},{8,12},{9,13},{10,... | collective-permute-start | bytes 393224 | tf_op jit(solution)/shard_map/ppermute | solution.py:294
  53.6 12.0 %collective-permute-start.14 = (bf16[128,512]{0,1:T(8,128)(2,1)}, bf16[128,512]{0,1:T(8,128)(2,1)S(1)}, u32[]{:S(2)}, u32[]{:S(2)}) collective-permute-start(bf16[128,512]{0,1:T(8,128)(2,1)} %bitcast.499), channel_id=1, source_target_pairs={{0,6},{1,7},{2,0},{3,1},{4,2},{5,3},{6,4},{7,5},{8,14},{9,15},{10,... | collective-permute-start | bytes 393224 | tf_op jit(solution)/shard_map/ppermute | solution.py:294
  53.7 16.3 %collective-permute-start.12 = (bf16[128,512]{0,1:T(8,128)(2,1)}, bf16[128,512]{0,1:T(8,128)(2,1)}, u32[]{:S(2)}, u32[]{:S(2)}) collective-permute-start(bf16[128,512]{0,1:T(8,128)(2,1)} %bitcast.500), channel_id=1, source_target_pairs={{0,2},{1,3},{2,4},{3,5},{4,6},{5,7},{6,0},{7,1},{8,10},{9,11},{10,... | collective-permute-start | bytes 393224 | tf_op jit(solution)/shard_map/ppermute | solution.py:294
  57.4 17.4 %collective-permute-start.9 = (bf16[128,1024]{1,0:T(8,128)(2,1)}, bf16[128,1024]{1,0:T(8,128)(2,1)}, u32[]{:S(2)}, u32[]{:S(2)}) collective-permute-start(bf16[128,1024]{1,0:T(8,128)(2,1)} %param.22), channel_id=1, source_target_pairs={{0,1},{2,3},{4,5},{6,7},{9,8},{11,10},{13,12},{15,14},{16,17},{18,... | collective-permute-start | bytes 786440 | tf_op jit(solution)/shard_map/ppermute | solution.py:294
  61.9 40.9 %collective-permute-start.26 = (bf16[256,1024]{1,0:T(8,128)(2,1)S(1)}, bf16[256,1024]{1,0:T(8,128)(2,1)}, u32[]{:S(2)}, u32[]{:S(2)}) collective-permute-start(bf16[256,1024]{1,0:T(8,128)(2,1)S(1)} %copy-done.9), channel_id=1, source_target_pairs={{0,18},{1,19},{2,16},{3,17},{4,22},{5,23},{6,20},{7,21},{8,26},{9,... | collective-permute-start | bytes 1572872 | tf_op jit(solution)/shard_map/ppermute | solution.py:294
  65.6 38.6 %collective-permute-start.25 = (bf16[256,1024]{1,0:T(8,128)(2,1)S(1)}, bf16[256,1024]{1,0:T(8,128)(2,1)}, u32[]{:S(2)}, u32[]{:S(2)}) collective-permute-start(bf16[256,1024]{1,0:T(8,128)(2,1)S(1)} %copy-done.9), channel_id=1, source_target_pairs={{0,16},{1,17},{2,18},{3,19},{4,20},{5,21},{6,22},{7,23},{8,24},{9,... | collective-permute-start | bytes 1572872 | tf_op jit(solution)/shard_map/ppermute | solution.py:294
  70.0 10.9 %collective-permute-start.8 = (bf16[3,144,384]{2,1,0:T(8,128)(2,1)}, bf16[3,144,384]{2,1,0:T(8,128)(2,1)}, u32[]{:S(2)}, u32[]{:S(2)}) collective-permute-start(bf16[3,144,384]{2,1,0:T(8,128)(2,1)} %copy.115), channel_id=1, source_target_pairs={{0,1},{1,0},{2,3},{3,2},{4,5},{5,4},{6,7},{7,6},{8,9},{9,8},{10,11... | collective-permute-start | bytes 995336 | tf_op jit(solution)/shard_map/ppermute | solution.py:294
  74.9 38.9 %collective-permute-start.1 = (bf16[272,1024]{1,0:T(8,128)(2,1)}, bf16[272,1024]{1,0:T(8,128)(2,1)}, u32[]{:S(2)}, u32[]{:S(2)}) collective-permute-start(bf16[272,1024]{1,0:T(8,128)(2,1)} %get-tuple-element.100), channel_id=1, source_target_pairs={{0,16},{1,17},{2,18},{3,19},{4,20},{5,21},{6,22},{7,23},{8,24},{9,... | collective-permute-start | bytes 1671176 | tf_op jit(solution)/shard_map/ppermute | solution.py:294
  80.9 17.6 %collective-permute-start.15 = (bf16[3,128,512]{1,2,0:T(8,128)(2,1)}, bf16[3,128,512]{1,2,0:T(8,128)(2,1)}, u32[]{:S(2)}, u32[]{:S(2)}) collective-permute-start(bf16[3,128,512]{1,2,0:T(8,128)(2,1)} %pad_maximum_fusion.8), channel_id=1, source_target_pairs={{0,1},{1,0},{2,3},{3,2},{4,5},{5,4},{6,7},{7,6},{8,9},{9,8},{10,11... | collective-permute-start | bytes 1179656 | tf_op jit(solution)/shard_map/ppermute | solution.py:294
  98.6 10.3 %collective-permute-start.20 = (bf16[3,64,1024]{2,1,0:T(8,128)(2,1)}, bf16[3,64,1024]{2,1,0:T(8,128)(2,1)}, u32[]{:S(2)}, u32[]{:S(2)}) collective-permute-start(bf16[3,64,1024]{2,1,0:T(8,128)(2,1)} %pad_maximum_fusion.9), channel_id=1, source_target_pairs={{0,1},{1,0},{2,3},{3,2},{4,5},{5,4},{6,7},{7,6},{8,9},{9,8},{10,11... | collective-permute-start | bytes 1179656 | tf_op jit(solution)/shard_map/ppermute | solution.py:294
  102.7 15.9 %collective-permute-start = (bf16[272,1024]{1,0:T(8,128)(2,1)}, bf16[272,1024]{1,0:T(8,128)(2,1)S(1)}, u32[]{:S(2)}, u32[]{:S(2)}) collective-permute-start(bf16[272,1024]{1,0:T(8,128)(2,1)} %get-tuple-element.100), channel_id=1, source_target_pairs={{0,2},{1,3},{2,0},{3,1},{4,6},{5,7},{6,4},{7,5},{8,10},{9,11},{10,... | collective-permute-start | bytes 1671176 | tf_op jit(solution)/shard_map/ppermute | solution.py:294
  102.7 16.9 %collective-permute-start.2 = (bf16[272,1024]{1,0:T(8,128)(2,1)}, bf16[272,1024]{1,0:T(8,128)(2,1)}, u32[]{:S(2)}, u32[]{:S(2)}) collective-permute-start(bf16[272,1024]{1,0:T(8,128)(2,1)} %get-tuple-element.100), channel_id=1, source_target_pairs={{0,18},{1,19},{2,16},{3,17},{4,22},{5,23},{6,20},{7,21},{8,26},{9,... | collective-permute-start | bytes 1671176 | tf_op jit(solution)/shard_map/ppermute | solution.py:294
  104.1 29.4 %collective-permute-start.10 = (bf16[128,1024]{1,0:T(8,128)(2,1)S(1)}, bf16[128,1024]{1,0:T(8,128)(2,1)}, u32[]{:S(2)}, u32[]{:S(2)}) collective-permute-start(bf16[128,1024]{1,0:T(8,128)(2,1)S(1)} %broadcast_select_fusion.4), channel_id=1, source_target_pairs={{0,4},{1,5},{2,6},{3,7},{8,12},{9,13},{10,14},{11,15},{20,16},{21,... | collective-permute-start | bytes 786440 | tf_op jit(solution)/shard_map/ppermute | solution.py:294
  108.8 22.9 %collective-permute-start.27 = (bf16[4,256,1024]{2,1,0:T(8,128)(2,1)}, bf16[4,256,1024]{2,1,0:T(8,128)(2,1)}, u32[]{:S(2)}, u32[]{:S(2)}) collective-permute-start(bf16[4,256,1024]{2,1,0:T(8,128)(2,1)} %pad_maximum_fusion.1), channel_id=1, source_target_pairs={{0,8},{1,9},{2,10},{3,11},{4,12},{5,13},{6,14},{7,15},{8,0},{9,1},... | collective-permute-start | bytes 6291464 | tf_op jit(solution)/shard_map/ppermute | solution.py:294
  122.5 17.4 %collective-permute-start.3 = (bf16[4,272,1024]{2,1,0:T(8,128)(2,1)}, bf16[4,272,1024]{2,1,0:T(8,128)(2,1)}, u32[]{:S(2)}, u32[]{:S(2)}) collective-permute-start(bf16[4,272,1024]{2,1,0:T(8,128)(2,1)} %pad_maximum_fusion), channel_id=1, source_target_pairs={{0,8},{1,9},{2,10},{3,11},{4,12},{5,13},{6,14},{7,15},{8,0},{9,1},... | collective-permute-start | bytes 6684680 | tf_op jit(solution)/shard_map/ppermute | solution.py:294
  213.4 89.8 %collective-permute-start.50 = (bf16[2,2,64,1024]{3,2,1,0:T(8,128)(2,1)S(1)}, bf16[2,2,64,1024]{3,2,1,0:T(8,128)(2,1)}, u32[]{:S(2)}, u32[]{:S(2)}) collective-permute-start(bf16[2,2,64,1024]{3,2,1,0:T(8,128)(2,1)S(1)} %fusion.58), channel_id=1, source_target_pairs={{0,1},{1,0},{2,3},{3,2},{4,5},{5,4},{6,7},{7,6},{8,9},{9,8},{10,11... | collective-permute-start | bytes 1572872 | tf_op jit(solution)/shard_map/ppermute | solution.py:294
  216.4 79.1 %collective-permute-start.41 = (bf16[128,1024]{1,0:T(8,128)(2,1)}, bf16[128,1024]{1,0:T(8,128)(2,1)S(1)}, u32[]{:S(2)}, u32[]{:S(2)}) collective-permute-start(bf16[128,1024]{1,0:T(8,128)(2,1)} %get-tuple-element.141), channel_id=1, source_target_pairs={{1,0},{3,2},{5,4},{7,6},{8,9},{10,11},{12,13},{14,15},{17,16},{19,... | collective-permute-start | bytes 786440 | tf_op jit(solution)/shard_map/ppermute | solution.py:294
  238.8 159.9 %collective-permute-start.21 = (bf16[4,256,1024]{2,1,0:T(8,128)(2,1)}, bf16[4,256,1024]{2,1,0:T(8,128)(2,1)}, u32[]{:S(2)}, u32[]{:S(2)}) collective-permute-start(bf16[4,256,1024]{2,1,0:T(8,128)(2,1)} %bitcast.61), channel_id=1, source_target_pairs={{0,8},{1,9},{2,10},{3,11},{4,12},{5,13},{6,14},{7,15},{8,0},{9,1},... | collective-permute-start | bytes 6291464 | tf_op jit(solution)/shard_map/ppermute | solution.py:294
  274.8 37.3 %collective-permute-start.45 = (bf16[2,2,128,512]{3,2,1,0:T(8,128)(2,1)}, bf16[2,2,128,512]{3,2,1,0:T(8,128)(2,1)}, u32[]{:S(2)}, u32[]{:S(2)}) collective-permute-start(bf16[2,2,128,512]{3,2,1,0:T(8,128)(2,1)} %fusion.57), channel_id=1, source_target_pairs={{0,1},{1,0},{2,3},{3,2},{4,5},{5,4},{6,7},{7,6},{8,9},{9,8},{10,11... | collective-permute-start | bytes 1572872 | tf_op jit(solution)/shard_map/ppermute | solution.py:294
  289.4 11.1 %collective-permute-start.36 = (bf16[2,2,128,384]{3,2,1,0:T(8,128)(2,1)}, bf16[2,2,128,384]{3,2,1,0:T(8,128)(2,1)}, u32[]{:S(2)}, u32[]{:S(2)}) collective-permute-start(bf16[2,2,128,384]{3,2,1,0:T(8,128)(2,1)} %fusion.66), channel_id=1, source_target_pairs={{0,1},{1,0},{2,3},{3,2},{4,5},{5,4},{6,7},{7,6},{8,9},{9,8},{10,11... | collective-permute-start | bytes 1179656 | tf_op jit(solution)/shard_map/ppermute | solution.py:294
  295.5 70.3 %collective-permute-start.28 = (bf16[4,256,1024]{2,1,0:T(8,128)(2,1)}, bf16[4,256,1024]{2,1,0:T(8,128)(2,1)S(1)}, u32[]{:S(2)}, u32[]{:S(2)}) collective-permute-start(bf16[4,256,1024]{2,1,0:T(8,128)(2,1)} %bitcast.470), channel_id=1, source_target_pairs={{0,8},{1,9},{2,10},{3,11},{4,12},{5,13},{6,14},{7,15},{8,0},{9,1},... | collective-permute-start | bytes 6291464 | tf_op jit(solution)/shard_map/ppermute | solution.py:294
  303.2 11.6 %collective-permute-start.37 = (bf16[2,128,384]{2,1,0:T(8,128)(2,1)S(1)}, bf16[2,128,384]{2,1,0:T(8,128)(2,1)S(1)}, u32[]{:S(2)}, u32[]{:S(2)}) collective-permute-start(bf16[2,128,384]{2,1,0:T(8,128)(2,1)S(1)} %fusion.76), channel_id=1, source_target_pairs={{0,4},{1,5},{2,6},{3,7},{4,0},{5,1},{6,2},{7,3},{8,12},{9,13},{10,... | collective-permute-start | bytes 589832 | tf_op jit(solution)/shard_map/ppermute | solution.py:294
  308.6 27.9 %collective-permute-start.51 = (bf16[2,64,1024]{2,1,0:T(8,128)(2,1)S(1)}, bf16[2,64,1024]{2,1,0:T(8,128)(2,1)S(1)}, u32[]{:S(2)}, u32[]{:S(2)}) collective-permute-start(bf16[2,64,1024]{2,1,0:T(8,128)(2,1)S(1)} %fusion.73), channel_id=1, source_target_pairs={{0,4},{1,5},{2,6},{3,7},{4,0},{5,1},{6,2},{7,3},{8,12},{9,13},{10,... | collective-permute-start | bytes 786440 | tf_op jit(solution)/shard_map/ppermute | solution.py:294
  312.1 25.2 %collective-permute-start.43 = (bf16[128,1024]{1,0:T(8,128)(2,1)S(1)}, bf16[128,1024]{1,0:T(8,128)(2,1)S(1)}, u32[]{:S(2)}, u32[]{:S(2)}) collective-permute-start(bf16[128,1024]{1,0:T(8,128)(2,1)S(1)} %add_convert_fusion.5), channel_id=1, source_target_pairs={{0,16},{1,17},{2,18},{3,19},{8,24},{9,25},{10,26},{11,27},{20,4},{... | collective-permute-start | bytes 786440 | tf_op jit(solution)/shard_map/ppermute | solution.py:294
  314.9 17.5 %collective-permute-start.38 = (bf16[128,384]{1,0:T(8,128)(2,1)S(1)}, bf16[128,384]{1,0:T(8,128)(2,1)S(1)}, u32[]{:S(2)}, u32[]{:S(2)}) collective-permute-start(bf16[128,384]{1,0:T(8,128)(2,1)S(1)} %dynamic-slice_bitcast_fusion.4), channel_id=1, source_target_pairs={{0,2},{1,3},{2,0},{3,1},{4,6},{5,7},{6,4},{7,5},{8,10},{9,11},{10,... | collective-permute-start | bytes 294920 | tf_op jit(solution)/shard_map/ppermute | solution.py:294
  332.4 16.1 %collective-permute-start.46 = (bf16[2,128,512]{2,1,0:T(8,128)(2,1)S(1)}, bf16[2,128,512]{2,1,0:T(8,128)(2,1)S(1)}, u32[]{:S(2)}, u32[]{:S(2)}) collective-permute-start(bf16[2,128,512]{2,1,0:T(8,128)(2,1)S(1)} %fusion.72), channel_id=1, source_target_pairs={{0,4},{1,5},{2,6},{3,7},{4,0},{5,1},{6,2},{7,3},{8,12},{9,13},{10,... | collective-permute-start | bytes 786440 | tf_op jit(solution)/shard_map/ppermute | solution.py:294
  336.4 13.7 %collective-permute-start.39 = (bf16[2,128,384]{2,1,0:T(8,128)(2,1)S(1)}, bf16[2,128,384]{2,1,0:T(8,128)(2,1)S(1)}, u32[]{:S(2)}, u32[]{:S(2)}) collective-permute-start(bf16[2,128,384]{2,1,0:T(8,128)(2,1)S(1)} %pad_maximum_fusion.15), channel_id=1, source_target_pairs={{0,16},{1,17},{2,18},{3,19},{4,20},{5,21},{6,22},{7,23},{8,24},{9,... | collective-permute-start | bytes 589832 | tf_op jit(solution)/shard_map/ppermute | solution.py:294
  337.3 13.7 %collective-permute-start.52 = (bf16[64,1024]{1,0:T(8,128)(2,1)S(1)}, bf16[64,1024]{1,0:T(8,128)(2,1)S(1)}, u32[]{:S(2)}, u32[]{:S(2)}) collective-permute-start(bf16[64,1024]{1,0:T(8,128)(2,1)S(1)} %dynamic-slice_bitcast_fusion), channel_id=1, source_target_pairs={{0,2},{1,3},{2,0},{3,1},{4,6},{5,7},{6,4},{7,5},{8,10},{9,11},{10,... | collective-permute-start | bytes 393224 | tf_op jit(solution)/shard_map/ppermute | solution.py:294
  348.5 10.3 %collective-permute-start.44 = (bf16[128,1024]{1,0:T(8,128)(2,1)S(1)}, bf16[128,1024]{1,0:T(8,128)(2,1)S(1)}, u32[]{:S(2)}, u32[]{:S(2)}) collective-permute-start(bf16[128,1024]{1,0:T(8,128)(2,1)S(1)} %broadcast_select_fusion.5), channel_id=1, source_target_pairs={{0,8},{2,10},{4,12},{6,14},{9,1},{11,3},{13,5},{15,7},{16,24},{18,... | collective-permute-start | bytes 786440 | tf_op jit(solution)/shard_map/ppermute | solution.py:294
  351.0 23.3 %collective-permute-start.40 = (bf16[2,2,128,384]{3,2,1,0:T(8,128)(2,1)S(1)}, bf16[2,2,128,384]{3,2,1,0:T(8,128)(2,1)S(1)}, u32[]{:S(2)}, u32[]{:S(2)}) collective-permute-start(bf16[2,2,128,384]{3,2,1,0:T(8,128)(2,1)S(1)} %pad_maximum_fusion.10), channel_id=1, source_target_pairs={{0,8},{1,9},{2,10},{3,11},{4,12},{5,13},{6,14},{7,15},{8,0},{9,1},... | collective-permute-start | bytes 1179656 | tf_op jit(solution)/shard_map/ppermute | solution.py:294
  356.4 9.4 %collective-permute-start.53 = (bf16[2,64,1024]{2,1,0:T(8,128)(2,1)S(1)}, bf16[2,64,1024]{2,1,0:T(8,128)(2,1)S(1)}, u32[]{:S(2)}, u32[]{:S(2)}) collective-permute-start(bf16[2,64,1024]{2,1,0:T(8,128)(2,1)S(1)} %pad_maximum_fusion.12), channel_id=1, source_target_pairs={{0,16},{1,17},{2,18},{3,19},{4,20},{5,21},{6,22},{7,23},{8,24},{9,... | collective-permute-start | bytes 786440 | tf_op jit(solution)/shard_map/ppermute | solution.py:294
  358.8 14.1 %collective-permute-start.48 = (bf16[2,128,512]{2,1,0:T(8,128)(2,1)S(1)}, bf16[2,128,512]{2,1,0:T(8,128)(2,1)S(1)}, u32[]{:S(2)}, u32[]{:S(2)}) collective-permute-start(bf16[2,128,512]{2,1,0:T(8,128)(2,1)S(1)} %pad_maximum_fusion.11), channel_id=1, source_target_pairs={{0,16},{1,17},{2,18},{3,19},{4,20},{5,21},{6,22},{7,23},{8,24},{9,... | collective-permute-start | bytes 786440 | tf_op jit(solution)/shard_map/ppermute | solution.py:294
  370.0 24.5 %collective-permute-start.29 = (bf16[2,256,1024]{2,1,0:T(8,128)(2,1)}, bf16[2,256,1024]{2,1,0:T(8,128)(2,1)}, u32[]{:S(2)}, u32[]{:S(2)}) collective-permute-start(bf16[2,256,1024]{2,1,0:T(8,128)(2,1)} %slice.369), channel_id=1, source_target_pairs={{0,16},{1,17},{2,18},{3,19},{4,20},{5,21},{6,22},{7,23},{8,24},{9,... | collective-permute-start | bytes 3145736 | tf_op jit(solution)/shard_map/ppermute | solution.py:294
  372.9 10.9 %collective-permute-start.54 = (bf16[2,2,64,1024]{3,2,1,0:T(8,128)(2,1)}, bf16[2,2,64,1024]{3,2,1,0:T(8,128)(2,1)}, u32[]{:S(2)}, u32[]{:S(2)}) collective-permute-start(bf16[2,2,64,1024]{3,2,1,0:T(8,128)(2,1)} %pad_maximum_fusion.7), channel_id=1, source_target_pairs={{0,8},{1,9},{2,10},{3,11},{4,12},{5,13},{6,14},{7,15},{8,0},{9,1},... | collective-permute-start | bytes 1572872 | tf_op jit(solution)/shard_map/ppermute | solution.py:294
  373.8 23.0 %collective-permute-start.49 = (bf16[2,2,128,512]{3,2,1,0:T(8,128)(2,1)}, bf16[2,2,128,512]{3,2,1,0:T(8,128)(2,1)}, u32[]{:S(2)}, u32[]{:S(2)}) collective-permute-start(bf16[2,2,128,512]{3,2,1,0:T(8,128)(2,1)} %pad_maximum_fusion.6), channel_id=1, source_target_pairs={{0,8},{1,9},{2,10},{3,11},{4,12},{5,13},{6,14},{7,15},{8,0},{9,1},... | collective-permute-start | bytes 1572872 | tf_op jit(solution)/shard_map/ppermute | solution.py:294
  396.7 12.0 %collective-permute-start.30 = (bf16[256,1024]{1,0:T(8,128)(2,1)S(1)}, bf16[256,1024]{1,0:T(8,128)(2,1)S(1)}, u32[]{:S(2)}, u32[]{:S(2)}) collective-permute-start(bf16[256,1024]{1,0:T(8,128)(2,1)S(1)} %fusion.60), channel_id=1, source_target_pairs={{0,2},{1,3},{2,0},{3,1},{4,6},{5,7},{6,4},{7,5},{8,10},{9,11},{10,... | collective-permute-start | bytes 1572872 | tf_op jit(solution)/shard_map/ppermute | solution.py:294
  402.4 23.5 %collective-permute-start.22 = (bf16[2,256,1024]{2,1,0:T(8,128)(2,1)}, bf16[2,256,1024]{2,1,0:T(8,128)(2,1)}, u32[]{:S(2)}, u32[]{:S(2)}) collective-permute-start(bf16[2,256,1024]{2,1,0:T(8,128)(2,1)} %slice.370), channel_id=1, source_target_pairs={{0,16},{1,17},{2,18},{3,19},{4,20},{5,21},{6,22},{7,23},{8,24},{9,... | collective-permute-start | bytes 3145736 | tf_op jit(solution)/shard_map/ppermute | solution.py:294
  416.7 11.3 %collective-permute-start.32 = (bf16[2,12,128]{2,1,0:T(8,128)(2,1)S(1)}, bf16[2,12,128]{2,1,0:T(8,128)(2,1)S(1)}, u32[]{:S(2)}, u32[]{:S(2)}) collective-permute-start(bf16[2,12,128]{2,1,0:T(8,128)(2,1)S(1)} %fusion.91), channel_id=1, source_target_pairs={{0,4},{1,5},{2,6},{3,7},{4,0},{5,1},{6,2},{7,3},{8,12},{9,13},{10,... | collective-permute-start | bytes 18440 | tf_op jit(solution)/shard_map/ppermute | solution.py:294
  430.8 10.7 %collective-permute-start.23 = (bf16[256,1024]{1,0:T(8,128)(2,1)}, bf16[256,1024]{1,0:T(8,128)(2,1)S(1)}, u32[]{:S(2)}, u32[]{:S(2)}) collective-permute-start(bf16[256,1024]{1,0:T(8,128)(2,1)} %fusion.59), channel_id=1, source_target_pairs={{0,2},{1,3},{2,0},{3,1},{4,6},{5,7},{6,4},{7,5},{8,10},{9,11},{10,... | collective-permute-start | bytes 1572872 | tf_op jit(solution)/shard_map/ppermute | solution.py:294
  435.5 8.2 %collective-permute-start.35 = (bf16[12,128]{1,0:T(8,128)(2,1)S(1)}, bf16[12,128]{1,0:T(8,128)(2,1)S(1)}, u32[]{:S(2)}, u32[]{:S(2)}) collective-permute-start(bf16[12,128]{1,0:T(8,128)(2,1)S(1)} %add_convert_fusion.10), channel_id=1, source_target_pairs={{0,8},{1,9},{2,10},{3,11},{4,12},{5,13},{6,14},{7,15},{8,0},{9,1},... | collective-permute-start | bytes 9224 | tf_op jit(solution)/shard_map/ppermute | solution.py:294
  (67 other events, 663.3 us)

commit v2 on v0

--- a/solution.py
+++ b/solution.py
@@ -1,6 +1,9 @@
 import jax
 import jax.numpy as jnp
+import numpy as np
 from jax import lax
+from jax.experimental import pallas as pl
+from jax.experimental.pallas import tpu as pltpu
 from jax.sharding import PartitionSpec as P
 
 HEADS = 16
@@ -62,7 +65,7 @@
     return pullback(upstream)
 
 
-def local(
+def local_general(
     block_input,
     segments,
     cotangent,
@@ -272,9 +275,788 @@
     )
 
 
+TP_REP = 4
+TP_FSDP = 8
+GROUP = 8
+NEAR = (0, 2, 4, 6)
+MIX_COLS = 384
+HIDDEN = 512
+SMALL = 16
+LANES = 128
+FIRST_ROWS = MIX_COLS + SMALL + HIDDEN
+MIX_ROWS = MIX_COLS + SMALL
+FEED_ROWS = 2 * HIDDEN
+F32 = jnp.float32
+BF16 = jnp.bfloat16
+VMEM_LIMIT = 56 * 1024 * 1024
+
+
+def permute(value, target):
+    pairs = []
+    for rep in range(TP_REP):
+        for shard in range(TP_FSDP):
+            goal = target(rep // 2, rep % 2, shard // 4, (shard // 2) % 2, shard % 2)
+            if goal is not None:
+                x, core, high, low, y = goal
+                pairs.append((rep * TP_FSDP + shard, (2 * x + core) * TP_FSDP + 4 * high + 2 * low + y))
+    return lax.ppermute(value, ("rep", "fsdp"), pairs)
+
+
+def swap(value, x=0, core=0, high=0, low=0, y=0):
+    return permute(value, lambda a, b, c, d, e: (a ^ x, b ^ core, c ^ high, d ^ low, e ^ y))
+
+
+def nt(left, right):
+    return lax.dot_general(left, right, (((1,), (1,)), ((), ())), preferred_element_type=F32)
+
+
+def nn(left, right):
+    return lax.dot_general(left, right, (((1,), (0,)), ((), ())), preferred_element_type=F32)
+
+
+def tn(left, right):
+    return lax.dot_general(left, right, (((0,), (0,)), ((), ())), preferred_element_type=F32)
+
+
+def whole(shape):
+    return pl.BlockSpec(shape, lambda *_: (0,) * len(shape))
+
+
+def call(body, info, operands, in_specs, outs, out_specs, grid=(1,), scratch=(), aliases=None, micros=4):
+    return pl.pallas_call(
+        body,
+        grid_spec=pltpu.PrefetchScalarGridSpec(
+            num_scalar_prefetch=1,
+            grid=grid,
+            in_specs=in_specs,
+            out_specs=out_specs,
+            scratch_shapes=list(scratch),
+        ),
+        out_shape=[jax.ShapeDtypeStruct(shape, dtype) for shape, dtype in outs],
+        input_output_aliases=aliases or {},
+        compiler_params=pltpu.CompilerParams(vmem_limit_bytes=VMEM_LIMIT),
+        cost_estimate=pl.CostEstimate(flops=micros * 10**9, bytes_accessed=micros * 3 * 10**6, transcendentals=0),
+    )(info, *operands)
+
+
+def as_columns(matrix):
+    size = matrix.shape[1]
+    rows = lax.broadcasted_iota(jnp.int32, (size, size), 0)
+    cols = lax.broadcasted_iota(jnp.int32, (size, size), 1)
+    return nt((rows == cols).astype(BF16), matrix)
+
+
+def aligned(index, unit):
+    return pl.ds(pl.multiple_of(index * unit, unit), unit)
+
+
+def cut_body(info, mix, expand, shrink, dense, cot, *rest):
+    vectors, (own, other, own_last, other_last, other_shrink), small = rest[:8], rest[8:13], rest[13]
+    row = 0
+    small[...] = jnp.zeros_like(small)
+    for vector in vectors:
+        count = vector.shape[0]
+        small[row : row + count, :] = vector[...].astype(F32)
+        row = row + count if row + count != 6 else 8
+    lane = lax.broadcasted_iota(jnp.int32, (LANES, LANES), 1)
+    for out, rank in ((own, info[1]), (other, info[1] ^ 2)):
+        for part in range(3):
+            out[part * LANES : (part + 1) * LANES, :] = mix[:, aligned(8 * part + rank, LANES)]
+        out[MIX_COLS:MIX_ROWS, :] = small[...].astype(BF16)
+        upper = jnp.bitwise_and(rank, 1) == 1
+        for pair in range(4):
+            first = expand[:, aligned(8 * pair + rank // 2, LANES)].astype(F32)
+            second = expand[:, aligned(8 * pair + 4 + rank // 2, LANES)].astype(F32)
+            first = jnp.where(upper, pltpu.roll(first, 64, 1), first)
+            second = jnp.where(upper, second, pltpu.roll(second, 64, 1))
+            joined = jnp.where(lane < 64, first, second).astype(BF16)
+            out[MIX_ROWS + pair * LANES : MIX_ROWS + (pair + 1) * LANES, :] = joined
+    rows = cot.shape[0] // 2
+    own_last[:64, :] = shrink[aligned(info[1], 64), :]
+    own_last[64:, :] = dense[...]
+    other_shrink[...] = shrink[aligned(info[1] ^ 2, 64), :]
+    other_last[:64, :] = other_shrink[...]
+    other_last[64:, :] = cot[rows:, :]
+
+
+def cut_slices(info, mix, expand, shrink, dense, cot, vectors):
+    operands = [mix, expand, shrink, dense, cot] + [vector.reshape(-1, LANES) for vector in vectors]
+    width = shrink.shape[1]
+    outs = [((FIRST_ROWS, LANES), BF16)] * 2
+    outs += [((64 + rows, width), BF16) for rows in (dense.shape[0], cot.shape[0] // 2, 0)]
+    return call(
+        cut_body,
+        info,
+        operands,
+        [whole(operand.shape) for operand in operands],
+        outs,
+        [whole(shape) for shape, _ in outs],
+        scratch=[pltpu.VMEM((SMALL, LANES), F32)],
+    )
+
+
+def turn(heads, cos, sin, lane):
+    ahead = pltpu.roll(heads, LANES - 8, 1)
+    behind = pltpu.roll(heads, 8, 1)
+    return heads * cos + jnp.where(lane % HEAD < 8, -ahead, behind) * sin
+
+
+def spread_tables(table, frequency):
+    spread = frequency[8:16, :].astype(BF16)
+    high = table.astype(BF16)
+    low = (table - high.astype(F32)).astype(BF16)
+    cos = tn(high[:8], spread) + tn(low[:8], spread) + frequency[16:17, :]
+    return cos, tn(high[8:], spread) + tn(low[8:], spread)
+
+
+def gelu_parts(hidden):
+    bell = jnp.exp(hidden * hidden * -0.5)
+    point = 1.0 / (1.0 + (0.3275911 * 0.5**0.5) * jnp.abs(hidden))
+    series = 1.061405429 * point - 1.453152027
+    for factor in (1.421413741, -0.284496736, 0.254829592):
+        series = series * point + factor
+    tail = 0.5 * series * point * bell
+    normal = jnp.where(hidden < 0.0, tail, 1.0 - tail)
+    return normal, hidden * bell * ((2.0 * np.pi) ** -0.5)
+
+
+def near_forward_body(info, inputs, along, across, frequency, *outs):
+    mix, expand, vectors, bias = outs[7:]
+    shard, rank = info[0], info[1]
+
+    @pl.when(pl.program_id(0) == 0)
+    def _():
+        for number in range(8):
+            piece = (across if number % 2 else along).at[number // 2]
+            block = aligned(shard ^ number, LANES)
+            for part in range(3):
+                mix[block, part * LANES : (part + 1) * LANES] = piece[part * LANES : (part + 1) * LANES, :]
+            vectors[:, block] = piece[MIX_COLS:MIX_ROWS, :].astype(F32)
+            for pair in range(4):
+                start = MIX_ROWS + pair * LANES
+                expand[block, pair * LANES : (pair + 1) * LANES] = piece[start : start + LANES, :]
+        lane = lax.broadcasted_iota(jnp.int32, (8, LANES), 1)
+        upper = jnp.bitwise_and(rank, 1) == 1
+        bias[...] = jnp.zeros_like(bias)
+        line = lax.broadcasted_iota(jnp.int32, (8, LANES), 0)
+
+        def chosen_row(block, number):
+            row = jnp.sum(jnp.where(line == number, block, 0.0), axis=0, keepdims=True)
+            return jnp.broadcast_to(row, (8, LANES))
+
+        for pair in range(4):
+            one = chosen_row(vectors[8:16, 2 * pair * LANES : (2 * pair + 1) * LANES], 3 + rank // 2)
+            two = chosen_row(vectors[8:16, (2 * pair + 1) * LANES : (2 * pair + 2) * LANES], 3 + rank // 2)
+            one = jnp.where(upper, pltpu.roll(one, 64, 1), one)
+            two = jnp.where(upper, two, pltpu.roll(two, 64, 1))
+            joined = jnp.where(lane < 64, one, two)
+            bias[0:1, pair * LANES : (pair + 1) * LANES] = joined[0:1, :]
+        for part in range(3):
+            place = 8 * part + rank
+            held = chosen_row(vectors[8:16, aligned(place // 3, LANES)], place % 3)
+            bias[1:2, part * LANES : (part + 1) * LANES] = held[0:1, :]
+
+    forward_step(inputs, frequency, mix, expand, vectors, bias, *outs[:7])
+
+
+def far_forward_body(info, inputs, mix, expand, vectors, bias, frequency, *rest):
+    forward_step(inputs, frequency, mix, expand, vectors, bias, *rest[7:])
+
+
+def forward_step(
+    rows, frequency, mix, expand, vectors, bias,
+    normed_out, heads_out, tables_out, probs_out, context_out, act_out, slope_out,
+):
+    tokens = normed_out.shape[1]
+    flat = (2 * tokens, normed_out.shape[2])
+    rows = rows[...]
+    inputs = rows[:, :tokens].reshape(flat).astype(F32)
+    average = jnp.mean(inputs, axis=-1, keepdims=True)
+    centred = inputs - average
+    variance = jnp.mean(centred * centred, axis=-1, keepdims=True)
+    normed = centred * lax.rsqrt(variance + EPSILON)
+    one = (normed * vectors[0:1, :] + vectors[1:2, :]).astype(BF16)
+    two = (normed * vectors[2:3, :] + vectors[3:4, :]).astype(BF16)
+    normed_out[...] = normed.astype(BF16).reshape(normed_out.shape)
+    mixed = nn(one, mix[...]) + bias[1:2, :MIX_COLS]
+
+    row_index = lax.broadcasted_iota(jnp.int32, (tokens, tokens), 0)
+    col_index = lax.broadcasted_iota(jnp.int32, (tokens, tokens), 1)
+    lane = lax.broadcasted_iota(jnp.int32, (tokens, LANES), 1)
+    for sequence in range(2):
+        marks = rows[sequence, tokens : tokens + 16, :tokens].astype(F32)[0:1, :]
+        across_marks = jnp.broadcast_to(marks, (tokens, tokens))
+        same = across_marks == across_marks.T
+        allowed = same & (col_index <= row_index)
+        position = jnp.sum(jnp.where(same & (row_index < col_index), 1.0, 0.0), axis=0, keepdims=True)
+        phases = jnp.broadcast_to(position, (8, tokens)) * frequency[0:8, 0:1]
+        table = jnp.concatenate([jnp.cos(phases), jnp.sin(phases)], axis=0)
+        tables_out[sequence] = table
+        cos, sin = spread_tables(table, frequency)
+        part = mixed[sequence * tokens : (sequence + 1) * tokens]
+        queries = turn(part[:, :LANES], cos, sin, lane).astype(BF16)
+        keys = turn(part[:, LANES : 2 * LANES], cos, sin, lane).astype(BF16)
+        values = part[:, 2 * LANES :].astype(BF16)
+        heads_out[sequence, :, :LANES] = queries
+        heads_out[sequence, :, LANES : 2 * LANES] = keys
+        heads_out[sequence, :, 2 * LANES :] = values
+        context = jnp.zeros((tokens, LANES), F32)
+        for head in range(2):
+            chosen = lane // HEAD == head
+            scores = nt(jnp.where(chosen, queries, 0).astype(BF16), keys) * HEAD ** (-0.5)
+            scores = jnp.where(allowed, scores, -1e30)
+            weights = jnp.exp(scores - jnp.max(scores, axis=-1, keepdims=True))
+            probs = weights * (1.0 / jnp.sum(weights, axis=-1, keepdims=True))
+            probs_out[sequence, head] = probs
+            context = context + nn(probs.astype(BF16), jnp.where(chosen, values, 0).astype(BF16))
+        context_out[sequence] = context.astype(BF16)
+
+    hidden = nn(two, expand[...]) + bias[0:1, :]
+    normal, slope = gelu_parts(hidden)
+    act_out[...] = (hidden * normal).astype(BF16).reshape(act_out.shape)
+    slope_out[...] = (normal + slope).reshape(slope_out.shape)
+
+
+def turn_constants():
+    frequency = np.zeros((24, LANES), np.float32)
+    powers = np.power(np.float32(10000.0), -2.0 * np.arange(ROT // 2, dtype=np.float32) / np.float32(ROT))
+    frequency[0:8, :] = powers[:, None]
+    for lane in range(LANES):
+        if lane % HEAD < ROT:
+            frequency[8 + lane % 8, lane] = 1.0
+        else:
+            frequency[16, lane] = 1.0
+    return frequency
+
+
+def forward(info, inputs, weights, frequency, tokens, width, held=None):
+    far = held is not None
+    outs = [
+        ((GROUP, tokens, width), BF16),
+        ((GROUP, tokens, MIX_COLS), BF16),
+        ((GROUP, 2 * 8, tokens), F32),
+        ((GROUP, 2, tokens, tokens), F32),
+        ((GROUP, tokens, LANES), BF16),
+        ((GROUP, tokens, HIDDEN), BF16),
+        ((GROUP, tokens, HIDDEN), F32),
+    ]
+    fixed = [((width, MIX_COLS), BF16), ((width, HIDDEN), BF16), ((SMALL, width), F32), ((8, HIDDEN), F32)]
+    operands = [inputs] + list(weights) + [frequency]
+    in_specs = [pairs(inputs.shape)] + [whole(operand.shape) for operand in operands[1:]]
+    out_specs = [pairs(shape, 2 * far) for shape, _ in outs]
+    if far:
+        aliases = {1 + len(operands) + number: number for number in range(len(outs))}
+        in_specs += [pl.BlockSpec(memory_space=pl.ANY)] * len(outs)
+        return call(
+            far_forward_body, info, operands + list(held), in_specs, outs, out_specs, grid=(2,), aliases=aliases, micros=10
+        )
+    out_specs += [whole(shape) for shape, _ in fixed]
+    return call(near_forward_body, info, operands, in_specs, outs + fixed, out_specs, grid=(2,), micros=10)
+
+
+def pairs(shape, first=0):
+    rest = (0,) * (len(shape) - 1)
+    return pl.BlockSpec((2,) + shape[1:], lambda i, _: (i + first,) + rest)
+
+
+def far_project_body(info, context, act, dense, along, across, out, shrink):
+    @pl.when(pl.program_id(0) == 0)
+    def _():
+        for number in range(8):
+            piece = across if number % 2 else along
+            start = 64 * (number // 2)
+            shrink[aligned(info[0] ^ number, 64), :] = piece[start : start + 64, :]
+
+    near_project_body(info, context, act, dense, shrink, out)
+
+
+def near_project_body(info, context, act, dense, shrink, out):
+    rows = 2 * context.shape[1]
+    total = nn(context[...].reshape(rows, LANES), dense[...]) + nn(act[...].reshape(rows, HIDDEN), shrink[...])
+    out[...] = total.astype(BF16).reshape(out.shape)
+
+
+def project(info, context, act, dense, shrink, far):
+    tokens, width = context.shape[1], dense.shape[1]
+    operands = [context, act, dense] + (list(shrink) if far else [shrink])
+    in_specs = [pairs(context.shape, 2 * far), pairs(act.shape, 2 * far)]
+    in_specs += [whole(operand.shape) for operand in operands[2:]]
+    outs = [((4, tokens, width), BF16)] + [((HIDDEN, width), BF16)] * far
+    out_specs = [pairs(outs[0][0])] + [whole((HIDDEN, width))] * far
+    body = far_project_body if far else near_project_body
+    return call(body, info, operands, in_specs, outs, out_specs, grid=(2,), micros=5)
+
+
+def halves(near, far):
+    block = (2,) + near.shape[1:]
+    return [
+        pl.BlockSpec(block, lambda i, _: (jnp.minimum(i, 1), 0, 0)),
+        pl.BlockSpec(block, lambda i, _: (jnp.maximum(i - 2, 0), 0, 0)),
+    ]
+
+
+def chosen_half(near, far):
+    rows = jnp.where(pl.program_id(0) < 2, near[...], far[...])
+    return rows.reshape(rows.shape[0] * rows.shape[1], rows.shape[2])
+
+
+def flat(ref):
+    return ref[...].reshape(ref.shape[0] * ref.shape[1], ref.shape[2])
+
+
+def clear(*refs):
+    @pl.when(pl.program_id(0) == 0)
+    def _():
+        for ref in refs:
+            ref[...] = jnp.zeros_like(ref)
+
+
+def each_shard(info, mine, other):
+    unit = mine.shape[0] // 4
+    for place, z in enumerate((1, 0, 3, 2)):
+        rows = pl.ds(place * unit, unit)
+        yield info[0] ^ (2 * z), mine.at[rows]
+        yield info[0] ^ (2 * z + 1), other.at[rows]
+
+
+def last_grad_body(info, near, far, act, context, mine, other, total, dense_total):
+    clear(total, dense_total)
+    cot = chosen_half(near, far)
+    total[...] += tn(flat(act), cot)
+    dense_total[...] += tn(flat(context), cot)
+
+    @pl.when(pl.program_id(0) == 3)
+    def _():
+        shrink_rows = 4 * HIDDEN
+        for shard, out in each_shard(info, mine.at[:shrink_rows], other.at[:shrink_rows]):
+            for part in range(8):
+                rows = total[aligned(shard, 64), part * LANES : (part + 1) * LANES]
+                out[64 * part : 64 * (part + 1), :] = rows.astype(BF16)
+        for part in range(8):
+            start = shrink_rows + LANES * part
+            block = dense_total[:, part * LANES : (part + 1) * LANES].astype(BF16)
+            mine[start : start + LANES, :] = block
+            other[start : start + LANES, :] = block
+
+
+def last_backward(info, near, far, act, context):
+    width = near.shape[2]
+    outs = [((4 * HIDDEN + width, LANES), BF16)] * 2
+    return call(
+        last_grad_body,
+        info,
+        [near, far, act, context],
+        halves(near, far) + [pairs(act.shape), pairs(context.shape)],
+        outs,
+        [whole(shape) for shape, _ in outs],
+        grid=(4,),
+        scratch=[pltpu.VMEM((HIDDEN, width), F32), pltpu.VMEM((LANES, width), F32)],
+        micros=8,
+    )
+
+
+def norm_products(total, column, weight, gain, shift):
+    lines = as_columns(weight)
+    column = column[:, 0:1]
+    grad = total * gain + column * shift
+    return grad, jnp.sum(lines * total, axis=0, keepdims=True), jnp.sum(lines * column, axis=0, keepdims=True)
+
+
+def expand_grad_body(
+    info, near, far, slope, normed, shrink, expand, vectors, pre_out, bias_out, sums, mine, other, total, column
+):
+    clear(total, column, bias_out, sums)
+    grad_act = nt(chosen_half(near, far), shrink[...])
+    grad_pre = (grad_act * flat(slope)).astype(BF16)
+    pre_out[...] = grad_pre.reshape(pre_out.shape)
+    bias_out[...] += jnp.broadcast_to(jnp.sum(grad_pre.astype(F32), axis=0, keepdims=True), bias_out.shape)
+    total[...] += tn(grad_pre, flat(normed))
+    column[...] += tn(grad_pre, jnp.ones((grad_pre.shape[0], LANES), BF16))
+
+    @pl.when(pl.program_id(0) == 3)
+    def _():
+        grad, sums[0:1, :], sums[1:2, :] = norm_products(
+            total[...], column, expand[...], vectors[2:3, :], vectors[3:4, :]
+        )
+        total[...] = grad
+        for shard, out in each_shard(info, mine, other):
+            out[...] = total[:, aligned(shard, LANES)].astype(BF16)
+
+
+def expand_backward(info, near, far, slope, normed, shrink, expand, vectors):
+    tokens, width = near.shape[1:]
+    operands = [near, far, slope, normed, shrink, expand, vectors]
+    in_specs = halves(near, far) + [pairs(slope.shape), pairs(normed.shape)]
+    in_specs += [whole(operand.shape) for operand in operands[4:]]
+    outs = [((GROUP, tokens, HIDDEN), BF16), ((8, HIDDEN), F32), ((8, width), F32)] + [((4 * HIDDEN, LANES), BF16)] * 2
+    out_specs = [pairs(outs[0][0])] + [whole(shape) for shape, _ in outs[1:]]
+    scratch = [pltpu.VMEM((HIDDEN, width), F32), pltpu.VMEM((HIDDEN, LANES), F32)]
+    return call(expand_grad_body, info, operands, in_specs, outs, out_specs, grid=(4,), scratch=scratch, micros=12)
+
+
+def attention_grad_body(
+    info, near, far, normed, heads, tables, probs, dense, mix, vectors, bias_grad, feed_sums, frequency,
+    mixed_out, mine, other, total, column, sums, piece,
+):
+    step = pl.program_id(0)
+    rank = info[1]
+    tokens = near.shape[1]
+    clear(total, column, sums)
+    cot = chosen_half(near, far)
+    lane = lax.broadcasted_iota(jnp.int32, (tokens, LANES), 1)
+    grad_context = nt(cot, dense[...]).astype(BF16)
+    grad_mixed = []
+    for sequence in range(2):
+        queries = heads[sequence, :, :LANES]
+        keys = heads[sequence, :, LANES : 2 * LANES]
+        values = heads[sequence, :, 2 * LANES :]
+        grad_queries = jnp.zeros((tokens, LANES), F32)
+        grad_keys = jnp.zeros((tokens, LANES), F32)
+        grad_values = jnp.zeros((tokens, LANES), F32)
+        for head in range(2):
+            chosen = lane // HEAD == head
+            exact = probs[sequence, head]
+            part = grad_context[sequence * tokens : (sequence + 1) * tokens]
+            part = jnp.where(chosen, part, 0).astype(BF16)
+            grad_probs = nt(part, values)
+            grad_scores = exact * (grad_probs - jnp.sum(exact * grad_probs, axis=-1, keepdims=True))
+            grad_scores = grad_scores.astype(BF16)
+            grad_values = grad_values + tn(exact.astype(BF16), part)
+            grad_queries = grad_queries + nn(grad_scores, jnp.where(chosen, keys, 0).astype(BF16))
+            grad_keys = grad_keys + tn(grad_scores, jnp.where(chosen, queries, 0).astype(BF16))
+        cos, sin = spread_tables(tables[sequence], frequency)
+        joined = [
+            turn(grad_queries * HEAD ** (-0.5), cos, -sin, lane),
+            turn(grad_keys * HEAD ** (-0.5), cos, -sin, lane),
+            grad_values,
+        ]
+        grad_mixed.append(jnp.concatenate(joined, axis=1).astype(BF16))
+    grad_mixed = jnp.concatenate(grad_mixed, axis=0)
+    mixed_out[...] = grad_mixed.reshape(mixed_out.shape)
+    total[...] += tn(grad_mixed, flat(normed))
+    column[...] += tn(grad_mixed, jnp.ones((grad_mixed.shape[0], LANES), BF16))
+    sums[5:6, :MIX_COLS] += jnp.sum(grad_mixed.astype(F32), axis=0, keepdims=True)
+
+    @pl.when(step == 0)
+    def _():
+        sums[4:5, :] = jnp.sum(near[0].astype(F32), axis=0, keepdims=True)
+
+    @pl.when(step == 3)
+    def _():
+        grad, sums[0:1, :], sums[1:2, :] = norm_products(
+            total[...], column, mix[...], vectors[0:1, :], vectors[1:2, :]
+        )
+        total[...] = grad
+        sums[2:4, :] = feed_sums[0:2, :]
+        line = lax.broadcasted_iota(jnp.int32, (8, LANES), 1)
+        for shard, out in each_shard(info, mine, other):
+            block = aligned(shard, LANES)
+            out[:MIX_COLS, :] = total[:, block].astype(BF16)
+            piece[...] = jnp.zeros_like(piece)
+            piece[0:5, :] = sums[0:5, block]
+            for row in range(3):
+                place = 3 * shard + row
+                spread = jnp.zeros((1, LANES), F32)
+                for part in range(3):
+                    held = sums[5:6, part * LANES : (part + 1) * LANES]
+                    spread = spread + jnp.where(place == 8 * part + rank, held, 0.0)
+                piece[5 + row : 6 + row, :] = spread
+            packed = bias_grad[:, aligned(shard // 2, LANES)]
+            moved = jnp.where(jnp.bitwise_and(shard ^ rank, 1) == 1, pltpu.roll(packed, 64, 1), packed)
+            moved = jnp.where(line // 64 == jnp.bitwise_and(rank, 1), moved, 0.0)
+            for row in range(4):
+                piece[8 + row : 9 + row, :] = jnp.where(rank // 2 == row, moved[0:1, :], 0.0)
+            out[MIX_COLS:, :] = piece[...].astype(BF16)
+
+
+def attention_backward(info, near, far, saved, dense, fixed):
+    tokens, width = near.shape[1:]
+    operands = [near, far] + list(saved) + [dense] + list(fixed)
+    in_specs = halves(near, far) + [pairs(operand.shape) for operand in saved]
+    in_specs += [whole(operand.shape) for operand in operands[2 + len(saved) :]]
+    outs = [((GROUP, tokens, MIX_COLS), BF16)] + [((4 * MIX_ROWS, LANES), BF16)] * 2
+    out_specs = [pairs(outs[0][0])] + [whole(shape) for shape, _ in outs[1:]]
+    scratch = [
+        pltpu.VMEM((MIX_COLS, width), F32),
+        pltpu.VMEM((MIX_COLS, LANES), F32),
+        pltpu.VMEM((8, width), F32),
+        pltpu.VMEM((SMALL, LANES), F32),
+    ]
+    return call(attention_grad_body, info, operands, in_specs, outs, out_specs, grid=(4,), scratch=scratch, micros=14)
+
+
+def input_grad_body(info, mixed, pre, mix, expand, vectors, out):
+    total = nt(flat(mixed), mix[...]) * vectors[0:1, :] + nt(flat(pre), expand[...]) * vectors[2:3, :]
+    out[...] = total.astype(BF16).reshape(out.shape)
+
+
+def input_backward(info, mixed, pre, mix, expand, vectors, far):
+    tokens, width = mixed.shape[1], mix.shape[0]
+    operands = [mixed, pre, mix, expand, vectors]
+    in_specs = [pairs(mixed.shape, 2 * far), pairs(pre.shape, 2 * far)]
+    in_specs += [whole(operand.shape) for operand in operands[2:]]
+    shape = (4, tokens, width)
+    return call(input_grad_body, info, operands, in_specs, [(shape, BF16)], [pairs(shape)], grid=(2,), micros=6)[0]
+
+
+def norm_body(info, block, cot, upstream, out):
+    inputs = block[...].astype(F32)
+    average = jnp.mean(inputs, axis=-1, keepdims=True)
+    centred = inputs - average
+    scale = lax.rsqrt(jnp.mean(centred * centred, axis=-1, keepdims=True) + EPSILON)
+    normed = centred * scale
+    pulled = upstream[...]
+    pulled = pulled - jnp.mean(pulled, axis=-1, keepdims=True) - normed * jnp.mean(pulled * normed, axis=-1, keepdims=True)
+    out[...] = cot[...].astype(F32) + scale * pulled
+
+
+def each_rank(near, far, unit):
+    for place, number in enumerate(NEAR):
+        rows = pl.ds(place * unit, unit)
+        yield number, near.at[rows], far.at[rows]
+
+
+def expand_out_body(info, near, far, out):
+    rank = info[1]
+    upper = jnp.bitwise_and(rank, 1) == 1
+    for number, one, two in each_rank(near, far, HIDDEN):
+        place = (rank ^ number) // 2
+        for shard in range(8):
+            rows = slice(64 * shard, 64 * (shard + 1))
+            lower_rows = jnp.where(upper, two[rows, :], one[rows, :])
+            upper_rows = jnp.where(upper, one[rows, :], two[rows, :])
+            joined = jnp.concatenate([lower_rows, upper_rows], axis=0)
+            out[:, aligned(4 * shard + place, LANES)] = as_columns(joined)
+
+
+def last_out_body(info, near, far, own_dense, shrink_out, dense_out):
+    rank = info[1]
+    for number, one, two in each_rank(near, far, HIDDEN):
+        for piece, place in ((one, rank ^ number), (two, rank ^ number ^ 1)):
+            for part in range(8):
+                rows = piece[64 * part : 64 * (part + 1), :]
+                shrink_out[aligned(place, 64), part * LANES : (part + 1) * LANES] = rows.astype(F32)
+    for part in range(8):
+        start = 4 * HIDDEN + part * LANES
+        rows = jnp.where(own_dense[0] == 1, near[start : start + LANES, :], far[start : start + LANES, :])
+        dense_out[:, part * LANES : (part + 1) * LANES] = rows.astype(F32)
+
+
+def mix_out_body(info, near, far, mix_out):
+    rank = info[1]
+    for number, one, two in each_rank(near, far, MIX_ROWS):
+        for piece, place in ((one, rank ^ number), (two, rank ^ number ^ 1)):
+            for part in range(3):
+                mix_out[:, aligned(8 * part + place, LANES)] = as_columns(piece[part * LANES : (part + 1) * LANES, :])
+
+
+def after(value, *others):
+    return lax.optimization_barrier((value,) + others)[0]
+
+
+def gather_first(upper, lower):
+    return swap(upper, x=1), swap(lower, low=1)
+
+
+def gather_second(upper, lower, upper_x, lower_low):
+    upper_pair = swap(jnp.stack([upper, upper_x]), low=1)
+    lower_pair = swap(jnp.stack([lower, lower_low]), x=1)
+    return (
+        jnp.stack([upper, upper_pair[0], upper_x, upper_pair[1]]),
+        jnp.stack([lower, lower_low, lower_pair[0], lower_pair[1]]),
+    )
+
+
+def reduce_first(mine, other, unit):
+    got = swap(other, y=1)
+    total = mine.astype(F32) + got.astype(F32)
+    return total, total[2 * unit :].astype(BF16)
+
+
+def reduce_second(total, sent, unit):
+    kept = jnp.concatenate([total[: 2 * unit], total[4 * unit :]])
+    return (kept + swap(sent, high=1).astype(F32)).astype(BF16)
+
+
+def share_first(slices, unit):
+    away, own = slices[:unit], slices[unit:]
+    return own, swap(away, low=1), swap(own, x=1), swap(away, x=1, low=1)
+
+
+def scatter_first(near, far_got):
+    cut = near.shape[1] // 2
+    total = near.astype(F32) + far_got.astype(F32)
+    sent_x = total[2:, :cut].astype(BF16)
+    sent_low = total[1::2, cut:].astype(BF16)
+    return total[:2, :cut], sent_x, total[0::2, cut:], sent_low
+
+
+def scatter_second(kept_x, sent_x, kept_low, sent_low):
+    upper = kept_x + swap(sent_x, x=1).astype(F32)
+    lower = kept_low + swap(sent_low, low=1).astype(F32)
+    return upper[0], upper[1].astype(BF16), lower[0], lower[1].astype(BF16)
+
+
+def scatter_third(upper, sent_upper, lower, sent_lower):
+    upper = upper + swap(sent_upper, low=1).astype(F32)
+    lower = lower + swap(sent_lower, x=1).astype(F32)
+    return jnp.concatenate([upper, lower])
+
+
+def local(
+    block_input,
+    segments,
+    cotangent,
+    first_gain,
+    first_shift,
+    mix_weight,
+    mix_bias,
+    dense_weight,
+    dense_bias,
+    second_gain,
+    second_shift,
+    expand_weight,
+    expand_bias,
+    shrink_weight,
+    shrink_bias,
+):
+    rep = lax.axis_index("rep")
+    shard = lax.axis_index("fsdp")
+    x, core, high, low, y = rep // 2, rep % 2, shard // 4, (shard // 2) % 2, shard % 2
+    info = jnp.stack([shard, 4 * x + 2 * low + core]).astype(jnp.int32)
+    tokens, width = block_input.shape
+    rows = mix_weight.shape[0]
+
+    own_y, own_x = y == core, x == high
+
+    small = (first_gain, first_shift, second_gain, second_shift, dense_bias, shrink_bias, mix_bias, expand_bias)
+    cut = tokens // 2
+    marks = jnp.pad(segments.astype(BF16), ((0, 15), (0, width - tokens)))
+    upper, lower = block_input[:cut], jnp.concatenate([block_input[cut:], marks])
+    upper_x, lower_low = gather_first(upper, lower)
+    own, other, own_last, other_last, other_shrink = cut_slices(
+        info, mix_weight, expand_weight, shrink_weight, dense_weight, cotangent, small
+    )
+    along = swap(other, low=1), swap(own, high=1), swap(other, high=1, low=1)
+    upper_x, lower_low = after((upper_x, lower_low), own)
+    near = gather_second(upper, lower, upper_x, lower_low)
+    along = jnp.stack((own,) + along)
+    across = swap(along, y=1)
+    near = jnp.concatenate(after(near, along), axis=1)
+    far = swap(near, core=1)
+
+    own_last, other_last, other_shrink, cot_upper = after((own_last, other_last, other_shrink, cotangent[:cut]), near)
+    low_last = swap(other_last, low=1)
+    high_last = swap(own_last, high=1)
+    both_last = swap(other_shrink, high=1, low=1)
+    cot_upper_x = swap(cot_upper, x=1)
+
+    frequency = jnp.asarray(turn_constants())
+    *saved, mix, expand, vectors, bias = forward(info, near, (along, across), frequency, tokens, width)
+    dense_held = jnp.where(own_x, dense_weight, high_last[64:])
+    last = jnp.concatenate([own_last[:64], low_last[:64], high_last[:64], both_last, dense_held])
+    last = after(last, mix)
+    last_across = swap(last, y=1)
+    cot_upper_x, cot_lower_low = after((cot_upper_x, low_last[64:]), mix)
+    cot_near = gather_second(cot_upper, cotangent[cut:], cot_upper_x, cot_lower_low)
+    far = after(far, last, cot_upper_x, cot_lower_low)
+    saved = forward(info, far, (mix, expand, vectors, bias), frequency, tokens, width, saved)
+    normed, heads, tables, probs, context, act, slope = saved
+    last_across = after(last_across, context)
+    dense = jnp.where(own_y, dense_held, last_across[256:])
+    branch_far, shrink = project(info, context, act, dense, (last, last_across), True)
+    branch_got = swap(branch_far, core=1)
+    cot_near = jnp.concatenate(after(cot_near, branch_far), axis=1)
+    cot_far = swap(cot_near, core=1)
+    (branch_near,) = project(info, context, act, dense, after(shrink, cot_near), False)
+    branch = scatter_first(branch_near, branch_got)
+
+    cot_near, cot_far = after((cot_near, cot_far), branch[1], branch[3])
+    last_mine, last_other = last_backward(info, cot_near, cot_far, act, context)
+    grad_pre, bias_grad, feed_sums, expand_mine, expand_other = expand_backward(
+        info, cot_near, cot_far, slope, normed, after(shrink, last_mine), expand, vectors
+    )
+    branch = scatter_second(*branch)
+    last_part = reduce_first(last_mine, last_other, HIDDEN)
+    saved = (normed, heads, tables, probs)
+    fixed = (mix, vectors, bias_grad, feed_sums, frequency)
+    grad_mixed, mix_mine, mix_other = attention_backward(
+        info, cot_near, cot_far, saved, after(dense, branch[1], branch[3], last_part[1]), fixed
+    )
+    expand_part = reduce_first(expand_mine, expand_other, HIDDEN)
+    last_slices = reduce_second(*last_part, HIDDEN)
+    branch = scatter_third(*branch)
+    block_out = (block_input.astype(F32) + branch + (vectors[4] + vectors[5])).astype(BF16)
+    error_far = input_backward(
+        info, after(grad_mixed, expand_part[1], last_slices), grad_pre, mix, expand, vectors, True
+    )
+    error_got = swap(error_far, core=1)
+    own_part, low_part, x_part, both_part = share_first(last_slices, HIDDEN)
+    dense_part = jnp.where(own_x, own_part[HIDDEN:], x_part[HIDDEN:])
+    last_near = jnp.concatenate([own_part[:HIDDEN], low_part, x_part[:HIDDEN], both_part, dense_part])
+    last_far = swap(last_near, core=1)
+    error_near = input_backward(
+        info, after(grad_mixed, error_far, last_near), grad_pre, mix, expand, vectors, False
+    )
+    error = scatter_first(error_near, error_got)
+
+    mix_part = reduce_first(mix_mine, mix_other, MIX_ROWS)
+    mix_part = after(mix_part, error[1], error[3])
+    expand_slices = after(reduce_second(*expand_part, HIDDEN), mix_part[1])
+    expand_near = jnp.concatenate(share_first(expand_slices, HIDDEN))
+    expand_far = swap(expand_near, core=1)
+    mix_slices = reduce_second(*mix_part, MIX_ROWS)
+    mix_parts = share_first(mix_slices, MIX_ROWS)
+    mix_near = jnp.concatenate(mix_parts)
+    mix_sums = [part[MIX_COLS:].astype(F32) for part in mix_parts]
+    mix_sums = ((mix_sums[0] + mix_sums[1]) + (mix_sums[2] + mix_sums[3])).astype(BF16)
+    mix_near = jnp.concatenate([mix_near, mix_sums])
+    mix_far = swap(mix_near, core=1)
+    sums = mix_sums.astype(F32) + mix_far[4 * MIX_ROWS :].astype(F32)
+    upstream = scatter_third(*scatter_second(*error))
+
+    def out(body, near, far, shapes, flag=None):
+        operands = [near, far]
+        in_specs = [whole(near.shape), whole(far.shape)]
+        if flag is not None:
+            operands.append(flag)
+            in_specs.append(pl.BlockSpec(memory_space=pltpu.SMEM))
+        return call(body, info, operands, in_specs, [(shape, F32) for shape in shapes], [whole(shape) for shape in shapes])
+
+    flag = own_y.astype(jnp.int32).reshape(1)
+    shrink_out, dense_out = out(last_out_body, last_near, last_far, [shrink_weight.shape, dense_weight.shape], flag)
+    (expand_out,) = out(expand_out_body, expand_near, expand_far, [expand_weight.shape])
+    (mix_out,) = out(mix_out_body, mix_near, mix_far, [mix_weight.shape])
+    (input_grad,) = call(
+        norm_body,
+        info,
+        [block_input, cotangent, upstream],
+        [whole(block_input.shape)] * 3,
+        [(block_input.shape, F32)],
+        [whole(block_input.shape)],
+    )
+    return (
+        block_out,
+        input_grad,
+        sums[0],
+        sums[1],
+        mix_out,
+        sums[5:8].reshape(-1),
+        dense_out,
+        sums[4],
+        sums[2],
+        sums[3],
+        expand_out,
+        sums[8:12].reshape(-1),
+        shrink_out,
+        sums[4],
+    )
+
+
 def solution(mesh):
+    tensor_parallel = mesh.shape["rep"] == TP_REP and mesh.shape["fsdp"] == TP_FSDP
     return jax.shard_map(
-        local,
+        local if tensor_parallel else local_general,
         mesh=mesh,
         in_specs=(
             P(("rep", "fsdp"), None),

time: 1430 us -> 278 us (0.19)
  waiting for transfers between devices: 1080 us -> 90.5 us
  blocking collectives: 197 us -> 0 us
  Pallas kernels: 0 us -> 103 us
  matrix products: 85.3 us -> 0 us
  starting transfers between devices: 8.04 us -> 50.9 us
  between operations: 16.6 us -> 1.47 us
    reduce_scatter x4 -> x0, waiting for transfers between devices: 782 us -> none  [the longest x1 286 us: local(): lax.psum_scatter(expand_grad, 'fsdp', scatter_dimension=0, tiled=True)]
    all_gather x4 -> x0, waiting for transfers between devices: 225 us -> none  [the longest x1 117 us: local(): lax.all_gather(shrink_weight, 'fsdp', axis=0, tiled=True)]
    all_gather x8 -> x0, blocking collectives: 159 us -> none  [the longest x1 26.3 us: local(): lax.all_gather(mix_bias, 'fsdp', axis=0, tiled=True)]
    pallas_call x0 -> x14, Pallas kernels: none -> 103 us  [call(): pl.pallas_call(body, grid_spec=pltpu.PrefetchScalarGridSpec(num_scalar_pr...]
    ppermute x0 -> x45, waiting for transfers between devices: none -> 90.5 us  [permute(): return lax.ppermute(value, ('rep', 'fsdp'), pairs)]
    dot_general x18 -> x0, matrix products: 85.3 us -> none  [the longest x4 31.4 us: product_right(): lax.dot_general(left, right, (((1,), (1,)), ((), ())), preferred_element_...]
    psum x1 -> x0, waiting for transfers between devices: 66.3 us -> none  [local(): lax.psum((gain_one_sum, shift_one_sum, mix_sum, mix_bias_sum, dense_sum,...]
    ppermute x0 -> x45, starting transfers between devices: none -> 50.9 us  [permute(): return lax.ppermute(value, ('rep', 'fsdp'), pairs)]
  transfers between devices with their start and end apart: 9 -> 45, of which waited for: 7 -> 15; matrix products, arithmetic and copies ran while one was open for 8% -> 7% of each run, Pallas kernels for 0% -> 28%
where the time goes in v2:
time: 278 us; the launch traced here: 275 us
  Pallas kernels  103 us (37%)
  waiting for transfers between devices  90.5 us (33%)
  starting transfers between devices  50.9 us (18%)
  other arithmetic  18.5 us (7%)
  local copies, waits for them, and re-layouts  10.8 us (4%)
    pallas_call x14, Pallas kernels, call(): pl.pallas_call(body, grid_spec=pltpu.PrefetchScalarGridSpec(num_scalar_pr...  103 us
    ppermute x45, waiting for transfers between devices, permute(): return lax.ppermute(value, ('rep', 'fsdp'), pairs)  90.5 us
    ppermute x45, starting transfers between devices, permute(): return lax.ppermute(value, ('rep', 'fsdp'), pairs)  50.9 us
    unnamed x63, local copies, waits for them, and re-layouts  6.06 us
    add x2, other arithmetic, scatter_first(): total = near.astype(F32) + far_got.astype(F32)  5.66 us
  transfers between devices with their start and end apart: 45, of which 15 were waited for; matrix products, arithmetic and copies ran while one was open for 7% of the time, Pallas kernels for 28%

profile of v2, /device:TPU:6, one launch (start us, length us, event | category | flops | bytes accessed | tf_op | source)
XLA Modules:
  0.0 275.3 jit_solution(5354529592377667264)
XLA Ops:
  3.1 1.6 collective-permute-start.1
  5.4 4.1 %shard_map.263 = (bf16[912,128]{1,0:T(8,128)(2,1)}, bf16[912,128]{1,0:T(8,128)(2,1)}, bf16[192,1024]{1,0:T(8,128)(2,1)}, bf16[192,1024]{1,0:T(8,128)(2,1)}, bf16[64,1024]{1,0:T(8,128)(2,1)}) custom-call(s32[2]{0:T(128)} %pad_add_fusion.info, bf16[128,3072]{1,0:T(8,128)(2,1)} %mix.1, bf16[128,4096]{1,0:T(8,128)(2,1)} %expand.1, bf16[512,1024]{1,0:T(8,128)(2,1)} %shrink.1, ...), custom_call_target="tpu_custom_call" | custom-call | flops 4000000000 | bytes 12000000 | tf_op jit(solution)/shard_map/pallas_call | solution.py:326
  9.9 1.8 collective-permute-done.1
  12.5 1.6 collective-permute-start.2
  14.1 2.5 collective-permute-start.6
  18.5 1.6 collective-permute-start.3
  20.1 14.4 %collective-permute-done.6 = bf16[912,128]{1,0:T(8,128)(2,1)S(1)} collective-permute-done((bf16[912,128]{1,0:T(8,128)(2,1)}, bf16[912,128]{1,0:T(8,128)(2,1)S(1)}, u32[]{:S(2)}, u32[]{:S(2)}) %collective-permute-start.6) | collective-permute-done | bytes 233504 | tf_op jit(solution)/shard_map/ppermute | solution.py:302
  34.6 5.6 %collective-permute-done.4 = bf16[912,128]{1,0:T(8,128)(2,1)S(1)} collective-permute-done((bf16[912,128]{1,0:T(8,128)(2,1)}, bf16[912,128]{1,0:T(8,128)(2,1)S(1)}, u32[]{:S(2)}, u32[]{:S(2)}) %collective-permute-start.4) | collective-permute-done | bytes 233504 | tf_op jit(solution)/shard_map/ppermute | solution.py:302
  44.3 3.4 %collective-permute-start.10 = (bf16[64,1024]{1,0:T(8,128)(2,1)S(1)}, bf16[64,1024]{1,0:T(8,128)(2,1)S(1)}, u32[]{:S(2)}, u32[]{:S(2)}) collective-permute-start(bf16[64,1024]{1,0:T(8,128)(2,1)S(1)} %copy-done.24), channel_id=1, source_target_pairs={{0,6},{1,7},{2,4},{3,5},{4,2},{5,3},{6,0},{7,1},{8,14},{9,15},{10,... | collective-permute-start | bytes 393224 | tf_op jit(solution)/shard_map/ppermute | solution.py:302
  47.7 1.5 collective-permute-start.12
  49.8 11.9 %collective-permute-done.11.across = bf16[4,912,128]{2,1,0:T(8,128)(2,1)S(1)} collective-permute-done((bf16[4,912,128]{2,1,0:T(8,128)(2,1)S(1)}, bf16[4,912,128]{2,1,0:T(8,128)(2,1)S(1)}, u32[]{:S(2)}, u32[]{:S(2)}) %collective-permute-start.11) | collective-permute-done | bytes 933920 | tf_op jit(solution)/shard_map/ppermute | solution.py:302
  62.6 2.7 collective-permute-start.8
  65.3 12.1 %shard_map.264 = (bf16[8,256,1024]{2,1,0:T(8,128)(2,1)}, bf16[8,256,384]{2,1,0:T(8,128)(2,1)}, f32[8,16,256]{2,1,0:T(8,128)}, f32[8,2,256,256]{3,2,1,0:T(8,128)}...) custom-call(s32[2]{0:T(128)} %pad_add_fusion.info, ...), custom_call_target="tpu_custom_call" | custom-call | flops 10000000000 | bytes 30000000 | tf_op jit(solution)/shard_map/pallas_call | solution.py:326
  77.4 2.0 collective-permute-done.8
  79.8 1.5 collective-permute-start.15
  82.3 11.7 %shard_map.265 = (bf16[8,256,1024]{2,1,0:T(8,128)(2,1)}, bf16[8,256,384]{2,1,0:T(8,128)(2,1)}, f32[8,16,256]{2,1,0:T(8,128)}, f32[8,2,256,256]{3,2,1,0:T(8,128)}...) custom-call(s32[2]{0:T(128)} %pad_add_fusion.info, ...), custom_call_target="tpu_custom_call", output_to_operand_aliasing={{0}: (7, {}), {1}: (8, {}), {2}: (9, {}), {3}: (10, {}), {4... | custom-call | flops 10000000000 | bytes 30000000 | tf_op jit(solution)/shard_map/pallas_call | solution.py:326
  93.9 6.6 %collective-permute-done.13.across = bf16[384,1024]{1,0:T(8,128)(2,1)S(1)} collective-permute-done((bf16[384,1024]{1,0:T(8,128)(2,1)S(1)}, bf16[384,1024]{1,0:T(8,128)(2,1)S(1)}, u32[]{:S(2)}, u32[]{:S(2)}) %collective-permute-start.13) | collective-permute-done | bytes 786464 | tf_op jit(solution)/shard_map/ppermute | solution.py:302
  101.5 5.6 %shard_map.266 = (bf16[4,256,1024]{2,1,0:T(8,128)(2,1)}, bf16[512,1024]{1,0:T(8,128)(2,1)}) custom-call(s32[2]{0:T(128)} %pad_add_fusion.info, bf16[8,256,128]{2,1,0:T(8,128)(2,1)} %get-tuple-element.104.context, bf16[8,256,512]{2,1,0:T(8,128)(2,1)} %get-tuple-element.105.act, bf16[128,1024]{1,0:T(8,128)(2,1)} %slice_select_fusion.2.dense, ...), custom_call_target="tpu_custom_call" | custom-call | flops 5000000000 | bytes 15000000 | tf_op jit(solution)/shard_map/pallas_call | solution.py:326
  108.2 5.2 %shard_map.267 = bf16[4,256,1024]{2,1,0:T(8,128)(2,1)} custom-call(s32[2]{0:T(128)} %pad_add_fusion.info, bf16[8,256,128]{2,1,0:T(8,128)(2,1)} %get-tuple-element.104.context, bf16[8,256,512]{2,1,0:T(8,128)(2,1)} %get-tuple-element.105.act, bf16[128,1024]{1,0:T(8,128)(2,1)} %slice_select_fusion.2.dense, bf16[512,1024]{1,0:T(8,128)(2,1)} %get-tuple-element.122.shrink), custom_call_target="tpu_custom_call" | custom-call | flops 5000000000 | bytes 15000000 | tf_op jit(solution)/shard_map/pallas_call | solution.py:326
  113.4 4.6 %convert_add_fusion.1 = (f32[4,256,1024]{2,1,0:T(8,128)}, bf16[4,256,1024]{2,1,0:T(8,128)(2,1)S(1)}) fusion(bf16[4,256,1024]{2,1,0:T(8,128)(2,1)S(1)} %collective-permute-done.16, bf16[4,256,1024]{2,1,0:T(8,128)(2,1)} %shard_map.267), kind=kLoop, calls=%fused_computation.1 | loop fusion | flops 4194304 | bytes 10485760 | tf_op jit(solution)/shard_map/add | solution.py:888
  119.4 8.2 %shard_map.268 = (bf16[3072,128]{1,0:T(8,128)(2,1)}, bf16[3072,128]{1,0:T(8,128)(2,1)}) custom-call(s32[2]{0:T(128)} %pad_add_fusion.info, bf16[4,256,1024]{2,1,0:T(8,128)(2,1)} %copy-done.5, bf16[4,256,1024]{2,1,0:T(8,128)(2,1)} %copy-done.18, bf16[8,256,512]{2,1,0:T(8,128)(2,1)} %get-tuple-element.105.act, bf16[8,256,128]{2,1,0:T(8,128)(2,1)} %get-tuple-element.104.context), custom_call_target="tpu_custom_call" | custom-call | flops 8000000000 | bytes 24000000 | tf_op jit(solution)/shard_map/pallas_call | solution.py:326
  127.6 13.1 %shard_map.269 = (bf16[8,256,512]{2,1,0:T(8,128)(2,1)}, f32[8,512]{1,0:T(8,128)}, f32[8,1024]{1,0:T(8,128)}, bf16[2048,128]{1,0:T(8,128)(2,1)}, bf16[2048,128]{1,0:T(8,128)(2,1)}) custom-call(s32[2]{0:T(128)} %pad_add_fusion.info, bf16[4,256,1024]{2,1,0:T(8,128)(2,1)} %copy-done.5, bf16[4,256,1024]{2,1,0:T(8,128)(2,1)} %copy-done.18, ...), custom_call_target="tpu_custom_call" | custom-call | flops 12000000000 | bytes 36000000 | tf_op jit(solution)/shard_map/pallas_call | solution.py:326
  141.6 1.7 collective-permute-start.19
  144.2 1.8 collective-permute-start.22
  146.0 9.7 %collective-permute-done.23 = bf16[2048,128]{1,0:T(8,128)(2,1)S(1)} collective-permute-done((bf16[2048,128]{1,0:T(8,128)(2,1)}, bf16[2048,128]{1,0:T(8,128)(2,1)S(1)}, u32[]{:S(2)}, u32[]{:S(2)}) %collective-permute-start.23) | collective-permute-done | bytes 524320 | tf_op jit(solution)/shard_map/ppermute | solution.py:302
  156.9 1.9 collective-permute-start.40
  158.8 1.9 slice_add_fusion.1
  161.8 9.8 %collective-permute-done.22 = bf16[3072,128]{1,0:T(8,128)(2,1)S(1)} collective-permute-done((bf16[3072,128]{1,0:T(8,128)(2,1)S(1)}, bf16[3072,128]{1,0:T(8,128)(2,1)S(1)}, u32[]{:S(2)}, u32[]{:S(2)}) %collective-permute-start.22) | collective-permute-done | bytes 786464 | tf_op jit(solution)/shard_map/ppermute | solution.py:302
  171.8 2.0 collective-permute-start.24
  173.8 15.6 %shard_map.270 = (bf16[8,256,384]{2,1,0:T(8,128)(2,1)}, bf16[1600,128]{1,0:T(8,128)(2,1)}, bf16[1600,128]{1,0:T(8,128)(2,1)}) custom-call(s32[2]{0:T(128)} %pad_add_fusion.info, bf16[4,256,1024]{2,1,0:T(8,128)(2,1)} %copy-done.5, bf16[4,256,1024]{2,1,0:T(8,128)(2,1)} %copy-done.18, bf16[8,256,1024]{2,1,0:T(8,128)(2,1)} %get-tuple-element.114.normed, ...), custom_call_target="tpu_custom_call" | custom-call | flops 14000000000 | bytes 42000000 | tf_op jit(solution)/shard_map/pallas_call | solution.py:326
  192.5 4.5 %collective-permute-done.24 = bf16[2048,128]{1,0:T(8,128)(2,1)S(1)} collective-permute-done((bf16[2048,128]{1,0:T(8,128)(2,1)S(1)}, bf16[2048,128]{1,0:T(8,128)(2,1)S(1)}, u32[]{:S(2)}, u32[]{:S(2)}) %collective-permute-start.24) | collective-permute-done | bytes 524320 | tf_op jit(solution)/shard_map/ppermute | solution.py:302
  197.2 2.1 collective-permute-start.25
  200.7 6.2 %shard_map.271 = bf16[4,256,1024]{2,1,0:T(8,128)(2,1)} custom-call(s32[2]{0:T(128)} %pad_add_fusion.info, bf16[8,256,384]{2,1,0:T(8,128)(2,1)} %get-tuple-element.130.mixed, bf16[8,256,512]{2,1,0:T(8,128)(2,1)} %get-tuple-element.129.pre, bf16[1024,384]{1,0:T(8,128)(2,1)} %get-tuple-element.88.mix, bf16[1024,512]{1,0:T(8,128)(2,1)} %get-tuple-element.94.expand, ...), custom_call_target="tpu_custom_call" | custom-call | flops 6000000000 | bytes 18000000 | tf_op jit(solution)/shard_map/pallas_call | solution.py:326
  206.9 3.8 %collective-permute-done.26 = bf16[1536,128]{1,0:T(8,128)(2,1)S(1)} collective-permute-done((bf16[1536,128]{1,0:T(8,128)(2,1)S(1)}, bf16[1536,128]{1,0:T(8,128)(2,1)S(1)}, u32[]{:S(2)}, u32[]{:S(2)}) %collective-permute-start.26) | collective-permute-done | bytes 393248 | tf_op jit(solution)/shard_map/ppermute | solution.py:302
  211.1 6.1 %shard_map.272 = bf16[4,256,1024]{2,1,0:T(8,128)(2,1)} custom-call(s32[2]{0:T(128)} %pad_add_fusion.info, bf16[8,256,384]{2,1,0:T(8,128)(2,1)} %get-tuple-element.130.mixed, bf16[8,256,512]{2,1,0:T(8,128)(2,1)} %get-tuple-element.129.pre, bf16[1024,384]{1,0:T(8,128)(2,1)} %get-tuple-element.88.mix, bf16[1024,512]{1,0:T(8,128)(2,1)} %get-tuple-element.94.expand, ...), custom_call_target="tpu_custom_call" | custom-call | flops 6000000000 | bytes 18000000 | tf_op jit(solution)/shard_map/pallas_call | solution.py:326
  218.0 3.8 %shard_map.275 = (f32[512,1024]{1,0:T(8,128)}, f32[128,1024]{1,0:T(8,128)}) custom-call(s32[2]{0:T(128)} %pad_add_fusion.info, bf16[3072,128]{1,0:T(8,128)(2,1)} %copy-done.15, bf16[3072,128]{1,0:T(8,128)(2,1)} %copy-done.21, s32[1]{0:T(128)} %bitcast.34.own_dense), custom_call_target="tpu_custom_call" | custom-call | flops 4000000000 | bytes 12000000 | tf_op jit(solution)/shard_map/pallas_call | solution.py:326
  223.2 2.3 collective-permute-start.43
  226.9 2.0 collective-permute-start.31
  228.9 6.1 %collective-permute-done.34 = bf16[800,128]{1,0:T(8,128)(2,1)S(1)} collective-permute-done((bf16[800,128]{1,0:T(8,128)(2,1)S(1)}, bf16[800,128]{1,0:T(8,128)(2,1)S(1)}, u32[]{:S(2)}, u32[]{:S(2)}) %collective-permute-start.34) | collective-permute-done | bytes 204832 | tf_op jit(solution)/shard_map/ppermute | solution.py:302
  236.4 7.7 %collective-permute-done.42 = bf16[512,128]{1,0:T(8,128)(2,1)S(1)} collective-permute-done((bf16[512,128]{1,0:T(8,128)(2,1)S(1)}, bf16[512,128]{1,0:T(8,128)(2,1)S(1)}, u32[]{:S(2)}, u32[]{:S(2)}) %collective-permute-start.42) | collective-permute-done | bytes 131104 | tf_op jit(solution)/shard_map/ppermute | solution.py:302
  244.1 2.4 collective-permute-start.35
  247.6 2.3 collective-permute-done.35
  251.2 3.9 %collective-permute-done.36 = bf16[400,128]{1,0:T(8,128)(2,1)S(1)} collective-permute-done((bf16[400,128]{1,0:T(8,128)(2,1)S(1)}, bf16[400,128]{1,0:T(8,128)(2,1)S(1)}, u32[]{:S(2)}, u32[]{:S(2)}) %collective-permute-start.36) | collective-permute-done | bytes 102432 | tf_op jit(solution)/shard_map/ppermute | solution.py:302
  256.0 1.5 collective-permute-start.32
  257.5 1.8 collective-permute-start.30
  260.1 4.1 %shard_map.276 = f32[128,4096]{1,0:T(8,128)} custom-call(s32[2]{0:T(128)} %pad_add_fusion.info, bf16[2048,128]{1,0:T(8,128)(2,1)} %copy-done.7, bf16[2048,128]{1,0:T(8,128)(2,1)} %copy-done.22), custom_call_target="tpu_custom_call" | custom-call | flops 4000000000 | bytes 12000000 | tf_op jit(solution)/shard_map/pallas_call | solution.py:326
  265.0 3.6 %shard_map.274 = f32[128,3072]{1,0:T(8,128)} custom-call(s32[2]{0:T(128)} %pad_add_fusion.info, bf16[1616,128]{1,0:T(8,128)(2,1)} %copy-done.13, bf16[1616,128]{1,0:T(8,128)(2,1)} %copy-done.17), custom_call_target="tpu_custom_call" | custom-call | flops 4000000000 | bytes 12000000 | tf_op jit(solution)/shard_map/pallas_call | solution.py:326
  271.0 3.8 %shard_map.273 = f32[256,1024]{1,0:T(8,128)} custom-call(s32[2]{0:T(128)} %pad_add_fusion.info, bf16[256,1024]{1,0:T(8,128)(2,1)} %block.1, bf16[256,1024]{1,0:T(8,128)(2,1)} %cot.3, f32[256,1024]{1,0:T(8,128)} %pad_maximum_fusion.4.upstream), custom_call_target="tpu_custom_call" | custom-call | flops 4000000000 | bytes 12000000 | tf_op jit(solution)/shard_map/pallas_call | solution.py:326
  (178 shorter events, 38.3 us)
Async XLA Ops:
  1.8 8.1 %collective-permute-start = (bf16[128,1024]{1,0:T(8,128)(2,1)S(1)}, bf16[128,1024]{1,0:T(8,128)(2,1)S(1)}, u32[]{:S(2)}, u32[]{:S(2)}) collective-permute-start(bf16[128,1024]{1,0:T(8,128)(2,1)S(1)} %get-tuple-element.163), channel_id=1, source_target_pairs={{0,16},{1,17},{2,18},{3,19},{4,20},{5,21},{6,22},{7,23},{8,24},{9,... | collective-permute-start | bytes 786440 | tf_op jit(solution)/shard_map/ppermute | solution.py:302
  3.1 8.5 %collective-permute-start.1 = (bf16[144,1024]{1,0:T(8,128)(2,1)S(1)}, bf16[144,1024]{1,0:T(8,128)(2,1)S(1)}, u32[]{:S(2)}, u32[]{:S(2)}) collective-permute-start(bf16[144,1024]{1,0:T(8,128)(2,1)S(1)} %get-tuple-element.166), channel_id=1, source_target_pairs={{0,2},{1,3},{2,0},{3,1},{4,6},{5,7},{6,4},{7,5},{8,10},{9,11},{10,... | collective-permute-start | bytes 884744 | tf_op jit(solution)/shard_map/ppermute | solution.py:302
  9.4 30.7 %copy-start.10 = (bf16[912,128]{1,0:T(8,128)(2,1)S(1)}, bf16[912,128]{1,0:T(8,128)(2,1)}, u32[]{:S(2)}) copy-start(bf16[912,128]{1,0:T(8,128)(2,1)} %get-tuple-element.76) | copy-start | bytes 700420
  12.5 29.5 %collective-permute-start.2 = (bf16[2,128,1024]{2,1,0:T(8,128)(2,1)}, bf16[2,128,1024]{2,1,0:T(8,128)(2,1)}, u32[]{:S(2)}, u32[]{:S(2)}) collective-permute-start(bf16[2,128,1024]{2,1,0:T(8,128)(2,1)} %pad_maximum_fusion.7), channel_id=1, source_target_pairs={{0,2},{1,3},{2,0},{3,1},{4,6},{5,7},{6,4},{7,5},{8,10},{9,11},{10,... | collective-permute-start | bytes 1572872 | tf_op jit(solution)/shard_map/ppermute | solution.py:302
  14.1 20.5 %collective-permute-start.6 = (bf16[912,128]{1,0:T(8,128)(2,1)}, bf16[912,128]{1,0:T(8,128)(2,1)S(1)}, u32[]{:S(2)}, u32[]{:S(2)}) collective-permute-start(bf16[912,128]{1,0:T(8,128)(2,1)} %get-tuple-element.79), channel_id=1, source_target_pairs={{0,6},{1,7},{2,4},{3,5},{4,2},{5,3},{6,0},{7,1},{8,14},{9,15},{10,... | collective-permute-start | bytes 700424 | tf_op jit(solution)/shard_map/ppermute | solution.py:302
  16.5 23.6 %collective-permute-start.4 = (bf16[912,128]{1,0:T(8,128)(2,1)}, bf16[912,128]{1,0:T(8,128)(2,1)S(1)}, u32[]{:S(2)}, u32[]{:S(2)}) collective-permute-start(bf16[912,128]{1,0:T(8,128)(2,1)} %get-tuple-element.79), channel_id=1, source_target_pairs={{0,2},{1,3},{2,0},{3,1},{4,6},{5,7},{6,4},{7,5},{8,10},{9,11},{10,... | collective-permute-start | bytes 700424 | tf_op jit(solution)/shard_map/ppermute | solution.py:302
  17.2 23.0 %collective-permute-start.5 = (bf16[912,128]{1,0:T(8,128)(2,1)}, bf16[912,128]{1,0:T(8,128)(2,1)}, u32[]{:S(2)}, u32[]{:S(2)}) collective-permute-start(bf16[912,128]{1,0:T(8,128)(2,1)} %get-tuple-element.76), channel_id=1, source_target_pairs={{0,4},{1,5},{2,6},{3,7},{4,0},{5,1},{6,2},{7,3},{8,12},{9,13},{10,... | collective-permute-start | bytes 700424 | tf_op jit(solution)/shard_map/ppermute | solution.py:302
  18.5 24.7 %collective-permute-start.3 = (bf16[2,144,1024]{2,1,0:T(8,128)(2,1)S(1)}, bf16[2,144,1024]{2,1,0:T(8,128)(2,1)S(1)}, u32[]{:S(2)}, u32[]{:S(2)}) collective-permute-start(bf16[2,144,1024]{2,1,0:T(8,128)(2,1)S(1)} %pad_maximum_fusion.6), channel_id=1, source_target_pairs={{0,16},{1,17},{2,18},{3,19},{4,20},{5,21},{6,22},{7,23},{8,24},{9,... | collective-permute-start | bytes 1769480 | tf_op jit(solution)/shard_map/ppermute | solution.py:302
  41.3 20.4 %collective-permute-start.11 = (bf16[4,912,128]{2,1,0:T(8,128)(2,1)S(1)}, bf16[4,912,128]{2,1,0:T(8,128)(2,1)S(1)}, u32[]{:S(2)}, u32[]{:S(2)}) collective-permute-start(bf16[4,912,128]{2,1,0:T(8,128)(2,1)S(1)} %pad_maximum_fusion.5.along), channel_id=1, source_target_pairs={{0,1},{1,0},{2,3},{3,2},{4,5},{5,4},{6,7},{7,6},{8,9},{9,8},{10,11... | collective-permute-start | bytes 2801672 | tf_op jit(solution)/shard_map/ppermute | solution.py:302
  43.6 21.7 %copy-start.8 = (bf16[4,272,1024]{2,1,0:T(8,128)(2,1)}, bf16[4,272,1024]{2,1,0:T(8,128)(2,1)S(1)}, u32[]{:S(2)}) copy-start(bf16[4,272,1024]{2,1,0:T(8,128)(2,1)S(1)} %constant_dynamic-update-slice_fusion.inputs) | copy-start | bytes 6684676
  43.6 38.7 %collective-permute-start.7 = (bf16[4,272,1024]{2,1,0:T(8,128)(2,1)S(1)}, bf16[4,272,1024]{2,1,0:T(8,128)(2,1)}, u32[]{:S(2)}, u32[]{:S(2)}) collective-permute-start(bf16[4,272,1024]{2,1,0:T(8,128)(2,1)S(1)} %constant_dynamic-update-slice_fusion.inputs), channel_id=1, source_target_pairs={{0,8},{1,9},{2,10},{3,11},{4,12},{5,13},{6,14},{7,15},{8,0},{9,1},... | collective-permute-start | bytes 6684680 | tf_op jit(solution)/shard_map/ppermute | solution.py:302
  44.3 35.3 %collective-permute-start.10 = (bf16[64,1024]{1,0:T(8,128)(2,1)S(1)}, bf16[64,1024]{1,0:T(8,128)(2,1)S(1)}, u32[]{:S(2)}, u32[]{:S(2)}) collective-permute-start(bf16[64,1024]{1,0:T(8,128)(2,1)S(1)} %copy-done.24), channel_id=1, source_target_pairs={{0,6},{1,7},{2,4},{3,5},{4,2},{5,3},{6,0},{7,1},{8,14},{9,15},{10,... | collective-permute-start | bytes 393224 | tf_op jit(solution)/shard_map/ppermute | solution.py:302
  47.7 31.8 %collective-permute-start.12 = (bf16[128,1024]{1,0:T(8,128)(2,1)S(1)}, bf16[128,1024]{1,0:T(8,128)(2,1)S(1)}, u32[]{:S(2)}, u32[]{:S(2)}) collective-permute-start(bf16[128,1024]{1,0:T(8,128)(2,1)S(1)} %get-tuple-element.90), channel_id=1, source_target_pairs={{0,16},{1,17},{2,18},{3,19},{4,20},{5,21},{6,22},{7,23},{8,24},{9,... | collective-permute-start | bytes 786440 | tf_op jit(solution)/shard_map/ppermute | solution.py:302
  49.2 30.3 %collective-permute-start.9 = (bf16[192,1024]{1,0:T(8,128)(2,1)S(1)}, bf16[192,1024]{1,0:T(8,128)(2,1)S(1)}, u32[]{:S(2)}, u32[]{:S(2)}) collective-permute-start(bf16[192,1024]{1,0:T(8,128)(2,1)S(1)} %copy-done.12), channel_id=1, source_target_pairs={{0,4},{1,5},{2,6},{3,7},{4,0},{5,1},{6,2},{7,3},{8,12},{9,13},{10,... | collective-permute-start | bytes 1179656 | tf_op jit(solution)/shard_map/ppermute | solution.py:302
  49.8 29.8 %copy-start.2 = (bf16[128,1024]{1,0:T(8,128)(2,1)S(1)}, bf16[128,1024]{1,0:T(8,128)(2,1)}, u32[]{:S(2)}) copy-start(bf16[128,1024]{1,0:T(8,128)(2,1)} %dense.1) | copy-start | bytes 786436
  62.6 16.8 %collective-permute-start.8 = (bf16[192,1024]{1,0:T(8,128)(2,1)S(1)}, bf16[192,1024]{1,0:T(8,128)(2,1)S(1)}, u32[]{:S(2)}, u32[]{:S(2)}) collective-permute-start(bf16[192,1024]{1,0:T(8,128)(2,1)S(1)} %copy-done.23), channel_id=1, source_target_pairs={{0,2},{1,3},{2,0},{3,1},{4,6},{5,7},{6,4},{7,5},{8,10},{9,11},{10,... | collective-permute-start | bytes 1179656 | tf_op jit(solution)/shard_map/ppermute | solution.py:302
  79.7 27.4 %collective-permute-start.14 = (bf16[2,128,1024]{2,1,0:T(8,128)(2,1)S(1)}, bf16[2,128,1024]{2,1,0:T(8,128)(2,1)S(1)}, u32[]{:S(2)}, u32[]{:S(2)}) collective-permute-start(bf16[2,128,1024]{2,1,0:T(8,128)(2,1)S(1)} %pad_maximum_fusion.8), channel_id=1, source_target_pairs={{0,2},{1,3},{2,0},{3,1},{4,6},{5,7},{6,4},{7,5},{8,10},{9,11},{10,... | collective-permute-start | bytes 1572872 | tf_op jit(solution)/shard_map/ppermute | solution.py:302
  79.8 27.5 %collective-permute-start.15 = (bf16[2,128,1024]{2,1,0:T(8,128)(2,1)S(1)}, bf16[2,128,1024]{2,1,0:T(8,128)(2,1)S(1)}, u32[]{:S(2)}, u32[]{:S(2)}) collective-permute-start(bf16[2,128,1024]{2,1,0:T(8,128)(2,1)S(1)} %pad_maximum_fusion.9), channel_id=1, source_target_pairs={{0,16},{1,17},{2,18},{3,19},{4,20},{5,21},{6,22},{7,23},{8,24},{9,... | collective-permute-start | bytes 1572872 | tf_op jit(solution)/shard_map/ppermute | solution.py:302
  81.3 19.2 %collective-permute-start.13 = (bf16[384,1024]{1,0:T(8,128)(2,1)S(1)}, bf16[384,1024]{1,0:T(8,128)(2,1)S(1)}, u32[]{:S(2)}, u32[]{:S(2)}) collective-permute-start(bf16[384,1024]{1,0:T(8,128)(2,1)S(1)} %fusion.15.along), channel_id=1, source_target_pairs={{0,1},{1,0},{2,3},{3,2},{4,5},{5,4},{6,7},{7,6},{8,9},{9,8},{10,11... | collective-permute-start | bytes 2359304 | tf_op jit(solution)/shard_map/ppermute | solution.py:302
  107.1 6.3 %collective-permute-start.16 = (bf16[4,256,1024]{2,1,0:T(8,128)(2,1)}, bf16[4,256,1024]{2,1,0:T(8,128)(2,1)S(1)}, u32[]{:S(2)}, u32[]{:S(2)}) collective-permute-start(bf16[4,256,1024]{2,1,0:T(8,128)(2,1)} %get-tuple-element.108), channel_id=1, source_target_pairs={{0,8},{1,9},{2,10},{3,11},{4,12},{5,13},{6,14},{7,15},{8,0},{9,1},... | collective-permute-start | bytes 6291464 | tf_op jit(solution)/shard_map/ppermute | solution.py:302
  107.6 10.4 %collective-permute-start.21 = (bf16[4,256,1024]{2,1,0:T(8,128)(2,1)S(1)}, bf16[4,256,1024]{2,1,0:T(8,128)(2,1)S(1)}, u32[]{:S(2)}, u32[]{:S(2)}) collective-permute-start(bf16[4,256,1024]{2,1,0:T(8,128)(2,1)S(1)} %constant_dynamic-update-slice_fusion.3.near), channel_id=1, source_target_pairs={{0,8},{1,9},{2,10},{3,11},{4,12},{5,13},{6,14},{7,15},{8,0},{9,1},... | collective-permute-start | bytes 6291464 | tf_op jit(solution)/shard_map/ppermute | solution.py:302
  140.6 15.1 %collective-permute-start.23 = (bf16[2048,128]{1,0:T(8,128)(2,1)}, bf16[2048,128]{1,0:T(8,128)(2,1)S(1)}, u32[]{:S(2)}, u32[]{:S(2)}) collective-permute-start(bf16[2048,128]{1,0:T(8,128)(2,1)} %get-tuple-element.127), channel_id=1, source_target_pairs={{0,1},{1,0},{2,3},{3,2},{4,5},{5,4},{6,7},{7,6},{8,9},{9,8},{10,11... | collective-permute-start | bytes 1572872 | tf_op jit(solution)/shard_map/ppermute | solution.py:302
  141.0 17.8 %collective-permute-start.17 = (bf16[2,128,1024]{2,1,0:T(8,128)(2,1)S(1)}, bf16[2,128,1024]{2,1,0:T(8,128)(2,1)S(1)}, u32[]{:S(2)}, u32[]{:S(2)}) collective-permute-start(bf16[2,128,1024]{2,1,0:T(8,128)(2,1)S(1)} %get-tuple-element.150), channel_id=1, source_target_pairs={{0,16},{1,17},{2,18},{3,19},{4,20},{5,21},{6,22},{7,23},{8,24},{9,... | collective-permute-start | bytes 1572872 | tf_op jit(solution)/shard_map/ppermute | solution.py:302
  141.6 17.2 %collective-permute-start.19 = (bf16[2,128,1024]{2,1,0:T(8,128)(2,1)S(1)}, bf16[2,128,1024]{2,1,0:T(8,128)(2,1)S(1)}, u32[]{:S(2)}, u32[]{:S(2)}) collective-permute-start(bf16[2,128,1024]{2,1,0:T(8,128)(2,1)S(1)} %get-tuple-element.151), channel_id=1, source_target_pairs={{0,2},{1,3},{2,0},{3,1},{4,6},{5,7},{6,4},{7,5},{8,10},{9,11},{10,... | collective-permute-start | bytes 1572872 | tf_op jit(solution)/shard_map/ppermute | solution.py:302
  144.2 27.4 %collective-permute-start.22 = (bf16[3072,128]{1,0:T(8,128)(2,1)S(1)}, bf16[3072,128]{1,0:T(8,128)(2,1)S(1)}, u32[]{:S(2)}, u32[]{:S(2)}) collective-permute-start(bf16[3072,128]{1,0:T(8,128)(2,1)S(1)} %copy-done.20), channel_id=1, source_target_pairs={{0,1},{1,0},{2,3},{3,2},{4,5},{5,4},{6,7},{7,6},{8,9},{9,8},{10,11... | collective-permute-start | bytes 2359304 | tf_op jit(solution)/shard_map/ppermute | solution.py:302
  156.9 33.6 %collective-permute-start.40 = (bf16[1024,128]{1,0:T(8,128)(2,1)S(1)}, bf16[1024,128]{1,0:T(8,128)(2,1)}, u32[]{:S(2)}, u32[]{:S(2)}) collective-permute-start(bf16[1024,128]{1,0:T(8,128)(2,1)S(1)} %slice.379), channel_id=1, source_target_pairs={{0,4},{1,5},{2,6},{3,7},{4,0},{5,1},{6,2},{7,3},{8,12},{9,13},{10,... | collective-permute-start | bytes 786440 | tf_op jit(solution)/shard_map/ppermute | solution.py:302
  160.8 29.5 %collective-permute-start.20 = (bf16[128,1024]{1,0:T(8,128)(2,1)S(1)}, bf16[128,1024]{1,0:T(8,128)(2,1)S(1)}, u32[]{:S(2)}, u32[]{:S(2)}) collective-permute-start(bf16[128,1024]{1,0:T(8,128)(2,1)S(1)} %fusion.11), channel_id=1, source_target_pairs={{0,16},{1,17},{2,18},{3,19},{4,20},{5,21},{6,22},{7,23},{8,24},{9,... | collective-permute-start | bytes 786440 | tf_op jit(solution)/shard_map/ppermute | solution.py:302
  161.5 28.9 %collective-permute-start.18 = (bf16[128,1024]{1,0:T(8,128)(2,1)S(1)}, bf16[128,1024]{1,0:T(8,128)(2,1)S(1)}, u32[]{:S(2)}, u32[]{:S(2)}) collective-permute-start(bf16[128,1024]{1,0:T(8,128)(2,1)S(1)} %fusion.10), channel_id=1, source_target_pairs={{0,2},{1,3},{2,0},{3,1},{4,6},{5,7},{6,4},{7,5},{8,10},{9,11},{10,... | collective-permute-start | bytes 786440 | tf_op jit(solution)/shard_map/ppermute | solution.py:302
  171.8 25.2 %collective-permute-start.24 = (bf16[2048,128]{1,0:T(8,128)(2,1)S(1)}, bf16[2048,128]{1,0:T(8,128)(2,1)S(1)}, u32[]{:S(2)}, u32[]{:S(2)}) collective-permute-start(bf16[2048,128]{1,0:T(8,128)(2,1)S(1)} %slice.378), channel_id=1, source_target_pairs={{0,4},{1,5},{2,6},{3,7},{4,0},{5,1},{6,2},{7,3},{8,12},{9,13},{10,... | collective-permute-start | bytes 1572872 | tf_op jit(solution)/shard_map/ppermute | solution.py:302
  189.4 21.5 %collective-permute-start.33 = (bf16[1600,128]{1,0:T(8,128)(2,1)}, bf16[1600,128]{1,0:T(8,128)(2,1)S(1)}, u32[]{:S(2)}, u32[]{:S(2)}) collective-permute-start(bf16[1600,128]{1,0:T(8,128)(2,1)} %get-tuple-element.132), channel_id=1, source_target_pairs={{0,1},{1,0},{2,3},{3,2},{4,5},{5,4},{6,7},{7,6},{8,9},{9,8},{10,11... | collective-permute-start | bytes 1228808 | tf_op jit(solution)/shard_map/ppermute | solution.py:302
  197.2 13.6 %collective-permute-start.27 = (bf16[512,128]{1,0:T(8,128)(2,1)S(1)}, bf16[512,128]{1,0:T(8,128)(2,1)S(1)}, u32[]{:S(2)}, u32[]{:S(2)}) collective-permute-start(bf16[512,128]{1,0:T(8,128)(2,1)S(1)} %get-tuple-element.154), channel_id=1, source_target_pairs={{0,18},{1,19},{2,16},{3,17},{4,22},{5,23},{6,20},{7,21},{8,26},{9,... | collective-permute-start | bytes 393224 | tf_op jit(solution)/shard_map/ppermute | solution.py:302
  197.2 9.6 %collective-permute-start.25 = (bf16[512,128]{1,0:T(8,128)(2,1)S(1)}, bf16[512,128]{1,0:T(8,128)(2,1)S(1)}, u32[]{:S(2)}, u32[]{:S(2)}) collective-permute-start(bf16[512,128]{1,0:T(8,128)(2,1)S(1)} %get-tuple-element.154), channel_id=1, source_target_pairs={{0,2},{1,3},{2,0},{3,1},{4,6},{5,7},{6,4},{7,5},{8,10},{9,11},{10,... | collective-permute-start | bytes 393224 | tf_op jit(solution)/shard_map/ppermute | solution.py:302
  199.3 11.4 %collective-permute-start.26 = (bf16[1536,128]{1,0:T(8,128)(2,1)S(1)}, bf16[1536,128]{1,0:T(8,128)(2,1)S(1)}, u32[]{:S(2)}, u32[]{:S(2)}) collective-permute-start(bf16[1536,128]{1,0:T(8,128)(2,1)S(1)} %slice.285), channel_id=1, source_target_pairs={{0,16},{1,17},{2,18},{3,19},{4,20},{5,21},{6,22},{7,23},{8,24},{9,... | collective-permute-start | bytes 1179656 | tf_op jit(solution)/shard_map/ppermute | solution.py:302
  206.9 15.0 %collective-permute-start.28 = (bf16[4,256,1024]{2,1,0:T(8,128)(2,1)}, bf16[4,256,1024]{2,1,0:T(8,128)(2,1)S(1)}, u32[]{:S(2)}, u32[]{:S(2)}) collective-permute-start(bf16[4,256,1024]{2,1,0:T(8,128)(2,1)} %shard_map.271), channel_id=1, source_target_pairs={{0,8},{1,9},{2,10},{3,11},{4,12},{5,13},{6,14},{7,15},{8,0},{9,1},... | collective-permute-start | bytes 6291464 | tf_op jit(solution)/shard_map/ppermute | solution.py:302
  210.9 6.3 %collective-permute-start.39 = (bf16[3072,128]{1,0:T(8,128)(2,1)S(1)}, bf16[3072,128]{1,0:T(8,128)(2,1)S(1)}, u32[]{:S(2)}, u32[]{:S(2)}) collective-permute-start(bf16[3072,128]{1,0:T(8,128)(2,1)S(1)} %fusion.14.near), channel_id=1, source_target_pairs={{0,8},{1,9},{2,10},{3,11},{4,12},{5,13},{6,14},{7,15},{8,0},{9,1},... | collective-permute-start | bytes 2359304 | tf_op jit(solution)/shard_map/ppermute | solution.py:302
  223.0 11.9 %collective-permute-start.34 = (bf16[800,128]{1,0:T(8,128)(2,1)S(1)}, bf16[800,128]{1,0:T(8,128)(2,1)S(1)}, u32[]{:S(2)}, u32[]{:S(2)}) collective-permute-start(bf16[800,128]{1,0:T(8,128)(2,1)S(1)} %slice.380), channel_id=1, source_target_pairs={{0,4},{1,5},{2,6},{3,7},{4,0},{5,1},{6,2},{7,3},{8,12},{9,13},{10,... | collective-permute-start | bytes 614408 | tf_op jit(solution)/shard_map/ppermute | solution.py:302
  223.2 23.4 %collective-permute-start.43 = (bf16[512,128]{1,0:T(8,128)(2,1)S(1)}, bf16[512,128]{1,0:T(8,128)(2,1)S(1)}, u32[]{:S(2)}, u32[]{:S(2)}) collective-permute-start(bf16[512,128]{1,0:T(8,128)(2,1)S(1)} %get-tuple-element.168), channel_id=1, source_target_pairs={{0,18},{1,19},{2,16},{3,17},{4,22},{5,23},{6,20},{7,21},{8,26},{9,... | collective-permute-start | bytes 393224 | tf_op jit(solution)/shard_map/ppermute | solution.py:302
  225.5 21.1 %collective-permute-start.41 = (bf16[512,128]{1,0:T(8,128)(2,1)S(1)}, bf16[512,128]{1,0:T(8,128)(2,1)S(1)}, u32[]{:S(2)}, u32[]{:S(2)}) collective-permute-start(bf16[512,128]{1,0:T(8,128)(2,1)S(1)} %get-tuple-element.168), channel_id=1, source_target_pairs={{0,2},{1,3},{2,0},{3,1},{4,6},{5,7},{6,4},{7,5},{8,10},{9,11},{10,... | collective-permute-start | bytes 393224 | tf_op jit(solution)/shard_map/ppermute | solution.py:302
  225.7 29.5 %collective-permute-start.29 = (bf16[2,128,1024]{2,1,0:T(8,128)(2,1)S(1)}, bf16[2,128,1024]{2,1,0:T(8,128)(2,1)S(1)}, u32[]{:S(2)}, u32[]{:S(2)}) collective-permute-start(bf16[2,128,1024]{2,1,0:T(8,128)(2,1)S(1)} %get-tuple-element.148), channel_id=1, source_target_pairs={{0,16},{1,17},{2,18},{3,19},{4,20},{5,21},{6,22},{7,23},{8,24},{9,... | collective-permute-start | bytes 1572872 | tf_op jit(solution)/shard_map/ppermute | solution.py:302
  226.9 28.4 %collective-permute-start.31 = (bf16[2,128,1024]{2,1,0:T(8,128)(2,1)S(1)}, bf16[2,128,1024]{2,1,0:T(8,128)(2,1)S(1)}, u32[]{:S(2)}, u32[]{:S(2)}) collective-permute-start(bf16[2,128,1024]{2,1,0:T(8,128)(2,1)S(1)} %get-tuple-element.149), channel_id=1, source_target_pairs={{0,2},{1,3},{2,0},{3,1},{4,6},{5,7},{6,4},{7,5},{8,10},{9,11},{10,... | collective-permute-start | bytes 1572872 | tf_op jit(solution)/shard_map/ppermute | solution.py:302
  235.0 9.2 %collective-permute-start.42 = (bf16[512,128]{1,0:T(8,128)(2,1)S(1)}, bf16[512,128]{1,0:T(8,128)(2,1)S(1)}, u32[]{:S(2)}, u32[]{:S(2)}) collective-permute-start(bf16[512,128]{1,0:T(8,128)(2,1)S(1)} %get-tuple-element.167), channel_id=1, source_target_pairs={{0,16},{1,17},{2,18},{3,19},{4,20},{5,21},{6,22},{7,23},{8,24},{9,... | collective-permute-start | bytes 393224 | tf_op jit(solution)/shard_map/ppermute | solution.py:302
  244.1 5.8 %collective-permute-start.35 = (bf16[400,128]{1,0:T(8,128)(2,1)S(1)}, bf16[400,128]{1,0:T(8,128)(2,1)S(1)}, u32[]{:S(2)}, u32[]{:S(2)}) collective-permute-start(bf16[400,128]{1,0:T(8,128)(2,1)S(1)} %get-tuple-element.171), channel_id=1, source_target_pairs={{0,2},{1,3},{2,0},{3,1},{4,6},{5,7},{6,4},{7,5},{8,10},{9,11},{10,... | collective-permute-start | bytes 307208 | tf_op jit(solution)/shard_map/ppermute | solution.py:302
  246.6 12.7 %collective-permute-start.44 = (bf16[2048,128]{1,0:T(8,128)(2,1)S(1)}, bf16[2048,128]{1,0:T(8,128)(2,1)S(1)}, u32[]{:S(2)}, u32[]{:S(2)}) collective-permute-start(bf16[2048,128]{1,0:T(8,128)(2,1)S(1)} %pad_maximum_fusion.10.near), channel_id=1, source_target_pairs={{0,8},{1,9},{2,10},{3,11},{4,12},{5,13},{6,14},{7,15},{8,0},{9,1},... | collective-permute-start | bytes 1572872 | tf_op jit(solution)/shard_map/ppermute | solution.py:302
  246.7 8.4 %collective-permute-start.37 = (bf16[400,128]{1,0:T(8,128)(2,1)S(1)}, bf16[400,128]{1,0:T(8,128)(2,1)S(1)}, u32[]{:S(2)}, u32[]{:S(2)}) collective-permute-start(bf16[400,128]{1,0:T(8,128)(2,1)S(1)} %get-tuple-element.171), channel_id=1, source_target_pairs={{0,18},{1,19},{2,16},{3,17},{4,22},{5,23},{6,20},{7,21},{8,26},{9,... | collective-permute-start | bytes 307208 | tf_op jit(solution)/shard_map/ppermute | solution.py:302
  249.9 5.2 %collective-permute-start.36 = (bf16[400,128]{1,0:T(8,128)(2,1)S(1)}, bf16[400,128]{1,0:T(8,128)(2,1)S(1)}, u32[]{:S(2)}, u32[]{:S(2)}) collective-permute-start(bf16[400,128]{1,0:T(8,128)(2,1)S(1)} %get-tuple-element.169), channel_id=1, source_target_pairs={{0,16},{1,17},{2,18},{3,19},{4,20},{5,21},{6,22},{7,23},{8,24},{9,... | collective-permute-start | bytes 307208 | tf_op jit(solution)/shard_map/ppermute | solution.py:302
  255.2 9.0 %collective-permute-start.38 = (bf16[1616,128]{1,0:T(8,128)(2,1)S(1)}, bf16[1616,128]{1,0:T(8,128)(2,1)S(1)}, u32[]{:S(2)}, u32[]{:S(2)}) collective-permute-start(bf16[1616,128]{1,0:T(8,128)(2,1)S(1)} %get-tuple-element.138.near), channel_id=1, source_target_pairs={{0,8},{1,9},{2,10},{3,11},{4,12},{5,13},{6,14},{7,15},{8,0},{9,1},... | collective-permute-start | bytes 1241096 | tf_op jit(solution)/shard_map/ppermute | solution.py:302
  256.0 13.7 %collective-permute-start.32 = (bf16[128,1024]{1,0:T(8,128)(2,1)S(1)}, bf16[128,1024]{1,0:T(8,128)(2,1)S(1)}, u32[]{:S(2)}, u32[]{:S(2)}) collective-permute-start(bf16[128,1024]{1,0:T(8,128)(2,1)S(1)} %fusion.13), channel_id=1, source_target_pairs={{0,16},{1,17},{2,18},{3,19},{4,20},{5,21},{6,22},{7,23},{8,24},{9,... | collective-permute-start | bytes 786440 | tf_op jit(solution)/shard_map/ppermute | solution.py:302
  257.5 12.4 %collective-permute-start.30 = (bf16[128,1024]{1,0:T(8,128)(2,1)S(1)}, bf16[128,1024]{1,0:T(8,128)(2,1)S(1)}, u32[]{:S(2)}, u32[]{:S(2)}) collective-permute-start(bf16[128,1024]{1,0:T(8,128)(2,1)S(1)} %fusion.12), channel_id=1, source_target_pairs={{0,2},{1,3},{2,0},{3,1},{4,6},{5,7},{6,4},{7,5},{8,10},{9,11},{10,... | collective-permute-start | bytes 786440 | tf_op jit(solution)/shard_map/ppermute | solution.py:302
  (22 other events, 135.9 us)

commit v3 on v2

--- a/solution.py
+++ b/solution.py
@@ -288,7 +288,10 @@
 FEED_ROWS = 2 * HIDDEN
 F32 = jnp.float32
 BF16 = jnp.bfloat16
-VMEM_LIMIT = 56 * 1024 * 1024
+COST = 4000
+VMEM_LIMIT = 18 * 1024 * 1024
+VMEM_FIRST = 36 * 1024 * 1024
+VMEM_WHOLE = 56 * 1024 * 1024
 
 
 def permute(value, target):
@@ -322,7 +325,7 @@
     return pl.BlockSpec(shape, lambda *_: (0,) * len(shape))
 
 
-def call(body, info, operands, in_specs, outs, out_specs, grid=(1,), scratch=(), aliases=None, micros=4):
+def call(body, info, operands, in_specs, outs, out_specs, grid=(1,), scratch=(), micros=4, vmem=VMEM_LIMIT):
     return pl.pallas_call(
         body,
         grid_spec=pltpu.PrefetchScalarGridSpec(
@@ -333,9 +336,8 @@
             scratch_shapes=list(scratch),
         ),
         out_shape=[jax.ShapeDtypeStruct(shape, dtype) for shape, dtype in outs],
-        input_output_aliases=aliases or {},
-        compiler_params=pltpu.CompilerParams(vmem_limit_bytes=VMEM_LIMIT),
-        cost_estimate=pl.CostEstimate(flops=micros * 10**9, bytes_accessed=micros * 3 * 10**6, transcendentals=0),
+        compiler_params=pltpu.CompilerParams(vmem_limit_bytes=vmem),
+        cost_estimate=pl.CostEstimate(flops=micros * COST * 10**6, bytes_accessed=micros * COST * 3 * 10**3, transcendentals=0),
     )(info, *operands)
 
 
@@ -350,8 +352,8 @@
     return pl.ds(pl.multiple_of(index * unit, unit), unit)
 
 
-def cut_body(info, mix, expand, shrink, dense, cot, *rest):
-    vectors, (own, other, own_last, other_last, other_shrink), small = rest[:8], rest[8:13], rest[13]
+def cut_body(info, mix, expand, *rest):
+    vectors, (own, other), small = rest[:8], rest[8:10], rest[10]
     row = 0
     small[...] = jnp.zeros_like(small)
     for vector in vectors:
@@ -371,19 +373,10 @@
             second = jnp.where(upper, second, pltpu.roll(second, 64, 1))
             joined = jnp.where(lane < 64, first, second).astype(BF16)
             out[MIX_ROWS + pair * LANES : MIX_ROWS + (pair + 1) * LANES, :] = joined
-    rows = cot.shape[0] // 2
-    own_last[:64, :] = shrink[aligned(info[1], 64), :]
-    own_last[64:, :] = dense[...]
-    other_shrink[...] = shrink[aligned(info[1] ^ 2, 64), :]
-    other_last[:64, :] = other_shrink[...]
-    other_last[64:, :] = cot[rows:, :]
-
-
-def cut_slices(info, mix, expand, shrink, dense, cot, vectors):
-    operands = [mix, expand, shrink, dense, cot] + [vector.reshape(-1, LANES) for vector in vectors]
-    width = shrink.shape[1]
+
+def cut_slices(info, mix, expand, vectors):
+    operands = [mix, expand] + [vector.reshape(-1, LANES) for vector in vectors]
     outs = [((FIRST_ROWS, LANES), BF16)] * 2
-    outs += [((64 + rows, width), BF16) for rows in (dense.shape[0], cot.shape[0] // 2, 0)]
     return call(
         cut_body,
         info,
@@ -392,6 +385,54 @@
         outs,
         [whole(shape) for shape, _ in outs],
         scratch=[pltpu.VMEM((SMALL, LANES), F32)],
+        vmem=VMEM_WHOLE,
+    )
+
+
+def cut_last_body(info, shrink, dense, cot, own, other, other_shrink):
+    rows = cot.shape[0] // 2
+    own[:64, :] = shrink[aligned(info[1], 64), :]
+    own[64:, :] = dense[...]
+    rest = shrink[aligned(info[1] ^ 2, 64), :]
+    other_shrink[...] = rest
+    other[:64, :] = rest
+    other[64:, :] = cot[rows:, :]
+
+
+def cut_last(info, shrink, dense, cot):
+    operands = [shrink, dense, cot]
+    shapes = [(64 + rows, shrink.shape[1]) for rows in (dense.shape[0], cot.shape[0] // 2, 0)]
+    return call(
+        cut_last_body,
+        info,
+        operands,
+        [whole(operand.shape) for operand in operands],
+        [(shape, BF16) for shape in shapes],
+        [whole(shape) for shape in shapes],
+        vmem=VMEM_WHOLE,
+    )
+
+
+def pack_body(info, own, low, high, both, dense, out, dense_high):
+    out[:64, :] = own[:64, :]
+    out[64:128, :] = low[:64, :]
+    out[128:192, :] = high[:64, :]
+    out[192:256, :] = both[...]
+    same = info[1] // 4 == info[0] // 4
+    out[256:, :] = jnp.where(same, dense[...], high[64:, :])
+    dense_high[...] = out[256:, :]
+
+
+def pack_last(info, own, low, high, both, dense):
+    operands = [own, low, high, both, dense]
+    shapes = [(256 + dense.shape[0], dense.shape[1]), dense.shape]
+    return call(
+        pack_body,
+        info,
+        operands,
+        [whole(operand.shape) for operand in operands],
+        [(shape, BF16) for shape in shapes],
+        [whole(shape) for shape in shapes],
     )
 
 
@@ -410,24 +451,30 @@
 
 
 def gelu_parts(hidden):
-    bell = jnp.exp(hidden * hidden * -0.5)
-    point = 1.0 / (1.0 + (0.3275911 * 0.5**0.5) * jnp.abs(hidden))
-    series = 1.061405429 * point - 1.453152027
-    for factor in (1.421413741, -0.284496736, 0.254829592):
-        series = series * point + factor
-    tail = 0.5 * series * point * bell
-    normal = jnp.where(hidden < 0.0, tail, 1.0 - tail)
-    return normal, hidden * bell * ((2.0 * np.pi) ** -0.5)
-
-
-def near_forward_body(info, inputs, along, across, frequency, *outs):
+    normal = 0.5 + 0.5 * lax.erf(hidden * (0.5**0.5))
+    return normal, hidden * jnp.exp(hidden * hidden * -0.5) * ((2.0 * np.pi) ** -0.5)
+
+
+def by_head(rows, lane):
+    return jnp.concatenate([jnp.where(lane < HEAD, rows, 0), jnp.where(lane < HEAD, 0, rows)]).astype(BF16)
+
+
+def from_heads(rows, lane):
+    tokens = rows.shape[0] // 2
+    return jnp.where(lane < HEAD, rows[:tokens], rows[tokens:])
+
+
+def near_forward_body(info, inputs, own, over, along, across, frequency, *outs):
     mix, expand, vectors, bias = outs[7:]
     shard, rank = info[0], info[1]
 
     @pl.when(pl.program_id(0) == 0)
     def _():
         for number in range(8):
-            piece = (across if number % 2 else along).at[number // 2]
+            if number < 2:
+                piece = over if number else own
+            else:
+                piece = (across if number % 2 else along).at[number // 2 - 1]
             block = aligned(shard ^ number, LANES)
             for part in range(3):
                 mix[block, part * LANES : (part + 1) * LANES] = piece[part * LANES : (part + 1) * LANES, :]
@@ -459,8 +506,8 @@
     forward_step(inputs, frequency, mix, expand, vectors, bias, *outs[:7])
 
 
-def far_forward_body(info, inputs, mix, expand, vectors, bias, frequency, *rest):
-    forward_step(inputs, frequency, mix, expand, vectors, bias, *rest[7:])
+def far_forward_body(info, inputs, mix, expand, vectors, bias, frequency, *outs):
+    forward_step(inputs, frequency, mix, expand, vectors, bias, *outs)
 
 
 def forward_step(
@@ -500,21 +547,18 @@
         heads_out[sequence, :, :LANES] = queries
         heads_out[sequence, :, LANES : 2 * LANES] = keys
         heads_out[sequence, :, 2 * LANES :] = values
-        context = jnp.zeros((tokens, LANES), F32)
-        for head in range(2):
-            chosen = lane // HEAD == head
-            scores = nt(jnp.where(chosen, queries, 0).astype(BF16), keys) * HEAD ** (-0.5)
-            scores = jnp.where(allowed, scores, -1e30)
-            weights = jnp.exp(scores - jnp.max(scores, axis=-1, keepdims=True))
-            probs = weights * (1.0 / jnp.sum(weights, axis=-1, keepdims=True))
-            probs_out[sequence, head] = probs
-            context = context + nn(probs.astype(BF16), jnp.where(chosen, values, 0).astype(BF16))
-        context_out[sequence] = context.astype(BF16)
+        scores = nt(by_head(queries * HEAD ** (-0.5), lane), keys)
+        scores = jnp.where(jnp.concatenate([allowed, allowed]), scores, -1e30)
+        weights = jnp.exp(scores - jnp.max(scores, axis=-1, keepdims=True))
+        probs = weights * (1.0 / jnp.sum(weights, axis=-1, keepdims=True))
+        probs = probs.astype(BF16)
+        probs_out[sequence] = probs.reshape(2, tokens, tokens)
+        context_out[sequence] = from_heads(nn(probs, values), lane).astype(BF16)
 
     hidden = nn(two, expand[...]) + bias[0:1, :]
     normal, slope = gelu_parts(hidden)
     act_out[...] = (hidden * normal).astype(BF16).reshape(act_out.shape)
-    slope_out[...] = (normal + slope).reshape(slope_out.shape)
+    slope_out[...] = (normal + slope).astype(BF16).reshape(slope_out.shape)
 
 
 def turn_constants():
@@ -529,29 +573,27 @@
     return frequency
 
 
-def forward(info, inputs, weights, frequency, tokens, width, held=None):
-    far = held is not None
+def forward(info, inputs, weights, frequency, tokens, width, far=False):
+    count = inputs.shape[0]
     outs = [
-        ((GROUP, tokens, width), BF16),
-        ((GROUP, tokens, MIX_COLS), BF16),
-        ((GROUP, 2 * 8, tokens), F32),
-        ((GROUP, 2, tokens, tokens), F32),
-        ((GROUP, tokens, LANES), BF16),
-        ((GROUP, tokens, HIDDEN), BF16),
-        ((GROUP, tokens, HIDDEN), F32),
+        ((count, tokens, width), BF16),
+        ((count, tokens, MIX_COLS), BF16),
+        ((count, 2 * 8, tokens), F32),
+        ((count, 2, tokens, tokens), BF16),
+        ((count, tokens, LANES), BF16),
+        ((count, tokens, HIDDEN), BF16),
+        ((count, tokens, HIDDEN), BF16),
     ]
     fixed = [((width, MIX_COLS), BF16), ((width, HIDDEN), BF16), ((SMALL, width), F32), ((8, HIDDEN), F32)]
     operands = [inputs] + list(weights) + [frequency]
     in_specs = [pairs(inputs.shape)] + [whole(operand.shape) for operand in operands[1:]]
-    out_specs = [pairs(shape, 2 * far) for shape, _ in outs]
+    out_specs = [pairs(shape) for shape, _ in outs]
     if far:
-        aliases = {1 + len(operands) + number: number for number in range(len(outs))}
-        in_specs += [pl.BlockSpec(memory_space=pl.ANY)] * len(outs)
-        return call(
-            far_forward_body, info, operands + list(held), in_specs, outs, out_specs, grid=(2,), aliases=aliases, micros=10
-        )
+        return call(far_forward_body, info, operands, in_specs, outs, out_specs, grid=(2,), micros=9)
     out_specs += [whole(shape) for shape, _ in fixed]
-    return call(near_forward_body, info, operands, in_specs, outs + fixed, out_specs, grid=(2,), micros=10)
+    return call(
+        near_forward_body, info, operands, in_specs, outs + fixed, out_specs, grid=(2,), micros=9, vmem=VMEM_FIRST
+    )
 
 
 def pairs(shape, first=0):
@@ -579,25 +621,12 @@
 def project(info, context, act, dense, shrink, far):
     tokens, width = context.shape[1], dense.shape[1]
     operands = [context, act, dense] + (list(shrink) if far else [shrink])
-    in_specs = [pairs(context.shape, 2 * far), pairs(act.shape, 2 * far)]
+    in_specs = [pairs(context.shape), pairs(act.shape)]
     in_specs += [whole(operand.shape) for operand in operands[2:]]
     outs = [((4, tokens, width), BF16)] + [((HIDDEN, width), BF16)] * far
     out_specs = [pairs(outs[0][0])] + [whole((HIDDEN, width))] * far
     body = far_project_body if far else near_project_body
     return call(body, info, operands, in_specs, outs, out_specs, grid=(2,), micros=5)
-
-
-def halves(near, far):
-    block = (2,) + near.shape[1:]
-    return [
-        pl.BlockSpec(block, lambda i, _: (jnp.minimum(i, 1), 0, 0)),
-        pl.BlockSpec(block, lambda i, _: (jnp.maximum(i - 2, 0), 0, 0)),
-    ]
-
-
-def chosen_half(near, far):
-    rows = jnp.where(pl.program_id(0) < 2, near[...], far[...])
-    return rows.reshape(rows.shape[0] * rows.shape[1], rows.shape[2])
 
 
 def flat(ref):
@@ -619,134 +648,182 @@
         yield info[0] ^ (2 * z + 1), other.at[rows]
 
 
-def last_grad_body(info, near, far, act, context, mine, other, total, dense_total):
-    clear(total, dense_total)
-    cot = chosen_half(near, far)
-    total[...] += tn(flat(act), cot)
-    dense_total[...] += tn(flat(context), cot)
-
-    @pl.when(pl.program_id(0) == 3)
-    def _():
-        shrink_rows = 4 * HIDDEN
+def last_grad_body(info, near, far, act, far_act, context, far_context, mine, other, total, dense_total):
+    step = pl.program_id(0)
+    total[...] = tn(act[...], near[...]) + tn(far_act[...], far[...])
+    dense_total[...] = tn(context[...], near[...]) + tn(far_context[...], far[...])
+    shrink_rows = 4 * HIDDEN
+    for part in range(2):
+        cols = slice(part * LANES, (part + 1) * LANES)
         for shard, out in each_shard(info, mine.at[:shrink_rows], other.at[:shrink_rows]):
-            for part in range(8):
-                rows = total[aligned(shard, 64), part * LANES : (part + 1) * LANES]
-                out[64 * part : 64 * (part + 1), :] = rows.astype(BF16)
-        for part in range(8):
-            start = shrink_rows + LANES * part
-            block = dense_total[:, part * LANES : (part + 1) * LANES].astype(BF16)
-            mine[start : start + LANES, :] = block
-            other[start : start + LANES, :] = block
+            out[pl.ds(pl.multiple_of(64 * (2 * step + part), 64), 64), :] = total[aligned(shard, 64), cols].astype(BF16)
+        block = dense_total[:, cols].astype(BF16)
+        rows = pl.ds(pl.multiple_of(shrink_rows + LANES * (2 * step + part), LANES), LANES)
+        mine[rows, :] = block
+        other[rows, :] = block
 
 
 def last_backward(info, near, far, act, context):
-    width = near.shape[2]
+    operands = [array.reshape(-1, array.shape[2]) for array in (near, far) + act + context]
+    near = operands[0]
+    width = near.shape[1]
     outs = [((4 * HIDDEN + width, LANES), BF16)] * 2
+    columns = pl.BlockSpec((near.shape[0], 2 * LANES), lambda i, _: (0, i))
     return call(
         last_grad_body,
         info,
-        [near, far, act, context],
-        halves(near, far) + [pairs(act.shape), pairs(context.shape)],
+        operands,
+        [columns, columns] + [whole(operand.shape) for operand in operands[2:]],
         outs,
         [whole(shape) for shape, _ in outs],
-        grid=(4,),
-        scratch=[pltpu.VMEM((HIDDEN, width), F32), pltpu.VMEM((LANES, width), F32)],
-        micros=8,
-    )
-
-
-def norm_products(total, column, weight, gain, shift):
-    lines = as_columns(weight)
-    column = column[:, 0:1]
-    grad = total * gain + column * shift
-    return grad, jnp.sum(lines * total, axis=0, keepdims=True), jnp.sum(lines * column, axis=0, keepdims=True)
+        grid=(width // (2 * LANES),),
+        scratch=[pltpu.VMEM((HIDDEN, 2 * LANES), F32), pltpu.VMEM((LANES, 2 * LANES), F32)],
+        micros=5,
+    )
+
+
+def as_column(row):
+    size = row.shape[1]
+    high = row.astype(BF16)
+    middle = (row - high.astype(F32)).astype(BF16)
+    low = (row - high.astype(F32) - middle.astype(F32)).astype(BF16)
+    parts = jnp.concatenate([jnp.broadcast_to(part, (16, size)) for part in (high, middle, low)])
+    first = lax.broadcasted_iota(jnp.int32, (48, LANES), 0) % 16 == 0
+    return tn(parts, first.astype(BF16))
+
+
+def norm_products(block, grads, normed, far_normed, column, weight, vectors, row, total, sums):
+    count = normed.shape[0]
+    products = tn(grads[:count, :], normed[...]) + tn(grads[count:, :], far_normed[...])
+    lines = as_columns(weight[block, :])
+    shifts = column[:, 0:1]
+    total[:, block] = products * vectors[row : row + 1, block] + shifts * vectors[row + 1 : row + 2, block]
+    sums[0:1, block] = jnp.sum(lines * products, axis=0, keepdims=True)
+    sums[1:2, block] = jnp.sum(lines * shifts, axis=0, keepdims=True)
 
 
 def expand_grad_body(
-    info, near, far, slope, normed, shrink, expand, vectors, pre_out, bias_out, sums, mine, other, total, column
+    info, near, far, slope, far_slope, normed, far_normed, shrink, expand, vectors, pre_out, bias_out, sums, mine, other, held, total, column
 ):
-    clear(total, column, bias_out, sums)
-    grad_act = nt(chosen_half(near, far), shrink[...])
-    grad_pre = (grad_act * flat(slope)).astype(BF16)
-    pre_out[...] = grad_pre.reshape(pre_out.shape)
-    bias_out[...] += jnp.broadcast_to(jnp.sum(grad_pre.astype(F32), axis=0, keepdims=True), bias_out.shape)
-    total[...] += tn(grad_pre, flat(normed))
-    column[...] += tn(grad_pre, jnp.ones((grad_pre.shape[0], LANES), BF16))
-
-    @pl.when(pl.program_id(0) == 3)
+    step = pl.program_id(0)
+    clear(bias_out, sums)
+
+    @pl.when(step < 4)
     def _():
-        grad, sums[0:1, :], sums[1:2, :] = norm_products(
-            total[...], column, expand[...], vectors[2:3, :], vectors[3:4, :]
-        )
-        total[...] = grad
+        cot = jnp.where(step < 2, near[...], far[...])
+        grad_act = nt(cot.reshape(cot.shape[0] * cot.shape[1], cot.shape[2]), shrink[...])
+        slopes = jnp.where(step < 2, slope[...], far_slope[...]).reshape(grad_act.shape).astype(F32)
+        grad_pre = (grad_act * slopes).astype(BF16)
+        pre_out[...] = grad_pre.reshape(pre_out.shape)
+        held[pl.ds(pl.multiple_of(step * grad_pre.shape[0], grad_pre.shape[0]), grad_pre.shape[0]), :] = grad_pre
+        bias_out[...] += jnp.broadcast_to(jnp.sum(grad_pre.astype(F32), axis=0, keepdims=True), bias_out.shape)
+
+    @pl.when(step == 3)
+    def _():
+        column[...] = as_column(bias_out[0:1, :])
+
+    @pl.when(step >= 4)
+    def _():
+        block = aligned(step - 4, 2 * LANES)
+        norm_products(block, held, normed, far_normed, column, expand, vectors, 2, total, sums)
+
+    @pl.when(step == 7)
+    def _():
         for shard, out in each_shard(info, mine, other):
             out[...] = total[:, aligned(shard, LANES)].astype(BF16)
 
 
+def two_phases(pair):
+    shape = pair[0].shape
+    block, rest = (2,) + shape[1:], (0,) * (len(shape) - 1)
+    return [
+        pl.BlockSpec(block, lambda i, _: (jnp.minimum(i, 1),) + rest),
+        pl.BlockSpec(block, lambda i, _: (jnp.clip(i - 2, 0, 1),) + rest),
+    ]
+
+
+def all_tokens(rows):
+    return [pl.BlockSpec((rows, 2 * LANES), lambda i, _: (0, jnp.maximum(i - 4, 0)))] * 2
+
+
+def in_first_phase(shape):
+    rest = (0,) * (len(shape) - 1)
+    return pl.BlockSpec((2,) + shape[1:], lambda i, _: (jnp.minimum(i, 3),) + rest)
+
+
 def expand_backward(info, near, far, slope, normed, shrink, expand, vectors):
     tokens, width = near.shape[1:]
-    operands = [near, far, slope, normed, shrink, expand, vectors]
-    in_specs = halves(near, far) + [pairs(slope.shape), pairs(normed.shape)]
-    in_specs += [whole(operand.shape) for operand in operands[4:]]
+    columns = [half.reshape(-1, width) for half in normed]
+    operands = [near, far, *slope, *columns, shrink, expand, vectors]
+    in_specs = two_phases((near, far)) + two_phases(slope) + all_tokens(columns[0].shape[0])
+    in_specs += [whole(operand.shape) for operand in operands[6:]]
     outs = [((GROUP, tokens, HIDDEN), BF16), ((8, HIDDEN), F32), ((8, width), F32)] + [((4 * HIDDEN, LANES), BF16)] * 2
-    out_specs = [pairs(outs[0][0])] + [whole(shape) for shape, _ in outs[1:]]
-    scratch = [pltpu.VMEM((HIDDEN, width), F32), pltpu.VMEM((HIDDEN, LANES), F32)]
-    return call(expand_grad_body, info, operands, in_specs, outs, out_specs, grid=(4,), scratch=scratch, micros=12)
+    out_specs = [in_first_phase(outs[0][0])] + [whole(shape) for shape, _ in outs[1:]]
+    scratch = [
+        pltpu.VMEM((GROUP * tokens, HIDDEN), BF16),
+        pltpu.VMEM((HIDDEN, width), F32),
+        pltpu.VMEM((HIDDEN, LANES), F32),
+    ]
+    return call(expand_grad_body, info, operands, in_specs, outs, out_specs, grid=(8,), scratch=scratch, micros=9)
 
 
 def attention_grad_body(
-    info, near, far, normed, heads, tables, probs, dense, mix, vectors, bias_grad, feed_sums, frequency,
-    mixed_out, mine, other, total, column, sums, piece,
+    info, near, far, normed, far_normed, heads, far_heads, tables, far_tables, probs, far_probs,
+    dense, frequency, mix, vectors, bias_grad, feed_sums,
+    mixed_out, mine, other, mixed_held, total, column, sums, piece,
 ):
     step = pl.program_id(0)
     rank = info[1]
     tokens = near.shape[1]
-    clear(total, column, sums)
-    cot = chosen_half(near, far)
-    lane = lax.broadcasted_iota(jnp.int32, (tokens, LANES), 1)
-    grad_context = nt(cot, dense[...]).astype(BF16)
-    grad_mixed = []
-    for sequence in range(2):
-        queries = heads[sequence, :, :LANES]
-        keys = heads[sequence, :, LANES : 2 * LANES]
-        values = heads[sequence, :, 2 * LANES :]
-        grad_queries = jnp.zeros((tokens, LANES), F32)
-        grad_keys = jnp.zeros((tokens, LANES), F32)
-        grad_values = jnp.zeros((tokens, LANES), F32)
-        for head in range(2):
-            chosen = lane // HEAD == head
-            exact = probs[sequence, head]
-            part = grad_context[sequence * tokens : (sequence + 1) * tokens]
-            part = jnp.where(chosen, part, 0).astype(BF16)
+    clear(sums)
+
+    @pl.when(step == 0)
+    def _():
+        sums[4:5, :] = jnp.sum(near[0].astype(F32), axis=0, keepdims=True)
+
+    @pl.when(step < 4)
+    def _():
+        cot = jnp.where(step < 2, near[...], far[...])
+        all_heads = jnp.where(step < 2, heads[...], far_heads[...])
+        all_tables = jnp.where(step < 2, tables[...], far_tables[...])
+        all_probs = jnp.where(step < 2, probs[...], far_probs[...])
+        lane = lax.broadcasted_iota(jnp.int32, (tokens, LANES), 1)
+        grad_context = nt(cot.reshape(2 * tokens, cot.shape[2]), dense[...]).astype(BF16)
+        for sequence in range(2):
+            queries = all_heads[sequence, :, :LANES]
+            keys = all_heads[sequence, :, LANES : 2 * LANES]
+            values = all_heads[sequence, :, 2 * LANES :]
+            part = by_head(grad_context[sequence * tokens : (sequence + 1) * tokens], lane)
+            low = all_probs[sequence].reshape(2 * tokens, tokens)
+            exact = low.astype(F32)
             grad_probs = nt(part, values)
             grad_scores = exact * (grad_probs - jnp.sum(exact * grad_probs, axis=-1, keepdims=True))
             grad_scores = grad_scores.astype(BF16)
-            grad_values = grad_values + tn(exact.astype(BF16), part)
-            grad_queries = grad_queries + nn(grad_scores, jnp.where(chosen, keys, 0).astype(BF16))
-            grad_keys = grad_keys + tn(grad_scores, jnp.where(chosen, queries, 0).astype(BF16))
-        cos, sin = spread_tables(tables[sequence], frequency)
-        joined = [
-            turn(grad_queries * HEAD ** (-0.5), cos, -sin, lane),
-            turn(grad_keys * HEAD ** (-0.5), cos, -sin, lane),
-            grad_values,
-        ]
-        grad_mixed.append(jnp.concatenate(joined, axis=1).astype(BF16))
-    grad_mixed = jnp.concatenate(grad_mixed, axis=0)
-    mixed_out[...] = grad_mixed.reshape(mixed_out.shape)
-    total[...] += tn(grad_mixed, flat(normed))
-    column[...] += tn(grad_mixed, jnp.ones((grad_mixed.shape[0], LANES), BF16))
-    sums[5:6, :MIX_COLS] += jnp.sum(grad_mixed.astype(F32), axis=0, keepdims=True)
-
-    @pl.when(step == 0)
-    def _():
-        sums[4:5, :] = jnp.sum(near[0].astype(F32), axis=0, keepdims=True)
+            grad_values = tn(low, part)
+            grad_queries = from_heads(nn(grad_scores, keys), lane)
+            grad_keys = tn(grad_scores, by_head(queries, lane))
+            cos, sin = spread_tables(all_tables[sequence], frequency)
+            joined = [
+                turn(grad_queries * HEAD ** (-0.5), cos, -sin, lane),
+                turn(grad_keys * HEAD ** (-0.5), cos, -sin, lane),
+                grad_values,
+            ]
+            grad_mixed = jnp.concatenate(joined, axis=1).astype(BF16)
+            mixed_out[sequence] = grad_mixed
+            mixed_held[pl.ds(pl.multiple_of((2 * step + sequence) * tokens, tokens), tokens), :] = grad_mixed
+            sums[5:6, :MIX_COLS] += jnp.sum(grad_mixed.astype(F32), axis=0, keepdims=True)
 
     @pl.when(step == 3)
     def _():
-        grad, sums[0:1, :], sums[1:2, :] = norm_products(
-            total[...], column, mix[...], vectors[0:1, :], vectors[1:2, :]
-        )
-        total[...] = grad
+        column[...] = as_column(sums[5:6, :MIX_COLS])
+
+    @pl.when(step >= 4)
+    def _():
+        block = aligned(step - 4, 2 * LANES)
+        norm_products(block, mixed_held, normed, far_normed, column, mix, vectors, 0, total, sums)
+
+    @pl.when(step == 7)
+    def _():
         sums[2:4, :] = feed_sums[0:2, :]
         line = lax.broadcasted_iota(jnp.int32, (8, LANES), 1)
         for shard, out in each_shard(info, mine, other):
@@ -769,20 +846,29 @@
             out[MIX_COLS:, :] = piece[...].astype(BF16)
 
 
-def attention_backward(info, near, far, saved, dense, fixed):
+def attention_backward(info, near, far, saved, fixed):
     tokens, width = near.shape[1:]
-    operands = [near, far] + list(saved) + [dense] + list(fixed)
-    in_specs = halves(near, far) + [pairs(operand.shape) for operand in saved]
-    in_specs += [whole(operand.shape) for operand in operands[2 + len(saved) :]]
+    normed, *saved = saved
+    columns = [half.reshape(-1, width) for half in normed]
+    operands = [near, far, *columns]
+    in_specs = two_phases((near, far)) + all_tokens(columns[0].shape[0])
+    for pair in saved:
+        operands += pair
+        in_specs += two_phases(pair)
+    operands += list(fixed)
+    in_specs += [whole(operand.shape) for operand in fixed]
     outs = [((GROUP, tokens, MIX_COLS), BF16)] + [((4 * MIX_ROWS, LANES), BF16)] * 2
-    out_specs = [pairs(outs[0][0])] + [whole(shape) for shape, _ in outs[1:]]
+    out_specs = [in_first_phase(outs[0][0])] + [whole(shape) for shape, _ in outs[1:]]
     scratch = [
+        pltpu.VMEM((GROUP * tokens, MIX_COLS), BF16),
         pltpu.VMEM((MIX_COLS, width), F32),
         pltpu.VMEM((MIX_COLS, LANES), F32),
         pltpu.VMEM((8, width), F32),
         pltpu.VMEM((SMALL, LANES), F32),
     ]
-    return call(attention_grad_body, info, operands, in_specs, outs, out_specs, grid=(4,), scratch=scratch, micros=14)
+    return call(
+        attention_grad_body, info, operands, in_specs, outs, out_specs, grid=(8,), scratch=scratch, micros=13
+    )
 
 
 def input_grad_body(info, mixed, pre, mix, expand, vectors, out):
@@ -799,13 +885,15 @@
     return call(input_grad_body, info, operands, in_specs, [(shape, BF16)], [pairs(shape)], grid=(2,), micros=6)[0]
 
 
-def norm_body(info, block, cot, upstream, out):
+def norm_body(info, block, cot, upper, upper_got, lower, lower_got, out):
     inputs = block[...].astype(F32)
     average = jnp.mean(inputs, axis=-1, keepdims=True)
     centred = inputs - average
     scale = lax.rsqrt(jnp.mean(centred * centred, axis=-1, keepdims=True) + EPSILON)
     normed = centred * scale
-    pulled = upstream[...]
+    pulled = jnp.concatenate(
+        [upper[...] + upper_got[...].astype(F32), lower[...] + lower_got[...].astype(F32)]
+    )
     pulled = pulled - jnp.mean(pulled, axis=-1, keepdims=True) - normed * jnp.mean(pulled * normed, axis=-1, keepdims=True)
     out[...] = cot[...].astype(F32) + scale * pulled
 
@@ -816,7 +904,20 @@
         yield number, near.at[rows], far.at[rows]
 
 
-def expand_out_body(info, near, far, out):
+def last_out_body(info, near, far, own_dense, shrink_out, dense_out):
+    rank = info[1]
+    for number, one, two in each_rank(near, far, HIDDEN):
+        for piece, held in ((one, rank ^ number), (two, rank ^ number ^ 1)):
+            for part in range(8):
+                rows = piece[64 * part : 64 * (part + 1), :]
+                shrink_out[aligned(held, 64), part * LANES : (part + 1) * LANES] = rows.astype(F32)
+    for part in range(8):
+        start = 4 * HIDDEN + part * LANES
+        rows = jnp.where(own_dense[0] == 1, near[start : start + LANES, :], far[start : start + LANES, :])
+        dense_out[:, part * LANES : (part + 1) * LANES] = rows.astype(F32)
+
+
+def last_grads_out_body(info, near, far, expand_out, mix_out):
     rank = info[1]
     upper = jnp.bitwise_and(rank, 1) == 1
     for number, one, two in each_rank(near, far, HIDDEN):
@@ -826,32 +927,24 @@
             lower_rows = jnp.where(upper, two[rows, :], one[rows, :])
             upper_rows = jnp.where(upper, one[rows, :], two[rows, :])
             joined = jnp.concatenate([lower_rows, upper_rows], axis=0)
-            out[:, aligned(4 * shard + place, LANES)] = as_columns(joined)
-
-
-def last_out_body(info, near, far, own_dense, shrink_out, dense_out):
-    rank = info[1]
-    for number, one, two in each_rank(near, far, HIDDEN):
-        for piece, place in ((one, rank ^ number), (two, rank ^ number ^ 1)):
-            for part in range(8):
-                rows = piece[64 * part : 64 * (part + 1), :]
-                shrink_out[aligned(place, 64), part * LANES : (part + 1) * LANES] = rows.astype(F32)
-    for part in range(8):
-        start = 4 * HIDDEN + part * LANES
-        rows = jnp.where(own_dense[0] == 1, near[start : start + LANES, :], far[start : start + LANES, :])
-        dense_out[:, part * LANES : (part + 1) * LANES] = rows.astype(F32)
-
-
-def mix_out_body(info, near, far, mix_out):
-    rank = info[1]
-    for number, one, two in each_rank(near, far, MIX_ROWS):
+            expand_out[:, aligned(4 * shard + place, LANES)] = as_columns(joined)
+    size = 4 * HIDDEN
+    for number, one, two in each_rank(near.at[size:], far.at[size:], MIX_ROWS):
         for piece, place in ((one, rank ^ number), (two, rank ^ number ^ 1)):
             for part in range(3):
                 mix_out[:, aligned(8 * part + place, LANES)] = as_columns(piece[part * LANES : (part + 1) * LANES, :])
 
 
 def after(value, *others):
-    return lax.optimization_barrier((value,) + others)[0]
+    return jax.tree.map(lambda leaf: lax.optimization_barrier((leaf,) + others)[0], value)
+
+
+def mark_body(info, out):
+    out[...] = jnp.zeros_like(out) + info[0].astype(F32)
+
+
+def mark(info, *others):
+    return call(mark_body, after(info, *others), [], [], [((8, LANES), F32)], [whole((8, LANES))], micros=40)[0]
 
 
 def gather_first(upper, lower):
@@ -867,20 +960,26 @@
     )
 
 
-def reduce_first(mine, other, unit):
-    got = swap(other, y=1)
+def reduce_first(mine, other, unit, *late):
+    got = after(swap(other, y=1), *late)
     total = mine.astype(F32) + got.astype(F32)
     return total, total[2 * unit :].astype(BF16)
 
 
-def reduce_second(total, sent, unit):
+def reduce_second(total, sent, unit, *late):
     kept = jnp.concatenate([total[: 2 * unit], total[4 * unit :]])
-    return (kept + swap(sent, high=1).astype(F32)).astype(BF16)
+    return (kept + after(swap(sent, high=1), *late).astype(F32)).astype(BF16)
 
 
 def share_first(slices, unit):
     away, own = slices[:unit], slices[unit:]
     return own, swap(away, low=1), swap(own, x=1), swap(away, x=1, low=1)
+
+
+def share_last(slices, own_x, *late):
+    parts = after(share_first(slices, HIDDEN), *late)
+    dense_part = jnp.where(own_x, parts[0][HIDDEN:], parts[2][HIDDEN:])
+    return jnp.concatenate([part[:HIDDEN] for part in parts] + [dense_part])
 
 
 def scatter_first(near, far_got):
@@ -891,15 +990,15 @@
     return total[:2, :cut], sent_x, total[0::2, cut:], sent_low
 
 
-def scatter_second(kept_x, sent_x, kept_low, sent_low):
-    upper = kept_x + swap(sent_x, x=1).astype(F32)
-    lower = kept_low + swap(sent_low, low=1).astype(F32)
+def scatter_second(kept_x, sent_x, kept_low, sent_low, *late):
+    upper = kept_x + after(swap(sent_x, x=1), *late).astype(F32)
+    lower = kept_low + after(swap(sent_low, low=1), *late).astype(F32)
     return upper[0], upper[1].astype(BF16), lower[0], lower[1].astype(BF16)
 
 
-def scatter_third(upper, sent_upper, lower, sent_lower):
-    upper = upper + swap(sent_upper, low=1).astype(F32)
-    lower = lower + swap(sent_lower, x=1).astype(F32)
+def scatter_third(upper, sent_upper, lower, sent_lower, *late):
+    upper = upper + after(swap(sent_upper, low=1), *late).astype(F32)
+    lower = lower + after(swap(sent_lower, x=1), *late).astype(F32)
     return jnp.concatenate([upper, lower])
 
 
@@ -930,90 +1029,82 @@
     own_y, own_x = y == core, x == high
 
     small = (first_gain, first_shift, second_gain, second_shift, dense_bias, shrink_bias, mix_bias, expand_bias)
-    cut = tokens // 2
+    half = tokens // 2
+    own, other = cut_slices(info, mix_weight, expand_weight, small)
     marks = jnp.pad(segments.astype(BF16), ((0, 15), (0, width - tokens)))
-    upper, lower = block_input[:cut], jnp.concatenate([block_input[cut:], marks])
+    upper, lower = block_input[:half], jnp.concatenate([block_input[half:], marks])
+    along = swap(other, low=1), swap(own, high=1), swap(other, high=1, low=1)
     upper_x, lower_low = gather_first(upper, lower)
-    own, other, own_last, other_last, other_shrink = cut_slices(
-        info, mix_weight, expand_weight, shrink_weight, dense_weight, cotangent, small
-    )
-    along = swap(other, low=1), swap(own, high=1), swap(other, high=1, low=1)
-    upper_x, lower_low = after((upper_x, lower_low), own)
-    near = gather_second(upper, lower, upper_x, lower_low)
-    along = jnp.stack((own,) + along)
+    first = mark(info, own)
+    upper_x, lower_low = after((upper_x, lower_low), first)
+    over = swap(after(own, first), y=1)
+    upper_pair = swap(jnp.stack([upper, upper_x]), low=1)
+    lower_in = jnp.stack([lower, lower_low])
+    second = mark(info, upper_x, lower_in)
+    along = jnp.stack(after(along, second, over))
     across = swap(along, y=1)
-    near = jnp.concatenate(after(near, along), axis=1)
+    lower_pair = swap(after(lower_in, along), x=1)
+
+    high_in, low_in, other_shrink = cut_last(after(info, first), shrink_weight, dense_weight, cotangent)
+    high_last = swap(after(high_in, along), high=1)
+    low_last = swap(after(low_in, along), low=1)
+    third = mark(info, along, high_in, low_in)
+    upper_pair, lower_pair, across = after((upper_pair, lower_pair, across), third)
+    near = jnp.concatenate(
+        [
+            jnp.stack([upper, upper_pair[0], upper_x, upper_pair[1]]),
+            jnp.stack([lower, lower_low, lower_pair[0], lower_pair[1]]),
+        ],
+        axis=1,
+    )
+    both_last = swap(after(other_shrink, near), high=1, low=1)
     far = swap(near, core=1)
-
-    own_last, other_last, other_shrink, cot_upper = after((own_last, other_last, other_shrink, cotangent[:cut]), near)
-    low_last = swap(other_last, low=1)
-    high_last = swap(own_last, high=1)
-    both_last = swap(other_shrink, high=1, low=1)
+    cot_upper = after(cotangent[:half], near)
     cot_upper_x = swap(cot_upper, x=1)
-
     frequency = jnp.asarray(turn_constants())
-    *saved, mix, expand, vectors, bias = forward(info, near, (along, across), frequency, tokens, width)
-    dense_held = jnp.where(own_x, dense_weight, high_last[64:])
-    last = jnp.concatenate([own_last[:64], low_last[:64], high_last[:64], both_last, dense_held])
-    last = after(last, mix)
+    *near_saved, mix, expand, vectors, bias = forward(info, near, (own, over, along, across), frequency, tokens, width)
+    high_last, low_last, both_last, cot_upper_x, far = after((high_last, low_last, both_last, cot_upper_x, far), mix)
+    last, dense_held = pack_last(info, high_in, low_last, high_last, both_last, dense_weight)
     last_across = swap(last, y=1)
-    cot_upper_x, cot_lower_low = after((cot_upper_x, low_last[64:]), mix)
-    cot_near = gather_second(cot_upper, cotangent[cut:], cot_upper_x, cot_lower_low)
-    far = after(far, last, cot_upper_x, cot_lower_low)
-    saved = forward(info, far, (mix, expand, vectors, bias), frequency, tokens, width, saved)
-    normed, heads, tables, probs, context, act, slope = saved
-    last_across = after(last_across, context)
+    cot_near = gather_second(cot_upper, cotangent[half:], cot_upper_x, low_last[64:])
+    far = after(far, last, cot_upper_x)
+    far_saved = forward(info, far, (mix, expand, vectors, bias), frequency, tokens, width, True)
+    normed, heads, tables, probs, context, act, slope = zip(near_saved, far_saved)
+    last_across = after(last_across, context[1])
     dense = jnp.where(own_y, dense_held, last_across[256:])
-    branch_far, shrink = project(info, context, act, dense, (last, last_across), True)
+    branch_far, shrink = project(info, context[1], act[1], dense, (last, last_across), True)
     branch_got = swap(branch_far, core=1)
     cot_near = jnp.concatenate(after(cot_near, branch_far), axis=1)
     cot_far = swap(cot_near, core=1)
-    (branch_near,) = project(info, context, act, dense, after(shrink, cot_near), False)
-    branch = scatter_first(branch_near, branch_got)
-
-    cot_near, cot_far = after((cot_near, cot_far), branch[1], branch[3])
-    last_mine, last_other = last_backward(info, cot_near, cot_far, act, context)
+    (branch_near,) = project(info, context[0], act[0], dense, after(shrink, cot_near), False)
+    last_mine, last_other = last_backward(info, cot_near, after(cot_far, branch_near), act, context)
+    branch = scatter_first(after(branch_near, last_mine), branch_got)
     grad_pre, bias_grad, feed_sums, expand_mine, expand_other = expand_backward(
-        info, cot_near, cot_far, slope, normed, after(shrink, last_mine), expand, vectors
-    )
-    branch = scatter_second(*branch)
-    last_part = reduce_first(last_mine, last_other, HIDDEN)
-    saved = (normed, heads, tables, probs)
-    fixed = (mix, vectors, bias_grad, feed_sums, frequency)
+        info, cot_near, cot_far, slope, normed, after(shrink, last_mine, branch[1], branch[3]), expand, vectors
+    )
+    branch = scatter_second(*branch, grad_pre)
+    last_part = reduce_first(last_mine, last_other, HIDDEN, grad_pre)
     grad_mixed, mix_mine, mix_other = attention_backward(
-        info, cot_near, cot_far, saved, after(dense, branch[1], branch[3], last_part[1]), fixed
-    )
-    expand_part = reduce_first(expand_mine, expand_other, HIDDEN)
-    last_slices = reduce_second(*last_part, HIDDEN)
-    branch = scatter_third(*branch)
+        info,
+        cot_near,
+        cot_far,
+        (normed, heads, tables, probs),
+        (after(dense, last_part[1], branch[1], branch[3]), frequency, mix, vectors, bias_grad, feed_sums),
+    )
+    expand_part = reduce_first(expand_mine, expand_other, HIDDEN, grad_mixed)
+    branch = scatter_third(*branch, grad_mixed)
     block_out = (block_input.astype(F32) + branch + (vectors[4] + vectors[5])).astype(BF16)
-    error_far = input_backward(
-        info, after(grad_mixed, expand_part[1], last_slices), grad_pre, mix, expand, vectors, True
-    )
+    error_far = input_backward(info, after(grad_mixed, expand_part[1]), grad_pre, mix, expand, vectors, True)
     error_got = swap(error_far, core=1)
-    own_part, low_part, x_part, both_part = share_first(last_slices, HIDDEN)
-    dense_part = jnp.where(own_x, own_part[HIDDEN:], x_part[HIDDEN:])
-    last_near = jnp.concatenate([own_part[:HIDDEN], low_part, x_part[:HIDDEN], both_part, dense_part])
+    error_near = input_backward(info, after(grad_mixed, error_far), grad_pre, mix, expand, vectors, False)
+    error = scatter_first(error_near, error_got)
+    last_slices = reduce_second(*last_part, HIDDEN, error_near)
+    mix_part = reduce_first(mix_mine, mix_other, MIX_ROWS, error[1], error[3])
+    last_near = share_last(last_slices, own_x, error[1], error[3])
     last_far = swap(last_near, core=1)
-    error_near = input_backward(
-        info, after(grad_mixed, error_far, last_near), grad_pre, mix, expand, vectors, False
-    )
-    error = scatter_first(error_near, error_got)
-
-    mix_part = reduce_first(mix_mine, mix_other, MIX_ROWS)
-    mix_part = after(mix_part, error[1], error[3])
-    expand_slices = after(reduce_second(*expand_part, HIDDEN), mix_part[1])
-    expand_near = jnp.concatenate(share_first(expand_slices, HIDDEN))
-    expand_far = swap(expand_near, core=1)
-    mix_slices = reduce_second(*mix_part, MIX_ROWS)
-    mix_parts = share_first(mix_slices, MIX_ROWS)
-    mix_near = jnp.concatenate(mix_parts)
-    mix_sums = [part[MIX_COLS:].astype(F32) for part in mix_parts]
-    mix_sums = ((mix_sums[0] + mix_sums[1]) + (mix_sums[2] + mix_sums[3])).astype(BF16)
-    mix_near = jnp.concatenate([mix_near, mix_sums])
-    mix_far = swap(mix_near, core=1)
-    sums = mix_sums.astype(F32) + mix_far[4 * MIX_ROWS :].astype(F32)
-    upstream = scatter_third(*scatter_second(*error))
+    fourth = mark(info, error[1], mix_part[1], last_near)
+    expand_slices = reduce_second(*expand_part, HIDDEN, fourth)
+    error = scatter_second(*error, expand_slices)
 
     def out(body, near, far, shapes, flag=None):
         operands = [near, far]
@@ -1024,17 +1115,34 @@
         return call(body, info, operands, in_specs, [(shape, F32) for shape in shapes], [whole(shape) for shape in shapes])
 
     flag = own_y.astype(jnp.int32).reshape(1)
-    shrink_out, dense_out = out(last_out_body, last_near, last_far, [shrink_weight.shape, dense_weight.shape], flag)
-    (expand_out,) = out(expand_out_body, expand_near, expand_far, [expand_weight.shape])
-    (mix_out,) = out(mix_out_body, mix_near, mix_far, [mix_weight.shape])
+    shapes = [shrink_weight.shape, dense_weight.shape]
+    shrink_out, dense_out = out(last_out_body, last_near, after(last_far, fourth), shapes, flag)
+    mix_slices = reduce_second(*mix_part, MIX_ROWS, fourth)
+    slices = [expand_slices[:HIDDEN], mix_slices[:MIX_ROWS], expand_slices[HIDDEN:], mix_slices[MIX_ROWS:]]
+    slices = jnp.concatenate(slices)
+    parts = share_first(slices, HIDDEN + MIX_ROWS)
+    fifth = mark(info, slices, error[1], error[3])
+    parts = after(parts, fifth)
+    expand_near = jnp.concatenate([part[:HIDDEN] for part in parts])
+    mix_parts = [part[HIDDEN:] for part in parts]
+    mix_sums = [part[MIX_COLS:].astype(F32) for part in mix_parts]
+    mix_sums = ((mix_sums[0] + mix_sums[1]) + (mix_sums[2] + mix_sums[3])).astype(BF16)
+    near = jnp.concatenate([expand_near] + mix_parts + [mix_sums])
+    far = swap(near, core=1)
+    upper_got = after(swap(error[1], low=1), near)
+    lower_got = after(swap(error[3], x=1), near)
+    operands = [block_input, cotangent, error[0], upper_got, error[2], lower_got]
     (input_grad,) = call(
         norm_body,
         info,
-        [block_input, cotangent, upstream],
-        [whole(block_input.shape)] * 3,
+        operands,
+        [whole(operand.shape) for operand in operands],
         [(block_input.shape, F32)],
         [whole(block_input.shape)],
     )
+    far = after(far, input_grad)
+    sums = mix_sums.astype(F32) + far[4 * (HIDDEN + MIX_ROWS) :].astype(F32)
+    expand_out, mix_out = out(last_grads_out_body, near, far, [expand_weight.shape, mix_weight.shape])
     return (
         block_out,
         input_grad,

time: 278 us -> 215 us (0.77)
  Pallas kernels: 103 us -> 69.3 us
  starting transfers between devices: 50.9 us -> 37.3 us
  other arithmetic: 18.5 us -> 6.74 us
  local copies, waits for them, and re-layouts: 10.8 us -> 3.67 us
  waiting for transfers between devices: 90.5 us -> 93.6 us
    pallas_call x14 -> x15, Pallas kernels: 103 us -> 69.3 us  [call(): pl.pallas_call(body, grid_spec=pltpu.PrefetchScalarGridSpec(num_scalar_pr...]
    ppermute x45 -> x42, starting transfers between devices: 50.9 us -> 37.3 us  [permute(): return lax.ppermute(value, ('rep', 'fsdp'), pairs)]
    unnamed x63 -> x40, local copies, waits for them, and re-layouts: 6.06 us -> 1.12 us
    add x2 -> x1, other arithmetic: 5.66 us -> 1.06 us  [scatter_first(): total = near.astype(F32) + far_got.astype(F32)]
    ppermute x45 -> x42, waiting for transfers between devices: 90.5 us -> 93.6 us  [permute(): return lax.ppermute(value, ('rep', 'fsdp'), pairs)]
  transfers between devices with their start and end apart: 45 -> 42, of which waited for: 15 -> 19; matrix products, arithmetic and copies ran while one was open for 7% -> 3% of each run, Pallas kernels for 28% -> 28%
where the time goes in v3:
time: 215 us; the launch traced here: 212 us
  waiting for transfers between devices  93.6 us (44%)
  Pallas kernels  69.3 us (32%)
  starting transfers between devices  37.3 us (17%)
  other arithmetic  6.74 us (3%)
  local copies, waits for them, and re-layouts  3.67 us (2%)
    ppermute x42, waiting for transfers between devices, permute(): return lax.ppermute(value, ('rep', 'fsdp'), pairs)  93.6 us
    pallas_call x15, Pallas kernels, call(): pl.pallas_call(body, grid_spec=pltpu.PrefetchScalarGridSpec(num_scalar_pr...  69.3 us
    ppermute x42, starting transfers between devices, permute(): return lax.ppermute(value, ('rep', 'fsdp'), pairs)  37.3 us
  transfers between devices with their start and end apart: 42, of which 19 were waited for; matrix products, arithmetic and copies ran while one was open for 3% of the time, Pallas kernels for 28%

profile of v3, /device:TPU:6, one launch (start us, length us, event | category | flops | bytes accessed | tf_op | source)
XLA Modules:
  0.0 212.1 jit_solution(12321201027746955800)
XLA Ops:
  1.3 3.3 %shard_map.263 = (bf16[912,128]{1,0:T(8,128)(2,1)}, bf16[912,128]{1,0:T(8,128)(2,1)}) custom-call(s32[2]{0:T(128)} %pad_add_fusion.info, bf16[128,3072]{1,0:T(8,128)(2,1)} %mix.1, bf16[128,4096]{1,0:T(8,128)(2,1)} %expand.1, bf16[1,128]{1,0:T(2,128)(2,1)} %bitcast.93, bf16[1,128]{1,0:T(2,128)(2,1)} %bitcast.94, bf16[1,128]{1,0:T(2,128)(2,1)} %bitcast.95, ...), custom_call_target="tpu_custom_call" | custom-call | flops 16000000000 | bytes 48000000 | tf_op jit(solution)/shard_map/pallas_call | solution.py:329
  4.6 1.6 collective-permute-start.2
  6.2 2.5 %collective-permute-start.6 = (bf16[912,128]{1,0:T(8,128)(2,1)}, bf16[912,128]{1,0:T(8,128)(2,1)S(1)}, u32[]{:S(2)}, u32[]{:S(2)}) collective-permute-start(bf16[912,128]{1,0:T(8,128)(2,1)} %get-tuple-element.118), channel_id=1, source_target_pairs={{0,6},{1,7},{2,4},{3,5},{4,2},{5,3},{6,0},{7,1},{8,14},{9,15},{10,... | collective-permute-start | bytes 700424 | tf_op jit(solution)/shard_map/ppermute | solution.py:305
  8.8 0.7 collective-permute-start.3
  10.1 1.2 collective-permute-start.5
  11.3 3.1 %shard_map.264 = (bf16[192,1024]{1,0:T(8,128)(2,1)}, bf16[192,1024]{1,0:T(8,128)(2,1)}, bf16[64,1024]{1,0:T(8,128)(2,1)}) custom-call(s32[2]{0:T(128)} %pad_add_fusion.info, bf16[512,1024]{1,0:T(8,128)(2,1)} %shrink.1, bf16[128,1024]{1,0:T(8,128)(2,1)} %dense.3, bf16[256,1024]{1,0:T(8,128)(2,1)} %cot.3), custom_call_target="tpu_custom_call" | custom-call | flops 16000000000 | bytes 48000000 | tf_op jit(solution)/shard_map/pallas_call | solution.py:329
  14.4 2.3 %collective-permute-done = bf16[128,1024]{1,0:T(8,128)(2,1)S(1)} collective-permute-done((bf16[128,1024]{1,0:T(8,128)(2,1)S(1)}, bf16[128,1024]{1,0:T(8,128)(2,1)S(1)}, u32[]{:S(2)}, u32[]{:S(2)}) %collective-permute-start) | collective-permute-done | bytes 262176 | tf_op jit(solution)/shard_map/ppermute | solution.py:305
  17.3 11.2 %collective-permute-done.3 = bf16[144,1024]{1,0:T(8,128)(2,1)S(1)} collective-permute-done((bf16[144,1024]{1,0:T(8,128)(2,1)S(1)}, bf16[144,1024]{1,0:T(8,128)(2,1)S(1)}, u32[]{:S(2)}, u32[]{:S(2)}) %collective-permute-start.3) | collective-permute-done | bytes 294944 | tf_op jit(solution)/shard_map/ppermute | solution.py:305
  29.7 2.7 %collective-permute-start.9 = (bf16[192,1024]{1,0:T(8,128)(2,1)S(1)}, bf16[192,1024]{1,0:T(8,128)(2,1)S(1)}, u32[]{:S(2)}, u32[]{:S(2)}) collective-permute-start(bf16[192,1024]{1,0:T(8,128)(2,1)S(1)} %copy-done.11), channel_id=1, source_target_pairs={{0,2},{1,3},{2,0},{3,1},{4,6},{5,7},{6,4},{7,5},{8,10},{9,11},{10,... | collective-permute-start | bytes 1179656 | tf_op jit(solution)/shard_map/ppermute | solution.py:305
  32.4 1.7 collective-permute-start.10
  34.1 17.8 %collective-permute-done.1 = bf16[2,128,1024]{2,1,0:T(8,128)(2,1)S(1)} collective-permute-done((bf16[2,128,1024]{2,1,0:T(8,128)(2,1)S(1)}, bf16[2,128,1024]{2,1,0:T(8,128)(2,1)S(1)}, u32[]{:S(2)}, u32[]{:S(2)}) %collective-permute-start.1) | collective-permute-done | bytes 524320 | tf_op jit(solution)/shard_map/ppermute | solution.py:305
  52.9 3.6 %collective-permute-start.11 = (bf16[64,1024]{1,0:T(8,128)(2,1)S(1)}, bf16[64,1024]{1,0:T(8,128)(2,1)S(1)}, u32[]{:S(2)}, u32[]{:S(2)}) collective-permute-start(bf16[64,1024]{1,0:T(8,128)(2,1)S(1)} %copy-done.12), channel_id=1, source_target_pairs={{0,6},{1,7},{2,4},{3,5},{4,2},{5,3},{6,0},{7,1},{8,14},{9,15},{10,... | collective-permute-start | bytes 393224 | tf_op jit(solution)/shard_map/ppermute | solution.py:305
  56.5 7.9 %shard_map.265 = (bf16[4,256,1024]{2,1,0:T(8,128)(2,1)S(1)}, bf16[4,256,384]{2,1,0:T(8,128)(2,1)S(1)}, f32[4,16,256]{2,1,0:T(8,128)S(1)}, bf16[4,2,256,256]{3,2,...) custom-call(s32[2]{0:T(128)S(1)} %copy-done.7, ...), custom_call_target="tpu_custom_call" | custom-call | flops 35999997952 | bytes 108000000 | tf_op jit(solution)/shard_map/pallas_call | solution.py:329
  64.5 1.6 collective-permute-start.16
  67.6 10.7 %collective-permute-done.16 = bf16[2,128,1024]{2,1,0:T(8,128)(2,1)S(1)} collective-permute-done((bf16[2,128,1024]{2,1,0:T(8,128)(2,1)S(1)}, bf16[2,128,1024]{2,1,0:T(8,128)(2,1)S(1)}, u32[]{:S(2)}, u32[]{:S(2)}) %collective-permute-start.16) | collective-permute-done | bytes 524320 | tf_op jit(solution)/shard_map/ppermute | solution.py:305
  78.4 1.2 collective-permute-done.15
  79.8 7.5 %shard_map.267 = (bf16[4,256,1024]{2,1,0:T(8,128)(2,1)S(1)}, bf16[4,256,384]{2,1,0:T(8,128)(2,1)S(1)}, f32[4,16,256]{2,1,0:T(8,128)S(1)}, bf16[4,2,256,256]{3,2,...) custom-call(s32[2]{0:T(128)S(1)} %copy-done.7, ...), custom_call_target="tpu_custom_call" | custom-call | flops 35999997952 | bytes 108000000 | tf_op jit(solution)/shard_map/pallas_call | solution.py:329
  87.4 2.6 %shard_map.268 = (bf16[4,256,1024]{2,1,0:T(8,128)(2,1)S(1)}, bf16[512,1024]{1,0:T(8,128)(2,1)S(1)}) custom-call(s32[2]{0:T(128)S(1)} %copy-done.7, bf16[4,256,128]{2,1,0:T(8,128)(2,1)S(1)} %get-tuple-element.152.context, bf16[4,256,512]{2,1,0:T(8,128)(2,1)S(1)} %get-tuple-element.154.act, bf16[128,1024]{1,0:T(8,128)(2,1)S(1)} %slice_select_fusion.dense, ...), custom_call_target="tpu_custom_call" | custom-call | flops 20000000000 | bytes 60000000 | tf_op jit(solution)/shard_map/pallas_call | solution.py:329
  91.3 2.5 %shard_map.269 = bf16[4,256,1024]{2,1,0:T(8,128)(2,1)S(1)} custom-call(s32[2]{0:T(128)S(1)} %copy-done.7, bf16[4,256,128]{2,1,0:T(8,128)(2,1)S(1)} %get-tuple-element.133.context, bf16[4,256,512]{2,1,0:T(8,128)(2,1)S(1)} %get-tuple-element.134.act, bf16[128,1024]{1,0:T(8,128)(2,1)S(1)} %slice_select_fusion.dense, bf16[512,1024]{1,0:T(8,128)(2,1)S(1)} %get-tuple-element.167.shrink), custom_call_target="tpu_custom_call" | custom-call | flops 20000000000 | bytes 60000000 | tf_op jit(solution)/shard_map/pallas_call | solution.py:329
  94.4 4.8 %shard_map.270 = (bf16[3072,128]{1,0:T(8,128)(2,1)S(1)}, bf16[3072,128]{1,0:T(8,128)(2,1)S(1)}) custom-call(s32[2]{0:T(128)S(1)} %copy-done.7, bf16[1024,1024]{1,0:T(8,128)(2,1)S(1)} %bitcast.69, bf16[1024,1024]{1,0:T(8,128)(2,1)S(1)} %bitcast.70, bf16[1024,512]{1,0:T(8,128)(2,1)S(1)} %bitcast.75, bf16[1024,512]{1,0:T(8,128)(2,1)S(1)} %bitcast.76, ...), custom_call_target="tpu_custom_call" | custom-call | flops 20000000000 | bytes 60000000 | tf_op jit(solution)/shard_map/pallas_call | solution.py:329
  99.2 1.1 convert_add_fusion.1
  102.1 9.0 %shard_map.271 = (bf16[8,256,512]{2,1,0:T(8,128)(2,1)S(1)}, f32[8,512]{1,0:T(8,128)S(1)}, f32[8,1024]{1,0:T(8,128)S(1)}, bf16[2048,128]{1,0:T(8,128)(2,1)S(1)}, bf16[2048,128]{1,0:T(8,128)(2,1)S(1)}) custom-call(s32[2]{0:T(128)S(1)} %copy-done.7, bf16[4,256,1024]{2,1,0:T(8,128)(2,1)S(1)} %constant_dynamic-update-slice_fusion.near, ...), custom_call_target="tpu_custom_call" | custom-call | flops 35999997952 | bytes 108000000 | tf_op jit(solution)/shard_map/pallas_call | solution.py:329
  111.1 1.6 collective-permute-start.24
  112.7 1.7 collective-permute-done.22
  115.1 1.5 collective-permute-start.20
  117.2 4.8 %collective-permute-done.21 = bf16[3072,128]{1,0:T(8,128)(2,1)S(1)} collective-permute-done((bf16[3072,128]{1,0:T(8,128)(2,1)S(1)}, bf16[3072,128]{1,0:T(8,128)(2,1)S(1)}, u32[]{:S(2)}, u32[]{:S(2)}) %collective-permute-start.21) | collective-permute-done | bytes 786464 | tf_op jit(solution)/shard_map/ppermute | solution.py:305
  122.6 13.4 %shard_map.272 = (bf16[8,256,384]{2,1,0:T(8,128)(2,1)S(1)}, bf16[1600,128]{1,0:T(8,128)(2,1)S(1)}, bf16[1600,128]{1,0:T(8,128)(2,1)S(1)}) custom-call(s32[2]{0:T(128)S(1)} %copy-done.7, bf16[4,256,1024]{2,1,0:T(8,128)(2,1)S(1)} %constant_dynamic-update-slice_fusion.near, bf16[4,256,1024]{2,1,0:T(8,128)(2,1)S(1)} %collective-permute-done.17.far, ...), custom_call_target="tpu_custom_call" | custom-call | flops 51999997952 | bytes 156000000 | tf_op jit(solution)/shard_map/pallas_call | solution.py:329
  136.1 3.1 %shard_map.273 = bf16[4,256,1024]{2,1,0:T(8,128)(2,1)S(1)} custom-call(s32[2]{0:T(128)S(1)} %copy-done.7, bf16[8,256,384]{2,1,0:T(8,128)(2,1)S(1)} %get-tuple-element.189.mixed, bf16[8,256,512]{2,1,0:T(8,128)(2,1)S(1)} %get-tuple-element.168.pre, bf16[1024,384]{1,0:T(8,128)(2,1)S(1)} %get-tuple-element.136.mix, ...), custom_call_target="tpu_custom_call" | custom-call | flops 24000000000 | bytes 72000000 | tf_op jit(solution)/shard_map/pallas_call | solution.py:329
  139.4 2.7 %collective-permute-start.27 = (bf16[1024,128]{1,0:T(8,128)(2,1)S(1)}, bf16[1024,128]{1,0:T(8,128)(2,1)S(1)}, u32[]{:S(2)}, u32[]{:S(2)}) collective-permute-start(bf16[1024,128]{1,0:T(8,128)(2,1)S(1)} %slice.384), channel_id=1, source_target_pairs={{0,4},{1,5},{2,6},{3,7},{4,0},{5,1},{6,2},{7,3},{8,12},{9,13},{10,... | collective-permute-start | bytes 786440 | tf_op jit(solution)/shard_map/ppermute | solution.py:305
  142.1 3.4 %shard_map.274 = bf16[4,256,1024]{2,1,0:T(8,128)(2,1)S(1)} custom-call(s32[2]{0:T(128)S(1)} %copy-done.7, bf16[8,256,384]{2,1,0:T(8,128)(2,1)S(1)} %get-tuple-element.189.mixed, bf16[8,256,512]{2,1,0:T(8,128)(2,1)S(1)} %get-tuple-element.168.pre, bf16[1024,384]{1,0:T(8,128)(2,1)S(1)} %get-tuple-element.136.mix, ...), custom_call_target="tpu_custom_call" | custom-call | flops 24000000000 | bytes 72000000 | tf_op jit(solution)/shard_map/pallas_call | solution.py:329
  146.5 1.0 fusion.1
  147.5 4.6 %collective-permute-done.29 = bf16[2048,128]{1,0:T(8,128)(2,1)S(1)} collective-permute-done((bf16[2048,128]{1,0:T(8,128)(2,1)S(1)}, bf16[2048,128]{1,0:T(8,128)(2,1)S(1)}, u32[]{:S(2)}, u32[]{:S(2)}) %collective-permute-start.29) | collective-permute-done | bytes 524320 | tf_op jit(solution)/shard_map/ppermute | solution.py:305
  152.4 2.9 %collective-permute-start.30 = (bf16[512,128]{1,0:T(8,128)(2,1)S(1)}, bf16[512,128]{1,0:T(8,128)(2,1)S(1)}, u32[]{:S(2)}, u32[]{:S(2)}) collective-permute-start(bf16[512,128]{1,0:T(8,128)(2,1)S(1)} %slice.303), channel_id=1, source_target_pairs={{0,2},{1,3},{2,0},{3,1},{4,6},{5,7},{6,4},{7,5},{8,10},{9,11},{10,... | collective-permute-start | bytes 393224 | tf_op jit(solution)/shard_map/ppermute | solution.py:305
  155.8 1.1 fusion.15
  157.0 9.6 %collective-permute-done.31 = bf16[1536,128]{1,0:T(8,128)(2,1)S(1)} collective-permute-done((bf16[1536,128]{1,0:T(8,128)(2,1)S(1)}, bf16[1536,128]{1,0:T(8,128)(2,1)S(1)}, u32[]{:S(2)}, u32[]{:S(2)}) %collective-permute-start.31) | collective-permute-done | bytes 393248 | tf_op jit(solution)/shard_map/ppermute | solution.py:305
  167.8 10.5 %collective-permute-done.34 = bf16[800,128]{1,0:T(8,128)(2,1)S(1)} collective-permute-done((bf16[800,128]{1,0:T(8,128)(2,1)S(1)}, bf16[800,128]{1,0:T(8,128)(2,1)S(1)}, u32[]{:S(2)}, u32[]{:S(2)}) %collective-permute-start.34) | collective-permute-done | bytes 204832 | tf_op jit(solution)/shard_map/ppermute | solution.py:305
  178.5 2.1 collective-permute-start.36
  180.6 0.8 collective-permute-done.26
  182.1 4.8 %collective-permute-done.35 = bf16[2,128,1024]{2,1,0:T(8,128)(2,1)S(1)} collective-permute-done((bf16[2,128,1024]{2,1,0:T(8,128)(2,1)S(1)}, bf16[2,128,1024]{2,1,0:T(8,128)(2,1)S(1)}, u32[]{:S(2)}, u32[]{:S(2)}) %collective-permute-start.35) | collective-permute-done | bytes 524320 | tf_op jit(solution)/shard_map/ppermute | solution.py:305
  187.3 1.4 collective-permute-start.39
  188.7 4.0 %collective-permute-done.38 = bf16[912,128]{1,0:T(8,128)(2,1)S(1)} collective-permute-done((bf16[912,128]{1,0:T(8,128)(2,1)S(1)}, bf16[912,128]{1,0:T(8,128)(2,1)S(1)}, u32[]{:S(2)}, u32[]{:S(2)}) %collective-permute-start.38) | collective-permute-done | bytes 233504 | tf_op jit(solution)/shard_map/ppermute | solution.py:305
  192.7 2.3 %collective-permute-done.37 = bf16[912,128]{1,0:T(8,128)(2,1)S(1)} collective-permute-done((bf16[912,128]{1,0:T(8,128)(2,1)S(1)}, bf16[912,128]{1,0:T(8,128)(2,1)S(1)}, u32[]{:S(2)}, u32[]{:S(2)}) %collective-permute-start.37) | collective-permute-done | bytes 233504 | tf_op jit(solution)/shard_map/ppermute | solution.py:305
  195.0 1.8 collective-permute-done.36
  197.3 2.1 collective-permute-done.39.lower_got
  199.4 2.4 %collective-permute-done.33.upper_got = bf16[128,1024]{1,0:T(8,128)(2,1)S(1)} collective-permute-done((bf16[128,1024]{1,0:T(8,128)(2,1)S(1)}, bf16[128,1024]{1,0:T(8,128)(2,1)S(1)}, u32[]{:S(2)}, u32[]{:S(2)}) %collective-permute-start.33) | collective-permute-done | bytes 262176 | tf_op jit(solution)/shard_map/ppermute | solution.py:305
  201.8 2.2 %shard_map.277 = (f32[512,1024]{1,0:T(8,128)}, f32[128,1024]{1,0:T(8,128)}) custom-call(s32[2]{0:T(128)S(1)} %copy-done.7, bf16[3072,128]{1,0:T(8,128)(2,1)S(1)} %select_dynamic-update-slice_fusion.near, bf16[3072,128]{1,0:T(8,128)(2,1)S(1)} %collective-permute-done.41.far, s32[1]{0:T(128)} %bitcast.41.own_dense), custom_call_target="tpu_custom_call" | custom-call | flops 16000000000 | bytes 48000000 | tf_op jit(solution)/shard_map/pallas_call | solution.py:329
  204.0 2.2 %shard_map.275 = f32[256,1024]{1,0:T(8,128)} custom-call(s32[2]{0:T(128)S(1)} %copy-done.7, bf16[256,1024]{1,0:T(8,128)(2,1)S(1)} %copy-done.1, bf16[256,1024]{1,0:T(8,128)(2,1)S(1)} %copy-done.2, f32[128,1024]{1,0:T(8,128)S(1)} %get-tuple-element.253.upper, bf16[128,1024]{1,0:T(8,128)(2,1)S(1)} %collective-permute-done.33.upper_got, ...), custom_call_target="tpu_custom_call" | custom-call | flops 16000000000 | bytes 48000000 | tf_op jit(solution)/shard_map/pallas_call | solution.py:329
  206.2 3.7 %shard_map.276 = (f32[128,4096]{1,0:T(8,128)}, f32[128,3072]{1,0:T(8,128)}) custom-call(s32[2]{0:T(128)S(1)} %copy-done.7, bf16[3664,128]{1,0:T(8,128)(2,1)S(1)} %get-tuple-element.216.near, bf16[3664,128]{1,0:T(8,128)(2,1)S(1)} %collective-permute-done.40.far), custom_call_target="tpu_custom_call" | custom-call | flops 16000000000 | bytes 48000000 | tf_op jit(solution)/shard_map/pallas_call | solution.py:329
  (146 shorter events, 18.3 us)
Async XLA Ops:
  1.3 7.4 %copy-start = (bf16[256,1024]{1,0:T(8,128)(2,1)S(1)}, bf16[256,1024]{1,0:T(8,128)(2,1)}, u32[]{:S(2)}) copy-start(bf16[256,1024]{1,0:T(8,128)(2,1)} %block.1) | copy-start | bytes 1572868
  1.3 7.4 %copy-start.9 = (s32[1,256]{1,0:T(1,128)S(1)}, s32[1,256]{1,0:T(1,128)}, u32[]{:S(2)}) copy-start(s32[1,256]{1,0:T(1,128)} %param.17) | copy-start | bytes 3076
  4.6 5.5 %copy-start.5 = (bf16[912,128]{1,0:T(8,128)(2,1)S(1)}, bf16[912,128]{1,0:T(8,128)(2,1)}, u32[]{:S(2)}) copy-start(bf16[912,128]{1,0:T(8,128)(2,1)} %get-tuple-element.121.own) | copy-start | bytes 700420
  4.6 24.0 %collective-permute-start.2 = (bf16[912,128]{1,0:T(8,128)(2,1)}, bf16[912,128]{1,0:T(8,128)(2,1)S(1)}, u32[]{:S(2)}, u32[]{:S(2)}) collective-permute-start(bf16[912,128]{1,0:T(8,128)(2,1)} %get-tuple-element.118), channel_id=1, source_target_pairs={{0,2},{1,3},{2,0},{3,1},{4,6},{5,7},{6,4},{7,5},{8,10},{9,11},{10,... | collective-permute-start | bytes 700424 | tf_op jit(solution)/shard_map/ppermute | solution.py:305
  6.2 22.5 %collective-permute-start.6 = (bf16[912,128]{1,0:T(8,128)(2,1)}, bf16[912,128]{1,0:T(8,128)(2,1)S(1)}, u32[]{:S(2)}, u32[]{:S(2)}) collective-permute-start(bf16[912,128]{1,0:T(8,128)(2,1)} %get-tuple-element.118), channel_id=1, source_target_pairs={{0,6},{1,7},{2,4},{3,5},{4,2},{5,3},{6,0},{7,1},{8,14},{9,15},{10,... | collective-permute-start | bytes 700424 | tf_op jit(solution)/shard_map/ppermute | solution.py:305
  8.8 19.8 %collective-permute-start.3 = (bf16[144,1024]{1,0:T(8,128)(2,1)S(1)}, bf16[144,1024]{1,0:T(8,128)(2,1)S(1)}, u32[]{:S(2)}, u32[]{:S(2)}) collective-permute-start(bf16[144,1024]{1,0:T(8,128)(2,1)S(1)} %get-tuple-element.242), channel_id=1, source_target_pairs={{0,2},{1,3},{2,0},{3,1},{4,6},{5,7},{6,4},{7,5},{8,10},{9,11},{10,... | collective-permute-start | bytes 884744 | tf_op jit(solution)/shard_map/ppermute | solution.py:305
  9.6 7.2 %collective-permute-start = (bf16[128,1024]{1,0:T(8,128)(2,1)S(1)}, bf16[128,1024]{1,0:T(8,128)(2,1)S(1)}, u32[]{:S(2)}, u32[]{:S(2)}) collective-permute-start(bf16[128,1024]{1,0:T(8,128)(2,1)S(1)} %get-tuple-element.239), channel_id=1, source_target_pairs={{0,16},{1,17},{2,18},{3,19},{4,20},{5,21},{6,22},{7,23},{8,24},{9,... | collective-permute-start | bytes 786440 | tf_op jit(solution)/shard_map/ppermute | solution.py:305
  10.1 18.6 %collective-permute-start.5 = (bf16[912,128]{1,0:T(8,128)(2,1)S(1)}, bf16[912,128]{1,0:T(8,128)(2,1)S(1)}, u32[]{:S(2)}, u32[]{:S(2)}) collective-permute-start(bf16[912,128]{1,0:T(8,128)(2,1)S(1)} %copy-done.5), channel_id=1, source_target_pairs={{0,4},{1,5},{2,6},{3,7},{4,0},{5,1},{6,2},{7,3},{8,12},{9,13},{10,... | collective-permute-start | bytes 700424 | tf_op jit(solution)/shard_map/ppermute | solution.py:305
  14.4 15.3 %copy-start.11 = (bf16[192,1024]{1,0:T(8,128)(2,1)S(1)}, bf16[192,1024]{1,0:T(8,128)(2,1)}, u32[]{:S(2)}) copy-start(bf16[192,1024]{1,0:T(8,128)(2,1)} %get-tuple-element.135) | copy-start | bytes 1179652
  14.4 18.0 %copy-start.3 = (bf16[192,1024]{1,0:T(8,128)(2,1)S(1)}, bf16[192,1024]{1,0:T(8,128)(2,1)}, u32[]{:S(2)}) copy-start(bf16[192,1024]{1,0:T(8,128)(2,1)} %get-tuple-element.138.own) | copy-start | bytes 1179652
  16.8 11.9 %collective-permute-start.4 = (bf16[912,128]{1,0:T(8,128)(2,1)S(1)}, bf16[912,128]{1,0:T(8,128)(2,1)S(1)}, u32[]{:S(2)}, u32[]{:S(2)}) collective-permute-start(bf16[912,128]{1,0:T(8,128)(2,1)S(1)} %copy-done.5), channel_id=1, source_target_pairs={{0,1},{1,0},{2,3},{3,2},{4,5},{5,4},{6,7},{7,6},{8,9},{9,8},{10,11... | collective-permute-start | bytes 700424 | tf_op jit(solution)/shard_map/ppermute | solution.py:305
  28.6 23.3 %collective-permute-start.1 = (bf16[2,128,1024]{2,1,0:T(8,128)(2,1)S(1)}, bf16[2,128,1024]{2,1,0:T(8,128)(2,1)S(1)}, u32[]{:S(2)}, u32[]{:S(2)}) collective-permute-start(bf16[2,128,1024]{2,1,0:T(8,128)(2,1)S(1)} %pad_maximum_fusion.4), channel_id=1, source_target_pairs={{0,2},{1,3},{2,0},{3,1},{4,6},{5,7},{6,4},{7,5},{8,10},{9,11},{10,... | collective-permute-start | bytes 1572872 | tf_op jit(solution)/shard_map/ppermute | solution.py:305
  28.8 24.1 %collective-permute-start.8 = (bf16[3,912,128]{2,1,0:T(8,128)(2,1)S(1)}, bf16[3,912,128]{2,1,0:T(8,128)(2,1)S(1)}, u32[]{:S(2)}, u32[]{:S(2)}) collective-permute-start(bf16[3,912,128]{2,1,0:T(8,128)(2,1)S(1)} %pad_maximum_fusion.2.along), channel_id=1, source_target_pairs={{0,1},{1,0},{2,3},{3,2},{4,5},{5,4},{6,7},{7,6},{8,9},{9,8},{10,11... | collective-permute-start | bytes 2101256 | tf_op jit(solution)/shard_map/ppermute | solution.py:305
  29.3 22.6 %collective-permute-start.7 = (bf16[2,144,1024]{2,1,0:T(8,128)(2,1)S(1)}, bf16[2,144,1024]{2,1,0:T(8,128)(2,1)S(1)}, u32[]{:S(2)}, u32[]{:S(2)}) collective-permute-start(bf16[2,144,1024]{2,1,0:T(8,128)(2,1)S(1)} %pad_maximum_fusion.3), channel_id=1, source_target_pairs={{0,16},{1,17},{2,18},{3,19},{4,20},{5,21},{6,22},{7,23},{8,24},{9,... | collective-permute-start | bytes 1769480 | tf_op jit(solution)/shard_map/ppermute | solution.py:305
  29.7 34.7 %collective-permute-start.9 = (bf16[192,1024]{1,0:T(8,128)(2,1)S(1)}, bf16[192,1024]{1,0:T(8,128)(2,1)S(1)}, u32[]{:S(2)}, u32[]{:S(2)}) collective-permute-start(bf16[192,1024]{1,0:T(8,128)(2,1)S(1)} %copy-done.11), channel_id=1, source_target_pairs={{0,2},{1,3},{2,0},{3,1},{4,6},{5,7},{6,4},{7,5},{8,10},{9,11},{10,... | collective-permute-start | bytes 1179656 | tf_op jit(solution)/shard_map/ppermute | solution.py:305
  32.4 33.7 %collective-permute-start.10 = (bf16[192,1024]{1,0:T(8,128)(2,1)S(1)}, bf16[192,1024]{1,0:T(8,128)(2,1)S(1)}, u32[]{:S(2)}, u32[]{:S(2)}) collective-permute-start(bf16[192,1024]{1,0:T(8,128)(2,1)S(1)} %copy-done.3), channel_id=1, source_target_pairs={{0,4},{1,5},{2,6},{3,7},{4,0},{5,1},{6,2},{7,3},{8,12},{9,13},{10,... | collective-permute-start | bytes 1179656 | tf_op jit(solution)/shard_map/ppermute | solution.py:305
  51.9 4.6 %copy-start.6 = (f32[24,128]{1,0:T(8,128)S(1)}, f32[24,128]{1,0:T(8,128)}, u32[]{:S(2)}) copy-start(f32[24,128]{1,0:T(8,128)} %constant.63.clone.frequency) | copy-start | bytes 36868
  52.2 27.6 %collective-permute-start.13 = (bf16[4,272,1024]{2,1,0:T(8,128)(2,1)S(1)}, bf16[4,272,1024]{2,1,0:T(8,128)(2,1)S(1)}, u32[]{:S(2)}, u32[]{:S(2)}) collective-permute-start(bf16[4,272,1024]{2,1,0:T(8,128)(2,1)S(1)} %maximum_maximum_fusion.inputs), channel_id=1, source_target_pairs={{0,8},{1,9},{2,10},{3,11},{4,12},{5,13},{6,14},{7,15},{8,0},{9,1},... | collective-permute-start | bytes 6684680 | tf_op jit(solution)/shard_map/ppermute | solution.py:305
  52.3 13.8 %collective-permute-start.14 = (bf16[128,1024]{1,0:T(8,128)(2,1)S(1)}, bf16[128,1024]{1,0:T(8,128)(2,1)S(1)}, u32[]{:S(2)}, u32[]{:S(2)}) collective-permute-start(bf16[128,1024]{1,0:T(8,128)(2,1)S(1)} %get-tuple-element.146), channel_id=1, source_target_pairs={{0,16},{1,17},{2,18},{3,19},{4,20},{5,21},{6,22},{7,23},{8,24},{9,... | collective-permute-start | bytes 786440 | tf_op jit(solution)/shard_map/ppermute | solution.py:305
  52.9 13.2 %collective-permute-start.11 = (bf16[64,1024]{1,0:T(8,128)(2,1)S(1)}, bf16[64,1024]{1,0:T(8,128)(2,1)S(1)}, u32[]{:S(2)}, u32[]{:S(2)}) collective-permute-start(bf16[64,1024]{1,0:T(8,128)(2,1)S(1)} %copy-done.12), channel_id=1, source_target_pairs={{0,6},{1,7},{2,4},{3,5},{4,2},{5,3},{6,0},{7,1},{8,14},{9,15},{10,... | collective-permute-start | bytes 393224 | tf_op jit(solution)/shard_map/ppermute | solution.py:305
  64.5 13.8 %collective-permute-start.16 = (bf16[2,128,1024]{2,1,0:T(8,128)(2,1)S(1)}, bf16[2,128,1024]{2,1,0:T(8,128)(2,1)S(1)}, u32[]{:S(2)}, u32[]{:S(2)}) collective-permute-start(bf16[2,128,1024]{2,1,0:T(8,128)(2,1)S(1)} %pad_maximum_fusion.6), channel_id=1, source_target_pairs={{0,16},{1,17},{2,18},{3,19},{4,20},{5,21},{6,22},{7,23},{8,24},{9,... | collective-permute-start | bytes 1572872 | tf_op jit(solution)/shard_map/ppermute | solution.py:305
  66.1 13.5 %collective-permute-start.15 = (bf16[2,128,1024]{2,1,0:T(8,128)(2,1)S(1)}, bf16[2,128,1024]{2,1,0:T(8,128)(2,1)S(1)}, u32[]{:S(2)}, u32[]{:S(2)}) collective-permute-start(bf16[2,128,1024]{2,1,0:T(8,128)(2,1)S(1)} %pad_maximum_fusion.5), channel_id=1, source_target_pairs={{0,2},{1,3},{2,0},{3,1},{4,6},{5,7},{6,4},{7,5},{8,10},{9,11},{10,... | collective-permute-start | bytes 1572872 | tf_op jit(solution)/shard_map/ppermute | solution.py:305
  67.0 20.3 %collective-permute-start.12 = (bf16[384,1024]{1,0:T(8,128)(2,1)S(1)}, bf16[384,1024]{1,0:T(8,128)(2,1)S(1)}, u32[]{:S(2)}, u32[]{:S(2)}) collective-permute-start(bf16[384,1024]{1,0:T(8,128)(2,1)S(1)} %get-tuple-element.144.along), channel_id=1, source_target_pairs={{0,1},{1,0},{2,3},{3,2},{4,5},{5,4},{6,7},{7,6},{8,9},{9,8},{10,11... | collective-permute-start | bytes 2359304 | tf_op jit(solution)/shard_map/ppermute | solution.py:305
  90.2 4.2 %collective-permute-start.17 = (bf16[4,256,1024]{2,1,0:T(8,128)(2,1)S(1)}, bf16[4,256,1024]{2,1,0:T(8,128)(2,1)S(1)}, u32[]{:S(2)}, u32[]{:S(2)}) collective-permute-start(bf16[4,256,1024]{2,1,0:T(8,128)(2,1)S(1)} %constant_dynamic-update-slice_fusion.near), channel_id=1, source_target_pairs={{0,8},{1,9},{2,10},{3,11},{4,12},{5,13},{6,14},{7,15},{8,0},{9,1},... | collective-permute-start | bytes 6291464 | tf_op jit(solution)/shard_map/ppermute | solution.py:305
  90.8 8.3 %collective-permute-start.18 = (bf16[4,256,1024]{2,1,0:T(8,128)(2,1)S(1)}, bf16[4,256,1024]{2,1,0:T(8,128)(2,1)S(1)}, u32[]{:S(2)}, u32[]{:S(2)}) collective-permute-start(bf16[4,256,1024]{2,1,0:T(8,128)(2,1)S(1)} %get-tuple-element.156), channel_id=1, source_target_pairs={{0,8},{1,9},{2,10},{3,11},{4,12},{5,13},{6,14},{7,15},{8,0},{9,1},... | collective-permute-start | bytes 6291464 | tf_op jit(solution)/shard_map/ppermute | solution.py:305
  100.3 14.0 %collective-permute-start.22 = (bf16[2,128,1024]{2,1,0:T(8,128)(2,1)S(1)}, bf16[2,128,1024]{2,1,0:T(8,128)(2,1)S(1)}, u32[]{:S(2)}, u32[]{:S(2)}) collective-permute-start(bf16[2,128,1024]{2,1,0:T(8,128)(2,1)S(1)} %get-tuple-element.229), channel_id=1, source_target_pairs={{0,2},{1,3},{2,0},{3,1},{4,6},{5,7},{6,4},{7,5},{8,10},{9,11},{10,... | collective-permute-start | bytes 1572872 | tf_op jit(solution)/shard_map/ppermute | solution.py:305
  101.0 13.7 %collective-permute-start.19 = (bf16[2,128,1024]{2,1,0:T(8,128)(2,1)S(1)}, bf16[2,128,1024]{2,1,0:T(8,128)(2,1)S(1)}, u32[]{:S(2)}, u32[]{:S(2)}) collective-permute-start(bf16[2,128,1024]{2,1,0:T(8,128)(2,1)S(1)} %get-tuple-element.228), channel_id=1, source_target_pairs={{0,16},{1,17},{2,18},{3,19},{4,20},{5,21},{6,22},{7,23},{8,24},{9,... | collective-permute-start | bytes 1572872 | tf_op jit(solution)/shard_map/ppermute | solution.py:305
  101.6 20.5 %collective-permute-start.21 = (bf16[3072,128]{1,0:T(8,128)(2,1)S(1)}, bf16[3072,128]{1,0:T(8,128)(2,1)S(1)}, u32[]{:S(2)}, u32[]{:S(2)}) collective-permute-start(bf16[3072,128]{1,0:T(8,128)(2,1)S(1)} %get-tuple-element.176), channel_id=1, source_target_pairs={{0,1},{1,0},{2,3},{3,2},{4,5},{5,4},{6,7},{7,6},{8,9},{9,8},{10,11... | collective-permute-start | bytes 2359304 | tf_op jit(solution)/shard_map/ppermute | solution.py:305
  111.1 24.9 %collective-permute-start.24 = (bf16[2048,128]{1,0:T(8,128)(2,1)S(1)}, bf16[2048,128]{1,0:T(8,128)(2,1)S(1)}, u32[]{:S(2)}, u32[]{:S(2)}) collective-permute-start(bf16[2048,128]{1,0:T(8,128)(2,1)S(1)} %get-tuple-element.186), channel_id=1, source_target_pairs={{0,1},{1,0},{2,3},{3,2},{4,5},{5,4},{6,7},{7,6},{8,9},{9,8},{10,11... | collective-permute-start | bytes 1572872 | tf_op jit(solution)/shard_map/ppermute | solution.py:305
  115.1 30.4 %collective-permute-start.20 = (bf16[128,1024]{1,0:T(8,128)(2,1)S(1)}, bf16[128,1024]{1,0:T(8,128)(2,1)S(1)}, u32[]{:S(2)}, u32[]{:S(2)}) collective-permute-start(bf16[128,1024]{1,0:T(8,128)(2,1)S(1)} %fusion.9), channel_id=1, source_target_pairs={{0,2},{1,3},{2,0},{3,1},{4,6},{5,7},{6,4},{7,5},{8,10},{9,11},{10,... | collective-permute-start | bytes 786440 | tf_op jit(solution)/shard_map/ppermute | solution.py:305
  116.6 29.5 %collective-permute-start.23 = (bf16[128,1024]{1,0:T(8,128)(2,1)S(1)}, bf16[128,1024]{1,0:T(8,128)(2,1)S(1)}, u32[]{:S(2)}, u32[]{:S(2)}) collective-permute-start(bf16[128,1024]{1,0:T(8,128)(2,1)S(1)} %fusion.10), channel_id=1, source_target_pairs={{0,16},{1,17},{2,18},{3,19},{4,20},{5,21},{6,22},{7,23},{8,24},{9,... | collective-permute-start | bytes 786440 | tf_op jit(solution)/shard_map/ppermute | solution.py:305
  122.2 29.9 %collective-permute-start.29 = (bf16[2048,128]{1,0:T(8,128)(2,1)S(1)}, bf16[2048,128]{1,0:T(8,128)(2,1)S(1)}, u32[]{:S(2)}, u32[]{:S(2)}) collective-permute-start(bf16[2048,128]{1,0:T(8,128)(2,1)S(1)} %slice.383), channel_id=1, source_target_pairs={{0,4},{1,5},{2,6},{3,7},{4,0},{5,1},{6,2},{7,3},{8,12},{9,13},{10,... | collective-permute-start | bytes 1572872 | tf_op jit(solution)/shard_map/ppermute | solution.py:305
  139.3 16.0 %collective-permute-start.25 = (bf16[4,256,1024]{2,1,0:T(8,128)(2,1)S(1)}, bf16[4,256,1024]{2,1,0:T(8,128)(2,1)S(1)}, u32[]{:S(2)}, u32[]{:S(2)}) collective-permute-start(bf16[4,256,1024]{2,1,0:T(8,128)(2,1)S(1)} %shard_map.273), channel_id=1, source_target_pairs={{0,8},{1,9},{2,10},{3,11},{4,12},{5,13},{6,14},{7,15},{8,0},{9,1},... | collective-permute-start | bytes 6291464 | tf_op jit(solution)/shard_map/ppermute | solution.py:305
  139.4 28.4 %collective-permute-start.27 = (bf16[1024,128]{1,0:T(8,128)(2,1)S(1)}, bf16[1024,128]{1,0:T(8,128)(2,1)S(1)}, u32[]{:S(2)}, u32[]{:S(2)}) collective-permute-start(bf16[1024,128]{1,0:T(8,128)(2,1)S(1)} %slice.384), channel_id=1, source_target_pairs={{0,4},{1,5},{2,6},{3,7},{4,0},{5,1},{6,2},{7,3},{8,12},{9,13},{10,... | collective-permute-start | bytes 786440 | tf_op jit(solution)/shard_map/ppermute | solution.py:305
  145.5 21.4 %collective-permute-start.28 = (bf16[1600,128]{1,0:T(8,128)(2,1)S(1)}, bf16[1600,128]{1,0:T(8,128)(2,1)S(1)}, u32[]{:S(2)}, u32[]{:S(2)}) collective-permute-start(bf16[1600,128]{1,0:T(8,128)(2,1)S(1)} %get-tuple-element.191), channel_id=1, source_target_pairs={{0,1},{1,0},{2,3},{3,2},{4,5},{5,4},{6,7},{7,6},{8,9},{9,8},{10,11... | collective-permute-start | bytes 1228808 | tf_op jit(solution)/shard_map/ppermute | solution.py:305
  152.3 14.4 %collective-permute-start.32 = (bf16[512,128]{1,0:T(8,128)(2,1)S(1)}, bf16[512,128]{1,0:T(8,128)(2,1)S(1)}, u32[]{:S(2)}, u32[]{:S(2)}) collective-permute-start(bf16[512,128]{1,0:T(8,128)(2,1)S(1)} %slice.303), channel_id=1, source_target_pairs={{0,18},{1,19},{2,16},{3,17},{4,22},{5,23},{6,20},{7,21},{8,26},{9,... | collective-permute-start | bytes 393224 | tf_op jit(solution)/shard_map/ppermute | solution.py:305
  152.4 14.2 %collective-permute-start.30 = (bf16[512,128]{1,0:T(8,128)(2,1)S(1)}, bf16[512,128]{1,0:T(8,128)(2,1)S(1)}, u32[]{:S(2)}, u32[]{:S(2)}) collective-permute-start(bf16[512,128]{1,0:T(8,128)(2,1)S(1)} %slice.303), channel_id=1, source_target_pairs={{0,2},{1,3},{2,0},{3,1},{4,6},{5,7},{6,4},{7,5},{8,10},{9,11},{10,... | collective-permute-start | bytes 393224 | tf_op jit(solution)/shard_map/ppermute | solution.py:305
  155.3 11.3 %collective-permute-start.31 = (bf16[1536,128]{1,0:T(8,128)(2,1)S(1)}, bf16[1536,128]{1,0:T(8,128)(2,1)S(1)}, u32[]{:S(2)}, u32[]{:S(2)}) collective-permute-start(bf16[1536,128]{1,0:T(8,128)(2,1)S(1)} %slice.302), channel_id=1, source_target_pairs={{0,16},{1,17},{2,18},{3,19},{4,20},{5,21},{6,22},{7,23},{8,24},{9,... | collective-permute-start | bytes 1179656 | tf_op jit(solution)/shard_map/ppermute | solution.py:305
  166.8 30.5 %collective-permute-start.41 = (bf16[3072,128]{1,0:T(8,128)(2,1)S(1)}, bf16[3072,128]{1,0:T(8,128)(2,1)S(1)}, u32[]{:S(2)}, u32[]{:S(2)}) collective-permute-start(bf16[3072,128]{1,0:T(8,128)(2,1)S(1)} %select_dynamic-update-slice_fusion.near), channel_id=1, source_target_pairs={{0,8},{1,9},{2,10},{3,11},{4,12},{5,13},{6,14},{7,15},{8,0},{9,1},... | collective-permute-start | bytes 2359304 | tf_op jit(solution)/shard_map/ppermute | solution.py:305
  167.0 11.3 %collective-permute-start.34 = (bf16[800,128]{1,0:T(8,128)(2,1)S(1)}, bf16[800,128]{1,0:T(8,128)(2,1)S(1)}, u32[]{:S(2)}, u32[]{:S(2)}) collective-permute-start(bf16[800,128]{1,0:T(8,128)(2,1)S(1)} %slice.385), channel_id=1, source_target_pairs={{0,4},{1,5},{2,6},{3,7},{4,0},{5,1},{6,2},{7,3},{8,12},{9,13},{10,... | collective-permute-start | bytes 614408 | tf_op jit(solution)/shard_map/ppermute | solution.py:305
  167.1 14.4 %collective-permute-start.26 = (bf16[2,128,1024]{2,1,0:T(8,128)(2,1)S(1)}, bf16[2,128,1024]{2,1,0:T(8,128)(2,1)S(1)}, u32[]{:S(2)}, u32[]{:S(2)}) collective-permute-start(bf16[2,128,1024]{2,1,0:T(8,128)(2,1)S(1)} %get-tuple-element.227), channel_id=1, source_target_pairs={{0,16},{1,17},{2,18},{3,19},{4,20},{5,21},{6,22},{7,23},{8,24},{9,... | collective-permute-start | bytes 1572872 | tf_op jit(solution)/shard_map/ppermute | solution.py:305
  167.7 19.1 %collective-permute-start.35 = (bf16[2,128,1024]{2,1,0:T(8,128)(2,1)S(1)}, bf16[2,128,1024]{2,1,0:T(8,128)(2,1)S(1)}, u32[]{:S(2)}, u32[]{:S(2)}) collective-permute-start(bf16[2,128,1024]{2,1,0:T(8,128)(2,1)S(1)} %get-tuple-element.226), channel_id=1, source_target_pairs={{0,2},{1,3},{2,0},{3,1},{4,6},{5,7},{6,4},{7,5},{8,10},{9,11},{10,... | collective-permute-start | bytes 1572872 | tf_op jit(solution)/shard_map/ppermute | solution.py:305
  178.4 14.3 %collective-permute-start.38 = (bf16[912,128]{1,0:T(8,128)(2,1)S(1)}, bf16[912,128]{1,0:T(8,128)(2,1)S(1)}, u32[]{:S(2)}, u32[]{:S(2)}) collective-permute-start(bf16[912,128]{1,0:T(8,128)(2,1)S(1)} %pad_maximum_fusion.8), channel_id=1, source_target_pairs={{0,18},{1,19},{2,16},{3,17},{4,22},{5,23},{6,20},{7,21},{8,26},{9,... | collective-permute-start | bytes 700424 | tf_op jit(solution)/shard_map/ppermute | solution.py:305
  178.5 18.4 %collective-permute-start.36 = (bf16[912,128]{1,0:T(8,128)(2,1)S(1)}, bf16[912,128]{1,0:T(8,128)(2,1)S(1)}, u32[]{:S(2)}, u32[]{:S(2)}) collective-permute-start(bf16[912,128]{1,0:T(8,128)(2,1)S(1)} %pad_maximum_fusion.8), channel_id=1, source_target_pairs={{0,2},{1,3},{2,0},{3,1},{4,6},{5,7},{6,4},{7,5},{8,10},{9,11},{10,... | collective-permute-start | bytes 700424 | tf_op jit(solution)/shard_map/ppermute | solution.py:305
  181.4 13.6 %collective-permute-start.37 = (bf16[912,128]{1,0:T(8,128)(2,1)S(1)}, bf16[912,128]{1,0:T(8,128)(2,1)S(1)}, u32[]{:S(2)}, u32[]{:S(2)}) collective-permute-start(bf16[912,128]{1,0:T(8,128)(2,1)S(1)} %pad_maximum_fusion.7), channel_id=1, source_target_pairs={{0,16},{1,17},{2,18},{3,19},{4,20},{5,21},{6,22},{7,23},{8,24},{9,... | collective-permute-start | bytes 700424 | tf_op jit(solution)/shard_map/ppermute | solution.py:305
  187.3 12.1 %collective-permute-start.39 = (bf16[128,1024]{1,0:T(8,128)(2,1)S(1)}, bf16[128,1024]{1,0:T(8,128)(2,1)S(1)}, u32[]{:S(2)}, u32[]{:S(2)}) collective-permute-start(bf16[128,1024]{1,0:T(8,128)(2,1)S(1)} %fusion.12), channel_id=1, source_target_pairs={{0,16},{1,17},{2,18},{3,19},{4,20},{5,21},{6,22},{7,23},{8,24},{9,... | collective-permute-start | bytes 786440 | tf_op jit(solution)/shard_map/ppermute | solution.py:305
  192.7 9.1 %collective-permute-start.33 = (bf16[128,1024]{1,0:T(8,128)(2,1)S(1)}, bf16[128,1024]{1,0:T(8,128)(2,1)S(1)}, u32[]{:S(2)}, u32[]{:S(2)}) collective-permute-start(bf16[128,1024]{1,0:T(8,128)(2,1)S(1)} %fusion.11), channel_id=1, source_target_pairs={{0,2},{1,3},{2,0},{3,1},{4,6},{5,7},{6,4},{7,5},{8,10},{9,11},{10,... | collective-permute-start | bytes 786440 | tf_op jit(solution)/shard_map/ppermute | solution.py:305
  197.1 9.1 %collective-permute-start.40 = (bf16[3664,128]{1,0:T(8,128)(2,1)S(1)}, bf16[3664,128]{1,0:T(8,128)(2,1)S(1)}, u32[]{:S(2)}, u32[]{:S(2)}) collective-permute-start(bf16[3664,128]{1,0:T(8,128)(2,1)S(1)} %get-tuple-element.216.near), channel_id=1, source_target_pairs={{0,8},{1,9},{2,10},{3,11},{4,12},{5,13},{6,14},{7,15},{8,0},{9,1},... | collective-permute-start | bytes 2813960 | tf_op jit(solution)/shard_map/ppermute | solution.py:305
  (7 other events, 15.6 us)

commit v4 on v3

--- a/solution.py
+++ b/solution.py
@@ -288,9 +288,9 @@
 FEED_ROWS = 2 * HIDDEN
 F32 = jnp.float32
 BF16 = jnp.bfloat16
-COST = 4000
+COST = 5000
 VMEM_LIMIT = 18 * 1024 * 1024
-VMEM_FIRST = 36 * 1024 * 1024
+VMEM_FIRST = 28 * 1024 * 1024
 VMEM_WHOLE = 56 * 1024 * 1024
 
 
@@ -442,12 +442,15 @@
     return heads * cos + jnp.where(lane % HEAD < 8, -ahead, behind) * sin
 
 
-def spread_tables(table, frequency):
-    spread = frequency[8:16, :].astype(BF16)
+def spread_tables(table):
     high = table.astype(BF16)
     low = (table - high.astype(F32)).astype(BF16)
-    cos = tn(high[:8], spread) + tn(low[:8], spread) + frequency[16:17, :]
-    return cos, tn(high[8:], spread) + tn(low[8:], spread)
+    row = lax.broadcasted_iota(jnp.int32, (32, 2 * LANES), 0)
+    lane = lax.broadcasted_iota(jnp.int32, (32, 2 * LANES), 1)
+    goes = ((row // 8) % 2 == lane // LANES) & (lane % HEAD < ROT) & (lane % 8 == row % 8)
+    both = tn(jnp.concatenate([high, low]), goes.astype(BF16))
+    still = lax.broadcasted_iota(jnp.int32, (1, LANES), 1) % HEAD >= ROT
+    return both[:, :LANES] + still.astype(F32), both[:, LANES:]
 
 
 def gelu_parts(hidden):
@@ -539,7 +542,7 @@
         phases = jnp.broadcast_to(position, (8, tokens)) * frequency[0:8, 0:1]
         table = jnp.concatenate([jnp.cos(phases), jnp.sin(phases)], axis=0)
         tables_out[sequence] = table
-        cos, sin = spread_tables(table, frequency)
+        cos, sin = spread_tables(table)
         part = mixed[sequence * tokens : (sequence + 1) * tokens]
         queries = turn(part[:, :LANES], cos, sin, lane).astype(BF16)
         keys = turn(part[:, LANES : 2 * LANES], cos, sin, lane).astype(BF16)
@@ -562,15 +565,8 @@
 
 
 def turn_constants():
-    frequency = np.zeros((24, LANES), np.float32)
     powers = np.power(np.float32(10000.0), -2.0 * np.arange(ROT // 2, dtype=np.float32) / np.float32(ROT))
-    frequency[0:8, :] = powers[:, None]
-    for lane in range(LANES):
-        if lane % HEAD < ROT:
-            frequency[8 + lane % 8, lane] = 1.0
-        else:
-            frequency[16, lane] = 1.0
-    return frequency
+    return np.tile(powers[:, None].astype(np.float32), (1, LANES))
 
 
 def forward(info, inputs, weights, frequency, tokens, width, far=False):
@@ -648,26 +644,22 @@
         yield info[0] ^ (2 * z + 1), other.at[rows]
 
 
-def last_grad_body(info, near, far, act, far_act, context, far_context, mine, other, total, dense_total):
+def last_grad_body(info, near, far, act, far_act, context, far_context, mine, other, dense_out, total, dense_total):
     step = pl.program_id(0)
     total[...] = tn(act[...], near[...]) + tn(far_act[...], far[...])
     dense_total[...] = tn(context[...], near[...]) + tn(far_context[...], far[...])
-    shrink_rows = 4 * HIDDEN
     for part in range(2):
         cols = slice(part * LANES, (part + 1) * LANES)
-        for shard, out in each_shard(info, mine.at[:shrink_rows], other.at[:shrink_rows]):
+        for shard, out in each_shard(info, mine, other):
             out[pl.ds(pl.multiple_of(64 * (2 * step + part), 64), 64), :] = total[aligned(shard, 64), cols].astype(BF16)
-        block = dense_total[:, cols].astype(BF16)
-        rows = pl.ds(pl.multiple_of(shrink_rows + LANES * (2 * step + part), LANES), LANES)
-        mine[rows, :] = block
-        other[rows, :] = block
+        dense_out[pl.ds(pl.multiple_of(LANES * (2 * step + part), LANES), LANES), :] = dense_total[:, cols].astype(BF16)
 
 
 def last_backward(info, near, far, act, context):
     operands = [array.reshape(-1, array.shape[2]) for array in (near, far) + act + context]
     near = operands[0]
     width = near.shape[1]
-    outs = [((4 * HIDDEN + width, LANES), BF16)] * 2
+    outs = [((4 * HIDDEN, LANES), BF16)] * 2 + [((width, LANES), BF16)]
     columns = pl.BlockSpec((near.shape[0], 2 * LANES), lambda i, _: (0, i))
     return call(
         last_grad_body,
@@ -678,7 +670,7 @@
         [whole(shape) for shape, _ in outs],
         grid=(width // (2 * LANES),),
         scratch=[pltpu.VMEM((HIDDEN, 2 * LANES), F32), pltpu.VMEM((LANES, 2 * LANES), F32)],
-        micros=5,
+        micros=0,
     )
 
 
@@ -802,7 +794,7 @@
             grad_values = tn(low, part)
             grad_queries = from_heads(nn(grad_scores, keys), lane)
             grad_keys = tn(grad_scores, by_head(queries, lane))
-            cos, sin = spread_tables(all_tables[sequence], frequency)
+            cos, sin = spread_tables(all_tables[sequence])
             joined = [
                 turn(grad_queries * HEAD ** (-0.5), cos, -sin, lane),
                 turn(grad_keys * HEAD ** (-0.5), cos, -sin, lane),
@@ -867,7 +859,7 @@
         pltpu.VMEM((SMALL, LANES), F32),
     ]
     return call(
-        attention_grad_body, info, operands, in_specs, outs, out_specs, grid=(8,), scratch=scratch, micros=13
+        attention_grad_body, info, operands, in_specs, outs, out_specs, grid=(8,), scratch=scratch, micros=6
     )
 
 
@@ -882,7 +874,8 @@
     in_specs = [pairs(mixed.shape, 2 * far), pairs(pre.shape, 2 * far)]
     in_specs += [whole(operand.shape) for operand in operands[2:]]
     shape = (4, tokens, width)
-    return call(input_grad_body, info, operands, in_specs, [(shape, BF16)], [pairs(shape)], grid=(2,), micros=6)[0]
+    micros = 0 if far else 6
+    return call(input_grad_body, info, operands, in_specs, [(shape, BF16)], [pairs(shape)], grid=(2,), micros=micros)[0]
 
 
 def norm_body(info, block, cot, upper, upper_got, lower, lower_got, out):
@@ -917,7 +910,7 @@
         dense_out[:, part * LANES : (part + 1) * LANES] = rows.astype(F32)
 
 
-def last_grads_out_body(info, near, far, expand_out, mix_out):
+def expand_out_body(info, near, far, out):
     rank = info[1]
     upper = jnp.bitwise_and(rank, 1) == 1
     for number, one, two in each_rank(near, far, HIDDEN):
@@ -927,12 +920,15 @@
             lower_rows = jnp.where(upper, two[rows, :], one[rows, :])
             upper_rows = jnp.where(upper, one[rows, :], two[rows, :])
             joined = jnp.concatenate([lower_rows, upper_rows], axis=0)
-            expand_out[:, aligned(4 * shard + place, LANES)] = as_columns(joined)
-    size = 4 * HIDDEN
-    for number, one, two in each_rank(near.at[size:], far.at[size:], MIX_ROWS):
+            out[:, aligned(4 * shard + place, LANES)] = as_columns(joined)
+
+
+def mix_out_body(info, near, far, out):
+    rank = info[1]
+    for number, one, two in each_rank(near, far, MIX_ROWS):
         for piece, place in ((one, rank ^ number), (two, rank ^ number ^ 1)):
             for part in range(3):
-                mix_out[:, aligned(8 * part + place, LANES)] = as_columns(piece[part * LANES : (part + 1) * LANES, :])
+                out[:, aligned(8 * part + place, LANES)] = as_columns(piece[part * LANES : (part + 1) * LANES, :])
 
 
 def after(value, *others):
@@ -952,34 +948,35 @@
 
 
 def gather_second(upper, lower, upper_x, lower_low):
-    upper_pair = swap(jnp.stack([upper, upper_x]), low=1)
-    lower_pair = swap(jnp.stack([lower, lower_low]), x=1)
-    return (
-        jnp.stack([upper, upper_pair[0], upper_x, upper_pair[1]]),
-        jnp.stack([lower, lower_low, lower_pair[0], lower_pair[1]]),
+    return swap(jnp.stack([upper, upper_x]), low=1), swap(jnp.stack([lower, lower_low]), x=1)
+
+
+def gathered(upper, lower, upper_x, lower_low, upper_pair, lower_pair):
+    return jnp.concatenate(
+        [
+            jnp.stack([upper, upper_pair[0], upper_x, upper_pair[1]]),
+            jnp.stack([lower, lower_low, lower_pair[0], lower_pair[1]]),
+        ],
+        axis=1,
     )
 
 
 def reduce_first(mine, other, unit, *late):
     got = after(swap(other, y=1), *late)
     total = mine.astype(F32) + got.astype(F32)
-    return total, total[2 * unit :].astype(BF16)
-
-
-def reduce_second(total, sent, unit, *late):
-    kept = jnp.concatenate([total[: 2 * unit], total[4 * unit :]])
+    return total[: 2 * unit], total[2 * unit :].astype(BF16)
+
+
+def reduce_second(kept, sent, *late):
     return (kept + after(swap(sent, high=1), *late).astype(F32)).astype(BF16)
 
 
-def share_first(slices, unit):
-    away, own = slices[:unit], slices[unit:]
-    return own, swap(away, low=1), swap(own, x=1), swap(away, x=1, low=1)
-
-
-def share_last(slices, own_x, *late):
-    parts = after(share_first(slices, HIDDEN), *late)
-    dense_part = jnp.where(own_x, parts[0][HIDDEN:], parts[2][HIDDEN:])
-    return jnp.concatenate([part[:HIDDEN] for part in parts] + [dense_part])
+def share_first(slices, unit, *late):
+    return jnp.concatenate([slices[unit:], after(swap(slices[:unit], low=1), *late)])
+
+
+def share_second(pair, *late):
+    return after(swap(pair, x=1), *late)
 
 
 def scatter_first(near, far_got):
@@ -1050,13 +1047,7 @@
     low_last = swap(after(low_in, along), low=1)
     third = mark(info, along, high_in, low_in)
     upper_pair, lower_pair, across = after((upper_pair, lower_pair, across), third)
-    near = jnp.concatenate(
-        [
-            jnp.stack([upper, upper_pair[0], upper_x, upper_pair[1]]),
-            jnp.stack([lower, lower_low, lower_pair[0], lower_pair[1]]),
-        ],
-        axis=1,
-    )
+    near = gathered(upper, lower, upper_x, lower_low, upper_pair, lower_pair)
     both_last = swap(after(other_shrink, near), high=1, low=1)
     far = swap(near, core=1)
     cot_upper = after(cotangent[:half], near)
@@ -1066,45 +1057,68 @@
     high_last, low_last, both_last, cot_upper_x, far = after((high_last, low_last, both_last, cot_upper_x, far), mix)
     last, dense_held = pack_last(info, high_in, low_last, high_last, both_last, dense_weight)
     last_across = swap(last, y=1)
-    cot_near = gather_second(cot_upper, cotangent[half:], cot_upper_x, low_last[64:])
+    cot_pairs = gather_second(cot_upper, cotangent[half:], cot_upper_x, low_last[64:])
     far = after(far, last, cot_upper_x)
+    cot_near = gathered(cot_upper, cotangent[half:], cot_upper_x, low_last[64:], *cot_pairs)
+    cot_far = swap(cot_near, core=1)
+    far = after(far, cot_near)
     far_saved = forward(info, far, (mix, expand, vectors, bias), frequency, tokens, width, True)
     normed, heads, tables, probs, context, act, slope = zip(near_saved, far_saved)
+    last_mine, last_other, dense_grad = last_backward(info, cot_near, cot_far, act, context)
     last_across = after(last_across, context[1])
     dense = jnp.where(own_y, dense_held, last_across[256:])
-    branch_far, shrink = project(info, context[1], act[1], dense, (last, last_across), True)
+    branch_far, shrink = project(info, after(context[1], last_mine), act[1], dense, (last, last_across), True)
     branch_got = swap(branch_far, core=1)
-    cot_near = jnp.concatenate(after(cot_near, branch_far), axis=1)
-    cot_far = swap(cot_near, core=1)
-    (branch_near,) = project(info, context[0], act[0], dense, after(shrink, cot_near), False)
-    last_mine, last_other = last_backward(info, cot_near, after(cot_far, branch_near), act, context)
-    branch = scatter_first(after(branch_near, last_mine), branch_got)
+    (branch_near,) = project(info, context[0], act[0], dense, shrink, False)
+    branch_sum = (branch_near.astype(F32) + branch_got.astype(F32)).astype(BF16)
+    branch_kept, branch_sent = branch_sum[:2], branch_sum[2:]
     grad_pre, bias_grad, feed_sums, expand_mine, expand_other = expand_backward(
-        info, cot_near, cot_far, slope, normed, after(shrink, last_mine, branch[1], branch[3]), expand, vectors
-    )
-    branch = scatter_second(*branch, grad_pre)
+        info, cot_near, cot_far, slope, normed, after(shrink, branch_sent), expand, vectors
+    )
     last_part = reduce_first(last_mine, last_other, HIDDEN, grad_pre)
+    dense_got = after(swap(dense_grad, high=1), grad_pre)
+    dense_grad = (dense_grad.astype(F32) + dense_got.astype(F32)).astype(BF16)
     grad_mixed, mix_mine, mix_other = attention_backward(
         info,
         cot_near,
         cot_far,
         (normed, heads, tables, probs),
-        (after(dense, last_part[1], branch[1], branch[3]), frequency, mix, vectors, bias_grad, feed_sums),
-    )
+        (after(dense, last_part[1], dense_grad), frequency, mix, vectors, bias_grad, feed_sums),
+    )
+    branch = branch_kept.astype(F32) + after(swap(branch_sent, x=1), grad_mixed).astype(F32)
+    branch_own, branch_last = branch[0].astype(BF16), branch[1].astype(BF16)
+    last_slices = reduce_second(*last_part, grad_mixed)
+    dense_got = after(swap(dense_grad, y=1), grad_mixed)
+    dense_grad = (dense_grad.astype(F32) + dense_got.astype(F32)).astype(BF16)
     expand_part = reduce_first(expand_mine, expand_other, HIDDEN, grad_mixed)
-    branch = scatter_third(*branch, grad_mixed)
-    block_out = (block_input.astype(F32) + branch + (vectors[4] + vectors[5])).astype(BF16)
-    error_far = input_backward(info, after(grad_mixed, expand_part[1]), grad_pre, mix, expand, vectors, True)
+    error_far = input_backward(
+        info,
+        after(grad_mixed, branch_own, branch_last, last_slices, dense_grad, expand_part[1]),
+        grad_pre,
+        mix,
+        expand,
+        vectors,
+        True,
+    )
     error_got = swap(error_far, core=1)
-    error_near = input_backward(info, after(grad_mixed, error_far), grad_pre, mix, expand, vectors, False)
-    error = scatter_first(error_near, error_got)
-    last_slices = reduce_second(*last_part, HIDDEN, error_near)
-    mix_part = reduce_first(mix_mine, mix_other, MIX_ROWS, error[1], error[3])
-    last_near = share_last(last_slices, own_x, error[1], error[3])
-    last_far = swap(last_near, core=1)
-    fourth = mark(info, error[1], mix_part[1], last_near)
-    expand_slices = reduce_second(*expand_part, HIDDEN, fourth)
-    error = scatter_second(*error, expand_slices)
+    error_near = input_backward(
+        info, after(grad_mixed, error_far), grad_pre, mix, expand, vectors, False
+    )
+    mix_part = reduce_first(mix_mine, mix_other, MIX_ROWS, error_near)
+    last_pair = share_first(last_slices, HIDDEN, error_near)
+    dense_x = after(swap(dense_grad, x=1), error_near)
+    dense_part = jnp.where(own_x, dense_grad, dense_x)
+    error = scatter_first(after(error_near, mix_part[1], last_pair), error_got)
+    fourth = mark(info, last_pair, mix_part[1], error[1], error[3], dense_part)
+    expand_slices = reduce_second(*expand_part, fourth)
+    last_x = share_second(last_pair, fourth)
+    last_near = jnp.concatenate([last_pair, last_x, dense_part])
+    mix_slices = reduce_second(*mix_part, fourth)
+    error = scatter_second(*error, fourth)
+    fifth = mark(info, expand_slices, mix_slices, error[1], error[3], last_near)
+    expand_pair = share_first(expand_slices, HIDDEN, fifth)
+    mix_pair = share_first(mix_slices, MIX_ROWS, fifth)
+    last_far = swap(after(last_near, mix_pair), core=1)
 
     def out(body, near, far, shapes, flag=None):
         operands = [near, far]
@@ -1116,21 +1130,8 @@
 
     flag = own_y.astype(jnp.int32).reshape(1)
     shapes = [shrink_weight.shape, dense_weight.shape]
-    shrink_out, dense_out = out(last_out_body, last_near, after(last_far, fourth), shapes, flag)
-    mix_slices = reduce_second(*mix_part, MIX_ROWS, fourth)
-    slices = [expand_slices[:HIDDEN], mix_slices[:MIX_ROWS], expand_slices[HIDDEN:], mix_slices[MIX_ROWS:]]
-    slices = jnp.concatenate(slices)
-    parts = share_first(slices, HIDDEN + MIX_ROWS)
-    fifth = mark(info, slices, error[1], error[3])
-    parts = after(parts, fifth)
-    expand_near = jnp.concatenate([part[:HIDDEN] for part in parts])
-    mix_parts = [part[HIDDEN:] for part in parts]
-    mix_sums = [part[MIX_COLS:].astype(F32) for part in mix_parts]
-    mix_sums = ((mix_sums[0] + mix_sums[1]) + (mix_sums[2] + mix_sums[3])).astype(BF16)
-    near = jnp.concatenate([expand_near] + mix_parts + [mix_sums])
-    far = swap(near, core=1)
-    upper_got = after(swap(error[1], low=1), near)
-    lower_got = after(swap(error[3], x=1), near)
+    upper_got = after(swap(error[1], low=1), mix_pair, expand_pair)
+    lower_got = after(swap(error[3], x=1), mix_pair, expand_pair)
     operands = [block_input, cotangent, error[0], upper_got, error[2], lower_got]
     (input_grad,) = call(
         norm_body,
@@ -1140,9 +1141,20 @@
         [(block_input.shape, F32)],
         [whole(block_input.shape)],
     )
-    far = after(far, input_grad)
-    sums = mix_sums.astype(F32) + far[4 * (HIDDEN + MIX_ROWS) :].astype(F32)
-    expand_out, mix_out = out(last_grads_out_body, near, far, [expand_weight.shape, mix_weight.shape])
+    shrink_out, dense_out = out(last_out_body, last_near, after(last_far, input_grad), shapes, flag)
+    expand_near = jnp.concatenate([expand_pair, share_second(expand_pair, shrink_out)])
+    expand_far = swap(expand_near, core=1)
+    (expand_out,) = out(expand_out_body, expand_near, expand_far, [expand_weight.shape])
+    branch = branch_own.astype(F32) + after(swap(after(branch_last, mix_pair), low=1), expand_near).astype(F32)
+    block_out = (block_input.astype(F32) + branch + (vectors[4] + vectors[5])).astype(BF16)
+    mix_x = share_second(mix_pair, expand_near)
+    mix_parts = [mix_pair[:MIX_ROWS], mix_pair[MIX_ROWS:], mix_x[:MIX_ROWS], mix_x[MIX_ROWS:]]
+    mix_sums = [part[MIX_COLS:].astype(F32) for part in mix_parts]
+    mix_sums = ((mix_sums[0] + mix_sums[1]) + (mix_sums[2] + mix_sums[3])).astype(BF16)
+    near = jnp.concatenate(mix_parts + [mix_sums])
+    far = swap(near, core=1)
+    sums = mix_sums.astype(F32) + far[4 * MIX_ROWS :].astype(F32)
+    (mix_out,) = out(mix_out_body, near, far, [mix_weight.shape])
     return (
         block_out,
         input_grad,

time: 215 us -> 197 us (0.916)
  waiting for transfers between devices: 93.6 us -> 74.5 us
  starting transfers between devices: 37.3 us -> 39.8 us
    ppermute x42 -> x44, waiting for transfers between devices: 93.6 us -> 74.5 us  [permute(): return lax.ppermute(value, ('rep', 'fsdp'), pairs)]
    ppermute x42 -> x44, starting transfers between devices: 37.3 us -> 39.8 us  [permute(): return lax.ppermute(value, ('rep', 'fsdp'), pairs)]
    pallas_call x15 -> x16, Pallas kernels: 69.3 us -> 68.9 us  [call(): pl.pallas_call(body, grid_spec=pltpu.PrefetchScalarGridSpec(num_scalar_pr...]
  transfers between devices with their start and end apart: 42 -> 44, of which waited for: 19 -> 12; matrix products, arithmetic and copies ran while one was open for 3% -> 4% of each run, Pallas kernels for 28% -> 29%
where the time goes in v4:
time: 197 us; the launch traced here: 194 us
  waiting for transfers between devices  74.5 us (38%)
  Pallas kernels  68.9 us (35%)
  starting transfers between devices  39.8 us (20%)
  other arithmetic  6.22 us (3%)
  local copies, waits for them, and re-layouts  3.39 us (2%)
    ppermute x44, waiting for transfers between devices, permute(): return lax.ppermute(value, ('rep', 'fsdp'), pairs)  74.5 us
    pallas_call x16, Pallas kernels, call(): pl.pallas_call(body, grid_spec=pltpu.PrefetchScalarGridSpec(num_scalar_pr...  68.9 us
    ppermute x44, starting transfers between devices, permute(): return lax.ppermute(value, ('rep', 'fsdp'), pairs)  39.8 us
  transfers between devices with their start and end apart: 44, of which 12 were waited for; matrix products, arithmetic and copies ran while one was open for 4% of the time, Pallas kernels for 29%

profile of v4, /device:TPU:6, one launch (start us, length us, event | category | flops | bytes accessed | tf_op | source)
XLA Modules:
  0.0 194.2 jit_solution(9614617798104428481)
XLA Ops:
  1.3 3.3 %shard_map.263 = (bf16[912,128]{1,0:T(8,128)(2,1)}, bf16[912,128]{1,0:T(8,128)(2,1)}) custom-call(s32[2]{0:T(128)} %pad_add_fusion.info, bf16[128,3072]{1,0:T(8,128)(2,1)} %mix.1, bf16[128,4096]{1,0:T(8,128)(2,1)} %expand.1, bf16[1,128]{1,0:T(2,128)(2,1)} %bitcast.87, bf16[1,128]{1,0:T(2,128)(2,1)} %bitcast.88, bf16[1,128]{1,0:T(2,128)(2,1)} %bitcast.89, ...), custom_call_target="tpu_custom_call" | custom-call | flops 20000000000 | bytes 60000000 | tf_op jit(solution)/shard_map/pallas_call | solution.py:329
  4.6 3.6 %collective-permute-start.6 = (bf16[912,128]{1,0:T(8,128)(2,1)}, bf16[912,128]{1,0:T(8,128)(2,1)S(1)}, u32[]{:S(2)}, u32[]{:S(2)}) collective-permute-start(bf16[912,128]{1,0:T(8,128)(2,1)} %get-tuple-element.115), channel_id=1, source_target_pairs={{0,6},{1,7},{2,4},{3,5},{4,2},{5,3},{6,0},{7,1},{8,14},{9,15},{10,... | collective-permute-start | bytes 700424 | tf_op jit(solution)/shard_map/ppermute | solution.py:305
  8.4 2.1 %collective-permute-start.3 = (bf16[144,1024]{1,0:T(8,128)(2,1)S(1)}, bf16[144,1024]{1,0:T(8,128)(2,1)S(1)}, u32[]{:S(2)}, u32[]{:S(2)}) collective-permute-start(bf16[144,1024]{1,0:T(8,128)(2,1)S(1)} %get-tuple-element.226), channel_id=1, source_target_pairs={{0,2},{1,3},{2,0},{3,1},{4,6},{5,7},{6,4},{7,5},{8,10},{9,11},{10,... | collective-permute-start | bytes 884744 | tf_op jit(solution)/shard_map/ppermute | solution.py:305
  11.0 3.2 %shard_map.264 = (bf16[192,1024]{1,0:T(8,128)(2,1)}, bf16[192,1024]{1,0:T(8,128)(2,1)}, bf16[64,1024]{1,0:T(8,128)(2,1)}) custom-call(s32[2]{0:T(128)} %pad_add_fusion.info, bf16[512,1024]{1,0:T(8,128)(2,1)} %shrink.1, bf16[128,1024]{1,0:T(8,128)(2,1)} %dense.3, bf16[256,1024]{1,0:T(8,128)(2,1)} %cot.3), custom_call_target="tpu_custom_call" | custom-call | flops 20000000000 | bytes 60000000 | tf_op jit(solution)/shard_map/pallas_call | solution.py:329
  14.2 3.4 %collective-permute-done = bf16[128,1024]{1,0:T(8,128)(2,1)S(1)} collective-permute-done((bf16[128,1024]{1,0:T(8,128)(2,1)S(1)}, bf16[128,1024]{1,0:T(8,128)(2,1)S(1)}, u32[]{:S(2)}, u32[]{:S(2)}) %collective-permute-start) | collective-permute-done | bytes 262176 | tf_op jit(solution)/shard_map/ppermute | solution.py:305
  18.2 12.3 %collective-permute-done.3 = bf16[144,1024]{1,0:T(8,128)(2,1)S(1)} collective-permute-done((bf16[144,1024]{1,0:T(8,128)(2,1)S(1)}, bf16[144,1024]{1,0:T(8,128)(2,1)S(1)}, u32[]{:S(2)}, u32[]{:S(2)}) %collective-permute-start.3) | collective-permute-done | bytes 294944 | tf_op jit(solution)/shard_map/ppermute | solution.py:305
  31.8 2.0 %collective-permute-start.9 = (bf16[192,1024]{1,0:T(8,128)(2,1)S(1)}, bf16[192,1024]{1,0:T(8,128)(2,1)S(1)}, u32[]{:S(2)}, u32[]{:S(2)}) collective-permute-start(bf16[192,1024]{1,0:T(8,128)(2,1)S(1)} %copy-done.10), channel_id=1, source_target_pairs={{0,2},{1,3},{2,0},{3,1},{4,6},{5,7},{6,4},{7,5},{8,10},{9,11},{10,... | collective-permute-start | bytes 1179656 | tf_op jit(solution)/shard_map/ppermute | solution.py:305
  34.4 19.4 %collective-permute-done.1 = bf16[2,128,1024]{2,1,0:T(8,128)(2,1)S(1)} collective-permute-done((bf16[2,128,1024]{2,1,0:T(8,128)(2,1)S(1)}, bf16[2,128,1024]{2,1,0:T(8,128)(2,1)S(1)}, u32[]{:S(2)}, u32[]{:S(2)}) %collective-permute-start.1) | collective-permute-done | bytes 524320 | tf_op jit(solution)/shard_map/ppermute | solution.py:305
  54.7 1.7 collective-permute-start.11
  57.0 7.3 %shard_map.265 = (bf16[4,256,1024]{2,1,0:T(8,128)(2,1)S(1)}, bf16[4,256,384]{2,1,0:T(8,128)(2,1)S(1)}, f32[4,16,256]{2,1,0:T(8,128)S(1)}, bf16[4,2,256,256]{3,2,...) custom-call(s32[2]{0:T(128)S(1)} %copy-done.3, ...), custom_call_target="tpu_custom_call" | custom-call | flops 44999999488 | bytes 135000000 | tf_op jit(solution)/shard_map/pallas_call | solution.py:329
  64.4 1.6 collective-permute-start.16
  67.4 11.7 %collective-permute-done.15 = bf16[2,128,1024]{2,1,0:T(8,128)(2,1)S(1)} collective-permute-done((bf16[2,128,1024]{2,1,0:T(8,128)(2,1)S(1)}, bf16[2,128,1024]{2,1,0:T(8,128)(2,1)S(1)}, u32[]{:S(2)}, u32[]{:S(2)}) %collective-permute-start.15) | collective-permute-done | bytes 524320 | tf_op jit(solution)/shard_map/ppermute | solution.py:305
  79.5 6.9 %shard_map.267 = (bf16[4,256,1024]{2,1,0:T(8,128)(2,1)S(1)}, bf16[4,256,384]{2,1,0:T(8,128)(2,1)S(1)}, f32[4,16,256]{2,1,0:T(8,128)S(1)}, bf16[4,2,256,256]{3,2,...) custom-call(s32[2]{0:T(128)S(1)} %copy-done.3, ...), custom_call_target="tpu_custom_call" | custom-call | flops 44999999488 | bytes 135000000 | tf_op jit(solution)/shard_map/pallas_call | solution.py:329
  86.5 4.8 %shard_map.268 = (bf16[2048,128]{1,0:T(8,128)(2,1)S(1)}, bf16[2048,128]{1,0:T(8,128)(2,1)S(1)}, bf16[1024,128]{1,0:T(8,128)(2,1)S(1)}) custom-call(s32[2]{0:T(128)S(1)} %copy-done.3, bf16[1024,1024]{1,0:T(8,128)(2,1)S(1)} %bitcast.63, bf16[1024,1024]{1,0:T(8,128)(2,1)S(1)} %bitcast.64, bf16[1024,512]{1,0:T(8,128)(2,1)S(1)} %bitcast.65, ...), custom_call_target="tpu_custom_call" | custom-call | tf_op jit(solution)/shard_map/pallas_call | solution.py:329
  91.3 2.6 %shard_map.269 = (bf16[4,256,1024]{2,1,0:T(8,128)(2,1)S(1)}, bf16[512,1024]{1,0:T(8,128)(2,1)S(1)}) custom-call(s32[2]{0:T(128)S(1)} %copy-done.3, bf16[4,256,128]{2,1,0:T(8,128)(2,1)S(1)} %get-tuple-element.154.context, bf16[4,256,512]{2,1,0:T(8,128)(2,1)S(1)} %get-tuple-element.152.act, bf16[128,1024]{1,0:T(8,128)(2,1)S(1)} %slice_select_fusion.dense, ...), custom_call_target="tpu_custom_call" | custom-call | flops 24999999488 | bytes 75000000 | tf_op jit(solution)/shard_map/pallas_call | solution.py:329
  95.0 2.9 %collective-permute-start.21 = (bf16[1024,128]{1,0:T(8,128)(2,1)S(1)}, bf16[1024,128]{1,0:T(8,128)(2,1)S(1)}, u32[]{:S(2)}, u32[]{:S(2)}) collective-permute-start(bf16[1024,128]{1,0:T(8,128)(2,1)S(1)} %get-tuple-element.171), channel_id=1, source_target_pairs={{0,4},{1,5},{2,6},{3,7},{4,0},{5,1},{6,2},{7,3},{8,12},{9,13},{10,... | collective-permute-start | bytes 786440 | tf_op jit(solution)/shard_map/ppermute | solution.py:305
  97.9 2.5 %shard_map.270 = bf16[4,256,1024]{2,1,0:T(8,128)(2,1)S(1)} custom-call(s32[2]{0:T(128)S(1)} %copy-done.3, bf16[4,256,128]{2,1,0:T(8,128)(2,1)S(1)} %get-tuple-element.130.context, bf16[4,256,512]{2,1,0:T(8,128)(2,1)S(1)} %get-tuple-element.131.act, bf16[128,1024]{1,0:T(8,128)(2,1)S(1)} %slice_select_fusion.dense, bf16[512,1024]{1,0:T(8,128)(2,1)S(1)} %get-tuple-element.168.shrink), custom_call_target="tpu_custom_call" | custom-call | flops 24999999488 | bytes 75000000 | tf_op jit(solution)/shard_map/pallas_call | solution.py:329
  100.5 1.0 add_convert_fusion
  102.1 9.0 %shard_map.271 = (bf16[8,256,512]{2,1,0:T(8,128)(2,1)S(1)}, f32[8,512]{1,0:T(8,128)S(1)}, f32[8,1024]{1,0:T(8,128)S(1)}, bf16[2048,128]{1,0:T(8,128)(2,1)S(1)}, bf16[2048,128]{1,0:T(8,128)(2,1)S(1)}) custom-call(s32[2]{0:T(128)S(1)} %copy-done.3, bf16[4,256,1024]{2,1,0:T(8,128)(2,1)S(1)} %maximum_maximum_fusion.1.near, ...), custom_call_target="tpu_custom_call" | custom-call | flops 44999999488 | bytes 135000000 | tf_op jit(solution)/shard_map/pallas_call | solution.py:329
  111.4 0.8 collective-permute-start.23
  112.2 0.9 collective-permute-start.24
  113.0 1.2 collective-permute-start.25
  114.2 12.5 %shard_map.272 = (bf16[8,256,384]{2,1,0:T(8,128)(2,1)S(1)}, bf16[1600,128]{1,0:T(8,128)(2,1)S(1)}, bf16[1600,128]{1,0:T(8,128)(2,1)S(1)}) custom-call(s32[2]{0:T(128)S(1)} %copy-done.3, bf16[4,256,1024]{2,1,0:T(8,128)(2,1)S(1)} %maximum_maximum_fusion.1.near, bf16[4,256,1024]{2,1,0:T(8,128)(2,1)S(1)} %collective-permute-done.17.far, ...), custom_call_target="tpu_custom_call" | custom-call | flops 30000001024 | bytes 90000000 | tf_op jit(solution)/shard_map/pallas_call | solution.py:329
  126.7 0.9 collective-permute-start.22
  127.9 1.8 collective-permute-start.27
  129.6 0.7 collective-permute-start.29
  130.4 2.2 %collective-permute-done.25 = bf16[2048,128]{1,0:T(8,128)(2,1)S(1)} collective-permute-done((bf16[2048,128]{1,0:T(8,128)(2,1)S(1)}, bf16[2048,128]{1,0:T(8,128)(2,1)S(1)}, u32[]{:S(2)}, u32[]{:S(2)}) %collective-permute-start.25) | collective-permute-done | bytes 524320 | tf_op jit(solution)/shard_map/ppermute | solution.py:305
  132.8 2.3 %collective-permute-start.31 = (bf16[1024,128]{1,0:T(8,128)(2,1)S(1)}, bf16[1024,128]{1,0:T(8,128)(2,1)S(1)}, u32[]{:S(2)}, u32[]{:S(2)}) collective-permute-start(bf16[1024,128]{1,0:T(8,128)(2,1)S(1)} %slice.294), channel_id=1, source_target_pairs={{0,4},{1,5},{2,6},{3,7},{4,0},{5,1},{6,2},{7,3},{8,12},{9,13},{10,... | collective-permute-start | bytes 786440 | tf_op jit(solution)/shard_map/ppermute | solution.py:305
  135.5 3.1 %shard_map.273 = bf16[4,256,1024]{2,1,0:T(8,128)(2,1)S(1)} custom-call(s32[2]{0:T(128)S(1)} %copy-done.3, bf16[8,256,384]{2,1,0:T(8,128)(2,1)S(1)} %get-tuple-element.186.mixed, bf16[8,256,512]{2,1,0:T(8,128)(2,1)S(1)} %get-tuple-element.169.pre, bf16[1024,384]{1,0:T(8,128)(2,1)S(1)} %get-tuple-element.133.mix, ...), custom_call_target="tpu_custom_call" | custom-call | tf_op jit(solution)/shard_map/pallas_call | solution.py:329
  138.8 3.4 %shard_map.274 = bf16[4,256,1024]{2,1,0:T(8,128)(2,1)S(1)} custom-call(s32[2]{0:T(128)S(1)} %copy-done.3, bf16[8,256,384]{2,1,0:T(8,128)(2,1)S(1)} %get-tuple-element.186.mixed, bf16[8,256,512]{2,1,0:T(8,128)(2,1)S(1)} %get-tuple-element.169.pre, bf16[1024,384]{1,0:T(8,128)(2,1)S(1)} %get-tuple-element.133.mix, ...), custom_call_target="tpu_custom_call" | custom-call | flops 30000001024 | bytes 90000000 | tf_op jit(solution)/shard_map/pallas_call | solution.py:329
  142.3 0.7 collective-permute-start.26
  143.1 1.6 collective-permute-start.34
  144.7 1.0 convert_add_fusion
  146.5 1.0 collective-permute-start.32
  147.5 7.5 %collective-permute-done.26 = bf16[800,128]{1,0:T(8,128)(2,1)S(1)} collective-permute-done((bf16[800,128]{1,0:T(8,128)(2,1)S(1)}, bf16[800,128]{1,0:T(8,128)(2,1)S(1)}, u32[]{:S(2)}, u32[]{:S(2)}) %collective-permute-start.26) | collective-permute-done | bytes 204832 | tf_op jit(solution)/shard_map/ppermute | solution.py:305
  155.2 2.1 %collective-permute-start.36 = (bf16[512,128]{1,0:T(8,128)(2,1)S(1)}, bf16[512,128]{1,0:T(8,128)(2,1)S(1)}, u32[]{:S(2)}, u32[]{:S(2)}) collective-permute-start(bf16[512,128]{1,0:T(8,128)(2,1)S(1)} %get-tuple-element.228), channel_id=1, source_target_pairs={{0,2},{1,3},{2,0},{3,1},{4,6},{5,7},{6,4},{7,5},{8,10},{9,11},{10,... | collective-permute-start | bytes 393224 | tf_op jit(solution)/shard_map/ppermute | solution.py:305
  157.3 7.6 %collective-permute-done.33 = bf16[2,128,1024]{2,1,0:T(8,128)(2,1)S(1)} collective-permute-done((bf16[2,128,1024]{2,1,0:T(8,128)(2,1)S(1)}, bf16[2,128,1024]{2,1,0:T(8,128)(2,1)S(1)}, u32[]{:S(2)}, u32[]{:S(2)}) %collective-permute-start.33) | collective-permute-done | bytes 524320 | tf_op jit(solution)/shard_map/ppermute | solution.py:305
  165.4 1.8 collective-permute-done.30
  167.8 1.5 collective-permute-start.41
  169.3 1.9 %collective-permute-start.35 = (bf16[256,1024]{1,0:T(8,128)(2,1)S(1)}, bf16[256,1024]{1,0:T(8,128)(2,1)S(1)}, u32[]{:S(2)}, u32[]{:S(2)}) collective-permute-start(bf16[256,1024]{1,0:T(8,128)(2,1)S(1)} %slice_bitcast_fusion.2), channel_id=1, source_target_pairs={{0,2},{1,3},{2,0},{3,1},{4,6},{5,7},{6,4},{7,5},{8,10},{9,11},{10,... | collective-permute-start | bytes 1572872 | tf_op jit(solution)/shard_map/ppermute | solution.py:305
  172.0 4.5 %collective-permute-done.39.upper_got = bf16[128,1024]{1,0:T(8,128)(2,1)S(1)} collective-permute-done((bf16[128,1024]{1,0:T(8,128)(2,1)S(1)}, bf16[128,1024]{1,0:T(8,128)(2,1)S(1)}, u32[]{:S(2)}, u32[]{:S(2)}) %collective-permute-start.39) | collective-permute-done | bytes 262176 | tf_op jit(solution)/shard_map/ppermute | solution.py:305
  176.6 2.2 %shard_map.275 = f32[256,1024]{1,0:T(8,128)} custom-call(s32[2]{0:T(128)S(1)} %copy-done.3, bf16[256,1024]{1,0:T(8,128)(2,1)S(1)} %copy-done.1, bf16[256,1024]{1,0:T(8,128)(2,1)S(1)} %copy-done.2, f32[128,1024]{1,0:T(8,128)S(1)} %slice_bitcast_fusion.1.upper, bf16[128,1024]{1,0:T(8,128)(2,1)S(1)} %collective-permute-done.39.upper_got, ...), custom_call_target="tpu_custom_call" | custom-call | flops 20000000000 | bytes 60000000 | tf_op jit(solution)/shard_map/pallas_call | solution.py:329
  178.8 2.2 %shard_map.276 = (f32[512,1024]{1,0:T(8,128)}, f32[128,1024]{1,0:T(8,128)}) custom-call(s32[2]{0:T(128)S(1)} %copy-done.3, bf16[3072,128]{1,0:T(8,128)(2,1)S(1)} %pad_maximum_fusion.near, bf16[3072,128]{1,0:T(8,128)(2,1)S(1)} %collective-permute-done.38.far, s32[1]{0:T(128)} %bitcast.35.own_dense), custom_call_target="tpu_custom_call" | custom-call | flops 20000000000 | bytes 60000000 | tf_op jit(solution)/shard_map/pallas_call | solution.py:329
  181.0 2.6 %collective-permute-done.37 = bf16[1024,128]{1,0:T(8,128)(2,1)S(1)} collective-permute-done((bf16[1024,128]{1,0:T(8,128)(2,1)S(1)}, bf16[1024,128]{1,0:T(8,128)(2,1)S(1)}, u32[]{:S(2)}, u32[]{:S(2)}) %collective-permute-start.37) | collective-permute-done | bytes 262176 | tf_op jit(solution)/shard_map/ppermute | solution.py:305
  184.3 1.5 collective-permute-done.35
  185.8 1.1 add_convert_fusion.2
  186.8 2.4 %shard_map.277 = f32[128,3072]{1,0:T(8,128)} custom-call(s32[2]{0:T(128)S(1)} %copy-done.3, bf16[1616,128]{1,0:T(8,128)(2,1)S(1)} %pad_maximum_fusion.7.near, bf16[1616,128]{1,0:T(8,128)(2,1)S(1)} %collective-permute-done.42.far), custom_call_target="tpu_custom_call" | custom-call | flops 20000000000 | bytes 60000000 | tf_op jit(solution)/shard_map/pallas_call | solution.py:329
  190.9 2.7 %shard_map.278 = f32[128,4096]{1,0:T(8,128)} custom-call(s32[2]{0:T(128)S(1)} %copy-done.3, bf16[2048,128]{1,0:T(8,128)(2,1)S(1)} %pad_maximum_fusion.6.near, bf16[2048,128]{1,0:T(8,128)(2,1)S(1)} %collective-permute-done.43.far), custom_call_target="tpu_custom_call" | custom-call | flops 20000000000 | bytes 60000000 | tf_op jit(solution)/shard_map/pallas_call | solution.py:329
  (135 shorter events, 15.7 us)
Async XLA Ops:
  1.3 6.9 %copy-start = (bf16[256,1024]{1,0:T(8,128)(2,1)S(1)}, bf16[256,1024]{1,0:T(8,128)(2,1)}, u32[]{:S(2)}) copy-start(bf16[256,1024]{1,0:T(8,128)(2,1)} %block.1) | copy-start | bytes 1572868
  4.6 26.0 %collective-permute-start.6 = (bf16[912,128]{1,0:T(8,128)(2,1)}, bf16[912,128]{1,0:T(8,128)(2,1)S(1)}, u32[]{:S(2)}, u32[]{:S(2)}) collective-permute-start(bf16[912,128]{1,0:T(8,128)(2,1)} %get-tuple-element.115), channel_id=1, source_target_pairs={{0,6},{1,7},{2,4},{3,5},{4,2},{5,3},{6,0},{7,1},{8,14},{9,15},{10,... | collective-permute-start | bytes 700424 | tf_op jit(solution)/shard_map/ppermute | solution.py:305
  8.2 22.4 %collective-permute-start.2 = (bf16[912,128]{1,0:T(8,128)(2,1)}, bf16[912,128]{1,0:T(8,128)(2,1)S(1)}, u32[]{:S(2)}, u32[]{:S(2)}) collective-permute-start(bf16[912,128]{1,0:T(8,128)(2,1)} %get-tuple-element.115), channel_id=1, source_target_pairs={{0,2},{1,3},{2,0},{3,1},{4,6},{5,7},{6,4},{7,5},{8,10},{9,11},{10,... | collective-permute-start | bytes 700424 | tf_op jit(solution)/shard_map/ppermute | solution.py:305
  8.4 22.2 %collective-permute-start.3 = (bf16[144,1024]{1,0:T(8,128)(2,1)S(1)}, bf16[144,1024]{1,0:T(8,128)(2,1)S(1)}, u32[]{:S(2)}, u32[]{:S(2)}) collective-permute-start(bf16[144,1024]{1,0:T(8,128)(2,1)S(1)} %get-tuple-element.226), channel_id=1, source_target_pairs={{0,2},{1,3},{2,0},{3,1},{4,6},{5,7},{6,4},{7,5},{8,10},{9,11},{10,... | collective-permute-start | bytes 884744 | tf_op jit(solution)/shard_map/ppermute | solution.py:305
  10.4 7.2 %collective-permute-start = (bf16[128,1024]{1,0:T(8,128)(2,1)S(1)}, bf16[128,1024]{1,0:T(8,128)(2,1)S(1)}, u32[]{:S(2)}, u32[]{:S(2)}) collective-permute-start(bf16[128,1024]{1,0:T(8,128)(2,1)S(1)} %get-tuple-element.223), channel_id=1, source_target_pairs={{0,16},{1,17},{2,18},{3,19},{4,20},{5,21},{6,22},{7,23},{8,24},{9,... | collective-permute-start | bytes 786440 | tf_op jit(solution)/shard_map/ppermute | solution.py:305
  11.0 19.6 %collective-permute-start.5 = (bf16[912,128]{1,0:T(8,128)(2,1)}, bf16[912,128]{1,0:T(8,128)(2,1)S(1)}, u32[]{:S(2)}, u32[]{:S(2)}) collective-permute-start(bf16[912,128]{1,0:T(8,128)(2,1)} %get-tuple-element.118.own), channel_id=1, source_target_pairs={{0,4},{1,5},{2,6},{3,7},{4,0},{5,1},{6,2},{7,3},{8,12},{9,13},{10,... | collective-permute-start | bytes 700424 | tf_op jit(solution)/shard_map/ppermute | solution.py:305
  14.2 17.7 %copy-start.10 = (bf16[192,1024]{1,0:T(8,128)(2,1)S(1)}, bf16[192,1024]{1,0:T(8,128)(2,1)}, u32[]{:S(2)}) copy-start(bf16[192,1024]{1,0:T(8,128)(2,1)} %get-tuple-element.132) | copy-start | bytes 1179652
  14.2 19.7 %copy-start.4 = (bf16[192,1024]{1,0:T(8,128)(2,1)S(1)}, bf16[192,1024]{1,0:T(8,128)(2,1)}, u32[]{:S(2)}) copy-start(bf16[192,1024]{1,0:T(8,128)(2,1)} %get-tuple-element.135.own) | copy-start | bytes 1179652
  17.6 13.0 %collective-permute-start.4 = (bf16[912,128]{1,0:T(8,128)(2,1)S(1)}, bf16[912,128]{1,0:T(8,128)(2,1)S(1)}, u32[]{:S(2)}, u32[]{:S(2)}) collective-permute-start(bf16[912,128]{1,0:T(8,128)(2,1)S(1)} %copy-done.6), channel_id=1, source_target_pairs={{0,1},{1,0},{2,3},{3,2},{4,5},{5,4},{6,7},{7,6},{8,9},{9,8},{10,11... | collective-permute-start | bytes 700424 | tf_op jit(solution)/shard_map/ppermute | solution.py:305
  30.5 23.2 %collective-permute-start.1 = (bf16[2,128,1024]{2,1,0:T(8,128)(2,1)S(1)}, bf16[2,128,1024]{2,1,0:T(8,128)(2,1)S(1)}, u32[]{:S(2)}, u32[]{:S(2)}) collective-permute-start(bf16[2,128,1024]{2,1,0:T(8,128)(2,1)S(1)} %pad_maximum_fusion.3), channel_id=1, source_target_pairs={{0,2},{1,3},{2,0},{3,1},{4,6},{5,7},{6,4},{7,5},{8,10},{9,11},{10,... | collective-permute-start | bytes 1572872 | tf_op jit(solution)/shard_map/ppermute | solution.py:305
  30.7 25.7 %collective-permute-start.8 = (bf16[3,912,128]{2,1,0:T(8,128)(2,1)S(1)}, bf16[3,912,128]{2,1,0:T(8,128)(2,1)S(1)}, u32[]{:S(2)}, u32[]{:S(2)}) collective-permute-start(bf16[3,912,128]{2,1,0:T(8,128)(2,1)S(1)} %pad_maximum_fusion.1.along), channel_id=1, source_target_pairs={{0,1},{1,0},{2,3},{3,2},{4,5},{5,4},{6,7},{7,6},{8,9},{9,8},{10,11... | collective-permute-start | bytes 2101256 | tf_op jit(solution)/shard_map/ppermute | solution.py:305
  31.3 22.5 %collective-permute-start.7 = (bf16[2,144,1024]{2,1,0:T(8,128)(2,1)S(1)}, bf16[2,144,1024]{2,1,0:T(8,128)(2,1)S(1)}, u32[]{:S(2)}, u32[]{:S(2)}) collective-permute-start(bf16[2,144,1024]{2,1,0:T(8,128)(2,1)S(1)} %pad_maximum_fusion.2), channel_id=1, source_target_pairs={{0,16},{1,17},{2,18},{3,19},{4,20},{5,21},{6,22},{7,23},{8,24},{9,... | collective-permute-start | bytes 1769480 | tf_op jit(solution)/shard_map/ppermute | solution.py:305
  31.8 32.5 %collective-permute-start.9 = (bf16[192,1024]{1,0:T(8,128)(2,1)S(1)}, bf16[192,1024]{1,0:T(8,128)(2,1)S(1)}, u32[]{:S(2)}, u32[]{:S(2)}) collective-permute-start(bf16[192,1024]{1,0:T(8,128)(2,1)S(1)} %copy-done.10), channel_id=1, source_target_pairs={{0,2},{1,3},{2,0},{3,1},{4,6},{5,7},{6,4},{7,5},{8,10},{9,11},{10,... | collective-permute-start | bytes 1179656 | tf_op jit(solution)/shard_map/ppermute | solution.py:305
  33.8 30.5 %collective-permute-start.10 = (bf16[192,1024]{1,0:T(8,128)(2,1)S(1)}, bf16[192,1024]{1,0:T(8,128)(2,1)S(1)}, u32[]{:S(2)}, u32[]{:S(2)}) collective-permute-start(bf16[192,1024]{1,0:T(8,128)(2,1)S(1)} %copy-done.4), channel_id=1, source_target_pairs={{0,4},{1,5},{2,6},{3,7},{4,0},{5,1},{6,2},{7,3},{8,12},{9,13},{10,... | collective-permute-start | bytes 1179656 | tf_op jit(solution)/shard_map/ppermute | solution.py:305
  54.1 25.4 %collective-permute-start.13 = (bf16[4,272,1024]{2,1,0:T(8,128)(2,1)S(1)}, bf16[4,272,1024]{2,1,0:T(8,128)(2,1)S(1)}, u32[]{:S(2)}, u32[]{:S(2)}) collective-permute-start(bf16[4,272,1024]{2,1,0:T(8,128)(2,1)S(1)} %maximum_maximum_fusion.inputs), channel_id=1, source_target_pairs={{0,8},{1,9},{2,10},{3,11},{4,12},{5,13},{6,14},{7,15},{8,0},{9,1},... | collective-permute-start | bytes 6684680 | tf_op jit(solution)/shard_map/ppermute | solution.py:305
  54.7 11.3 %collective-permute-start.11 = (bf16[64,1024]{1,0:T(8,128)(2,1)S(1)}, bf16[64,1024]{1,0:T(8,128)(2,1)S(1)}, u32[]{:S(2)}, u32[]{:S(2)}) collective-permute-start(bf16[64,1024]{1,0:T(8,128)(2,1)S(1)} %copy-done.11), channel_id=1, source_target_pairs={{0,6},{1,7},{2,4},{3,5},{4,2},{5,3},{6,0},{7,1},{8,14},{9,15},{10,... | collective-permute-start | bytes 393224 | tf_op jit(solution)/shard_map/ppermute | solution.py:305
  56.4 9.6 %collective-permute-start.14 = (bf16[128,1024]{1,0:T(8,128)(2,1)S(1)}, bf16[128,1024]{1,0:T(8,128)(2,1)S(1)}, u32[]{:S(2)}, u32[]{:S(2)}) collective-permute-start(bf16[128,1024]{1,0:T(8,128)(2,1)S(1)} %get-tuple-element.143), channel_id=1, source_target_pairs={{0,16},{1,17},{2,18},{3,19},{4,20},{5,21},{6,22},{7,23},{8,24},{9,... | collective-permute-start | bytes 786440 | tf_op jit(solution)/shard_map/ppermute | solution.py:305
  64.4 14.7 %collective-permute-start.16 = (bf16[2,128,1024]{2,1,0:T(8,128)(2,1)S(1)}, bf16[2,128,1024]{2,1,0:T(8,128)(2,1)S(1)}, u32[]{:S(2)}, u32[]{:S(2)}) collective-permute-start(bf16[2,128,1024]{2,1,0:T(8,128)(2,1)S(1)} %pad_maximum_fusion.5), channel_id=1, source_target_pairs={{0,16},{1,17},{2,18},{3,19},{4,20},{5,21},{6,22},{7,23},{8,24},{9,... | collective-permute-start | bytes 1572872 | tf_op jit(solution)/shard_map/ppermute | solution.py:305
  66.0 13.1 %collective-permute-start.15 = (bf16[2,128,1024]{2,1,0:T(8,128)(2,1)S(1)}, bf16[2,128,1024]{2,1,0:T(8,128)(2,1)S(1)}, u32[]{:S(2)}, u32[]{:S(2)}) collective-permute-start(bf16[2,128,1024]{2,1,0:T(8,128)(2,1)S(1)} %pad_maximum_fusion.4), channel_id=1, source_target_pairs={{0,2},{1,3},{2,0},{3,1},{4,6},{5,7},{6,4},{7,5},{8,10},{9,11},{10,... | collective-permute-start | bytes 1572872 | tf_op jit(solution)/shard_map/ppermute | solution.py:305
  66.8 19.6 %collective-permute-start.12 = (bf16[384,1024]{1,0:T(8,128)(2,1)S(1)}, bf16[384,1024]{1,0:T(8,128)(2,1)S(1)}, u32[]{:S(2)}, u32[]{:S(2)}) collective-permute-start(bf16[384,1024]{1,0:T(8,128)(2,1)S(1)} %get-tuple-element.141.along), channel_id=1, source_target_pairs={{0,1},{1,0},{2,3},{3,2},{4,5},{5,4},{6,7},{7,6},{8,9},{9,8},{10,11... | collective-permute-start | bytes 2359304 | tf_op jit(solution)/shard_map/ppermute | solution.py:305
  79.4 7.1 %collective-permute-start.17 = (bf16[4,256,1024]{2,1,0:T(8,128)(2,1)S(1)}, bf16[4,256,1024]{2,1,0:T(8,128)(2,1)S(1)}, u32[]{:S(2)}, u32[]{:S(2)}) collective-permute-start(bf16[4,256,1024]{2,1,0:T(8,128)(2,1)S(1)} %maximum_maximum_fusion.1.near), channel_id=1, source_target_pairs={{0,8},{1,9},{2,10},{3,11},{4,12},{5,13},{6,14},{7,15},{8,0},{9,1},... | collective-permute-start | bytes 6291464 | tf_op jit(solution)/shard_map/ppermute | solution.py:305
  93.9 6.5 %collective-permute-start.18 = (bf16[4,256,1024]{2,1,0:T(8,128)(2,1)S(1)}, bf16[4,256,1024]{2,1,0:T(8,128)(2,1)S(1)}, u32[]{:S(2)}, u32[]{:S(2)}) collective-permute-start(bf16[4,256,1024]{2,1,0:T(8,128)(2,1)S(1)} %get-tuple-element.156), channel_id=1, source_target_pairs={{0,8},{1,9},{2,10},{3,11},{4,12},{5,13},{6,14},{7,15},{8,0},{9,1},... | collective-permute-start | bytes 6291464 | tf_op jit(solution)/shard_map/ppermute | solution.py:305
  94.5 16.6 %collective-permute-start.20 = (bf16[2048,128]{1,0:T(8,128)(2,1)S(1)}, bf16[2048,128]{1,0:T(8,128)(2,1)S(1)}, u32[]{:S(2)}, u32[]{:S(2)}) collective-permute-start(bf16[2048,128]{1,0:T(8,128)(2,1)S(1)} %get-tuple-element.165), channel_id=1, source_target_pairs={{0,1},{1,0},{2,3},{3,2},{4,5},{5,4},{6,7},{7,6},{8,9},{9,8},{10,11... | collective-permute-start | bytes 1572872 | tf_op jit(solution)/shard_map/ppermute | solution.py:305
  95.0 16.3 %collective-permute-start.21 = (bf16[1024,128]{1,0:T(8,128)(2,1)S(1)}, bf16[1024,128]{1,0:T(8,128)(2,1)S(1)}, u32[]{:S(2)}, u32[]{:S(2)}) collective-permute-start(bf16[1024,128]{1,0:T(8,128)(2,1)S(1)} %get-tuple-element.171), channel_id=1, source_target_pairs={{0,4},{1,5},{2,6},{3,7},{4,0},{5,1},{6,2},{7,3},{8,12},{9,13},{10,... | collective-permute-start | bytes 786440 | tf_op jit(solution)/shard_map/ppermute | solution.py:305
  101.5 33.5 %collective-permute-start.19 = (bf16[2,256,1024]{2,1,0:T(8,128)(2,1)S(1)}, bf16[2,256,1024]{2,1,0:T(8,128)(2,1)S(1)}, u32[]{:S(2)}, u32[]{:S(2)}) collective-permute-start(bf16[2,256,1024]{2,1,0:T(8,128)(2,1)S(1)} %slice.219), channel_id=1, source_target_pairs={{0,16},{1,17},{2,18},{3,19},{4,20},{5,21},{6,22},{7,23},{8,24},{9,... | collective-permute-start | bytes 3145736 | tf_op jit(solution)/shard_map/ppermute | solution.py:305
  111.4 16.3 %collective-permute-start.23 = (bf16[1024,128]{1,0:T(8,128)(2,1)S(1)}, bf16[1024,128]{1,0:T(8,128)(2,1)S(1)}, u32[]{:S(2)}, u32[]{:S(2)}) collective-permute-start(bf16[1024,128]{1,0:T(8,128)(2,1)S(1)} %slice.295), channel_id=1, source_target_pairs={{0,4},{1,5},{2,6},{3,7},{4,0},{5,1},{6,2},{7,3},{8,12},{9,13},{10,... | collective-permute-start | bytes 786440 | tf_op jit(solution)/shard_map/ppermute | solution.py:305
  112.2 15.5 %collective-permute-start.24 = (bf16[1024,128]{1,0:T(8,128)(2,1)S(1)}, bf16[1024,128]{1,0:T(8,128)(2,1)S(1)}, u32[]{:S(2)}, u32[]{:S(2)}) collective-permute-start(bf16[1024,128]{1,0:T(8,128)(2,1)S(1)} %add_convert_fusion.4), channel_id=1, source_target_pairs={{0,1},{1,0},{2,3},{3,2},{4,5},{5,4},{6,7},{7,6},{8,9},{9,8},{10,11... | collective-permute-start | bytes 786440 | tf_op jit(solution)/shard_map/ppermute | solution.py:305
  113.0 19.6 %collective-permute-start.25 = (bf16[2048,128]{1,0:T(8,128)(2,1)S(1)}, bf16[2048,128]{1,0:T(8,128)(2,1)S(1)}, u32[]{:S(2)}, u32[]{:S(2)}) collective-permute-start(bf16[2048,128]{1,0:T(8,128)(2,1)S(1)} %get-tuple-element.183), channel_id=1, source_target_pairs={{0,1},{1,0},{2,3},{3,2},{4,5},{5,4},{6,7},{7,6},{8,9},{9,8},{10,11... | collective-permute-start | bytes 1572872 | tf_op jit(solution)/shard_map/ppermute | solution.py:305
  126.7 15.4 %collective-permute-start.22 = (bf16[1600,128]{1,0:T(8,128)(2,1)S(1)}, bf16[1600,128]{1,0:T(8,128)(2,1)S(1)}, u32[]{:S(2)}, u32[]{:S(2)}) collective-permute-start(bf16[1600,128]{1,0:T(8,128)(2,1)S(1)} %get-tuple-element.179), channel_id=1, source_target_pairs={{0,1},{1,0},{2,3},{3,2},{4,5},{5,4},{6,7},{7,6},{8,9},{9,8},{10,11... | collective-permute-start | bytes 1228808 | tf_op jit(solution)/shard_map/ppermute | solution.py:305
  127.9 15.2 %collective-permute-start.27 = (bf16[512,128]{1,0:T(8,128)(2,1)S(1)}, bf16[512,128]{1,0:T(8,128)(2,1)S(1)}, u32[]{:S(2)}, u32[]{:S(2)}) collective-permute-start(bf16[512,128]{1,0:T(8,128)(2,1)S(1)} %get-tuple-element.230), channel_id=1, source_target_pairs={{0,2},{1,3},{2,0},{3,1},{4,6},{5,7},{6,4},{7,5},{8,10},{9,11},{10,... | collective-permute-start | bytes 393224 | tf_op jit(solution)/shard_map/ppermute | solution.py:305
  129.6 15.0 %collective-permute-start.29 = (bf16[1024,128]{1,0:T(8,128)(2,1)S(1)}, bf16[1024,128]{1,0:T(8,128)(2,1)S(1)}, u32[]{:S(2)}, u32[]{:S(2)}) collective-permute-start(bf16[1024,128]{1,0:T(8,128)(2,1)S(1)} %get-tuple-element.239), channel_id=1, source_target_pairs={{0,16},{1,17},{2,18},{3,19},{4,20},{5,21},{6,22},{7,23},{8,24},{9,... | collective-permute-start | bytes 786440 | tf_op jit(solution)/shard_map/ppermute | solution.py:305
  132.8 22.3 %collective-permute-start.31 = (bf16[1024,128]{1,0:T(8,128)(2,1)S(1)}, bf16[1024,128]{1,0:T(8,128)(2,1)S(1)}, u32[]{:S(2)}, u32[]{:S(2)}) collective-permute-start(bf16[1024,128]{1,0:T(8,128)(2,1)S(1)} %slice.294), channel_id=1, source_target_pairs={{0,4},{1,5},{2,6},{3,7},{4,0},{5,1},{6,2},{7,3},{8,12},{9,13},{10,... | collective-permute-start | bytes 786440 | tf_op jit(solution)/shard_map/ppermute | solution.py:305
  138.7 6.0 %collective-permute-start.28 = (bf16[4,256,1024]{2,1,0:T(8,128)(2,1)S(1)}, bf16[4,256,1024]{2,1,0:T(8,128)(2,1)S(1)}, u32[]{:S(2)}, u32[]{:S(2)}) collective-permute-start(bf16[4,256,1024]{2,1,0:T(8,128)(2,1)S(1)} %shard_map.273), channel_id=1, source_target_pairs={{0,8},{1,9},{2,10},{3,11},{4,12},{5,13},{6,14},{7,15},{8,0},{9,1},... | collective-permute-start | bytes 6291464 | tf_op jit(solution)/shard_map/ppermute | solution.py:305
  142.3 12.7 %collective-permute-start.26 = (bf16[800,128]{1,0:T(8,128)(2,1)S(1)}, bf16[800,128]{1,0:T(8,128)(2,1)S(1)}, u32[]{:S(2)}, u32[]{:S(2)}) collective-permute-start(bf16[800,128]{1,0:T(8,128)(2,1)S(1)} %slice.296), channel_id=1, source_target_pairs={{0,4},{1,5},{2,6},{3,7},{4,0},{5,1},{6,2},{7,3},{8,12},{9,13},{10,... | collective-permute-start | bytes 614408 | tf_op jit(solution)/shard_map/ppermute | solution.py:305
  143.1 12.1 %collective-permute-start.34 = (bf16[1024,128]{1,0:T(8,128)(2,1)S(1)}, bf16[1024,128]{1,0:T(8,128)(2,1)S(1)}, u32[]{:S(2)}, u32[]{:S(2)}) collective-permute-start(bf16[1024,128]{1,0:T(8,128)(2,1)S(1)} %pad_maximum_fusion.8), channel_id=1, source_target_pairs={{0,16},{1,17},{2,18},{3,19},{4,20},{5,21},{6,22},{7,23},{8,24},{9,... | collective-permute-start | bytes 786440 | tf_op jit(solution)/shard_map/ppermute | solution.py:305
  145.8 19.2 %collective-permute-start.33 = (bf16[2,128,1024]{2,1,0:T(8,128)(2,1)S(1)}, bf16[2,128,1024]{2,1,0:T(8,128)(2,1)S(1)}, u32[]{:S(2)}, u32[]{:S(2)}) collective-permute-start(bf16[2,128,1024]{2,1,0:T(8,128)(2,1)S(1)} %get-tuple-element.214), channel_id=1, source_target_pairs={{0,2},{1,3},{2,0},{3,1},{4,6},{5,7},{6,4},{7,5},{8,10},{9,11},{10,... | collective-permute-start | bytes 1572872 | tf_op jit(solution)/shard_map/ppermute | solution.py:305
  146.5 18.5 %collective-permute-start.32 = (bf16[2,128,1024]{2,1,0:T(8,128)(2,1)S(1)}, bf16[2,128,1024]{2,1,0:T(8,128)(2,1)S(1)}, u32[]{:S(2)}, u32[]{:S(2)}) collective-permute-start(bf16[2,128,1024]{2,1,0:T(8,128)(2,1)S(1)} %get-tuple-element.215), channel_id=1, source_target_pairs={{0,16},{1,17},{2,18},{3,19},{4,20},{5,21},{6,22},{7,23},{8,24},{9,... | collective-permute-start | bytes 1572872 | tf_op jit(solution)/shard_map/ppermute | solution.py:305
  155.0 12.1 %collective-permute-start.30 = (bf16[400,128]{1,0:T(8,128)(2,1)S(1)}, bf16[400,128]{1,0:T(8,128)(2,1)S(1)}, u32[]{:S(2)}, u32[]{:S(2)}) collective-permute-start(bf16[400,128]{1,0:T(8,128)(2,1)S(1)} %get-tuple-element.232), channel_id=1, source_target_pairs={{0,2},{1,3},{2,0},{3,1},{4,6},{5,7},{6,4},{7,5},{8,10},{9,11},{10,... | collective-permute-start | bytes 307208 | tf_op jit(solution)/shard_map/ppermute | solution.py:305
  155.2 16.1 %collective-permute-start.36 = (bf16[512,128]{1,0:T(8,128)(2,1)S(1)}, bf16[512,128]{1,0:T(8,128)(2,1)S(1)}, u32[]{:S(2)}, u32[]{:S(2)}) collective-permute-start(bf16[512,128]{1,0:T(8,128)(2,1)S(1)} %get-tuple-element.228), channel_id=1, source_target_pairs={{0,2},{1,3},{2,0},{3,1},{4,6},{5,7},{6,4},{7,5},{8,10},{9,11},{10,... | collective-permute-start | bytes 393224 | tf_op jit(solution)/shard_map/ppermute | solution.py:305
  165.3 11.3 %copy-start.1 = (bf16[256,1024]{1,0:T(8,128)(2,1)S(1)}, bf16[256,1024]{1,0:T(8,128)(2,1)}, u32[]{:S(2)}) copy-start(bf16[256,1024]{1,0:T(8,128)(2,1)} %block.1) | copy-start | bytes 1572868
  167.2 9.3 %collective-permute-start.39 = (bf16[128,1024]{1,0:T(8,128)(2,1)S(1)}, bf16[128,1024]{1,0:T(8,128)(2,1)S(1)}, u32[]{:S(2)}, u32[]{:S(2)}) collective-permute-start(bf16[128,1024]{1,0:T(8,128)(2,1)S(1)} %fusion.5), channel_id=1, source_target_pairs={{0,2},{1,3},{2,0},{3,1},{4,6},{5,7},{6,4},{7,5},{8,10},{9,11},{10,... | collective-permute-start | bytes 786440 | tf_op jit(solution)/shard_map/ppermute | solution.py:305
  167.2 9.3 %collective-permute-start.40 = (bf16[128,1024]{1,0:T(8,128)(2,1)S(1)}, bf16[128,1024]{1,0:T(8,128)(2,1)S(1)}, u32[]{:S(2)}, u32[]{:S(2)}) collective-permute-start(bf16[128,1024]{1,0:T(8,128)(2,1)S(1)} %fusion.6), channel_id=1, source_target_pairs={{0,16},{1,17},{2,18},{3,19},{4,20},{5,21},{6,22},{7,23},{8,24},{9,... | collective-permute-start | bytes 786440 | tf_op jit(solution)/shard_map/ppermute | solution.py:305
  167.8 15.8 %collective-permute-start.41 = (bf16[800,128]{1,0:T(8,128)(2,1)S(1)}, bf16[800,128]{1,0:T(8,128)(2,1)S(1)}, u32[]{:S(2)}, u32[]{:S(2)}) collective-permute-start(bf16[800,128]{1,0:T(8,128)(2,1)S(1)} %pad_maximum_fusion.10), channel_id=1, source_target_pairs={{0,16},{1,17},{2,18},{3,19},{4,20},{5,21},{6,22},{7,23},{8,24},{9,... | collective-permute-start | bytes 614408 | tf_op jit(solution)/shard_map/ppermute | solution.py:305
  169.3 16.4 %collective-permute-start.35 = (bf16[256,1024]{1,0:T(8,128)(2,1)S(1)}, bf16[256,1024]{1,0:T(8,128)(2,1)S(1)}, u32[]{:S(2)}, u32[]{:S(2)}) collective-permute-start(bf16[256,1024]{1,0:T(8,128)(2,1)S(1)} %slice_bitcast_fusion.2), channel_id=1, source_target_pairs={{0,2},{1,3},{2,0},{3,1},{4,6},{5,7},{6,4},{7,5},{8,10},{9,11},{10,... | collective-permute-start | bytes 1572872 | tf_op jit(solution)/shard_map/ppermute | solution.py:305
  171.4 12.2 %collective-permute-start.37 = (bf16[1024,128]{1,0:T(8,128)(2,1)S(1)}, bf16[1024,128]{1,0:T(8,128)(2,1)S(1)}, u32[]{:S(2)}, u32[]{:S(2)}) collective-permute-start(bf16[1024,128]{1,0:T(8,128)(2,1)S(1)} %pad_maximum_fusion.9), channel_id=1, source_target_pairs={{0,16},{1,17},{2,18},{3,19},{4,20},{5,21},{6,22},{7,23},{8,24},{9,... | collective-permute-start | bytes 786440 | tf_op jit(solution)/shard_map/ppermute | solution.py:305
  176.5 2.3 %collective-permute-start.38 = (bf16[3072,128]{1,0:T(8,128)(2,1)S(1)}, bf16[3072,128]{1,0:T(8,128)(2,1)S(1)}, u32[]{:S(2)}, u32[]{:S(2)}) collective-permute-start(bf16[3072,128]{1,0:T(8,128)(2,1)S(1)} %pad_maximum_fusion.near), channel_id=1, source_target_pairs={{0,8},{1,9},{2,10},{3,11},{4,12},{5,13},{6,14},{7,15},{8,0},{9,1},... | collective-permute-start | bytes 2359304 | tf_op jit(solution)/shard_map/ppermute | solution.py:305
  183.6 3.2 %collective-permute-start.42 = (bf16[1616,128]{1,0:T(8,128)(2,1)S(1)}, bf16[1616,128]{1,0:T(8,128)(2,1)S(1)}, u32[]{:S(2)}, u32[]{:S(2)}) collective-permute-start(bf16[1616,128]{1,0:T(8,128)(2,1)S(1)} %pad_maximum_fusion.7.near), channel_id=1, source_target_pairs={{0,8},{1,9},{2,10},{3,11},{4,12},{5,13},{6,14},{7,15},{8,0},{9,1},... | collective-permute-start | bytes 1241096 | tf_op jit(solution)/shard_map/ppermute | solution.py:305
  183.7 7.2 %collective-permute-start.43 = (bf16[2048,128]{1,0:T(8,128)(2,1)S(1)}, bf16[2048,128]{1,0:T(8,128)(2,1)S(1)}, u32[]{:S(2)}, u32[]{:S(2)}) collective-permute-start(bf16[2048,128]{1,0:T(8,128)(2,1)S(1)} %pad_maximum_fusion.6.near), channel_id=1, source_target_pairs={{0,8},{1,9},{2,10},{3,11},{4,12},{5,13},{6,14},{7,15},{8,0},{9,1},... | collective-permute-start | bytes 1572872 | tf_op jit(solution)/shard_map/ppermute | solution.py:305
  (8 other events, 29.9 us)

commit v5 on v4

--- a/solution.py
+++ b/solution.py
@@ -285,7 +285,7 @@
 LANES = 128
 FIRST_ROWS = MIX_COLS + SMALL + HIDDEN
 MIX_ROWS = MIX_COLS + SMALL
-FEED_ROWS = 2 * HIDDEN
+DENSE_START = FIRST_ROWS + HIDDEN
 F32 = jnp.float32
 BF16 = jnp.bfloat16
 COST = 5000
@@ -352,8 +352,8 @@
     return pl.ds(pl.multiple_of(index * unit, unit), unit)
 
 
-def cut_body(info, mix, expand, *rest):
-    vectors, (own, other), small = rest[:8], rest[8:10], rest[10]
+def cut_body(info, mix, expand, shrink, dense, *rest):
+    vectors, (own, other, own_all), small = rest[:8], rest[8:11], rest[11]
     row = 0
     small[...] = jnp.zeros_like(small)
     for vector in vectors:
@@ -373,10 +373,17 @@
             second = jnp.where(upper, second, pltpu.roll(second, 64, 1))
             joined = jnp.where(lane < 64, first, second).astype(BF16)
             out[MIX_ROWS + pair * LANES : MIX_ROWS + (pair + 1) * LANES, :] = joined
-
-def cut_slices(info, mix, expand, vectors):
-    operands = [mix, expand] + [vector.reshape(-1, LANES) for vector in vectors]
-    outs = [((FIRST_ROWS, LANES), BF16)] * 2
+    own_all[:FIRST_ROWS, :] = own[...]
+    rows = shrink[aligned(info[1], 64), :]
+    for part in range(8):
+        cols = slice(part * LANES, (part + 1) * LANES)
+        own_all[FIRST_ROWS + 64 * part : FIRST_ROWS + 64 * (part + 1), :] = rows[:, cols]
+        own_all[DENSE_START + LANES * part : DENSE_START + LANES * (part + 1), :] = dense[:, cols]
+
+
+def cut_slices(info, mix, expand, shrink, dense, vectors):
+    operands = [mix, expand, shrink, dense] + [vector.reshape(-1, LANES) for vector in vectors]
+    outs = [((rows, LANES), BF16) for rows in (FIRST_ROWS, FIRST_ROWS, DENSE_START + shrink.shape[1])]
     return call(
         cut_body,
         info,
@@ -389,18 +396,22 @@
     )
 
 
-def cut_last_body(info, shrink, dense, cot, own, other, other_shrink):
+def cut_last_body(info, shrink, dense, cot, over, own, other, other_shrink):
     rows = cot.shape[0] // 2
     own[:64, :] = shrink[aligned(info[1], 64), :]
-    own[64:, :] = dense[...]
+    mine = jnp.bitwise_and(info[0] ^ info[1], 1) == 0
+    for part in range(8):
+        cols = slice(part * LANES, (part + 1) * LANES)
+        start = DENSE_START + part * LANES
+        own[64:, cols] = jnp.where(mine, dense[:, cols], over[start : start + LANES, :])
     rest = shrink[aligned(info[1] ^ 2, 64), :]
     other_shrink[...] = rest
     other[:64, :] = rest
     other[64:, :] = cot[rows:, :]
 
 
-def cut_last(info, shrink, dense, cot):
-    operands = [shrink, dense, cot]
+def cut_last(info, shrink, dense, cot, over):
+    operands = [shrink, dense, cot, over]
     shapes = [(64 + rows, shrink.shape[1]) for rows in (dense.shape[0], cot.shape[0] // 2, 0)]
     return call(
         cut_last_body,
@@ -413,19 +424,18 @@
     )
 
 
-def pack_body(info, own, low, high, both, dense, out, dense_high):
-    out[:64, :] = own[:64, :]
-    out[64:128, :] = low[:64, :]
-    out[128:192, :] = high[:64, :]
-    out[192:256, :] = both[...]
+def pack_body(info, own, low, high, both, out, dense):
+    out[:64, :] = low[:64, :]
+    out[64:128, :] = high[:64, :]
+    out[128:, :] = both[...]
     same = info[1] // 4 == info[0] // 4
-    out[256:, :] = jnp.where(same, dense[...], high[64:, :])
-    dense_high[...] = out[256:, :]
-
-
-def pack_last(info, own, low, high, both, dense):
-    operands = [own, low, high, both, dense]
-    shapes = [(256 + dense.shape[0], dense.shape[1]), dense.shape]
+    dense[...] = jnp.where(same, own[64:, :], high[64:, :])
+
+
+def pack_last(info, own, low, high, both):
+    operands = [own, low, high, both]
+    width = own.shape[1]
+    shapes = [(192, width), (own.shape[0] - 64, width)]
     return call(
         pack_body,
         info,
@@ -597,12 +607,16 @@
     return pl.BlockSpec((2,) + shape[1:], lambda i, _: (i + first,) + rest)
 
 
-def far_project_body(info, context, act, dense, along, across, out, shrink):
+def far_project_body(info, context, act, dense, own, over, along, across, out, shrink):
     @pl.when(pl.program_id(0) == 0)
     def _():
-        for number in range(8):
+        shrink[aligned(info[0], 64), :] = own[:64, :]
+        for part in range(8):
+            start = FIRST_ROWS + 64 * part
+            shrink[aligned(info[0] ^ 1, 64), part * LANES : (part + 1) * LANES] = over[start : start + 64, :]
+        for number in range(2, 8):
             piece = across if number % 2 else along
-            start = 64 * (number // 2)
+            start = 64 * (number // 2 - 1)
             shrink[aligned(info[0] ^ number, 64), :] = piece[start : start + 64, :]
 
     near_project_body(info, context, act, dense, shrink, out)
@@ -684,10 +698,22 @@
     return tn(parts, first.astype(BF16))
 
 
-def norm_products(block, grads, normed, far_normed, column, weight, vectors, row, total, sums):
+def mirror_body(info, mix, expand, mix_lines, expand_lines):
+    mix_lines[...] = as_columns(mix[...]).astype(BF16)
+    expand_lines[...] = as_columns(expand[...]).astype(BF16)
+
+
+def mirror(info, mix, expand):
+    outs = [(weight.shape[::-1], BF16) for weight in (mix, expand)]
+    return call(
+        mirror_body, info, [mix, expand], [whole(mix.shape), whole(expand.shape)], outs, [whole(shape) for shape, _ in outs]
+    )
+
+
+def norm_products(block, grads, normed, far_normed, column, mirrored, vectors, row, total, sums):
     count = normed.shape[0]
     products = tn(grads[:count, :], normed[...]) + tn(grads[count:, :], far_normed[...])
-    lines = as_columns(weight[block, :])
+    lines = mirrored[:, block].astype(F32)
     shifts = column[:, 0:1]
     total[:, block] = products * vectors[row : row + 1, block] + shifts * vectors[row + 1 : row + 2, block]
     sums[0:1, block] = jnp.sum(lines * products, axis=0, keepdims=True)
@@ -1027,24 +1053,25 @@
 
     small = (first_gain, first_shift, second_gain, second_shift, dense_bias, shrink_bias, mix_bias, expand_bias)
     half = tokens // 2
-    own, other = cut_slices(info, mix_weight, expand_weight, small)
+    own, other, own_all = cut_slices(info, mix_weight, expand_weight, shrink_weight, dense_weight, small)
     marks = jnp.pad(segments.astype(BF16), ((0, 15), (0, width - tokens)))
     upper, lower = block_input[:half], jnp.concatenate([block_input[half:], marks])
     along = swap(other, low=1), swap(own, high=1), swap(other, high=1, low=1)
     upper_x, lower_low = gather_first(upper, lower)
     first = mark(info, own)
     upper_x, lower_low = after((upper_x, lower_low), first)
-    over = swap(after(own, first), y=1)
+    over = swap(own_all, y=1)
     upper_pair = swap(jnp.stack([upper, upper_x]), low=1)
     lower_in = jnp.stack([lower, lower_low])
     second = mark(info, upper_x, lower_in)
-    along = jnp.stack(after(along, second, over))
+    along = jnp.stack(after(along, second))
     across = swap(along, y=1)
     lower_pair = swap(after(lower_in, along), x=1)
 
-    high_in, low_in, other_shrink = cut_last(after(info, first), shrink_weight, dense_weight, cotangent)
-    high_last = swap(after(high_in, along), high=1)
-    low_last = swap(after(low_in, along), low=1)
+    over = after(over, along)
+    high_in, low_in, other_shrink = cut_last(info, shrink_weight, dense_weight, cotangent, over)
+    high_last = swap(high_in, high=1)
+    low_last = swap(low_in, low=1)
     third = mark(info, along, high_in, low_in)
     upper_pair, lower_pair, across = after((upper_pair, lower_pair, across), third)
     near = gathered(upper, lower, upper_x, lower_low, upper_pair, lower_pair)
@@ -1055,25 +1082,28 @@
     frequency = jnp.asarray(turn_constants())
     *near_saved, mix, expand, vectors, bias = forward(info, near, (own, over, along, across), frequency, tokens, width)
     high_last, low_last, both_last, cot_upper_x, far = after((high_last, low_last, both_last, cot_upper_x, far), mix)
-    last, dense_held = pack_last(info, high_in, low_last, high_last, both_last, dense_weight)
+    last, dense = pack_last(info, high_in, low_last, high_last, both_last)
     last_across = swap(last, y=1)
     cot_pairs = gather_second(cot_upper, cotangent[half:], cot_upper_x, low_last[64:])
     far = after(far, last, cot_upper_x)
-    cot_near = gathered(cot_upper, cotangent[half:], cot_upper_x, low_last[64:], *cot_pairs)
-    cot_far = swap(cot_near, core=1)
-    far = after(far, cot_near)
     far_saved = forward(info, far, (mix, expand, vectors, bias), frequency, tokens, width, True)
     normed, heads, tables, probs, context, act, slope = zip(near_saved, far_saved)
-    last_mine, last_other, dense_grad = last_backward(info, cot_near, cot_far, act, context)
-    last_across = after(last_across, context[1])
-    dense = jnp.where(own_y, dense_held, last_across[256:])
-    branch_far, shrink = project(info, after(context[1], last_mine), act[1], dense, (last, last_across), True)
+    mix_lines, expand_lines = mirror(info, after(mix, context[1]), expand)
+    cot_near = gathered(
+        cot_upper, cotangent[half:], cot_upper_x, low_last[64:], *after(cot_pairs, mix_lines)
+    )
+    cot_far = swap(cot_near, core=1)
+    last_across = after(last_across, cot_near)
+    branch_far, shrink = project(info, context[1], act[1], dense, (high_in, over, last, last_across), True)
     branch_got = swap(branch_far, core=1)
     (branch_near,) = project(info, context[0], act[0], dense, shrink, False)
+    cot_far = after(cot_far, branch_near)
+    last_mine, last_other, dense_grad = last_backward(info, cot_near, cot_far, act, context)
+    branch_near = after(branch_near, dense_grad)
     branch_sum = (branch_near.astype(F32) + branch_got.astype(F32)).astype(BF16)
     branch_kept, branch_sent = branch_sum[:2], branch_sum[2:]
     grad_pre, bias_grad, feed_sums, expand_mine, expand_other = expand_backward(
-        info, cot_near, cot_far, slope, normed, after(shrink, branch_sent), expand, vectors
+        info, cot_near, cot_far, slope, normed, after(shrink, branch_sent), expand_lines, vectors
     )
     last_part = reduce_first(last_mine, last_other, HIDDEN, grad_pre)
     dense_got = after(swap(dense_grad, high=1), grad_pre)
@@ -1083,32 +1113,30 @@
         cot_near,
         cot_far,
         (normed, heads, tables, probs),
-        (after(dense, last_part[1], dense_grad), frequency, mix, vectors, bias_grad, feed_sums),
-    )
-    branch = branch_kept.astype(F32) + after(swap(branch_sent, x=1), grad_mixed).astype(F32)
+        (after(dense, last_part[1], dense_grad), frequency, mix_lines, vectors, bias_grad, feed_sums),
+    )
+    error_far = input_backward(info, grad_mixed, grad_pre, mix, expand, vectors, True)
+    error_got = swap(error_far, core=1)
+    expand_part = reduce_first(expand_mine, expand_other, HIDDEN, error_far)
+    last_slices = reduce_second(*last_part, error_far)
+    dense_got = after(swap(dense_grad, y=1), error_far)
+    dense_grad = (dense_grad.astype(F32) + dense_got.astype(F32)).astype(BF16)
+    branch = branch_kept.astype(F32) + after(swap(branch_sent, x=1), error_far).astype(F32)
     branch_own, branch_last = branch[0].astype(BF16), branch[1].astype(BF16)
-    last_slices = reduce_second(*last_part, grad_mixed)
-    dense_got = after(swap(dense_grad, y=1), grad_mixed)
-    dense_grad = (dense_grad.astype(F32) + dense_got.astype(F32)).astype(BF16)
-    expand_part = reduce_first(expand_mine, expand_other, HIDDEN, grad_mixed)
-    error_far = input_backward(
+    error_near = input_backward(
         info,
-        after(grad_mixed, branch_own, branch_last, last_slices, dense_grad, expand_part[1]),
+        after(grad_mixed, error_far, branch_own, branch_last, last_slices, dense_grad, expand_part[1]),
         grad_pre,
         mix,
         expand,
         vectors,
-        True,
-    )
-    error_got = swap(error_far, core=1)
-    error_near = input_backward(
-        info, after(grad_mixed, error_far), grad_pre, mix, expand, vectors, False
-    )
-    mix_part = reduce_first(mix_mine, mix_other, MIX_ROWS, error_near)
-    last_pair = share_first(last_slices, HIDDEN, error_near)
+        False,
+    )
     dense_x = after(swap(dense_grad, x=1), error_near)
     dense_part = jnp.where(own_x, dense_grad, dense_x)
-    error = scatter_first(after(error_near, mix_part[1], last_pair), error_got)
+    mix_part = reduce_first(mix_mine, mix_other, MIX_ROWS, error_near)
+    error = scatter_first(after(error_near, dense_part, mix_part[1]), error_got)
+    last_pair = share_first(last_slices, HIDDEN, error[1], error[3])
     fourth = mark(info, last_pair, mix_part[1], error[1], error[3], dense_part)
     expand_slices = reduce_second(*expand_part, fourth)
     last_x = share_second(last_pair, fourth)

time: 197 us -> 194 us (0.985)
  waiting for transfers between devices: 74.5 us -> 66 us
  starting transfers between devices: 39.8 us -> 44.5 us
    ppermute x44, waiting for transfers between devices: 74.5 us -> 66 us  [permute(): return lax.ppermute(value, ('rep', 'fsdp'), pairs)]
    ppermute x44, starting transfers between devices: 39.8 us -> 44.5 us  [permute(): return lax.ppermute(value, ('rep', 'fsdp'), pairs)]
    pallas_call x16 -> x17, Pallas kernels: 68.9 us -> 70.7 us  [call(): pl.pallas_call(body, grid_spec=pltpu.PrefetchScalarGridSpec(num_scalar_pr...]
  transfers between devices with their start and end apart: 44 -> 44, of which waited for: 12 -> 15; matrix products, arithmetic and copies ran while one was open for 4% -> 4% of each run, Pallas kernels for 29% -> 33%
where the time goes in v5:
time: 194 us; the launch traced here: 193 us
  Pallas kernels  70.7 us (36%)
  waiting for transfers between devices  66 us (34%)
  starting transfers between devices  44.5 us (23%)
  other arithmetic  6.21 us (3%)
  local copies, waits for them, and re-layouts  4.22 us (2%)
    pallas_call x17, Pallas kernels, call(): pl.pallas_call(body, grid_spec=pltpu.PrefetchScalarGridSpec(num_scalar_pr...  70.7 us
    ppermute x44, waiting for transfers between devices, permute(): return lax.ppermute(value, ('rep', 'fsdp'), pairs)  66 us
    ppermute x44, starting transfers between devices, permute(): return lax.ppermute(value, ('rep', 'fsdp'), pairs)  44.5 us
  transfers between devices with their start and end apart: 44, of which 15 were waited for; matrix products, arithmetic and copies ran while one was open for 4% of the time, Pallas kernels for 33%

profile of v5, /device:TPU:6, one launch (start us, length us, event | category | flops | bytes accessed | tf_op | source)
XLA Modules:
  0.0 193.0 jit_solution(6710592138682951483)
XLA Ops:
  1.3 4.0 %shard_map.263 = (bf16[912,128]{1,0:T(8,128)(2,1)}, bf16[912,128]{1,0:T(8,128)(2,1)}, bf16[2448,128]{1,0:T(8,128)(2,1)}) custom-call(s32[2]{0:T(128)} %pad_add_fusion.info, bf16[128,3072]{1,0:T(8,128)(2,1)} %mix.1, bf16[128,4096]{1,0:T(8,128)(2,1)} %expand.1, bf16[512,1024]{1,0:T(8,128)(2,1)} %shrink.3, bf16[128,1024]{1,0:T(8,128)(2,1)} %dense.3, ...), custom_call_target="tpu_custom_call" | custom-call | flops 20000000000 | bytes 60000000 | tf_op jit(solution)/shard_map/pallas_call | solution.py:329
  5.3 3.7 %collective-permute-start.5 = (bf16[912,128]{1,0:T(8,128)(2,1)}, bf16[912,128]{1,0:T(8,128)(2,1)S(1)}, u32[]{:S(2)}, u32[]{:S(2)}) collective-permute-start(bf16[912,128]{1,0:T(8,128)(2,1)} %get-tuple-element.117), channel_id=1, source_target_pairs={{0,6},{1,7},{2,4},{3,5},{4,2},{5,3},{6,0},{7,1},{8,14},{9,15},{10,... | collective-permute-start | bytes 700424 | tf_op jit(solution)/shard_map/ppermute | solution.py:305
  9.1 2.1 %collective-permute-start.3 = (bf16[144,1024]{1,0:T(8,128)(2,1)S(1)}, bf16[144,1024]{1,0:T(8,128)(2,1)S(1)}, u32[]{:S(2)}, u32[]{:S(2)}) collective-permute-start(bf16[144,1024]{1,0:T(8,128)(2,1)S(1)} %get-tuple-element.230), channel_id=1, source_target_pairs={{0,2},{1,3},{2,0},{3,1},{4,6},{5,7},{6,4},{7,5},{8,10},{9,11},{10,... | collective-permute-start | bytes 884744 | tf_op jit(solution)/shard_map/ppermute | solution.py:305
  11.8 6.6 %collective-permute-done = bf16[128,1024]{1,0:T(8,128)(2,1)S(1)} collective-permute-done((bf16[128,1024]{1,0:T(8,128)(2,1)S(1)}, bf16[128,1024]{1,0:T(8,128)(2,1)S(1)}, u32[]{:S(2)}, u32[]{:S(2)}) %collective-permute-start) | collective-permute-done | bytes 262176 | tf_op jit(solution)/shard_map/ppermute | solution.py:305
  19.0 12.3 %collective-permute-done.3 = bf16[144,1024]{1,0:T(8,128)(2,1)S(1)} collective-permute-done((bf16[144,1024]{1,0:T(8,128)(2,1)S(1)}, bf16[144,1024]{1,0:T(8,128)(2,1)S(1)}, u32[]{:S(2)}, u32[]{:S(2)}) %collective-permute-start.3) | collective-permute-done | bytes 294944 | tf_op jit(solution)/shard_map/ppermute | solution.py:305
  33.4 3.3 %shard_map.264 = (bf16[192,1024]{1,0:T(8,128)(2,1)}, bf16[192,1024]{1,0:T(8,128)(2,1)}, bf16[64,1024]{1,0:T(8,128)(2,1)}) custom-call(s32[2]{0:T(128)} %pad_add_fusion.info, bf16[512,1024]{1,0:T(8,128)(2,1)} %shrink.3, bf16[128,1024]{1,0:T(8,128)(2,1)} %dense.3, bf16[256,1024]{1,0:T(8,128)(2,1)} %cot.3, bf16[2448,128]{1,0:T(8,128)(2,1)} %copy-done.5), custom_call_target="tpu_custom_call" | custom-call | flops 20000000000 | bytes 60000000 | tf_op jit(solution)/shard_map/pallas_call | solution.py:329
  36.7 2.0 %collective-permute-start.9 = (bf16[192,1024]{1,0:T(8,128)(2,1)}, bf16[192,1024]{1,0:T(8,128)(2,1)S(1)}, u32[]{:S(2)}, u32[]{:S(2)}) collective-permute-start(bf16[192,1024]{1,0:T(8,128)(2,1)} %get-tuple-element.126), channel_id=1, source_target_pairs={{0,2},{1,3},{2,0},{3,1},{4,6},{5,7},{6,4},{7,5},{8,10},{9,11},{10,... | collective-permute-start | bytes 1179656 | tf_op jit(solution)/shard_map/ppermute | solution.py:305
  39.2 15.3 %collective-permute-done.1 = bf16[2,128,1024]{2,1,0:T(8,128)(2,1)S(1)} collective-permute-done((bf16[2,128,1024]{2,1,0:T(8,128)(2,1)S(1)}, bf16[2,128,1024]{2,1,0:T(8,128)(2,1)S(1)}, u32[]{:S(2)}, u32[]{:S(2)}) %collective-permute-start.1) | collective-permute-done | bytes 524320 | tf_op jit(solution)/shard_map/ppermute | solution.py:305
  55.5 1.8 collective-permute-start.11
  57.8 7.3 %shard_map.265 = (bf16[4,256,1024]{2,1,0:T(8,128)(2,1)S(1)}, bf16[4,256,384]{2,1,0:T(8,128)(2,1)S(1)}, f32[4,16,256]{2,1,0:T(8,128)S(1)}, bf16[4,2,256,256]{3,2,...) custom-call(s32[2]{0:T(128)S(1)} %copy-done.4, ...), custom_call_target="tpu_custom_call" | custom-call | flops 44999999488 | bytes 135000000 | tf_op jit(solution)/shard_map/pallas_call | solution.py:329
  66.4 1.6 collective-permute-start.16
  68.1 1.0 collective-permute-start.15
  69.1 6.9 %shard_map.267 = (bf16[4,256,1024]{2,1,0:T(8,128)(2,1)S(1)}, bf16[4,256,384]{2,1,0:T(8,128)(2,1)S(1)}, f32[4,16,256]{2,1,0:T(8,128)S(1)}, bf16[4,2,256,256]{3,2,...) custom-call(s32[2]{0:T(128)S(1)} %copy-done.4, ...), custom_call_target="tpu_custom_call" | custom-call | flops 44999999488 | bytes 135000000 | tf_op jit(solution)/shard_map/pallas_call | solution.py:329
  76.0 1.7 shard_map.268
  77.7 3.1 %collective-permute-done.15 = bf16[2,128,1024]{2,1,0:T(8,128)(2,1)S(1)} collective-permute-done((bf16[2,128,1024]{2,1,0:T(8,128)(2,1)S(1)}, bf16[2,128,1024]{2,1,0:T(8,128)(2,1)S(1)}, u32[]{:S(2)}, u32[]{:S(2)}) %collective-permute-start.15) | collective-permute-done | bytes 524320 | tf_op jit(solution)/shard_map/ppermute | solution.py:305
  81.2 2.6 %shard_map.269 = (bf16[4,256,1024]{2,1,0:T(8,128)(2,1)S(1)}, bf16[512,1024]{1,0:T(8,128)(2,1)S(1)}) custom-call(s32[2]{0:T(128)S(1)} %copy-done.4, bf16[4,256,128]{2,1,0:T(8,128)(2,1)S(1)} %get-tuple-element.149.context, bf16[4,256,512]{2,1,0:T(8,128)(2,1)S(1)} %get-tuple-element.150.act, bf16[128,1024]{1,0:T(8,128)(2,1)S(1)} %get-tuple-element.178.dense, ...), custom_call_target="tpu_custom_call" | custom-call | flops 24999999488 | bytes 75000000 | tf_op jit(solution)/shard_map/pallas_call | solution.py:329
  84.4 2.5 %shard_map.270 = bf16[4,256,1024]{2,1,0:T(8,128)(2,1)S(1)} custom-call(s32[2]{0:T(128)S(1)} %copy-done.4, bf16[4,256,128]{2,1,0:T(8,128)(2,1)S(1)} %get-tuple-element.132.context, bf16[4,256,512]{2,1,0:T(8,128)(2,1)S(1)} %get-tuple-element.133.act, bf16[128,1024]{1,0:T(8,128)(2,1)S(1)} %get-tuple-element.178.dense, ...), custom_call_target="tpu_custom_call" | custom-call | flops 24999999488 | bytes 75000000 | tf_op jit(solution)/shard_map/pallas_call | solution.py:329
  87.0 4.8 %shard_map.271 = (bf16[2048,128]{1,0:T(8,128)(2,1)S(1)}, bf16[2048,128]{1,0:T(8,128)(2,1)S(1)}, bf16[1024,128]{1,0:T(8,128)(2,1)S(1)}) custom-call(s32[2]{0:T(128)S(1)} %copy-done.4, bf16[1024,1024]{1,0:T(8,128)(2,1)S(1)} %bitcast.63, bf16[1024,1024]{1,0:T(8,128)(2,1)S(1)} %bitcast.64, bf16[1024,512]{1,0:T(8,128)(2,1)S(1)} %bitcast.65, ...), custom_call_target="tpu_custom_call" | custom-call | tf_op jit(solution)/shard_map/pallas_call | solution.py:329
  92.9 1.2 collective-permute-start.19
  94.1 3.6 %collective-permute-start.21 = (bf16[1024,128]{1,0:T(8,128)(2,1)S(1)}, bf16[1024,128]{1,0:T(8,128)(2,1)S(1)}, u32[]{:S(2)}, u32[]{:S(2)}) collective-permute-start(bf16[1024,128]{1,0:T(8,128)(2,1)S(1)} %get-tuple-element.158), channel_id=1, source_target_pairs={{0,4},{1,5},{2,6},{3,7},{4,0},{5,1},{6,2},{7,3},{8,12},{9,13},{10,... | collective-permute-start | bytes 786440 | tf_op jit(solution)/shard_map/ppermute | solution.py:305
  97.7 1.5 collective-permute-start.20
  99.2 8.6 %shard_map.272 = (bf16[8,256,512]{2,1,0:T(8,128)(2,1)S(1)}, f32[8,512]{1,0:T(8,128)S(1)}, f32[8,1024]{1,0:T(8,128)S(1)}, bf16[2048,128]{1,0:T(8,128)(2,1)S(1)}, bf16[2048,128]{1,0:T(8,128)(2,1)S(1)}) custom-call(s32[2]{0:T(128)S(1)} %copy-done.4, bf16[4,256,1024]{2,1,0:T(8,128)(2,1)S(1)} %maximum_maximum_fusion.1.near, ...), custom_call_target="tpu_custom_call" | custom-call | flops 44999999488 | bytes 135000000 | tf_op jit(solution)/shard_map/pallas_call | solution.py:329
  108.4 1.1 collective-permute-done.21
  109.6 1.6 collective-permute-start.24
  112.7 12.2 %shard_map.273 = (bf16[8,256,384]{2,1,0:T(8,128)(2,1)S(1)}, bf16[1600,128]{1,0:T(8,128)(2,1)S(1)}, bf16[1600,128]{1,0:T(8,128)(2,1)S(1)}) custom-call(s32[2]{0:T(128)S(1)} %copy-done.4, bf16[4,256,1024]{2,1,0:T(8,128)(2,1)S(1)} %maximum_maximum_fusion.1.near, bf16[4,256,1024]{2,1,0:T(8,128)(2,1)S(1)} %collective-permute-done.17.far, ...), custom_call_target="tpu_custom_call" | custom-call | flops 30000001024 | bytes 90000000 | tf_op jit(solution)/shard_map/pallas_call | solution.py:329
  125.0 3.1 %shard_map.274 = bf16[4,256,1024]{2,1,0:T(8,128)(2,1)S(1)} custom-call(s32[2]{0:T(128)S(1)} %copy-done.4, bf16[8,256,384]{2,1,0:T(8,128)(2,1)S(1)} %get-tuple-element.190.mixed, bf16[8,256,512]{2,1,0:T(8,128)(2,1)S(1)} %get-tuple-element.175.pre, bf16[1024,384]{1,0:T(8,128)(2,1)S(1)} %get-tuple-element.151.mix, ...), custom_call_target="tpu_custom_call" | custom-call | tf_op jit(solution)/shard_map/pallas_call | solution.py:329
  128.1 1.7 collective-permute-start.22
  130.0 3.0 %collective-permute-start.31 = (bf16[1024,128]{1,0:T(8,128)(2,1)S(1)}, bf16[1024,128]{1,0:T(8,128)(2,1)S(1)}, u32[]{:S(2)}, u32[]{:S(2)}) collective-permute-start(bf16[1024,128]{1,0:T(8,128)(2,1)S(1)} %slice.287), channel_id=1, source_target_pairs={{0,4},{1,5},{2,6},{3,7},{4,0},{5,1},{6,2},{7,3},{8,12},{9,13},{10,... | collective-permute-start | bytes 786440 | tf_op jit(solution)/shard_map/ppermute | solution.py:305
  134.5 3.4 %shard_map.275 = bf16[4,256,1024]{2,1,0:T(8,128)(2,1)S(1)} custom-call(s32[2]{0:T(128)S(1)} %copy-done.4, bf16[8,256,384]{2,1,0:T(8,128)(2,1)S(1)} %get-tuple-element.190.mixed, bf16[8,256,512]{2,1,0:T(8,128)(2,1)S(1)} %get-tuple-element.175.pre, bf16[1024,384]{1,0:T(8,128)(2,1)S(1)} %get-tuple-element.151.mix, ...), custom_call_target="tpu_custom_call" | custom-call | flops 30000001024 | bytes 90000000 | tf_op jit(solution)/shard_map/pallas_call | solution.py:329
  138.0 2.6 %collective-permute-start.26 = (bf16[800,128]{1,0:T(8,128)(2,1)S(1)}, bf16[800,128]{1,0:T(8,128)(2,1)S(1)}, u32[]{:S(2)}, u32[]{:S(2)}) collective-permute-start(bf16[800,128]{1,0:T(8,128)(2,1)S(1)} %slice.289), channel_id=1, source_target_pairs={{0,4},{1,5},{2,6},{3,7},{4,0},{5,1},{6,2},{7,3},{8,12},{9,13},{10,... | collective-permute-start | bytes 614408 | tf_op jit(solution)/shard_map/ppermute | solution.py:305
  140.6 1.1 collective-permute-done.28
  141.7 1.0 convert_add_fusion
  142.9 1.7 collective-permute-start.33
  145.1 1.6 collective-permute-start.34
  146.7 7.7 %collective-permute-done.26 = bf16[800,128]{1,0:T(8,128)(2,1)S(1)} collective-permute-done((bf16[800,128]{1,0:T(8,128)(2,1)S(1)}, bf16[800,128]{1,0:T(8,128)(2,1)S(1)}, u32[]{:S(2)}, u32[]{:S(2)}) %collective-permute-start.26) | collective-permute-done | bytes 204832 | tf_op jit(solution)/shard_map/ppermute | solution.py:305
  154.7 2.1 %collective-permute-start.36 = (bf16[512,128]{1,0:T(8,128)(2,1)S(1)}, bf16[512,128]{1,0:T(8,128)(2,1)S(1)}, u32[]{:S(2)}, u32[]{:S(2)}) collective-permute-start(bf16[512,128]{1,0:T(8,128)(2,1)S(1)} %get-tuple-element.232), channel_id=1, source_target_pairs={{0,2},{1,3},{2,0},{3,1},{4,6},{5,7},{6,4},{7,5},{8,10},{9,11},{10,... | collective-permute-start | bytes 393224 | tf_op jit(solution)/shard_map/ppermute | solution.py:305
  156.7 6.1 %collective-permute-done.34 = bf16[1024,128]{1,0:T(8,128)(2,1)S(1)} collective-permute-done((bf16[1024,128]{1,0:T(8,128)(2,1)S(1)}, bf16[1024,128]{1,0:T(8,128)(2,1)S(1)}, u32[]{:S(2)}, u32[]{:S(2)}) %collective-permute-start.34) | collective-permute-done | bytes 262176 | tf_op jit(solution)/shard_map/ppermute | solution.py:305
  162.9 1.7 collective-permute-done.33
  165.1 1.8 collective-permute-done.30
  167.2 1.9 collective-permute-start.41
  169.0 1.9 %collective-permute-start.35 = (bf16[256,1024]{1,0:T(8,128)(2,1)S(1)}, bf16[256,1024]{1,0:T(8,128)(2,1)S(1)}, u32[]{:S(2)}, u32[]{:S(2)}) collective-permute-start(bf16[256,1024]{1,0:T(8,128)(2,1)S(1)} %slice_bitcast_fusion.2), channel_id=1, source_target_pairs={{0,2},{1,3},{2,0},{3,1},{4,6},{5,7},{6,4},{7,5},{8,10},{9,11},{10,... | collective-permute-start | bytes 1572872 | tf_op jit(solution)/shard_map/ppermute | solution.py:305
  171.3 4.8 %collective-permute-done.39.upper_got = bf16[128,1024]{1,0:T(8,128)(2,1)S(1)} collective-permute-done((bf16[128,1024]{1,0:T(8,128)(2,1)S(1)}, bf16[128,1024]{1,0:T(8,128)(2,1)S(1)}, u32[]{:S(2)}, u32[]{:S(2)}) %collective-permute-start.39) | collective-permute-done | bytes 262176 | tf_op jit(solution)/shard_map/ppermute | solution.py:305
  176.2 2.2 %shard_map.276 = f32[256,1024]{1,0:T(8,128)} custom-call(s32[2]{0:T(128)S(1)} %copy-done.4, bf16[256,1024]{1,0:T(8,128)(2,1)S(1)} %copy-done.1, bf16[256,1024]{1,0:T(8,128)(2,1)S(1)} %copy-done.3, f32[128,1024]{1,0:T(8,128)S(1)} %slice_bitcast_fusion.1.upper, bf16[128,1024]{1,0:T(8,128)(2,1)S(1)} %collective-permute-done.39.upper_got, ...), custom_call_target="tpu_custom_call" | custom-call | flops 20000000000 | bytes 60000000 | tf_op jit(solution)/shard_map/pallas_call | solution.py:329
  178.5 2.2 %shard_map.277 = (f32[512,1024]{1,0:T(8,128)}, f32[128,1024]{1,0:T(8,128)}) custom-call(s32[2]{0:T(128)S(1)} %copy-done.4, bf16[3072,128]{1,0:T(8,128)(2,1)S(1)} %pad_maximum_fusion.near, bf16[3072,128]{1,0:T(8,128)(2,1)S(1)} %collective-permute-done.38.far, s32[1]{0:T(128)} %bitcast.35.own_dense), custom_call_target="tpu_custom_call" | custom-call | flops 20000000000 | bytes 60000000 | tf_op jit(solution)/shard_map/pallas_call | solution.py:329
  182.4 2.3 %collective-permute-done.35 = bf16[256,1024]{1,0:T(8,128)(2,1)S(1)} collective-permute-done((bf16[256,1024]{1,0:T(8,128)(2,1)S(1)}, bf16[256,1024]{1,0:T(8,128)(2,1)S(1)}, u32[]{:S(2)}, u32[]{:S(2)}) %collective-permute-start.35) | collective-permute-done | bytes 524320 | tf_op jit(solution)/shard_map/ppermute | solution.py:305
  184.6 1.1 add_convert_fusion.2
  185.7 2.4 %shard_map.278 = f32[128,3072]{1,0:T(8,128)} custom-call(s32[2]{0:T(128)S(1)} %copy-done.4, bf16[1616,128]{1,0:T(8,128)(2,1)S(1)} %pad_maximum_fusion.7.near, bf16[1616,128]{1,0:T(8,128)(2,1)S(1)} %collective-permute-done.42.far), custom_call_target="tpu_custom_call" | custom-call | flops 20000000000 | bytes 60000000 | tf_op jit(solution)/shard_map/pallas_call | solution.py:329
  189.8 2.7 %shard_map.279 = f32[128,4096]{1,0:T(8,128)} custom-call(s32[2]{0:T(128)S(1)} %copy-done.4, bf16[2048,128]{1,0:T(8,128)(2,1)S(1)} %pad_maximum_fusion.6.near, bf16[2048,128]{1,0:T(8,128)(2,1)S(1)} %collective-permute-done.43.far), custom_call_target="tpu_custom_call" | custom-call | flops 20000000000 | bytes 60000000 | tf_op jit(solution)/shard_map/pallas_call | solution.py:329
  (139 shorter events, 19.0 us)
Async XLA Ops:
  5.3 13.1 %copy-start.12 = (bf16[2448,128]{1,0:T(8,128)(2,1)S(1)}, bf16[2448,128]{1,0:T(8,128)(2,1)}, u32[]{:S(2)}) copy-start(bf16[2448,128]{1,0:T(8,128)(2,1)} %get-tuple-element.123) | copy-start | bytes 1880068
  5.3 26.1 %collective-permute-start.5 = (bf16[912,128]{1,0:T(8,128)(2,1)}, bf16[912,128]{1,0:T(8,128)(2,1)S(1)}, u32[]{:S(2)}, u32[]{:S(2)}) collective-permute-start(bf16[912,128]{1,0:T(8,128)(2,1)} %get-tuple-element.117), channel_id=1, source_target_pairs={{0,6},{1,7},{2,4},{3,5},{4,2},{5,3},{6,0},{7,1},{8,14},{9,15},{10,... | collective-permute-start | bytes 700424 | tf_op jit(solution)/shard_map/ppermute | solution.py:305
  9.0 22.4 %collective-permute-start.2 = (bf16[912,128]{1,0:T(8,128)(2,1)}, bf16[912,128]{1,0:T(8,128)(2,1)S(1)}, u32[]{:S(2)}, u32[]{:S(2)}) collective-permute-start(bf16[912,128]{1,0:T(8,128)(2,1)} %get-tuple-element.117), channel_id=1, source_target_pairs={{0,2},{1,3},{2,0},{3,1},{4,6},{5,7},{6,4},{7,5},{8,10},{9,11},{10,... | collective-permute-start | bytes 700424 | tf_op jit(solution)/shard_map/ppermute | solution.py:305
  9.1 22.1 %collective-permute-start.3 = (bf16[144,1024]{1,0:T(8,128)(2,1)S(1)}, bf16[144,1024]{1,0:T(8,128)(2,1)S(1)}, u32[]{:S(2)}, u32[]{:S(2)}) collective-permute-start(bf16[144,1024]{1,0:T(8,128)(2,1)S(1)} %get-tuple-element.230), channel_id=1, source_target_pairs={{0,2},{1,3},{2,0},{3,1},{4,6},{5,7},{6,4},{7,5},{8,10},{9,11},{10,... | collective-permute-start | bytes 884744 | tf_op jit(solution)/shard_map/ppermute | solution.py:305
  11.2 7.2 %collective-permute-start = (bf16[128,1024]{1,0:T(8,128)(2,1)S(1)}, bf16[128,1024]{1,0:T(8,128)(2,1)S(1)}, u32[]{:S(2)}, u32[]{:S(2)}) collective-permute-start(bf16[128,1024]{1,0:T(8,128)(2,1)S(1)} %get-tuple-element.227), channel_id=1, source_target_pairs={{0,16},{1,17},{2,18},{3,19},{4,20},{5,21},{6,22},{7,23},{8,24},{9,... | collective-permute-start | bytes 786440 | tf_op jit(solution)/shard_map/ppermute | solution.py:305
  11.7 19.6 %collective-permute-start.4 = (bf16[912,128]{1,0:T(8,128)(2,1)}, bf16[912,128]{1,0:T(8,128)(2,1)S(1)}, u32[]{:S(2)}, u32[]{:S(2)}) collective-permute-start(bf16[912,128]{1,0:T(8,128)(2,1)} %get-tuple-element.114.own), channel_id=1, source_target_pairs={{0,4},{1,5},{2,6},{3,7},{4,0},{5,1},{6,2},{7,3},{8,12},{9,13},{10,... | collective-permute-start | bytes 700424 | tf_op jit(solution)/shard_map/ppermute | solution.py:305
  18.4 14.1 %collective-permute-start.6 = (bf16[2448,128]{1,0:T(8,128)(2,1)S(1)}, bf16[2448,128]{1,0:T(8,128)(2,1)S(1)}, u32[]{:S(2)}, u32[]{:S(2)}) collective-permute-start(bf16[2448,128]{1,0:T(8,128)(2,1)S(1)} %copy-done.12), channel_id=1, source_target_pairs={{0,1},{1,0},{2,3},{3,2},{4,5},{5,4},{6,7},{7,6},{8,9},{9,8},{10,11... | collective-permute-start | bytes 1880072 | tf_op jit(solution)/shard_map/ppermute | solution.py:305
  31.3 23.2 %collective-permute-start.1 = (bf16[2,128,1024]{2,1,0:T(8,128)(2,1)S(1)}, bf16[2,128,1024]{2,1,0:T(8,128)(2,1)S(1)}, u32[]{:S(2)}, u32[]{:S(2)}) collective-permute-start(bf16[2,128,1024]{2,1,0:T(8,128)(2,1)S(1)} %pad_maximum_fusion.3), channel_id=1, source_target_pairs={{0,2},{1,3},{2,0},{3,1},{4,6},{5,7},{6,4},{7,5},{8,10},{9,11},{10,... | collective-permute-start | bytes 1572872 | tf_op jit(solution)/shard_map/ppermute | solution.py:305
  31.5 25.8 %collective-permute-start.8 = (bf16[3,912,128]{2,1,0:T(8,128)(2,1)S(1)}, bf16[3,912,128]{2,1,0:T(8,128)(2,1)S(1)}, u32[]{:S(2)}, u32[]{:S(2)}) collective-permute-start(bf16[3,912,128]{2,1,0:T(8,128)(2,1)S(1)} %pad_maximum_fusion.1.along), channel_id=1, source_target_pairs={{0,1},{1,0},{2,3},{3,2},{4,5},{5,4},{6,7},{7,6},{8,9},{9,8},{10,11... | collective-permute-start | bytes 2101256 | tf_op jit(solution)/shard_map/ppermute | solution.py:305
  32.0 22.5 %collective-permute-start.7 = (bf16[2,144,1024]{2,1,0:T(8,128)(2,1)S(1)}, bf16[2,144,1024]{2,1,0:T(8,128)(2,1)S(1)}, u32[]{:S(2)}, u32[]{:S(2)}) collective-permute-start(bf16[2,144,1024]{2,1,0:T(8,128)(2,1)S(1)} %pad_maximum_fusion.2), channel_id=1, source_target_pairs={{0,16},{1,17},{2,18},{3,19},{4,20},{5,21},{6,22},{7,23},{8,24},{9,... | collective-permute-start | bytes 1769480 | tf_op jit(solution)/shard_map/ppermute | solution.py:305
  36.7 28.4 %collective-permute-start.9 = (bf16[192,1024]{1,0:T(8,128)(2,1)}, bf16[192,1024]{1,0:T(8,128)(2,1)S(1)}, u32[]{:S(2)}, u32[]{:S(2)}) collective-permute-start(bf16[192,1024]{1,0:T(8,128)(2,1)} %get-tuple-element.126), channel_id=1, source_target_pairs={{0,2},{1,3},{2,0},{3,1},{4,6},{5,7},{6,4},{7,5},{8,10},{9,11},{10,... | collective-permute-start | bytes 1179656 | tf_op jit(solution)/shard_map/ppermute | solution.py:305
  38.7 26.4 %collective-permute-start.10 = (bf16[192,1024]{1,0:T(8,128)(2,1)}, bf16[192,1024]{1,0:T(8,128)(2,1)S(1)}, u32[]{:S(2)}, u32[]{:S(2)}) collective-permute-start(bf16[192,1024]{1,0:T(8,128)(2,1)} %get-tuple-element.125.own), channel_id=1, source_target_pairs={{0,4},{1,5},{2,6},{3,7},{4,0},{5,1},{6,2},{7,3},{8,12},{9,13},{10,... | collective-permute-start | bytes 1179656 | tf_op jit(solution)/shard_map/ppermute | solution.py:305
  54.9 14.2 %collective-permute-start.12 = (bf16[4,272,1024]{2,1,0:T(8,128)(2,1)S(1)}, bf16[4,272,1024]{2,1,0:T(8,128)(2,1)S(1)}, u32[]{:S(2)}, u32[]{:S(2)}) collective-permute-start(bf16[4,272,1024]{2,1,0:T(8,128)(2,1)S(1)} %maximum_maximum_fusion.inputs), channel_id=1, source_target_pairs={{0,8},{1,9},{2,10},{3,11},{4,12},{5,13},{6,14},{7,15},{8,0},{9,1},... | collective-permute-start | bytes 6684680 | tf_op jit(solution)/shard_map/ppermute | solution.py:305
  55.5 9.7 %collective-permute-start.11 = (bf16[64,1024]{1,0:T(8,128)(2,1)S(1)}, bf16[64,1024]{1,0:T(8,128)(2,1)S(1)}, u32[]{:S(2)}, u32[]{:S(2)}) collective-permute-start(bf16[64,1024]{1,0:T(8,128)(2,1)S(1)} %copy-done.13), channel_id=1, source_target_pairs={{0,6},{1,7},{2,4},{3,5},{4,2},{5,3},{6,0},{7,1},{8,14},{9,15},{10,... | collective-permute-start | bytes 393224 | tf_op jit(solution)/shard_map/ppermute | solution.py:305
  57.2 7.9 %copy-start.7 = (bf16[192,1024]{1,0:T(8,128)(2,1)S(1)}, bf16[192,1024]{1,0:T(8,128)(2,1)}, u32[]{:S(2)}) copy-start(bf16[192,1024]{1,0:T(8,128)(2,1)} %get-tuple-element.125.own) | copy-start | bytes 1179652
  57.3 10.7 %collective-permute-start.13 = (bf16[128,1024]{1,0:T(8,128)(2,1)S(1)}, bf16[128,1024]{1,0:T(8,128)(2,1)S(1)}, u32[]{:S(2)}, u32[]{:S(2)}) collective-permute-start(bf16[128,1024]{1,0:T(8,128)(2,1)S(1)} %get-tuple-element.143), channel_id=1, source_target_pairs={{0,16},{1,17},{2,18},{3,19},{4,20},{5,21},{6,22},{7,23},{8,24},{9,... | collective-permute-start | bytes 786440 | tf_op jit(solution)/shard_map/ppermute | solution.py:305
  65.8 15.5 %collective-permute-start.14 = (bf16[192,1024]{1,0:T(8,128)(2,1)S(1)}, bf16[192,1024]{1,0:T(8,128)(2,1)S(1)}, u32[]{:S(2)}, u32[]{:S(2)}) collective-permute-start(bf16[192,1024]{1,0:T(8,128)(2,1)S(1)} %get-tuple-element.142.along), channel_id=1, source_target_pairs={{0,1},{1,0},{2,3},{3,2},{4,5},{5,4},{6,7},{7,6},{8,9},{9,8},{10,11... | collective-permute-start | bytes 1179656 | tf_op jit(solution)/shard_map/ppermute | solution.py:305
  66.4 14.4 %collective-permute-start.16 = (bf16[2,128,1024]{2,1,0:T(8,128)(2,1)S(1)}, bf16[2,128,1024]{2,1,0:T(8,128)(2,1)S(1)}, u32[]{:S(2)}, u32[]{:S(2)}) collective-permute-start(bf16[2,128,1024]{2,1,0:T(8,128)(2,1)S(1)} %pad_maximum_fusion.5), channel_id=1, source_target_pairs={{0,16},{1,17},{2,18},{3,19},{4,20},{5,21},{6,22},{7,23},{8,24},{9,... | collective-permute-start | bytes 1572872 | tf_op jit(solution)/shard_map/ppermute | solution.py:305
  68.1 12.8 %collective-permute-start.15 = (bf16[2,128,1024]{2,1,0:T(8,128)(2,1)S(1)}, bf16[2,128,1024]{2,1,0:T(8,128)(2,1)S(1)}, u32[]{:S(2)}, u32[]{:S(2)}) collective-permute-start(bf16[2,128,1024]{2,1,0:T(8,128)(2,1)S(1)} %pad_maximum_fusion.4), channel_id=1, source_target_pairs={{0,2},{1,3},{2,0},{3,1},{4,6},{5,7},{6,4},{7,5},{8,10},{9,11},{10,... | collective-permute-start | bytes 1572872 | tf_op jit(solution)/shard_map/ppermute | solution.py:305
  81.2 5.8 %collective-permute-start.17 = (bf16[4,256,1024]{2,1,0:T(8,128)(2,1)S(1)}, bf16[4,256,1024]{2,1,0:T(8,128)(2,1)S(1)}, u32[]{:S(2)}, u32[]{:S(2)}) collective-permute-start(bf16[4,256,1024]{2,1,0:T(8,128)(2,1)S(1)} %maximum_maximum_fusion.1.near), channel_id=1, source_target_pairs={{0,8},{1,9},{2,10},{3,11},{4,12},{5,13},{6,14},{7,15},{8,0},{9,1},... | collective-permute-start | bytes 6291464 | tf_op jit(solution)/shard_map/ppermute | solution.py:305
  83.9 7.9 %collective-permute-start.18 = (bf16[4,256,1024]{2,1,0:T(8,128)(2,1)S(1)}, bf16[4,256,1024]{2,1,0:T(8,128)(2,1)S(1)}, u32[]{:S(2)}, u32[]{:S(2)}) collective-permute-start(bf16[4,256,1024]{2,1,0:T(8,128)(2,1)S(1)} %get-tuple-element.160), channel_id=1, source_target_pairs={{0,8},{1,9},{2,10},{3,11},{4,12},{5,13},{6,14},{7,15},{8,0},{9,1},... | collective-permute-start | bytes 6291464 | tf_op jit(solution)/shard_map/ppermute | solution.py:305
  92.9 40.6 %collective-permute-start.19 = (bf16[2,256,1024]{2,1,0:T(8,128)(2,1)S(1)}, bf16[2,256,1024]{2,1,0:T(8,128)(2,1)S(1)}, u32[]{:S(2)}, u32[]{:S(2)}) collective-permute-start(bf16[2,256,1024]{2,1,0:T(8,128)(2,1)S(1)} %slice.213), channel_id=1, source_target_pairs={{0,16},{1,17},{2,18},{3,19},{4,20},{5,21},{6,22},{7,23},{8,24},{9,... | collective-permute-start | bytes 3145736 | tf_op jit(solution)/shard_map/ppermute | solution.py:305
  94.1 15.4 %collective-permute-start.21 = (bf16[1024,128]{1,0:T(8,128)(2,1)S(1)}, bf16[1024,128]{1,0:T(8,128)(2,1)S(1)}, u32[]{:S(2)}, u32[]{:S(2)}) collective-permute-start(bf16[1024,128]{1,0:T(8,128)(2,1)S(1)} %get-tuple-element.158), channel_id=1, source_target_pairs={{0,4},{1,5},{2,6},{3,7},{4,0},{5,1},{6,2},{7,3},{8,12},{9,13},{10,... | collective-permute-start | bytes 786440 | tf_op jit(solution)/shard_map/ppermute | solution.py:305
  97.7 14.5 %collective-permute-start.20 = (bf16[2048,128]{1,0:T(8,128)(2,1)S(1)}, bf16[2048,128]{1,0:T(8,128)(2,1)S(1)}, u32[]{:S(2)}, u32[]{:S(2)}) collective-permute-start(bf16[2048,128]{1,0:T(8,128)(2,1)S(1)} %get-tuple-element.170), channel_id=1, source_target_pairs={{0,1},{1,0},{2,3},{3,2},{4,5},{5,4},{6,7},{7,6},{8,9},{9,8},{10,11... | collective-permute-start | bytes 1572872 | tf_op jit(solution)/shard_map/ppermute | solution.py:305
  107.8 21.9 %collective-permute-start.25 = (bf16[2048,128]{1,0:T(8,128)(2,1)S(1)}, bf16[2048,128]{1,0:T(8,128)(2,1)S(1)}, u32[]{:S(2)}, u32[]{:S(2)}) collective-permute-start(bf16[2048,128]{1,0:T(8,128)(2,1)S(1)} %get-tuple-element.188), channel_id=1, source_target_pairs={{0,1},{1,0},{2,3},{3,2},{4,5},{5,4},{6,7},{7,6},{8,9},{9,8},{10,11... | collective-permute-start | bytes 1572872 | tf_op jit(solution)/shard_map/ppermute | solution.py:305
  109.6 20.4 %collective-permute-start.24 = (bf16[1024,128]{1,0:T(8,128)(2,1)S(1)}, bf16[1024,128]{1,0:T(8,128)(2,1)S(1)}, u32[]{:S(2)}, u32[]{:S(2)}) collective-permute-start(bf16[1024,128]{1,0:T(8,128)(2,1)S(1)} %add_convert_fusion.4), channel_id=1, source_target_pairs={{0,1},{1,0},{2,3},{3,2},{4,5},{5,4},{6,7},{7,6},{8,9},{9,8},{10,11... | collective-permute-start | bytes 786440 | tf_op jit(solution)/shard_map/ppermute | solution.py:305
  112.3 20.6 %collective-permute-start.23 = (bf16[1024,128]{1,0:T(8,128)(2,1)S(1)}, bf16[1024,128]{1,0:T(8,128)(2,1)S(1)}, u32[]{:S(2)}, u32[]{:S(2)}) collective-permute-start(bf16[1024,128]{1,0:T(8,128)(2,1)S(1)} %slice.288), channel_id=1, source_target_pairs={{0,4},{1,5},{2,6},{3,7},{4,0},{5,1},{6,2},{7,3},{8,12},{9,13},{10,... | collective-permute-start | bytes 786440 | tf_op jit(solution)/shard_map/ppermute | solution.py:305
  128.1 9.7 %collective-permute-start.22 = (bf16[1600,128]{1,0:T(8,128)(2,1)S(1)}, bf16[1600,128]{1,0:T(8,128)(2,1)S(1)}, u32[]{:S(2)}, u32[]{:S(2)}) collective-permute-start(bf16[1600,128]{1,0:T(8,128)(2,1)S(1)} %get-tuple-element.184), channel_id=1, source_target_pairs={{0,1},{1,0},{2,3},{3,2},{4,5},{5,4},{6,7},{7,6},{8,9},{9,8},{10,11... | collective-permute-start | bytes 1228808 | tf_op jit(solution)/shard_map/ppermute | solution.py:305
  129.8 11.9 %collective-permute-start.29 = (bf16[4,256,1024]{2,1,0:T(8,128)(2,1)S(1)}, bf16[4,256,1024]{2,1,0:T(8,128)(2,1)S(1)}, u32[]{:S(2)}, u32[]{:S(2)}) collective-permute-start(bf16[4,256,1024]{2,1,0:T(8,128)(2,1)S(1)} %shard_map.274), channel_id=1, source_target_pairs={{0,8},{1,9},{2,10},{3,11},{4,12},{5,13},{6,14},{7,15},{8,0},{9,1},... | collective-permute-start | bytes 6291464 | tf_op jit(solution)/shard_map/ppermute | solution.py:305
  130.0 24.6 %collective-permute-start.31 = (bf16[1024,128]{1,0:T(8,128)(2,1)S(1)}, bf16[1024,128]{1,0:T(8,128)(2,1)S(1)}, u32[]{:S(2)}, u32[]{:S(2)}) collective-permute-start(bf16[1024,128]{1,0:T(8,128)(2,1)S(1)} %slice.287), channel_id=1, source_target_pairs={{0,4},{1,5},{2,6},{3,7},{4,0},{5,1},{6,2},{7,3},{8,12},{9,13},{10,... | collective-permute-start | bytes 786440 | tf_op jit(solution)/shard_map/ppermute | solution.py:305
  133.1 12.0 %collective-permute-start.27 = (bf16[512,128]{1,0:T(8,128)(2,1)S(1)}, bf16[512,128]{1,0:T(8,128)(2,1)S(1)}, u32[]{:S(2)}, u32[]{:S(2)}) collective-permute-start(bf16[512,128]{1,0:T(8,128)(2,1)S(1)} %get-tuple-element.234), channel_id=1, source_target_pairs={{0,2},{1,3},{2,0},{3,1},{4,6},{5,7},{6,4},{7,5},{8,10},{9,11},{10,... | collective-permute-start | bytes 393224 | tf_op jit(solution)/shard_map/ppermute | solution.py:305
  133.5 8.2 %collective-permute-start.28 = (bf16[1024,128]{1,0:T(8,128)(2,1)S(1)}, bf16[1024,128]{1,0:T(8,128)(2,1)S(1)}, u32[]{:S(2)}, u32[]{:S(2)}) collective-permute-start(bf16[1024,128]{1,0:T(8,128)(2,1)S(1)} %get-tuple-element.243), channel_id=1, source_target_pairs={{0,16},{1,17},{2,18},{3,19},{4,20},{5,21},{6,22},{7,23},{8,24},{9,... | collective-permute-start | bytes 786440 | tf_op jit(solution)/shard_map/ppermute | solution.py:305
  138.0 16.4 %collective-permute-start.26 = (bf16[800,128]{1,0:T(8,128)(2,1)S(1)}, bf16[800,128]{1,0:T(8,128)(2,1)S(1)}, u32[]{:S(2)}, u32[]{:S(2)}) collective-permute-start(bf16[800,128]{1,0:T(8,128)(2,1)S(1)} %slice.289), channel_id=1, source_target_pairs={{0,4},{1,5},{2,6},{3,7},{4,0},{5,1},{6,2},{7,3},{8,12},{9,13},{10,... | collective-permute-start | bytes 614408 | tf_op jit(solution)/shard_map/ppermute | solution.py:305
  142.9 21.8 %collective-permute-start.33 = (bf16[2,128,1024]{2,1,0:T(8,128)(2,1)S(1)}, bf16[2,128,1024]{2,1,0:T(8,128)(2,1)S(1)}, u32[]{:S(2)}, u32[]{:S(2)}) collective-permute-start(bf16[2,128,1024]{2,1,0:T(8,128)(2,1)S(1)} %get-tuple-element.218), channel_id=1, source_target_pairs={{0,2},{1,3},{2,0},{3,1},{4,6},{5,7},{6,4},{7,5},{8,10},{9,11},{10,... | collective-permute-start | bytes 1572872 | tf_op jit(solution)/shard_map/ppermute | solution.py:305
  144.6 20.1 %collective-permute-start.32 = (bf16[2,128,1024]{2,1,0:T(8,128)(2,1)S(1)}, bf16[2,128,1024]{2,1,0:T(8,128)(2,1)S(1)}, u32[]{:S(2)}, u32[]{:S(2)}) collective-permute-start(bf16[2,128,1024]{2,1,0:T(8,128)(2,1)S(1)} %get-tuple-element.219), channel_id=1, source_target_pairs={{0,16},{1,17},{2,18},{3,19},{4,20},{5,21},{6,22},{7,23},{8,24},{9,... | collective-permute-start | bytes 1572872 | tf_op jit(solution)/shard_map/ppermute | solution.py:305
  145.1 17.7 %collective-permute-start.34 = (bf16[1024,128]{1,0:T(8,128)(2,1)S(1)}, bf16[1024,128]{1,0:T(8,128)(2,1)S(1)}, u32[]{:S(2)}, u32[]{:S(2)}) collective-permute-start(bf16[1024,128]{1,0:T(8,128)(2,1)S(1)} %pad_maximum_fusion.8), channel_id=1, source_target_pairs={{0,16},{1,17},{2,18},{3,19},{4,20},{5,21},{6,22},{7,23},{8,24},{9,... | collective-permute-start | bytes 786440 | tf_op jit(solution)/shard_map/ppermute | solution.py:305
  154.5 12.3 %collective-permute-start.30 = (bf16[400,128]{1,0:T(8,128)(2,1)S(1)}, bf16[400,128]{1,0:T(8,128)(2,1)S(1)}, u32[]{:S(2)}, u32[]{:S(2)}) collective-permute-start(bf16[400,128]{1,0:T(8,128)(2,1)S(1)} %get-tuple-element.236), channel_id=1, source_target_pairs={{0,2},{1,3},{2,0},{3,1},{4,6},{5,7},{6,4},{7,5},{8,10},{9,11},{10,... | collective-permute-start | bytes 307208 | tf_op jit(solution)/shard_map/ppermute | solution.py:305
  154.7 16.3 %collective-permute-start.36 = (bf16[512,128]{1,0:T(8,128)(2,1)S(1)}, bf16[512,128]{1,0:T(8,128)(2,1)S(1)}, u32[]{:S(2)}, u32[]{:S(2)}) collective-permute-start(bf16[512,128]{1,0:T(8,128)(2,1)S(1)} %get-tuple-element.232), channel_id=1, source_target_pairs={{0,2},{1,3},{2,0},{3,1},{4,6},{5,7},{6,4},{7,5},{8,10},{9,11},{10,... | collective-permute-start | bytes 393224 | tf_op jit(solution)/shard_map/ppermute | solution.py:305
  165.0 11.3 %copy-start.1 = (bf16[256,1024]{1,0:T(8,128)(2,1)S(1)}, bf16[256,1024]{1,0:T(8,128)(2,1)}, u32[]{:S(2)}) copy-start(bf16[256,1024]{1,0:T(8,128)(2,1)} %block.1) | copy-start | bytes 1572868
  165.0 11.3 %copy-start.3 = (bf16[256,1024]{1,0:T(8,128)(2,1)S(1)}, bf16[256,1024]{1,0:T(8,128)(2,1)}, u32[]{:S(2)}) copy-start(bf16[256,1024]{1,0:T(8,128)(2,1)} %cot.3) | copy-start | bytes 1572868
  166.9 9.3 %collective-permute-start.39 = (bf16[128,1024]{1,0:T(8,128)(2,1)S(1)}, bf16[128,1024]{1,0:T(8,128)(2,1)S(1)}, u32[]{:S(2)}, u32[]{:S(2)}) collective-permute-start(bf16[128,1024]{1,0:T(8,128)(2,1)S(1)} %fusion.5), channel_id=1, source_target_pairs={{0,2},{1,3},{2,0},{3,1},{4,6},{5,7},{6,4},{7,5},{8,10},{9,11},{10,... | collective-permute-start | bytes 786440 | tf_op jit(solution)/shard_map/ppermute | solution.py:305
  166.9 9.3 %collective-permute-start.40 = (bf16[128,1024]{1,0:T(8,128)(2,1)S(1)}, bf16[128,1024]{1,0:T(8,128)(2,1)S(1)}, u32[]{:S(2)}, u32[]{:S(2)}) collective-permute-start(bf16[128,1024]{1,0:T(8,128)(2,1)S(1)} %fusion.6), channel_id=1, source_target_pairs={{0,16},{1,17},{2,18},{3,19},{4,20},{5,21},{6,22},{7,23},{8,24},{9,... | collective-permute-start | bytes 786440 | tf_op jit(solution)/shard_map/ppermute | solution.py:305
  167.2 14.5 %collective-permute-start.41 = (bf16[800,128]{1,0:T(8,128)(2,1)S(1)}, bf16[800,128]{1,0:T(8,128)(2,1)S(1)}, u32[]{:S(2)}, u32[]{:S(2)}) collective-permute-start(bf16[800,128]{1,0:T(8,128)(2,1)S(1)} %pad_maximum_fusion.10), channel_id=1, source_target_pairs={{0,16},{1,17},{2,18},{3,19},{4,20},{5,21},{6,22},{7,23},{8,24},{9,... | collective-permute-start | bytes 614408 | tf_op jit(solution)/shard_map/ppermute | solution.py:305
  169.0 15.6 %collective-permute-start.35 = (bf16[256,1024]{1,0:T(8,128)(2,1)S(1)}, bf16[256,1024]{1,0:T(8,128)(2,1)S(1)}, u32[]{:S(2)}, u32[]{:S(2)}) collective-permute-start(bf16[256,1024]{1,0:T(8,128)(2,1)S(1)} %slice_bitcast_fusion.2), channel_id=1, source_target_pairs={{0,2},{1,3},{2,0},{3,1},{4,6},{5,7},{6,4},{7,5},{8,10},{9,11},{10,... | collective-permute-start | bytes 1572872 | tf_op jit(solution)/shard_map/ppermute | solution.py:305
  171.1 10.5 %collective-permute-start.37 = (bf16[1024,128]{1,0:T(8,128)(2,1)S(1)}, bf16[1024,128]{1,0:T(8,128)(2,1)S(1)}, u32[]{:S(2)}, u32[]{:S(2)}) collective-permute-start(bf16[1024,128]{1,0:T(8,128)(2,1)S(1)} %pad_maximum_fusion.9), channel_id=1, source_target_pairs={{0,16},{1,17},{2,18},{3,19},{4,20},{5,21},{6,22},{7,23},{8,24},{9,... | collective-permute-start | bytes 786440 | tf_op jit(solution)/shard_map/ppermute | solution.py:305
  176.2 2.3 %collective-permute-start.38 = (bf16[3072,128]{1,0:T(8,128)(2,1)S(1)}, bf16[3072,128]{1,0:T(8,128)(2,1)S(1)}, u32[]{:S(2)}, u32[]{:S(2)}) collective-permute-start(bf16[3072,128]{1,0:T(8,128)(2,1)S(1)} %pad_maximum_fusion.near), channel_id=1, source_target_pairs={{0,8},{1,9},{2,10},{3,11},{4,12},{5,13},{6,14},{7,15},{8,0},{9,1},... | collective-permute-start | bytes 2359304 | tf_op jit(solution)/shard_map/ppermute | solution.py:305
  181.7 4.0 %collective-permute-start.42 = (bf16[1616,128]{1,0:T(8,128)(2,1)S(1)}, bf16[1616,128]{1,0:T(8,128)(2,1)S(1)}, u32[]{:S(2)}, u32[]{:S(2)}) collective-permute-start(bf16[1616,128]{1,0:T(8,128)(2,1)S(1)} %pad_maximum_fusion.7.near), channel_id=1, source_target_pairs={{0,8},{1,9},{2,10},{3,11},{4,12},{5,13},{6,14},{7,15},{8,0},{9,1},... | collective-permute-start | bytes 1241096 | tf_op jit(solution)/shard_map/ppermute | solution.py:305
  181.8 8.0 %collective-permute-start.43 = (bf16[2048,128]{1,0:T(8,128)(2,1)S(1)}, bf16[2048,128]{1,0:T(8,128)(2,1)S(1)}, u32[]{:S(2)}, u32[]{:S(2)}) collective-permute-start(bf16[2048,128]{1,0:T(8,128)(2,1)S(1)} %pad_maximum_fusion.6.near), channel_id=1, source_target_pairs={{0,8},{1,9},{2,10},{3,11},{4,12},{5,13},{6,14},{7,15},{8,0},{9,1},... | collective-permute-start | bytes 1572872 | tf_op jit(solution)/shard_map/ppermute | solution.py:305
  (10 other events, 40.4 us)

commit v6 on v5

--- a/solution.py
+++ b/solution.py
@@ -352,8 +352,8 @@
     return pl.ds(pl.multiple_of(index * unit, unit), unit)
 
 
-def cut_body(info, mix, expand, shrink, dense, *rest):
-    vectors, (own, other, own_all), small = rest[:8], rest[8:11], rest[11]
+def cut_body(info, mix, expand, *rest):
+    vectors, (own, other), small = rest[:8], rest[8:10], rest[10]
     row = 0
     small[...] = jnp.zeros_like(small)
     for vector in vectors:
@@ -373,6 +373,9 @@
             second = jnp.where(upper, second, pltpu.roll(second, 64, 1))
             joined = jnp.where(lane < 64, first, second).astype(BF16)
             out[MIX_ROWS + pair * LANES : MIX_ROWS + (pair + 1) * LANES, :] = joined
+
+
+def cut_all_body(info, own, shrink, dense, own_all):
     own_all[:FIRST_ROWS, :] = own[...]
     rows = shrink[aligned(info[1], 64), :]
     for part in range(8):
@@ -381,9 +384,16 @@
         own_all[DENSE_START + LANES * part : DENSE_START + LANES * (part + 1), :] = dense[:, cols]
 
 
-def cut_slices(info, mix, expand, shrink, dense, vectors):
-    operands = [mix, expand, shrink, dense] + [vector.reshape(-1, LANES) for vector in vectors]
-    outs = [((rows, LANES), BF16) for rows in (FIRST_ROWS, FIRST_ROWS, DENSE_START + shrink.shape[1])]
+def cut_all(info, own, shrink, dense):
+    operands = [own, shrink, dense]
+    shape = (DENSE_START + shrink.shape[1], LANES)
+    in_specs = [whole(operand.shape) for operand in operands]
+    return call(cut_all_body, info, operands, in_specs, [(shape, BF16)], [whole(shape)], vmem=VMEM_WHOLE)[0]
+
+
+def cut_slices(info, mix, expand, vectors):
+    operands = [mix, expand] + [vector.reshape(-1, LANES) for vector in vectors]
+    outs = [((FIRST_ROWS, LANES), BF16)] * 2
     return call(
         cut_body,
         info,
@@ -1053,14 +1063,14 @@
 
     small = (first_gain, first_shift, second_gain, second_shift, dense_bias, shrink_bias, mix_bias, expand_bias)
     half = tokens // 2
-    own, other, own_all = cut_slices(info, mix_weight, expand_weight, shrink_weight, dense_weight, small)
+    own, other = cut_slices(info, mix_weight, expand_weight, small)
     marks = jnp.pad(segments.astype(BF16), ((0, 15), (0, width - tokens)))
     upper, lower = block_input[:half], jnp.concatenate([block_input[half:], marks])
     along = swap(other, low=1), swap(own, high=1), swap(other, high=1, low=1)
     upper_x, lower_low = gather_first(upper, lower)
     first = mark(info, own)
     upper_x, lower_low = after((upper_x, lower_low), first)
-    over = swap(own_all, y=1)
+    over = swap(cut_all(info, after(own, first), shrink_weight, dense_weight), y=1)
     upper_pair = swap(jnp.stack([upper, upper_x]), low=1)
     lower_in = jnp.stack([lower, lower_low])
     second = mark(info, upper_x, lower_in)
@@ -1102,11 +1112,12 @@
     branch_near = after(branch_near, dense_grad)
     branch_sum = (branch_near.astype(F32) + branch_got.astype(F32)).astype(BF16)
     branch_kept, branch_sent = branch_sum[:2], branch_sum[2:]
+    dense_sent = after(dense_grad, mark(info, branch_sent))
     grad_pre, bias_grad, feed_sums, expand_mine, expand_other = expand_backward(
         info, cot_near, cot_far, slope, normed, after(shrink, branch_sent), expand_lines, vectors
     )
     last_part = reduce_first(last_mine, last_other, HIDDEN, grad_pre)
-    dense_got = after(swap(dense_grad, high=1), grad_pre)
+    dense_got = after(swap(dense_sent, high=1), grad_pre)
     dense_grad = (dense_grad.astype(F32) + dense_got.astype(F32)).astype(BF16)
     grad_mixed, mix_mine, mix_other = attention_backward(
         info,

time: 194 us -> 192 us (0.990)
  waiting for transfers between devices: 66 us -> 63.2 us
  Pallas kernels: 70.7 us -> 73.1 us
  starting transfers between devices: 44.5 us -> 42.5 us
    ppermute x44, waiting for transfers between devices: 66 us -> 63.2 us  [permute(): return lax.ppermute(value, ('rep', 'fsdp'), pairs)]
    pallas_call x17 -> x18, Pallas kernels: 70.7 us -> 73.1 us  [call(): pl.pallas_call(body, grid_spec=pltpu.PrefetchScalarGridSpec(num_scalar_pr...]
    ppermute x44, starting transfers between devices: 44.5 us -> 42.5 us  [permute(): return lax.ppermute(value, ('rep', 'fsdp'), pairs)]
  transfers between devices with their start and end apart: 44 -> 44, of which waited for: 15 -> 15; matrix products, arithmetic and copies ran while one was open for 4% -> 4% of each run, Pallas kernels for 33% -> 35%
where the time goes in v6:
time: 192 us; the launch traced here: 191 us
  Pallas kernels  73.1 us (38%)
  waiting for transfers between devices  63.2 us (33%)
  starting transfers between devices  42.5 us (22%)
  other arithmetic  6.2 us (3%)
  local copies, waits for them, and re-layouts  4.22 us (2%)
    pallas_call x18, Pallas kernels, call(): pl.pallas_call(body, grid_spec=pltpu.PrefetchScalarGridSpec(num_scalar_pr...  73.1 us
    ppermute x44, waiting for transfers between devices, permute(): return lax.ppermute(value, ('rep', 'fsdp'), pairs)  63.2 us
    ppermute x44, starting transfers between devices, permute(): return lax.ppermute(value, ('rep', 'fsdp'), pairs)  42.5 us
  transfers between devices with their start and end apart: 44, of which 15 were waited for; matrix products, arithmetic and copies ran while one was open for 4% of the time, Pallas kernels for 35%

profile of v6, /device:TPU:6, one launch (start us, length us, event | category | flops | bytes accessed | tf_op | source)
XLA Modules:
  0.0 190.6 jit_solution(9288873455537899507)
XLA Ops:
  1.3 3.3 %shard_map.263 = (bf16[912,128]{1,0:T(8,128)(2,1)}, bf16[912,128]{1,0:T(8,128)(2,1)}) custom-call(s32[2]{0:T(128)} %pad_add_fusion.info, bf16[128,3072]{1,0:T(8,128)(2,1)} %mix.1, bf16[128,4096]{1,0:T(8,128)(2,1)} %expand.1, bf16[1,128]{1,0:T(2,128)(2,1)} %bitcast.87, bf16[1,128]{1,0:T(2,128)(2,1)} %bitcast.88, bf16[1,128]{1,0:T(2,128)(2,1)} %bitcast.89, ...), custom_call_target="tpu_custom_call" | custom-call | flops 20000000000 | bytes 60000000 | tf_op jit(solution)/shard_map/pallas_call | solution.py:329
  4.6 3.6 %collective-permute-start.5 = (bf16[912,128]{1,0:T(8,128)(2,1)}, bf16[912,128]{1,0:T(8,128)(2,1)S(1)}, u32[]{:S(2)}, u32[]{:S(2)}) collective-permute-start(bf16[912,128]{1,0:T(8,128)(2,1)} %get-tuple-element.117), channel_id=1, source_target_pairs={{0,6},{1,7},{2,4},{3,5},{4,2},{5,3},{6,0},{7,1},{8,14},{9,15},{10,... | collective-permute-start | bytes 700424 | tf_op jit(solution)/shard_map/ppermute | solution.py:305
  8.4 2.1 %collective-permute-start.3 = (bf16[144,1024]{1,0:T(8,128)(2,1)S(1)}, bf16[144,1024]{1,0:T(8,128)(2,1)S(1)}, u32[]{:S(2)}, u32[]{:S(2)}) collective-permute-start(bf16[144,1024]{1,0:T(8,128)(2,1)S(1)} %get-tuple-element.230), channel_id=1, source_target_pairs={{0,2},{1,3},{2,0},{3,1},{4,6},{5,7},{6,4},{7,5},{8,10},{9,11},{10,... | collective-permute-start | bytes 884744 | tf_op jit(solution)/shard_map/ppermute | solution.py:305
  11.0 3.0 %shard_map.264 = bf16[2448,128]{1,0:T(8,128)(2,1)} custom-call(s32[2]{0:T(128)} %pad_add_fusion.info, bf16[912,128]{1,0:T(8,128)(2,1)} %get-tuple-element.123.own, bf16[512,1024]{1,0:T(8,128)(2,1)} %shrink.3, bf16[128,1024]{1,0:T(8,128)(2,1)} %dense.3), custom_call_target="tpu_custom_call" | custom-call | flops 20000000000 | bytes 60000000 | tf_op jit(solution)/shard_map/pallas_call | solution.py:329
  14.1 3.6 %collective-permute-done = bf16[128,1024]{1,0:T(8,128)(2,1)S(1)} collective-permute-done((bf16[128,1024]{1,0:T(8,128)(2,1)S(1)}, bf16[128,1024]{1,0:T(8,128)(2,1)S(1)}, u32[]{:S(2)}, u32[]{:S(2)}) %collective-permute-start) | collective-permute-done | bytes 262176 | tf_op jit(solution)/shard_map/ppermute | solution.py:305
  18.2 12.3 %collective-permute-done.3 = bf16[144,1024]{1,0:T(8,128)(2,1)S(1)} collective-permute-done((bf16[144,1024]{1,0:T(8,128)(2,1)S(1)}, bf16[144,1024]{1,0:T(8,128)(2,1)S(1)}, u32[]{:S(2)}, u32[]{:S(2)}) %collective-permute-start.3) | collective-permute-done | bytes 294944 | tf_op jit(solution)/shard_map/ppermute | solution.py:305
  32.8 3.3 %shard_map.265 = (bf16[192,1024]{1,0:T(8,128)(2,1)}, bf16[192,1024]{1,0:T(8,128)(2,1)}, bf16[64,1024]{1,0:T(8,128)(2,1)}) custom-call(s32[2]{0:T(128)} %pad_add_fusion.info, bf16[512,1024]{1,0:T(8,128)(2,1)} %shrink.3, bf16[128,1024]{1,0:T(8,128)(2,1)} %dense.3, bf16[256,1024]{1,0:T(8,128)(2,1)} %cot.3, bf16[2448,128]{1,0:T(8,128)(2,1)} %copy-done.5), custom_call_target="tpu_custom_call" | custom-call | flops 20000000000 | bytes 60000000 | tf_op jit(solution)/shard_map/pallas_call | solution.py:329
  36.1 1.9 collective-permute-start.9
  38.5 15.3 %collective-permute-done.1 = bf16[2,128,1024]{2,1,0:T(8,128)(2,1)S(1)} collective-permute-done((bf16[2,128,1024]{2,1,0:T(8,128)(2,1)S(1)}, bf16[2,128,1024]{2,1,0:T(8,128)(2,1)S(1)}, u32[]{:S(2)}, u32[]{:S(2)}) %collective-permute-start.1) | collective-permute-done | bytes 524320 | tf_op jit(solution)/shard_map/ppermute | solution.py:305
  54.7 1.7 collective-permute-start.11
  57.0 7.3 %shard_map.266 = (bf16[4,256,1024]{2,1,0:T(8,128)(2,1)S(1)}, bf16[4,256,384]{2,1,0:T(8,128)(2,1)S(1)}, f32[4,16,256]{2,1,0:T(8,128)S(1)}, bf16[4,2,256,256]{3,2,...) custom-call(s32[2]{0:T(128)S(1)} %copy-done.4, ...), custom_call_target="tpu_custom_call" | custom-call | flops 44999999488 | bytes 135000000 | tf_op jit(solution)/shard_map/pallas_call | solution.py:329
  65.6 1.6 collective-permute-start.16
  68.2 6.9 %shard_map.268 = (bf16[4,256,1024]{2,1,0:T(8,128)(2,1)S(1)}, bf16[4,256,384]{2,1,0:T(8,128)(2,1)S(1)}, f32[4,16,256]{2,1,0:T(8,128)S(1)}, bf16[4,2,256,256]{3,2,...) custom-call(s32[2]{0:T(128)S(1)} %copy-done.4, ...), custom_call_target="tpu_custom_call" | custom-call | flops 44999999488 | bytes 135000000 | tf_op jit(solution)/shard_map/pallas_call | solution.py:329
  75.2 1.7 shard_map.269
  76.9 3.2 %collective-permute-done.15 = bf16[2,128,1024]{2,1,0:T(8,128)(2,1)S(1)} collective-permute-done((bf16[2,128,1024]{2,1,0:T(8,128)(2,1)S(1)}, bf16[2,128,1024]{2,1,0:T(8,128)(2,1)S(1)}, u32[]{:S(2)}, u32[]{:S(2)}) %collective-permute-start.15) | collective-permute-done | bytes 524320 | tf_op jit(solution)/shard_map/ppermute | solution.py:305
  80.4 2.6 %shard_map.270 = (bf16[4,256,1024]{2,1,0:T(8,128)(2,1)S(1)}, bf16[512,1024]{1,0:T(8,128)(2,1)S(1)}) custom-call(s32[2]{0:T(128)S(1)} %copy-done.4, bf16[4,256,128]{2,1,0:T(8,128)(2,1)S(1)} %get-tuple-element.149.context, bf16[4,256,512]{2,1,0:T(8,128)(2,1)S(1)} %get-tuple-element.150.act, bf16[128,1024]{1,0:T(8,128)(2,1)S(1)} %get-tuple-element.178.dense, ...), custom_call_target="tpu_custom_call" | custom-call | flops 24999999488 | bytes 75000000 | tf_op jit(solution)/shard_map/pallas_call | solution.py:329
  83.6 2.5 %shard_map.271 = bf16[4,256,1024]{2,1,0:T(8,128)(2,1)S(1)} custom-call(s32[2]{0:T(128)S(1)} %copy-done.4, bf16[4,256,128]{2,1,0:T(8,128)(2,1)S(1)} %get-tuple-element.132.context, bf16[4,256,512]{2,1,0:T(8,128)(2,1)S(1)} %get-tuple-element.133.act, bf16[128,1024]{1,0:T(8,128)(2,1)S(1)} %get-tuple-element.178.dense, ...), custom_call_target="tpu_custom_call" | custom-call | flops 24999999488 | bytes 75000000 | tf_op jit(solution)/shard_map/pallas_call | solution.py:329
  86.2 4.8 %shard_map.272 = (bf16[2048,128]{1,0:T(8,128)(2,1)S(1)}, bf16[2048,128]{1,0:T(8,128)(2,1)S(1)}, bf16[1024,128]{1,0:T(8,128)(2,1)S(1)}) custom-call(s32[2]{0:T(128)S(1)} %copy-done.4, bf16[1024,1024]{1,0:T(8,128)(2,1)S(1)} %bitcast.63, bf16[1024,1024]{1,0:T(8,128)(2,1)S(1)} %bitcast.64, bf16[1024,512]{1,0:T(8,128)(2,1)S(1)} %bitcast.65, ...), custom_call_target="tpu_custom_call" | custom-call | tf_op jit(solution)/shard_map/pallas_call | solution.py:329
  92.1 1.2 collective-permute-start.19
  93.2 1.5 collective-permute-start.20
  94.8 3.7 %collective-permute-start.21 = (bf16[1024,128]{1,0:T(8,128)(2,1)S(1)}, bf16[1024,128]{1,0:T(8,128)(2,1)S(1)}, u32[]{:S(2)}, u32[]{:S(2)}) collective-permute-start(bf16[1024,128]{1,0:T(8,128)(2,1)S(1)} %get-tuple-element.158), channel_id=1, source_target_pairs={{0,4},{1,5},{2,6},{3,7},{4,0},{5,1},{6,2},{7,3},{8,12},{9,13},{10,... | collective-permute-start | bytes 786440 | tf_op jit(solution)/shard_map/ppermute | solution.py:305
  98.4 8.6 %shard_map.273 = (bf16[8,256,512]{2,1,0:T(8,128)(2,1)S(1)}, f32[8,512]{1,0:T(8,128)S(1)}, f32[8,1024]{1,0:T(8,128)S(1)}, bf16[2048,128]{1,0:T(8,128)(2,1)S(1)}, bf16[2048,128]{1,0:T(8,128)(2,1)S(1)}) custom-call(s32[2]{0:T(128)S(1)} %copy-done.4, bf16[4,256,1024]{2,1,0:T(8,128)(2,1)S(1)} %maximum_maximum_fusion.1.near, ...), custom_call_target="tpu_custom_call" | custom-call | flops 44999999488 | bytes 135000000 | tf_op jit(solution)/shard_map/pallas_call | solution.py:329
  107.6 2.3 %collective-permute-done.21 = bf16[1024,128]{1,0:T(8,128)(2,1)S(1)} collective-permute-done((bf16[1024,128]{1,0:T(8,128)(2,1)S(1)}, bf16[1024,128]{1,0:T(8,128)(2,1)S(1)}, u32[]{:S(2)}, u32[]{:S(2)}) %collective-permute-start.21) | collective-permute-done | bytes 262176 | tf_op jit(solution)/shard_map/ppermute | solution.py:305
  110.8 1.2 collective-permute-start.23
  112.0 12.2 %shard_map.274 = (bf16[8,256,384]{2,1,0:T(8,128)(2,1)S(1)}, bf16[1600,128]{1,0:T(8,128)(2,1)S(1)}, bf16[1600,128]{1,0:T(8,128)(2,1)S(1)}) custom-call(s32[2]{0:T(128)S(1)} %copy-done.4, bf16[4,256,1024]{2,1,0:T(8,128)(2,1)S(1)} %maximum_maximum_fusion.1.near, bf16[4,256,1024]{2,1,0:T(8,128)(2,1)S(1)} %collective-permute-done.17.far, ...), custom_call_target="tpu_custom_call" | custom-call | flops 30000001024 | bytes 90000000 | tf_op jit(solution)/shard_map/pallas_call | solution.py:329
  124.2 3.1 %shard_map.275 = bf16[4,256,1024]{2,1,0:T(8,128)(2,1)S(1)} custom-call(s32[2]{0:T(128)S(1)} %copy-done.4, bf16[8,256,384]{2,1,0:T(8,128)(2,1)S(1)} %get-tuple-element.190.mixed, bf16[8,256,512]{2,1,0:T(8,128)(2,1)S(1)} %get-tuple-element.175.pre, bf16[1024,384]{1,0:T(8,128)(2,1)S(1)} %get-tuple-element.151.mix, ...), custom_call_target="tpu_custom_call" | custom-call | tf_op jit(solution)/shard_map/pallas_call | solution.py:329
  127.4 1.6 collective-permute-start.22
  129.1 1.9 collective-permute-start.31
  132.3 3.4 %shard_map.276 = bf16[4,256,1024]{2,1,0:T(8,128)(2,1)S(1)} custom-call(s32[2]{0:T(128)S(1)} %copy-done.4, bf16[8,256,384]{2,1,0:T(8,128)(2,1)S(1)} %get-tuple-element.190.mixed, bf16[8,256,512]{2,1,0:T(8,128)(2,1)S(1)} %get-tuple-element.175.pre, bf16[1024,384]{1,0:T(8,128)(2,1)S(1)} %get-tuple-element.151.mix, ...), custom_call_target="tpu_custom_call" | custom-call | flops 30000001024 | bytes 90000000 | tf_op jit(solution)/shard_map/pallas_call | solution.py:329
  135.7 1.6 collective-permute-done.22
  137.4 2.7 %collective-permute-start.26 = (bf16[800,128]{1,0:T(8,128)(2,1)S(1)}, bf16[800,128]{1,0:T(8,128)(2,1)S(1)}, u32[]{:S(2)}, u32[]{:S(2)}) collective-permute-start(bf16[800,128]{1,0:T(8,128)(2,1)S(1)} %slice.289), channel_id=1, source_target_pairs={{0,4},{1,5},{2,6},{3,7},{4,0},{5,1},{6,2},{7,3},{8,12},{9,13},{10,... | collective-permute-start | bytes 614408 | tf_op jit(solution)/shard_map/ppermute | solution.py:305
  140.2 1.0 convert_add_fusion
  141.3 1.4 collective-permute-start.33
  143.2 1.6 collective-permute-start.34
  144.8 8.5 %collective-permute-done.26 = bf16[800,128]{1,0:T(8,128)(2,1)S(1)} collective-permute-done((bf16[800,128]{1,0:T(8,128)(2,1)S(1)}, bf16[800,128]{1,0:T(8,128)(2,1)S(1)}, u32[]{:S(2)}, u32[]{:S(2)}) %collective-permute-start.26) | collective-permute-done | bytes 204832 | tf_op jit(solution)/shard_map/ppermute | solution.py:305
  153.6 2.1 %collective-permute-start.36 = (bf16[512,128]{1,0:T(8,128)(2,1)S(1)}, bf16[512,128]{1,0:T(8,128)(2,1)S(1)}, u32[]{:S(2)}, u32[]{:S(2)}) collective-permute-start(bf16[512,128]{1,0:T(8,128)(2,1)S(1)} %get-tuple-element.232), channel_id=1, source_target_pairs={{0,2},{1,3},{2,0},{3,1},{4,6},{5,7},{6,4},{7,5},{8,10},{9,11},{10,... | collective-permute-start | bytes 393224 | tf_op jit(solution)/shard_map/ppermute | solution.py:305
  155.7 5.3 %collective-permute-done.34 = bf16[1024,128]{1,0:T(8,128)(2,1)S(1)} collective-permute-done((bf16[1024,128]{1,0:T(8,128)(2,1)S(1)}, bf16[1024,128]{1,0:T(8,128)(2,1)S(1)}, u32[]{:S(2)}, u32[]{:S(2)}) %collective-permute-start.34) | collective-permute-done | bytes 262176 | tf_op jit(solution)/shard_map/ppermute | solution.py:305
  162.4 1.8 collective-permute-done.30
  164.7 1.7 collective-permute-start.41
  166.4 1.9 %collective-permute-start.35 = (bf16[256,1024]{1,0:T(8,128)(2,1)S(1)}, bf16[256,1024]{1,0:T(8,128)(2,1)S(1)}, u32[]{:S(2)}, u32[]{:S(2)}) collective-permute-start(bf16[256,1024]{1,0:T(8,128)(2,1)S(1)} %slice_bitcast_fusion.2), channel_id=1, source_target_pairs={{0,2},{1,3},{2,0},{3,1},{4,6},{5,7},{6,4},{7,5},{8,10},{9,11},{10,... | collective-permute-start | bytes 1572872 | tf_op jit(solution)/shard_map/ppermute | solution.py:305
  168.9 4.6 %collective-permute-done.39.upper_got = bf16[128,1024]{1,0:T(8,128)(2,1)S(1)} collective-permute-done((bf16[128,1024]{1,0:T(8,128)(2,1)S(1)}, bf16[128,1024]{1,0:T(8,128)(2,1)S(1)}, u32[]{:S(2)}, u32[]{:S(2)}) %collective-permute-start.39) | collective-permute-done | bytes 262176 | tf_op jit(solution)/shard_map/ppermute | solution.py:305
  173.6 2.2 %shard_map.277 = f32[256,1024]{1,0:T(8,128)} custom-call(s32[2]{0:T(128)S(1)} %copy-done.4, bf16[256,1024]{1,0:T(8,128)(2,1)S(1)} %copy-done.1, bf16[256,1024]{1,0:T(8,128)(2,1)S(1)} %copy-done.3, f32[128,1024]{1,0:T(8,128)S(1)} %slice_bitcast_fusion.1.upper, bf16[128,1024]{1,0:T(8,128)(2,1)S(1)} %collective-permute-done.39.upper_got, ...), custom_call_target="tpu_custom_call" | custom-call | flops 20000000000 | bytes 60000000 | tf_op jit(solution)/shard_map/pallas_call | solution.py:329
  175.8 2.2 %shard_map.278 = (f32[512,1024]{1,0:T(8,128)}, f32[128,1024]{1,0:T(8,128)}) custom-call(s32[2]{0:T(128)S(1)} %copy-done.4, bf16[3072,128]{1,0:T(8,128)(2,1)S(1)} %pad_maximum_fusion.near, bf16[3072,128]{1,0:T(8,128)(2,1)S(1)} %collective-permute-done.38.far, s32[1]{0:T(128)} %bitcast.35.own_dense), custom_call_target="tpu_custom_call" | custom-call | flops 20000000000 | bytes 60000000 | tf_op jit(solution)/shard_map/pallas_call | solution.py:329
  178.0 1.2 collective-permute-done.37
  180.0 2.1 %collective-permute-done.35 = bf16[256,1024]{1,0:T(8,128)(2,1)S(1)} collective-permute-done((bf16[256,1024]{1,0:T(8,128)(2,1)S(1)}, bf16[256,1024]{1,0:T(8,128)(2,1)S(1)}, u32[]{:S(2)}, u32[]{:S(2)}) %collective-permute-start.35) | collective-permute-done | bytes 524320 | tf_op jit(solution)/shard_map/ppermute | solution.py:305
  182.2 1.1 add_convert_fusion.2
  183.2 2.4 %shard_map.279 = f32[128,3072]{1,0:T(8,128)} custom-call(s32[2]{0:T(128)S(1)} %copy-done.4, bf16[1616,128]{1,0:T(8,128)(2,1)S(1)} %pad_maximum_fusion.7.near, bf16[1616,128]{1,0:T(8,128)(2,1)S(1)} %collective-permute-done.42.far), custom_call_target="tpu_custom_call" | custom-call | flops 20000000000 | bytes 60000000 | tf_op jit(solution)/shard_map/pallas_call | solution.py:329
  187.3 2.7 %shard_map.280 = f32[128,4096]{1,0:T(8,128)} custom-call(s32[2]{0:T(128)S(1)} %copy-done.4, bf16[2048,128]{1,0:T(8,128)(2,1)S(1)} %pad_maximum_fusion.6.near, bf16[2048,128]{1,0:T(8,128)(2,1)S(1)} %collective-permute-done.43.far), custom_call_target="tpu_custom_call" | custom-call | flops 20000000000 | bytes 60000000 | tf_op jit(solution)/shard_map/pallas_call | solution.py:329
  (138 shorter events, 19.6 us)
Async XLA Ops:
  1.3 6.9 %copy-start = (bf16[256,1024]{1,0:T(8,128)(2,1)S(1)}, bf16[256,1024]{1,0:T(8,128)(2,1)}, u32[]{:S(2)}) copy-start(bf16[256,1024]{1,0:T(8,128)(2,1)} %block.1) | copy-start | bytes 1572868
  4.6 26.0 %collective-permute-start.5 = (bf16[912,128]{1,0:T(8,128)(2,1)}, bf16[912,128]{1,0:T(8,128)(2,1)S(1)}, u32[]{:S(2)}, u32[]{:S(2)}) collective-permute-start(bf16[912,128]{1,0:T(8,128)(2,1)} %get-tuple-element.117), channel_id=1, source_target_pairs={{0,6},{1,7},{2,4},{3,5},{4,2},{5,3},{6,0},{7,1},{8,14},{9,15},{10,... | collective-permute-start | bytes 700424 | tf_op jit(solution)/shard_map/ppermute | solution.py:305
  8.2 22.4 %collective-permute-start.2 = (bf16[912,128]{1,0:T(8,128)(2,1)}, bf16[912,128]{1,0:T(8,128)(2,1)S(1)}, u32[]{:S(2)}, u32[]{:S(2)}) collective-permute-start(bf16[912,128]{1,0:T(8,128)(2,1)} %get-tuple-element.117), channel_id=1, source_target_pairs={{0,2},{1,3},{2,0},{3,1},{4,6},{5,7},{6,4},{7,5},{8,10},{9,11},{10,... | collective-permute-start | bytes 700424 | tf_op jit(solution)/shard_map/ppermute | solution.py:305
  8.4 22.1 %collective-permute-start.3 = (bf16[144,1024]{1,0:T(8,128)(2,1)S(1)}, bf16[144,1024]{1,0:T(8,128)(2,1)S(1)}, u32[]{:S(2)}, u32[]{:S(2)}) collective-permute-start(bf16[144,1024]{1,0:T(8,128)(2,1)S(1)} %get-tuple-element.230), channel_id=1, source_target_pairs={{0,2},{1,3},{2,0},{3,1},{4,6},{5,7},{6,4},{7,5},{8,10},{9,11},{10,... | collective-permute-start | bytes 884744 | tf_op jit(solution)/shard_map/ppermute | solution.py:305
  10.5 7.2 %collective-permute-start = (bf16[128,1024]{1,0:T(8,128)(2,1)S(1)}, bf16[128,1024]{1,0:T(8,128)(2,1)S(1)}, u32[]{:S(2)}, u32[]{:S(2)}) collective-permute-start(bf16[128,1024]{1,0:T(8,128)(2,1)S(1)} %get-tuple-element.227), channel_id=1, source_target_pairs={{0,16},{1,17},{2,18},{3,19},{4,20},{5,21},{6,22},{7,23},{8,24},{9,... | collective-permute-start | bytes 786440 | tf_op jit(solution)/shard_map/ppermute | solution.py:305
  11.0 19.6 %collective-permute-start.4 = (bf16[912,128]{1,0:T(8,128)(2,1)}, bf16[912,128]{1,0:T(8,128)(2,1)S(1)}, u32[]{:S(2)}, u32[]{:S(2)}) collective-permute-start(bf16[912,128]{1,0:T(8,128)(2,1)} %get-tuple-element.123.own), channel_id=1, source_target_pairs={{0,4},{1,5},{2,6},{3,7},{4,0},{5,1},{6,2},{7,3},{8,12},{9,13},{10,... | collective-permute-start | bytes 700424 | tf_op jit(solution)/shard_map/ppermute | solution.py:305
  17.7 14.3 %collective-permute-start.6 = (bf16[2448,128]{1,0:T(8,128)(2,1)}, bf16[2448,128]{1,0:T(8,128)(2,1)S(1)}, u32[]{:S(2)}, u32[]{:S(2)}) collective-permute-start(bf16[2448,128]{1,0:T(8,128)(2,1)} %shard_map.264), channel_id=1, source_target_pairs={{0,1},{1,0},{2,3},{3,2},{4,5},{5,4},{6,7},{7,6},{8,9},{9,8},{10,11... | collective-permute-start | bytes 1880072 | tf_op jit(solution)/shard_map/ppermute | solution.py:305
  30.5 23.2 %collective-permute-start.1 = (bf16[2,128,1024]{2,1,0:T(8,128)(2,1)S(1)}, bf16[2,128,1024]{2,1,0:T(8,128)(2,1)S(1)}, u32[]{:S(2)}, u32[]{:S(2)}) collective-permute-start(bf16[2,128,1024]{2,1,0:T(8,128)(2,1)S(1)} %pad_maximum_fusion.3), channel_id=1, source_target_pairs={{0,2},{1,3},{2,0},{3,1},{4,6},{5,7},{6,4},{7,5},{8,10},{9,11},{10,... | collective-permute-start | bytes 1572872 | tf_op jit(solution)/shard_map/ppermute | solution.py:305
  30.7 25.7 %collective-permute-start.8 = (bf16[3,912,128]{2,1,0:T(8,128)(2,1)S(1)}, bf16[3,912,128]{2,1,0:T(8,128)(2,1)S(1)}, u32[]{:S(2)}, u32[]{:S(2)}) collective-permute-start(bf16[3,912,128]{2,1,0:T(8,128)(2,1)S(1)} %pad_maximum_fusion.1.along), channel_id=1, source_target_pairs={{0,1},{1,0},{2,3},{3,2},{4,5},{5,4},{6,7},{7,6},{8,9},{9,8},{10,11... | collective-permute-start | bytes 2101256 | tf_op jit(solution)/shard_map/ppermute | solution.py:305
  31.3 22.5 %collective-permute-start.7 = (bf16[2,144,1024]{2,1,0:T(8,128)(2,1)S(1)}, bf16[2,144,1024]{2,1,0:T(8,128)(2,1)S(1)}, u32[]{:S(2)}, u32[]{:S(2)}) collective-permute-start(bf16[2,144,1024]{2,1,0:T(8,128)(2,1)S(1)} %pad_maximum_fusion.2), channel_id=1, source_target_pairs={{0,16},{1,17},{2,18},{3,19},{4,20},{5,21},{6,22},{7,23},{8,24},{9,... | collective-permute-start | bytes 1769480 | tf_op jit(solution)/shard_map/ppermute | solution.py:305
  36.1 28.2 %collective-permute-start.9 = (bf16[192,1024]{1,0:T(8,128)(2,1)}, bf16[192,1024]{1,0:T(8,128)(2,1)S(1)}, u32[]{:S(2)}, u32[]{:S(2)}) collective-permute-start(bf16[192,1024]{1,0:T(8,128)(2,1)} %get-tuple-element.126), channel_id=1, source_target_pairs={{0,2},{1,3},{2,0},{3,1},{4,6},{5,7},{6,4},{7,5},{8,10},{9,11},{10,... | collective-permute-start | bytes 1179656 | tf_op jit(solution)/shard_map/ppermute | solution.py:305
  38.0 26.4 %collective-permute-start.10 = (bf16[192,1024]{1,0:T(8,128)(2,1)}, bf16[192,1024]{1,0:T(8,128)(2,1)S(1)}, u32[]{:S(2)}, u32[]{:S(2)}) collective-permute-start(bf16[192,1024]{1,0:T(8,128)(2,1)} %get-tuple-element.125.own), channel_id=1, source_target_pairs={{0,4},{1,5},{2,6},{3,7},{4,0},{5,1},{6,2},{7,3},{8,12},{9,13},{10,... | collective-permute-start | bytes 1179656 | tf_op jit(solution)/shard_map/ppermute | solution.py:305
  54.1 14.1 %collective-permute-start.12 = (bf16[4,272,1024]{2,1,0:T(8,128)(2,1)S(1)}, bf16[4,272,1024]{2,1,0:T(8,128)(2,1)S(1)}, u32[]{:S(2)}, u32[]{:S(2)}) collective-permute-start(bf16[4,272,1024]{2,1,0:T(8,128)(2,1)S(1)} %maximum_maximum_fusion.inputs), channel_id=1, source_target_pairs={{0,8},{1,9},{2,10},{3,11},{4,12},{5,13},{6,14},{7,15},{8,0},{9,1},... | collective-permute-start | bytes 6684680 | tf_op jit(solution)/shard_map/ppermute | solution.py:305
  54.7 9.6 %collective-permute-start.11 = (bf16[64,1024]{1,0:T(8,128)(2,1)S(1)}, bf16[64,1024]{1,0:T(8,128)(2,1)S(1)}, u32[]{:S(2)}, u32[]{:S(2)}) collective-permute-start(bf16[64,1024]{1,0:T(8,128)(2,1)S(1)} %copy-done.12), channel_id=1, source_target_pairs={{0,6},{1,7},{2,4},{3,5},{4,2},{5,3},{6,0},{7,1},{8,14},{9,15},{10,... | collective-permute-start | bytes 393224 | tf_op jit(solution)/shard_map/ppermute | solution.py:305
  56.4 7.9 %copy-start.7 = (bf16[192,1024]{1,0:T(8,128)(2,1)S(1)}, bf16[192,1024]{1,0:T(8,128)(2,1)}, u32[]{:S(2)}) copy-start(bf16[192,1024]{1,0:T(8,128)(2,1)} %get-tuple-element.125.own) | copy-start | bytes 1179652
  56.4 10.8 %collective-permute-start.13 = (bf16[128,1024]{1,0:T(8,128)(2,1)S(1)}, bf16[128,1024]{1,0:T(8,128)(2,1)S(1)}, u32[]{:S(2)}, u32[]{:S(2)}) collective-permute-start(bf16[128,1024]{1,0:T(8,128)(2,1)S(1)} %get-tuple-element.143), channel_id=1, source_target_pairs={{0,16},{1,17},{2,18},{3,19},{4,20},{5,21},{6,22},{7,23},{8,24},{9,... | collective-permute-start | bytes 786440 | tf_op jit(solution)/shard_map/ppermute | solution.py:305
  65.0 15.5 %collective-permute-start.14 = (bf16[192,1024]{1,0:T(8,128)(2,1)S(1)}, bf16[192,1024]{1,0:T(8,128)(2,1)S(1)}, u32[]{:S(2)}, u32[]{:S(2)}) collective-permute-start(bf16[192,1024]{1,0:T(8,128)(2,1)S(1)} %get-tuple-element.142.along), channel_id=1, source_target_pairs={{0,1},{1,0},{2,3},{3,2},{4,5},{5,4},{6,7},{7,6},{8,9},{9,8},{10,11... | collective-permute-start | bytes 1179656 | tf_op jit(solution)/shard_map/ppermute | solution.py:305
  65.6 14.4 %collective-permute-start.16 = (bf16[2,128,1024]{2,1,0:T(8,128)(2,1)S(1)}, bf16[2,128,1024]{2,1,0:T(8,128)(2,1)S(1)}, u32[]{:S(2)}, u32[]{:S(2)}) collective-permute-start(bf16[2,128,1024]{2,1,0:T(8,128)(2,1)S(1)} %pad_maximum_fusion.5), channel_id=1, source_target_pairs={{0,16},{1,17},{2,18},{3,19},{4,20},{5,21},{6,22},{7,23},{8,24},{9,... | collective-permute-start | bytes 1572872 | tf_op jit(solution)/shard_map/ppermute | solution.py:305
  67.2 12.8 %collective-permute-start.15 = (bf16[2,128,1024]{2,1,0:T(8,128)(2,1)S(1)}, bf16[2,128,1024]{2,1,0:T(8,128)(2,1)S(1)}, u32[]{:S(2)}, u32[]{:S(2)}) collective-permute-start(bf16[2,128,1024]{2,1,0:T(8,128)(2,1)S(1)} %pad_maximum_fusion.4), channel_id=1, source_target_pairs={{0,2},{1,3},{2,0},{3,1},{4,6},{5,7},{6,4},{7,5},{8,10},{9,11},{10,... | collective-permute-start | bytes 1572872 | tf_op jit(solution)/shard_map/ppermute | solution.py:305
  80.3 5.8 %collective-permute-start.17 = (bf16[4,256,1024]{2,1,0:T(8,128)(2,1)S(1)}, bf16[4,256,1024]{2,1,0:T(8,128)(2,1)S(1)}, u32[]{:S(2)}, u32[]{:S(2)}) collective-permute-start(bf16[4,256,1024]{2,1,0:T(8,128)(2,1)S(1)} %maximum_maximum_fusion.1.near), channel_id=1, source_target_pairs={{0,8},{1,9},{2,10},{3,11},{4,12},{5,13},{6,14},{7,15},{8,0},{9,1},... | collective-permute-start | bytes 6291464 | tf_op jit(solution)/shard_map/ppermute | solution.py:305
  83.1 7.9 %collective-permute-start.18 = (bf16[4,256,1024]{2,1,0:T(8,128)(2,1)S(1)}, bf16[4,256,1024]{2,1,0:T(8,128)(2,1)S(1)}, u32[]{:S(2)}, u32[]{:S(2)}) collective-permute-start(bf16[4,256,1024]{2,1,0:T(8,128)(2,1)S(1)} %get-tuple-element.160), channel_id=1, source_target_pairs={{0,8},{1,9},{2,10},{3,11},{4,12},{5,13},{6,14},{7,15},{8,0},{9,1},... | collective-permute-start | bytes 6291464 | tf_op jit(solution)/shard_map/ppermute | solution.py:305
  92.1 39.2 %collective-permute-start.19 = (bf16[2,256,1024]{2,1,0:T(8,128)(2,1)S(1)}, bf16[2,256,1024]{2,1,0:T(8,128)(2,1)S(1)}, u32[]{:S(2)}, u32[]{:S(2)}) collective-permute-start(bf16[2,256,1024]{2,1,0:T(8,128)(2,1)S(1)} %slice.213), channel_id=1, source_target_pairs={{0,16},{1,17},{2,18},{3,19},{4,20},{5,21},{6,22},{7,23},{8,24},{9,... | collective-permute-start | bytes 3145736 | tf_op jit(solution)/shard_map/ppermute | solution.py:305
  93.2 17.4 %collective-permute-start.20 = (bf16[2048,128]{1,0:T(8,128)(2,1)S(1)}, bf16[2048,128]{1,0:T(8,128)(2,1)S(1)}, u32[]{:S(2)}, u32[]{:S(2)}) collective-permute-start(bf16[2048,128]{1,0:T(8,128)(2,1)S(1)} %get-tuple-element.170), channel_id=1, source_target_pairs={{0,1},{1,0},{2,3},{3,2},{4,5},{5,4},{6,7},{7,6},{8,9},{9,8},{10,11... | collective-permute-start | bytes 1572872 | tf_op jit(solution)/shard_map/ppermute | solution.py:305
  94.8 15.2 %collective-permute-start.21 = (bf16[1024,128]{1,0:T(8,128)(2,1)S(1)}, bf16[1024,128]{1,0:T(8,128)(2,1)S(1)}, u32[]{:S(2)}, u32[]{:S(2)}) collective-permute-start(bf16[1024,128]{1,0:T(8,128)(2,1)S(1)} %get-tuple-element.158), channel_id=1, source_target_pairs={{0,4},{1,5},{2,6},{3,7},{4,0},{5,1},{6,2},{7,3},{8,12},{9,13},{10,... | collective-permute-start | bytes 786440 | tf_op jit(solution)/shard_map/ppermute | solution.py:305
  107.1 21.9 %collective-permute-start.25 = (bf16[2048,128]{1,0:T(8,128)(2,1)S(1)}, bf16[2048,128]{1,0:T(8,128)(2,1)S(1)}, u32[]{:S(2)}, u32[]{:S(2)}) collective-permute-start(bf16[2048,128]{1,0:T(8,128)(2,1)S(1)} %get-tuple-element.188), channel_id=1, source_target_pairs={{0,1},{1,0},{2,3},{3,2},{4,5},{5,4},{6,7},{7,6},{8,9},{9,8},{10,11... | collective-permute-start | bytes 1572872 | tf_op jit(solution)/shard_map/ppermute | solution.py:305
  110.1 19.1 %collective-permute-start.24 = (bf16[1024,128]{1,0:T(8,128)(2,1)S(1)}, bf16[1024,128]{1,0:T(8,128)(2,1)S(1)}, u32[]{:S(2)}, u32[]{:S(2)}) collective-permute-start(bf16[1024,128]{1,0:T(8,128)(2,1)S(1)} %add_convert_fusion.4), channel_id=1, source_target_pairs={{0,1},{1,0},{2,3},{3,2},{4,5},{5,4},{6,7},{7,6},{8,9},{9,8},{10,11... | collective-permute-start | bytes 786440 | tf_op jit(solution)/shard_map/ppermute | solution.py:305
  110.8 20.2 %collective-permute-start.23 = (bf16[1024,128]{1,0:T(8,128)(2,1)S(1)}, bf16[1024,128]{1,0:T(8,128)(2,1)S(1)}, u32[]{:S(2)}, u32[]{:S(2)}) collective-permute-start(bf16[1024,128]{1,0:T(8,128)(2,1)S(1)} %slice.288), channel_id=1, source_target_pairs={{0,4},{1,5},{2,6},{3,7},{4,0},{5,1},{6,2},{7,3},{8,12},{9,13},{10,... | collective-permute-start | bytes 786440 | tf_op jit(solution)/shard_map/ppermute | solution.py:305
  127.4 9.9 %collective-permute-start.22 = (bf16[1600,128]{1,0:T(8,128)(2,1)S(1)}, bf16[1600,128]{1,0:T(8,128)(2,1)S(1)}, u32[]{:S(2)}, u32[]{:S(2)}) collective-permute-start(bf16[1600,128]{1,0:T(8,128)(2,1)S(1)} %get-tuple-element.184), channel_id=1, source_target_pairs={{0,1},{1,0},{2,3},{3,2},{4,5},{5,4},{6,7},{7,6},{8,9},{9,8},{10,11... | collective-permute-start | bytes 1228808 | tf_op jit(solution)/shard_map/ppermute | solution.py:305
  129.0 11.2 %collective-permute-start.29 = (bf16[4,256,1024]{2,1,0:T(8,128)(2,1)S(1)}, bf16[4,256,1024]{2,1,0:T(8,128)(2,1)S(1)}, u32[]{:S(2)}, u32[]{:S(2)}) collective-permute-start(bf16[4,256,1024]{2,1,0:T(8,128)(2,1)S(1)} %shard_map.275), channel_id=1, source_target_pairs={{0,8},{1,9},{2,10},{3,11},{4,12},{5,13},{6,14},{7,15},{8,0},{9,1},... | collective-permute-start | bytes 6291464 | tf_op jit(solution)/shard_map/ppermute | solution.py:305
  129.1 24.3 %collective-permute-start.31 = (bf16[1024,128]{1,0:T(8,128)(2,1)S(1)}, bf16[1024,128]{1,0:T(8,128)(2,1)S(1)}, u32[]{:S(2)}, u32[]{:S(2)}) collective-permute-start(bf16[1024,128]{1,0:T(8,128)(2,1)S(1)} %slice.287), channel_id=1, source_target_pairs={{0,4},{1,5},{2,6},{3,7},{4,0},{5,1},{6,2},{7,3},{8,12},{9,13},{10,... | collective-permute-start | bytes 786440 | tf_op jit(solution)/shard_map/ppermute | solution.py:305
  131.2 12.0 %collective-permute-start.27 = (bf16[512,128]{1,0:T(8,128)(2,1)S(1)}, bf16[512,128]{1,0:T(8,128)(2,1)S(1)}, u32[]{:S(2)}, u32[]{:S(2)}) collective-permute-start(bf16[512,128]{1,0:T(8,128)(2,1)S(1)} %get-tuple-element.234), channel_id=1, source_target_pairs={{0,2},{1,3},{2,0},{3,1},{4,6},{5,7},{6,4},{7,5},{8,10},{9,11},{10,... | collective-permute-start | bytes 393224 | tf_op jit(solution)/shard_map/ppermute | solution.py:305
  131.3 8.8 %collective-permute-start.28 = (bf16[1024,128]{1,0:T(8,128)(2,1)S(1)}, bf16[1024,128]{1,0:T(8,128)(2,1)S(1)}, u32[]{:S(2)}, u32[]{:S(2)}) collective-permute-start(bf16[1024,128]{1,0:T(8,128)(2,1)S(1)} %get-tuple-element.243), channel_id=1, source_target_pairs={{0,16},{1,17},{2,18},{3,19},{4,20},{5,21},{6,22},{7,23},{8,24},{9,... | collective-permute-start | bytes 786440 | tf_op jit(solution)/shard_map/ppermute | solution.py:305
  137.4 15.9 %collective-permute-start.26 = (bf16[800,128]{1,0:T(8,128)(2,1)S(1)}, bf16[800,128]{1,0:T(8,128)(2,1)S(1)}, u32[]{:S(2)}, u32[]{:S(2)}) collective-permute-start(bf16[800,128]{1,0:T(8,128)(2,1)S(1)} %slice.289), channel_id=1, source_target_pairs={{0,4},{1,5},{2,6},{3,7},{4,0},{5,1},{6,2},{7,3},{8,12},{9,13},{10,... | collective-permute-start | bytes 614408 | tf_op jit(solution)/shard_map/ppermute | solution.py:305
  141.3 20.7 %collective-permute-start.33 = (bf16[2,128,1024]{2,1,0:T(8,128)(2,1)S(1)}, bf16[2,128,1024]{2,1,0:T(8,128)(2,1)S(1)}, u32[]{:S(2)}, u32[]{:S(2)}) collective-permute-start(bf16[2,128,1024]{2,1,0:T(8,128)(2,1)S(1)} %get-tuple-element.218), channel_id=1, source_target_pairs={{0,2},{1,3},{2,0},{3,1},{4,6},{5,7},{6,4},{7,5},{8,10},{9,11},{10,... | collective-permute-start | bytes 1572872 | tf_op jit(solution)/shard_map/ppermute | solution.py:305
  142.7 19.3 %collective-permute-start.32 = (bf16[2,128,1024]{2,1,0:T(8,128)(2,1)S(1)}, bf16[2,128,1024]{2,1,0:T(8,128)(2,1)S(1)}, u32[]{:S(2)}, u32[]{:S(2)}) collective-permute-start(bf16[2,128,1024]{2,1,0:T(8,128)(2,1)S(1)} %get-tuple-element.219), channel_id=1, source_target_pairs={{0,16},{1,17},{2,18},{3,19},{4,20},{5,21},{6,22},{7,23},{8,24},{9,... | collective-permute-start | bytes 1572872 | tf_op jit(solution)/shard_map/ppermute | solution.py:305
  143.2 17.7 %collective-permute-start.34 = (bf16[1024,128]{1,0:T(8,128)(2,1)S(1)}, bf16[1024,128]{1,0:T(8,128)(2,1)S(1)}, u32[]{:S(2)}, u32[]{:S(2)}) collective-permute-start(bf16[1024,128]{1,0:T(8,128)(2,1)S(1)} %pad_maximum_fusion.8), channel_id=1, source_target_pairs={{0,16},{1,17},{2,18},{3,19},{4,20},{5,21},{6,22},{7,23},{8,24},{9,... | collective-permute-start | bytes 786440 | tf_op jit(solution)/shard_map/ppermute | solution.py:305
  153.4 10.8 %collective-permute-start.30 = (bf16[400,128]{1,0:T(8,128)(2,1)S(1)}, bf16[400,128]{1,0:T(8,128)(2,1)S(1)}, u32[]{:S(2)}, u32[]{:S(2)}) collective-permute-start(bf16[400,128]{1,0:T(8,128)(2,1)S(1)} %get-tuple-element.236), channel_id=1, source_target_pairs={{0,2},{1,3},{2,0},{3,1},{4,6},{5,7},{6,4},{7,5},{8,10},{9,11},{10,... | collective-permute-start | bytes 307208 | tf_op jit(solution)/shard_map/ppermute | solution.py:305
  153.6 14.8 %collective-permute-start.36 = (bf16[512,128]{1,0:T(8,128)(2,1)S(1)}, bf16[512,128]{1,0:T(8,128)(2,1)S(1)}, u32[]{:S(2)}, u32[]{:S(2)}) collective-permute-start(bf16[512,128]{1,0:T(8,128)(2,1)S(1)} %get-tuple-element.232), channel_id=1, source_target_pairs={{0,2},{1,3},{2,0},{3,1},{4,6},{5,7},{6,4},{7,5},{8,10},{9,11},{10,... | collective-permute-start | bytes 393224 | tf_op jit(solution)/shard_map/ppermute | solution.py:305
  162.3 11.3 %copy-start.1 = (bf16[256,1024]{1,0:T(8,128)(2,1)S(1)}, bf16[256,1024]{1,0:T(8,128)(2,1)}, u32[]{:S(2)}) copy-start(bf16[256,1024]{1,0:T(8,128)(2,1)} %block.1) | copy-start | bytes 1572868
  162.3 11.3 %copy-start.3 = (bf16[256,1024]{1,0:T(8,128)(2,1)S(1)}, bf16[256,1024]{1,0:T(8,128)(2,1)}, u32[]{:S(2)}) copy-start(bf16[256,1024]{1,0:T(8,128)(2,1)} %cot.3) | copy-start | bytes 1572868
  164.2 9.3 %collective-permute-start.39 = (bf16[128,1024]{1,0:T(8,128)(2,1)S(1)}, bf16[128,1024]{1,0:T(8,128)(2,1)S(1)}, u32[]{:S(2)}, u32[]{:S(2)}) collective-permute-start(bf16[128,1024]{1,0:T(8,128)(2,1)S(1)} %fusion.5), channel_id=1, source_target_pairs={{0,2},{1,3},{2,0},{3,1},{4,6},{5,7},{6,4},{7,5},{8,10},{9,11},{10,... | collective-permute-start | bytes 786440 | tf_op jit(solution)/shard_map/ppermute | solution.py:305
  164.3 9.3 %collective-permute-start.40 = (bf16[128,1024]{1,0:T(8,128)(2,1)S(1)}, bf16[128,1024]{1,0:T(8,128)(2,1)S(1)}, u32[]{:S(2)}, u32[]{:S(2)}) collective-permute-start(bf16[128,1024]{1,0:T(8,128)(2,1)S(1)} %fusion.6), channel_id=1, source_target_pairs={{0,16},{1,17},{2,18},{3,19},{4,20},{5,21},{6,22},{7,23},{8,24},{9,... | collective-permute-start | bytes 786440 | tf_op jit(solution)/shard_map/ppermute | solution.py:305
  164.7 14.6 %collective-permute-start.41 = (bf16[800,128]{1,0:T(8,128)(2,1)S(1)}, bf16[800,128]{1,0:T(8,128)(2,1)S(1)}, u32[]{:S(2)}, u32[]{:S(2)}) collective-permute-start(bf16[800,128]{1,0:T(8,128)(2,1)S(1)} %pad_maximum_fusion.10), channel_id=1, source_target_pairs={{0,16},{1,17},{2,18},{3,19},{4,20},{5,21},{6,22},{7,23},{8,24},{9,... | collective-permute-start | bytes 614408 | tf_op jit(solution)/shard_map/ppermute | solution.py:305
  166.4 15.8 %collective-permute-start.35 = (bf16[256,1024]{1,0:T(8,128)(2,1)S(1)}, bf16[256,1024]{1,0:T(8,128)(2,1)S(1)}, u32[]{:S(2)}, u32[]{:S(2)}) collective-permute-start(bf16[256,1024]{1,0:T(8,128)(2,1)S(1)} %slice_bitcast_fusion.2), channel_id=1, source_target_pairs={{0,2},{1,3},{2,0},{3,1},{4,6},{5,7},{6,4},{7,5},{8,10},{9,11},{10,... | collective-permute-start | bytes 1572872 | tf_op jit(solution)/shard_map/ppermute | solution.py:305
  168.4 10.9 %collective-permute-start.37 = (bf16[1024,128]{1,0:T(8,128)(2,1)S(1)}, bf16[1024,128]{1,0:T(8,128)(2,1)S(1)}, u32[]{:S(2)}, u32[]{:S(2)}) collective-permute-start(bf16[1024,128]{1,0:T(8,128)(2,1)S(1)} %pad_maximum_fusion.9), channel_id=1, source_target_pairs={{0,16},{1,17},{2,18},{3,19},{4,20},{5,21},{6,22},{7,23},{8,24},{9,... | collective-permute-start | bytes 786440 | tf_op jit(solution)/shard_map/ppermute | solution.py:305
  173.5 2.3 %collective-permute-start.38 = (bf16[3072,128]{1,0:T(8,128)(2,1)S(1)}, bf16[3072,128]{1,0:T(8,128)(2,1)S(1)}, u32[]{:S(2)}, u32[]{:S(2)}) collective-permute-start(bf16[3072,128]{1,0:T(8,128)(2,1)S(1)} %pad_maximum_fusion.near), channel_id=1, source_target_pairs={{0,8},{1,9},{2,10},{3,11},{4,12},{5,13},{6,14},{7,15},{8,0},{9,1},... | collective-permute-start | bytes 2359304 | tf_op jit(solution)/shard_map/ppermute | solution.py:305
  179.4 3.9 %collective-permute-start.42 = (bf16[1616,128]{1,0:T(8,128)(2,1)S(1)}, bf16[1616,128]{1,0:T(8,128)(2,1)S(1)}, u32[]{:S(2)}, u32[]{:S(2)}) collective-permute-start(bf16[1616,128]{1,0:T(8,128)(2,1)S(1)} %pad_maximum_fusion.7.near), channel_id=1, source_target_pairs={{0,8},{1,9},{2,10},{3,11},{4,12},{5,13},{6,14},{7,15},{8,0},{9,1},... | collective-permute-start | bytes 1241096 | tf_op jit(solution)/shard_map/ppermute | solution.py:305
  179.5 7.8 %collective-permute-start.43 = (bf16[2048,128]{1,0:T(8,128)(2,1)S(1)}, bf16[2048,128]{1,0:T(8,128)(2,1)S(1)}, u32[]{:S(2)}, u32[]{:S(2)}) collective-permute-start(bf16[2048,128]{1,0:T(8,128)(2,1)S(1)} %pad_maximum_fusion.6.near), channel_id=1, source_target_pairs={{0,8},{1,9},{2,10},{3,11},{4,12},{5,13},{6,14},{7,15},{8,0},{9,1},... | collective-permute-start | bytes 1572872 | tf_op jit(solution)/shard_map/ppermute | solution.py:305
  (9 other events, 28.3 us)

commit v7 on v6

--- a/solution.py
+++ b/solution.py
@@ -289,7 +289,7 @@
 F32 = jnp.float32
 BF16 = jnp.bfloat16
 COST = 5000
-VMEM_LIMIT = 18 * 1024 * 1024
+VMEM_LIMIT = 16 * 1024 * 1024
 VMEM_FIRST = 28 * 1024 * 1024
 VMEM_WHOLE = 56 * 1024 * 1024
 
@@ -1194,6 +1194,7 @@
     far = swap(near, core=1)
     sums = mix_sums.astype(F32) + far[4 * MIX_ROWS :].astype(F32)
     (mix_out,) = out(mix_out_body, near, far, [mix_weight.shape])
+    again = lax.optimization_barrier(sums)
     return (
         block_out,
         input_grad,
@@ -1208,7 +1209,7 @@
         expand_out,
         sums[8:12].reshape(-1),
         shrink_out,
-        sums[4],
+        again[4],
     )
 
 

time: 192 us -> 192 us (level)
  no operation moved by 1% of the time
where the time goes in v7:
time: 192 us; the launch traced here: 190 us
  Pallas kernels  73 us (38%)
  waiting for transfers between devices  63.2 us (33%)
  starting transfers between devices  42.5 us (22%)
  other arithmetic  6.12 us (3%)
  local copies, waits for them, and re-layouts  4.21 us (2%)
    pallas_call x18, Pallas kernels, call(): pl.pallas_call(body, grid_spec=pltpu.PrefetchScalarGridSpec(num_scalar_pr...  73 us
    ppermute x44, waiting for transfers between devices, permute(): return lax.ppermute(value, ('rep', 'fsdp'), pairs)  63.2 us
    ppermute x44, starting transfers between devices, permute(): return lax.ppermute(value, ('rep', 'fsdp'), pairs)  42.5 us
  transfers between devices with their start and end apart: 44, of which 15 were waited for; matrix products, arithmetic and copies ran while one was open for 4% of the time, Pallas kernels for 35%

profile of v7, /device:TPU:6, one launch (start us, length us, event | category | flops | bytes accessed | tf_op | source)
XLA Modules:
  0.0 190.5 jit_solution(10937708952649129805)
XLA Ops:
  1.3 3.3 %shard_map.263 = (bf16[912,128]{1,0:T(8,128)(2,1)}, bf16[912,128]{1,0:T(8,128)(2,1)}) custom-call(s32[2]{0:T(128)} %pad_add_fusion.info, bf16[128,3072]{1,0:T(8,128)(2,1)} %mix.1, bf16[128,4096]{1,0:T(8,128)(2,1)} %expand.1, bf16[1,128]{1,0:T(2,128)(2,1)} %bitcast.89, bf16[1,128]{1,0:T(2,128)(2,1)} %bitcast.90, bf16[1,128]{1,0:T(2,128)(2,1)} %bitcast.91, ...), custom_call_target="tpu_custom_call" | custom-call | flops 20000000000 | bytes 60000000 | tf_op jit(solution)/shard_map/pallas_call | solution.py:329
  4.6 3.6 %collective-permute-start.5 = (bf16[912,128]{1,0:T(8,128)(2,1)}, bf16[912,128]{1,0:T(8,128)(2,1)S(1)}, u32[]{:S(2)}, u32[]{:S(2)}) collective-permute-start(bf16[912,128]{1,0:T(8,128)(2,1)} %get-tuple-element.117), channel_id=1, source_target_pairs={{0,6},{1,7},{2,4},{3,5},{4,2},{5,3},{6,0},{7,1},{8,14},{9,15},{10,... | collective-permute-start | bytes 700424 | tf_op jit(solution)/shard_map/ppermute | solution.py:305
  8.4 2.1 %collective-permute-start.3 = (bf16[144,1024]{1,0:T(8,128)(2,1)S(1)}, bf16[144,1024]{1,0:T(8,128)(2,1)S(1)}, u32[]{:S(2)}, u32[]{:S(2)}) collective-permute-start(bf16[144,1024]{1,0:T(8,128)(2,1)S(1)} %get-tuple-element.230), channel_id=1, source_target_pairs={{0,2},{1,3},{2,0},{3,1},{4,6},{5,7},{6,4},{7,5},{8,10},{9,11},{10,... | collective-permute-start | bytes 884744 | tf_op jit(solution)/shard_map/ppermute | solution.py:305
  11.0 3.0 %shard_map.264 = bf16[2448,128]{1,0:T(8,128)(2,1)} custom-call(s32[2]{0:T(128)} %pad_add_fusion.info, bf16[912,128]{1,0:T(8,128)(2,1)} %get-tuple-element.123.own, bf16[512,1024]{1,0:T(8,128)(2,1)} %shrink.3, bf16[128,1024]{1,0:T(8,128)(2,1)} %dense.3), custom_call_target="tpu_custom_call" | custom-call | flops 20000000000 | bytes 60000000 | tf_op jit(solution)/shard_map/pallas_call | solution.py:329
  14.1 3.6 %collective-permute-done = bf16[128,1024]{1,0:T(8,128)(2,1)S(1)} collective-permute-done((bf16[128,1024]{1,0:T(8,128)(2,1)S(1)}, bf16[128,1024]{1,0:T(8,128)(2,1)S(1)}, u32[]{:S(2)}, u32[]{:S(2)}) %collective-permute-start) | collective-permute-done | bytes 262176 | tf_op jit(solution)/shard_map/ppermute | solution.py:305
  18.2 12.3 %collective-permute-done.3 = bf16[144,1024]{1,0:T(8,128)(2,1)S(1)} collective-permute-done((bf16[144,1024]{1,0:T(8,128)(2,1)S(1)}, bf16[144,1024]{1,0:T(8,128)(2,1)S(1)}, u32[]{:S(2)}, u32[]{:S(2)}) %collective-permute-start.3) | collective-permute-done | bytes 294944 | tf_op jit(solution)/shard_map/ppermute | solution.py:305
  32.8 3.3 %shard_map.265 = (bf16[192,1024]{1,0:T(8,128)(2,1)}, bf16[192,1024]{1,0:T(8,128)(2,1)}, bf16[64,1024]{1,0:T(8,128)(2,1)}) custom-call(s32[2]{0:T(128)} %pad_add_fusion.info, bf16[512,1024]{1,0:T(8,128)(2,1)} %shrink.3, bf16[128,1024]{1,0:T(8,128)(2,1)} %dense.3, bf16[256,1024]{1,0:T(8,128)(2,1)} %cot.3, bf16[2448,128]{1,0:T(8,128)(2,1)} %copy-done.5), custom_call_target="tpu_custom_call" | custom-call | flops 20000000000 | bytes 60000000 | tf_op jit(solution)/shard_map/pallas_call | solution.py:329
  36.1 1.9 collective-permute-start.9
  38.4 15.3 %collective-permute-done.1 = bf16[2,128,1024]{2,1,0:T(8,128)(2,1)S(1)} collective-permute-done((bf16[2,128,1024]{2,1,0:T(8,128)(2,1)S(1)}, bf16[2,128,1024]{2,1,0:T(8,128)(2,1)S(1)}, u32[]{:S(2)}, u32[]{:S(2)}) %collective-permute-start.1) | collective-permute-done | bytes 524320 | tf_op jit(solution)/shard_map/ppermute | solution.py:305
  54.7 1.7 collective-permute-start.11
  57.0 7.3 %shard_map.266 = (bf16[4,256,1024]{2,1,0:T(8,128)(2,1)S(1)}, bf16[4,256,384]{2,1,0:T(8,128)(2,1)S(1)}, f32[4,16,256]{2,1,0:T(8,128)S(1)}, bf16[4,2,256,256]{3,2,...) custom-call(s32[2]{0:T(128)S(1)} %copy-done.4, ...), custom_call_target="tpu_custom_call" | custom-call | flops 44999999488 | bytes 135000000 | tf_op jit(solution)/shard_map/pallas_call | solution.py:329
  65.6 1.6 collective-permute-start.16
  68.2 6.9 %shard_map.268 = (bf16[4,256,1024]{2,1,0:T(8,128)(2,1)S(1)}, bf16[4,256,384]{2,1,0:T(8,128)(2,1)S(1)}, f32[4,16,256]{2,1,0:T(8,128)S(1)}, bf16[4,2,256,256]{3,2,...) custom-call(s32[2]{0:T(128)S(1)} %copy-done.4, ...), custom_call_target="tpu_custom_call" | custom-call | flops 44999999488 | bytes 135000000 | tf_op jit(solution)/shard_map/pallas_call | solution.py:329
  75.2 1.7 shard_map.269
  76.8 3.2 %collective-permute-done.15 = bf16[2,128,1024]{2,1,0:T(8,128)(2,1)S(1)} collective-permute-done((bf16[2,128,1024]{2,1,0:T(8,128)(2,1)S(1)}, bf16[2,128,1024]{2,1,0:T(8,128)(2,1)S(1)}, u32[]{:S(2)}, u32[]{:S(2)}) %collective-permute-start.15) | collective-permute-done | bytes 524320 | tf_op jit(solution)/shard_map/ppermute | solution.py:305
  80.4 2.6 %shard_map.270 = (bf16[4,256,1024]{2,1,0:T(8,128)(2,1)S(1)}, bf16[512,1024]{1,0:T(8,128)(2,1)S(1)}) custom-call(s32[2]{0:T(128)S(1)} %copy-done.4, bf16[4,256,128]{2,1,0:T(8,128)(2,1)S(1)} %get-tuple-element.149.context, bf16[4,256,512]{2,1,0:T(8,128)(2,1)S(1)} %get-tuple-element.150.act, bf16[128,1024]{1,0:T(8,128)(2,1)S(1)} %get-tuple-element.178.dense, ...), custom_call_target="tpu_custom_call" | custom-call | flops 24999999488 | bytes 75000000 | tf_op jit(solution)/shard_map/pallas_call | solution.py:329
  83.6 2.5 %shard_map.271 = bf16[4,256,1024]{2,1,0:T(8,128)(2,1)S(1)} custom-call(s32[2]{0:T(128)S(1)} %copy-done.4, bf16[4,256,128]{2,1,0:T(8,128)(2,1)S(1)} %get-tuple-element.132.context, bf16[4,256,512]{2,1,0:T(8,128)(2,1)S(1)} %get-tuple-element.133.act, bf16[128,1024]{1,0:T(8,128)(2,1)S(1)} %get-tuple-element.178.dense, ...), custom_call_target="tpu_custom_call" | custom-call | flops 24999999488 | bytes 75000000 | tf_op jit(solution)/shard_map/pallas_call | solution.py:329
  86.2 4.8 %shard_map.272 = (bf16[2048,128]{1,0:T(8,128)(2,1)S(1)}, bf16[2048,128]{1,0:T(8,128)(2,1)S(1)}, bf16[1024,128]{1,0:T(8,128)(2,1)S(1)}) custom-call(s32[2]{0:T(128)S(1)} %copy-done.4, bf16[1024,1024]{1,0:T(8,128)(2,1)S(1)} %bitcast.65, bf16[1024,1024]{1,0:T(8,128)(2,1)S(1)} %bitcast.66, bf16[1024,512]{1,0:T(8,128)(2,1)S(1)} %bitcast.67, ...), custom_call_target="tpu_custom_call" | custom-call | tf_op jit(solution)/shard_map/pallas_call | solution.py:329
  92.0 1.2 collective-permute-start.19
  93.2 1.5 collective-permute-start.20
  94.7 3.7 %collective-permute-start.21 = (bf16[1024,128]{1,0:T(8,128)(2,1)S(1)}, bf16[1024,128]{1,0:T(8,128)(2,1)S(1)}, u32[]{:S(2)}, u32[]{:S(2)}) collective-permute-start(bf16[1024,128]{1,0:T(8,128)(2,1)S(1)} %get-tuple-element.158), channel_id=1, source_target_pairs={{0,4},{1,5},{2,6},{3,7},{4,0},{5,1},{6,2},{7,3},{8,12},{9,13},{10,... | collective-permute-start | bytes 786440 | tf_op jit(solution)/shard_map/ppermute | solution.py:305
  98.4 8.6 %shard_map.273 = (bf16[8,256,512]{2,1,0:T(8,128)(2,1)S(1)}, f32[8,512]{1,0:T(8,128)S(1)}, f32[8,1024]{1,0:T(8,128)S(1)}, bf16[2048,128]{1,0:T(8,128)(2,1)S(1)}, bf16[2048,128]{1,0:T(8,128)(2,1)S(1)}) custom-call(s32[2]{0:T(128)S(1)} %copy-done.4, bf16[4,256,1024]{2,1,0:T(8,128)(2,1)S(1)} %maximum_maximum_fusion.1.near, ...), custom_call_target="tpu_custom_call" | custom-call | flops 44999999488 | bytes 135000000 | tf_op jit(solution)/shard_map/pallas_call | solution.py:329
  107.6 2.3 %collective-permute-done.21 = bf16[1024,128]{1,0:T(8,128)(2,1)S(1)} collective-permute-done((bf16[1024,128]{1,0:T(8,128)(2,1)S(1)}, bf16[1024,128]{1,0:T(8,128)(2,1)S(1)}, u32[]{:S(2)}, u32[]{:S(2)}) %collective-permute-start.21) | collective-permute-done | bytes 262176 | tf_op jit(solution)/shard_map/ppermute | solution.py:305
  110.8 1.2 collective-permute-start.23
  111.9 12.2 %shard_map.274 = (bf16[8,256,384]{2,1,0:T(8,128)(2,1)S(1)}, bf16[1600,128]{1,0:T(8,128)(2,1)S(1)}, bf16[1600,128]{1,0:T(8,128)(2,1)S(1)}) custom-call(s32[2]{0:T(128)S(1)} %copy-done.4, bf16[4,256,1024]{2,1,0:T(8,128)(2,1)S(1)} %maximum_maximum_fusion.1.near, bf16[4,256,1024]{2,1,0:T(8,128)(2,1)S(1)} %collective-permute-done.17.far, ...), custom_call_target="tpu_custom_call" | custom-call | flops 30000001024 | bytes 90000000 | tf_op jit(solution)/shard_map/pallas_call | solution.py:329
  124.1 3.1 %shard_map.275 = bf16[4,256,1024]{2,1,0:T(8,128)(2,1)S(1)} custom-call(s32[2]{0:T(128)S(1)} %copy-done.4, bf16[8,256,384]{2,1,0:T(8,128)(2,1)S(1)} %get-tuple-element.190.mixed, bf16[8,256,512]{2,1,0:T(8,128)(2,1)S(1)} %get-tuple-element.175.pre, bf16[1024,384]{1,0:T(8,128)(2,1)S(1)} %get-tuple-element.151.mix, ...), custom_call_target="tpu_custom_call" | custom-call | tf_op jit(solution)/shard_map/pallas_call | solution.py:329
  127.3 1.6 collective-permute-start.22
  129.0 1.9 collective-permute-start.31
  132.2 3.4 %shard_map.276 = bf16[4,256,1024]{2,1,0:T(8,128)(2,1)S(1)} custom-call(s32[2]{0:T(128)S(1)} %copy-done.4, bf16[8,256,384]{2,1,0:T(8,128)(2,1)S(1)} %get-tuple-element.190.mixed, bf16[8,256,512]{2,1,0:T(8,128)(2,1)S(1)} %get-tuple-element.175.pre, bf16[1024,384]{1,0:T(8,128)(2,1)S(1)} %get-tuple-element.151.mix, ...), custom_call_target="tpu_custom_call" | custom-call | flops 30000001024 | bytes 90000000 | tf_op jit(solution)/shard_map/pallas_call | solution.py:329
  135.6 1.6 collective-permute-done.22
  137.3 2.7 %collective-permute-start.26 = (bf16[800,128]{1,0:T(8,128)(2,1)S(1)}, bf16[800,128]{1,0:T(8,128)(2,1)S(1)}, u32[]{:S(2)}, u32[]{:S(2)}) collective-permute-start(bf16[800,128]{1,0:T(8,128)(2,1)S(1)} %slice.294), channel_id=1, source_target_pairs={{0,4},{1,5},{2,6},{3,7},{4,0},{5,1},{6,2},{7,3},{8,12},{9,13},{10,... | collective-permute-start | bytes 614408 | tf_op jit(solution)/shard_map/ppermute | solution.py:305
  141.2 1.4 collective-permute-start.33
  143.1 1.5 collective-permute-start.34
  144.7 8.5 %collective-permute-done.26 = bf16[800,128]{1,0:T(8,128)(2,1)S(1)} collective-permute-done((bf16[800,128]{1,0:T(8,128)(2,1)S(1)}, bf16[800,128]{1,0:T(8,128)(2,1)S(1)}, u32[]{:S(2)}, u32[]{:S(2)}) %collective-permute-start.26) | collective-permute-done | bytes 204832 | tf_op jit(solution)/shard_map/ppermute | solution.py:305
  153.5 2.1 %collective-permute-start.36 = (bf16[512,128]{1,0:T(8,128)(2,1)S(1)}, bf16[512,128]{1,0:T(8,128)(2,1)S(1)}, u32[]{:S(2)}, u32[]{:S(2)}) collective-permute-start(bf16[512,128]{1,0:T(8,128)(2,1)S(1)} %get-tuple-element.232), channel_id=1, source_target_pairs={{0,2},{1,3},{2,0},{3,1},{4,6},{5,7},{6,4},{7,5},{8,10},{9,11},{10,... | collective-permute-start | bytes 393224 | tf_op jit(solution)/shard_map/ppermute | solution.py:305
  155.5 5.3 %collective-permute-done.34 = bf16[1024,128]{1,0:T(8,128)(2,1)S(1)} collective-permute-done((bf16[1024,128]{1,0:T(8,128)(2,1)S(1)}, bf16[1024,128]{1,0:T(8,128)(2,1)S(1)}, u32[]{:S(2)}, u32[]{:S(2)}) %collective-permute-start.34) | collective-permute-done | bytes 262176 | tf_op jit(solution)/shard_map/ppermute | solution.py:305
  160.9 1.0 collective-permute-done.33
  162.4 1.8 collective-permute-done.30
  164.6 1.7 collective-permute-start.41
  166.3 1.9 %collective-permute-start.35 = (bf16[256,1024]{1,0:T(8,128)(2,1)S(1)}, bf16[256,1024]{1,0:T(8,128)(2,1)S(1)}, u32[]{:S(2)}, u32[]{:S(2)}) collective-permute-start(bf16[256,1024]{1,0:T(8,128)(2,1)S(1)} %slice_bitcast_fusion.2), channel_id=1, source_target_pairs={{0,2},{1,3},{2,0},{3,1},{4,6},{5,7},{6,4},{7,5},{8,10},{9,11},{10,... | collective-permute-start | bytes 1572872 | tf_op jit(solution)/shard_map/ppermute | solution.py:305
  168.8 4.6 %collective-permute-done.39.upper_got = bf16[128,1024]{1,0:T(8,128)(2,1)S(1)} collective-permute-done((bf16[128,1024]{1,0:T(8,128)(2,1)S(1)}, bf16[128,1024]{1,0:T(8,128)(2,1)S(1)}, u32[]{:S(2)}, u32[]{:S(2)}) %collective-permute-start.39) | collective-permute-done | bytes 262176 | tf_op jit(solution)/shard_map/ppermute | solution.py:305
  173.5 2.2 %shard_map.277 = f32[256,1024]{1,0:T(8,128)} custom-call(s32[2]{0:T(128)S(1)} %copy-done.4, bf16[256,1024]{1,0:T(8,128)(2,1)S(1)} %copy-done.1, bf16[256,1024]{1,0:T(8,128)(2,1)S(1)} %copy-done.3, f32[128,1024]{1,0:T(8,128)S(1)} %slice_bitcast_fusion.1.upper, bf16[128,1024]{1,0:T(8,128)(2,1)S(1)} %collective-permute-done.39.upper_got, ...), custom_call_target="tpu_custom_call" | custom-call | flops 20000000000 | bytes 60000000 | tf_op jit(solution)/shard_map/pallas_call | solution.py:329
  175.7 2.2 %shard_map.278 = (f32[512,1024]{1,0:T(8,128)}, f32[128,1024]{1,0:T(8,128)}) custom-call(s32[2]{0:T(128)S(1)} %copy-done.4, bf16[3072,128]{1,0:T(8,128)(2,1)S(1)} %pad_maximum_fusion.near, bf16[3072,128]{1,0:T(8,128)(2,1)S(1)} %collective-permute-done.38.far, s32[1]{0:T(128)} %bitcast.35.own_dense), custom_call_target="tpu_custom_call" | custom-call | flops 20000000000 | bytes 60000000 | tf_op jit(solution)/shard_map/pallas_call | solution.py:329
  177.9 1.2 collective-permute-done.37
  179.9 2.1 %collective-permute-done.35 = bf16[256,1024]{1,0:T(8,128)(2,1)S(1)} collective-permute-done((bf16[256,1024]{1,0:T(8,128)(2,1)S(1)}, bf16[256,1024]{1,0:T(8,128)(2,1)S(1)}, u32[]{:S(2)}, u32[]{:S(2)}) %collective-permute-start.35) | collective-permute-done | bytes 524320 | tf_op jit(solution)/shard_map/ppermute | solution.py:305
  182.1 1.1 add_convert_fusion.2
  183.7 2.4 %shard_map.279 = f32[128,3072]{1,0:T(8,128)} custom-call(s32[2]{0:T(128)S(1)} %copy-done.4, bf16[1616,128]{1,0:T(8,128)(2,1)S(1)} %pad_maximum_fusion.7.near, bf16[1616,128]{1,0:T(8,128)(2,1)S(1)} %collective-permute-done.42.far), custom_call_target="tpu_custom_call" | custom-call | flops 20000000000 | bytes 60000000 | tf_op jit(solution)/shard_map/pallas_call | solution.py:329
  187.7 2.7 %shard_map.280 = f32[128,4096]{1,0:T(8,128)} custom-call(s32[2]{0:T(128)S(1)} %copy-done.4, bf16[2048,128]{1,0:T(8,128)(2,1)S(1)} %pad_maximum_fusion.6.near, bf16[2048,128]{1,0:T(8,128)(2,1)S(1)} %collective-permute-done.43.far), custom_call_target="tpu_custom_call" | custom-call | flops 20000000000 | bytes 60000000 | tf_op jit(solution)/shard_map/pallas_call | solution.py:329
  (136 shorter events, 19.6 us)
Async XLA Ops:
  1.3 6.9 %copy-start = (bf16[256,1024]{1,0:T(8,128)(2,1)S(1)}, bf16[256,1024]{1,0:T(8,128)(2,1)}, u32[]{:S(2)}) copy-start(bf16[256,1024]{1,0:T(8,128)(2,1)} %block.1) | copy-start | bytes 1572868
  4.6 26.0 %collective-permute-start.5 = (bf16[912,128]{1,0:T(8,128)(2,1)}, bf16[912,128]{1,0:T(8,128)(2,1)S(1)}, u32[]{:S(2)}, u32[]{:S(2)}) collective-permute-start(bf16[912,128]{1,0:T(8,128)(2,1)} %get-tuple-element.117), channel_id=1, source_target_pairs={{0,6},{1,7},{2,4},{3,5},{4,2},{5,3},{6,0},{7,1},{8,14},{9,15},{10,... | collective-permute-start | bytes 700424 | tf_op jit(solution)/shard_map/ppermute | solution.py:305
  8.2 22.4 %collective-permute-start.2 = (bf16[912,128]{1,0:T(8,128)(2,1)}, bf16[912,128]{1,0:T(8,128)(2,1)S(1)}, u32[]{:S(2)}, u32[]{:S(2)}) collective-permute-start(bf16[912,128]{1,0:T(8,128)(2,1)} %get-tuple-element.117), channel_id=1, source_target_pairs={{0,2},{1,3},{2,0},{3,1},{4,6},{5,7},{6,4},{7,5},{8,10},{9,11},{10,... | collective-permute-start | bytes 700424 | tf_op jit(solution)/shard_map/ppermute | solution.py:305
  8.4 22.1 %collective-permute-start.3 = (bf16[144,1024]{1,0:T(8,128)(2,1)S(1)}, bf16[144,1024]{1,0:T(8,128)(2,1)S(1)}, u32[]{:S(2)}, u32[]{:S(2)}) collective-permute-start(bf16[144,1024]{1,0:T(8,128)(2,1)S(1)} %get-tuple-element.230), channel_id=1, source_target_pairs={{0,2},{1,3},{2,0},{3,1},{4,6},{5,7},{6,4},{7,5},{8,10},{9,11},{10,... | collective-permute-start | bytes 884744 | tf_op jit(solution)/shard_map/ppermute | solution.py:305
  10.5 7.2 %collective-permute-start = (bf16[128,1024]{1,0:T(8,128)(2,1)S(1)}, bf16[128,1024]{1,0:T(8,128)(2,1)S(1)}, u32[]{:S(2)}, u32[]{:S(2)}) collective-permute-start(bf16[128,1024]{1,0:T(8,128)(2,1)S(1)} %get-tuple-element.227), channel_id=1, source_target_pairs={{0,16},{1,17},{2,18},{3,19},{4,20},{5,21},{6,22},{7,23},{8,24},{9,... | collective-permute-start | bytes 786440 | tf_op jit(solution)/shard_map/ppermute | solution.py:305
  11.0 19.6 %collective-permute-start.4 = (bf16[912,128]{1,0:T(8,128)(2,1)}, bf16[912,128]{1,0:T(8,128)(2,1)S(1)}, u32[]{:S(2)}, u32[]{:S(2)}) collective-permute-start(bf16[912,128]{1,0:T(8,128)(2,1)} %get-tuple-element.123.own), channel_id=1, source_target_pairs={{0,4},{1,5},{2,6},{3,7},{4,0},{5,1},{6,2},{7,3},{8,12},{9,13},{10,... | collective-permute-start | bytes 700424 | tf_op jit(solution)/shard_map/ppermute | solution.py:305
  17.7 14.3 %collective-permute-start.6 = (bf16[2448,128]{1,0:T(8,128)(2,1)}, bf16[2448,128]{1,0:T(8,128)(2,1)S(1)}, u32[]{:S(2)}, u32[]{:S(2)}) collective-permute-start(bf16[2448,128]{1,0:T(8,128)(2,1)} %shard_map.264), channel_id=1, source_target_pairs={{0,1},{1,0},{2,3},{3,2},{4,5},{5,4},{6,7},{7,6},{8,9},{9,8},{10,11... | collective-permute-start | bytes 1880072 | tf_op jit(solution)/shard_map/ppermute | solution.py:305
  30.5 23.2 %collective-permute-start.1 = (bf16[2,128,1024]{2,1,0:T(8,128)(2,1)S(1)}, bf16[2,128,1024]{2,1,0:T(8,128)(2,1)S(1)}, u32[]{:S(2)}, u32[]{:S(2)}) collective-permute-start(bf16[2,128,1024]{2,1,0:T(8,128)(2,1)S(1)} %pad_maximum_fusion.3), channel_id=1, source_target_pairs={{0,2},{1,3},{2,0},{3,1},{4,6},{5,7},{6,4},{7,5},{8,10},{9,11},{10,... | collective-permute-start | bytes 1572872 | tf_op jit(solution)/shard_map/ppermute | solution.py:305
  30.7 25.7 %collective-permute-start.8 = (bf16[3,912,128]{2,1,0:T(8,128)(2,1)S(1)}, bf16[3,912,128]{2,1,0:T(8,128)(2,1)S(1)}, u32[]{:S(2)}, u32[]{:S(2)}) collective-permute-start(bf16[3,912,128]{2,1,0:T(8,128)(2,1)S(1)} %pad_maximum_fusion.1.along), channel_id=1, source_target_pairs={{0,1},{1,0},{2,3},{3,2},{4,5},{5,4},{6,7},{7,6},{8,9},{9,8},{10,11... | collective-permute-start | bytes 2101256 | tf_op jit(solution)/shard_map/ppermute | solution.py:305
  31.3 22.5 %collective-permute-start.7 = (bf16[2,144,1024]{2,1,0:T(8,128)(2,1)S(1)}, bf16[2,144,1024]{2,1,0:T(8,128)(2,1)S(1)}, u32[]{:S(2)}, u32[]{:S(2)}) collective-permute-start(bf16[2,144,1024]{2,1,0:T(8,128)(2,1)S(1)} %pad_maximum_fusion.2), channel_id=1, source_target_pairs={{0,16},{1,17},{2,18},{3,19},{4,20},{5,21},{6,22},{7,23},{8,24},{9,... | collective-permute-start | bytes 1769480 | tf_op jit(solution)/shard_map/ppermute | solution.py:305
  36.1 28.2 %collective-permute-start.9 = (bf16[192,1024]{1,0:T(8,128)(2,1)}, bf16[192,1024]{1,0:T(8,128)(2,1)S(1)}, u32[]{:S(2)}, u32[]{:S(2)}) collective-permute-start(bf16[192,1024]{1,0:T(8,128)(2,1)} %get-tuple-element.126), channel_id=1, source_target_pairs={{0,2},{1,3},{2,0},{3,1},{4,6},{5,7},{6,4},{7,5},{8,10},{9,11},{10,... | collective-permute-start | bytes 1179656 | tf_op jit(solution)/shard_map/ppermute | solution.py:305
  38.0 26.4 %collective-permute-start.10 = (bf16[192,1024]{1,0:T(8,128)(2,1)}, bf16[192,1024]{1,0:T(8,128)(2,1)S(1)}, u32[]{:S(2)}, u32[]{:S(2)}) collective-permute-start(bf16[192,1024]{1,0:T(8,128)(2,1)} %get-tuple-element.125.own), channel_id=1, source_target_pairs={{0,4},{1,5},{2,6},{3,7},{4,0},{5,1},{6,2},{7,3},{8,12},{9,13},{10,... | collective-permute-start | bytes 1179656 | tf_op jit(solution)/shard_map/ppermute | solution.py:305
  54.1 14.1 %collective-permute-start.12 = (bf16[4,272,1024]{2,1,0:T(8,128)(2,1)S(1)}, bf16[4,272,1024]{2,1,0:T(8,128)(2,1)S(1)}, u32[]{:S(2)}, u32[]{:S(2)}) collective-permute-start(bf16[4,272,1024]{2,1,0:T(8,128)(2,1)S(1)} %maximum_maximum_fusion.inputs), channel_id=1, source_target_pairs={{0,8},{1,9},{2,10},{3,11},{4,12},{5,13},{6,14},{7,15},{8,0},{9,1},... | collective-permute-start | bytes 6684680 | tf_op jit(solution)/shard_map/ppermute | solution.py:305
  54.7 9.6 %collective-permute-start.11 = (bf16[64,1024]{1,0:T(8,128)(2,1)S(1)}, bf16[64,1024]{1,0:T(8,128)(2,1)S(1)}, u32[]{:S(2)}, u32[]{:S(2)}) collective-permute-start(bf16[64,1024]{1,0:T(8,128)(2,1)S(1)} %copy-done.11), channel_id=1, source_target_pairs={{0,6},{1,7},{2,4},{3,5},{4,2},{5,3},{6,0},{7,1},{8,14},{9,15},{10,... | collective-permute-start | bytes 393224 | tf_op jit(solution)/shard_map/ppermute | solution.py:305
  56.4 7.9 %copy-start.7 = (bf16[192,1024]{1,0:T(8,128)(2,1)S(1)}, bf16[192,1024]{1,0:T(8,128)(2,1)}, u32[]{:S(2)}) copy-start(bf16[192,1024]{1,0:T(8,128)(2,1)} %get-tuple-element.125.own) | copy-start | bytes 1179652
  56.4 10.8 %collective-permute-start.13 = (bf16[128,1024]{1,0:T(8,128)(2,1)S(1)}, bf16[128,1024]{1,0:T(8,128)(2,1)S(1)}, u32[]{:S(2)}, u32[]{:S(2)}) collective-permute-start(bf16[128,1024]{1,0:T(8,128)(2,1)S(1)} %get-tuple-element.143), channel_id=1, source_target_pairs={{0,16},{1,17},{2,18},{3,19},{4,20},{5,21},{6,22},{7,23},{8,24},{9,... | collective-permute-start | bytes 786440 | tf_op jit(solution)/shard_map/ppermute | solution.py:305
  65.0 15.5 %collective-permute-start.14 = (bf16[192,1024]{1,0:T(8,128)(2,1)S(1)}, bf16[192,1024]{1,0:T(8,128)(2,1)S(1)}, u32[]{:S(2)}, u32[]{:S(2)}) collective-permute-start(bf16[192,1024]{1,0:T(8,128)(2,1)S(1)} %get-tuple-element.142.along), channel_id=1, source_target_pairs={{0,1},{1,0},{2,3},{3,2},{4,5},{5,4},{6,7},{7,6},{8,9},{9,8},{10,11... | collective-permute-start | bytes 1179656 | tf_op jit(solution)/shard_map/ppermute | solution.py:305
  65.6 14.5 %collective-permute-start.16 = (bf16[2,128,1024]{2,1,0:T(8,128)(2,1)S(1)}, bf16[2,128,1024]{2,1,0:T(8,128)(2,1)S(1)}, u32[]{:S(2)}, u32[]{:S(2)}) collective-permute-start(bf16[2,128,1024]{2,1,0:T(8,128)(2,1)S(1)} %pad_maximum_fusion.5), channel_id=1, source_target_pairs={{0,16},{1,17},{2,18},{3,19},{4,20},{5,21},{6,22},{7,23},{8,24},{9,... | collective-permute-start | bytes 1572872 | tf_op jit(solution)/shard_map/ppermute | solution.py:305
  67.2 12.8 %collective-permute-start.15 = (bf16[2,128,1024]{2,1,0:T(8,128)(2,1)S(1)}, bf16[2,128,1024]{2,1,0:T(8,128)(2,1)S(1)}, u32[]{:S(2)}, u32[]{:S(2)}) collective-permute-start(bf16[2,128,1024]{2,1,0:T(8,128)(2,1)S(1)} %pad_maximum_fusion.4), channel_id=1, source_target_pairs={{0,2},{1,3},{2,0},{3,1},{4,6},{5,7},{6,4},{7,5},{8,10},{9,11},{10,... | collective-permute-start | bytes 1572872 | tf_op jit(solution)/shard_map/ppermute | solution.py:305
  80.4 5.8 %collective-permute-start.17 = (bf16[4,256,1024]{2,1,0:T(8,128)(2,1)S(1)}, bf16[4,256,1024]{2,1,0:T(8,128)(2,1)S(1)}, u32[]{:S(2)}, u32[]{:S(2)}) collective-permute-start(bf16[4,256,1024]{2,1,0:T(8,128)(2,1)S(1)} %maximum_maximum_fusion.1.near), channel_id=1, source_target_pairs={{0,8},{1,9},{2,10},{3,11},{4,12},{5,13},{6,14},{7,15},{8,0},{9,1},... | collective-permute-start | bytes 6291464 | tf_op jit(solution)/shard_map/ppermute | solution.py:305
  83.1 7.9 %collective-permute-start.18 = (bf16[4,256,1024]{2,1,0:T(8,128)(2,1)S(1)}, bf16[4,256,1024]{2,1,0:T(8,128)(2,1)S(1)}, u32[]{:S(2)}, u32[]{:S(2)}) collective-permute-start(bf16[4,256,1024]{2,1,0:T(8,128)(2,1)S(1)} %get-tuple-element.160), channel_id=1, source_target_pairs={{0,8},{1,9},{2,10},{3,11},{4,12},{5,13},{6,14},{7,15},{8,0},{9,1},... | collective-permute-start | bytes 6291464 | tf_op jit(solution)/shard_map/ppermute | solution.py:305
  92.0 39.2 %collective-permute-start.19 = (bf16[2,256,1024]{2,1,0:T(8,128)(2,1)S(1)}, bf16[2,256,1024]{2,1,0:T(8,128)(2,1)S(1)}, u32[]{:S(2)}, u32[]{:S(2)}) collective-permute-start(bf16[2,256,1024]{2,1,0:T(8,128)(2,1)S(1)} %slice.216), channel_id=1, source_target_pairs={{0,16},{1,17},{2,18},{3,19},{4,20},{5,21},{6,22},{7,23},{8,24},{9,... | collective-permute-start | bytes 3145736 | tf_op jit(solution)/shard_map/ppermute | solution.py:305
  93.2 17.4 %collective-permute-start.20 = (bf16[2048,128]{1,0:T(8,128)(2,1)S(1)}, bf16[2048,128]{1,0:T(8,128)(2,1)S(1)}, u32[]{:S(2)}, u32[]{:S(2)}) collective-permute-start(bf16[2048,128]{1,0:T(8,128)(2,1)S(1)} %get-tuple-element.170), channel_id=1, source_target_pairs={{0,1},{1,0},{2,3},{3,2},{4,5},{5,4},{6,7},{7,6},{8,9},{9,8},{10,11... | collective-permute-start | bytes 1572872 | tf_op jit(solution)/shard_map/ppermute | solution.py:305
  94.7 15.2 %collective-permute-start.21 = (bf16[1024,128]{1,0:T(8,128)(2,1)S(1)}, bf16[1024,128]{1,0:T(8,128)(2,1)S(1)}, u32[]{:S(2)}, u32[]{:S(2)}) collective-permute-start(bf16[1024,128]{1,0:T(8,128)(2,1)S(1)} %get-tuple-element.158), channel_id=1, source_target_pairs={{0,4},{1,5},{2,6},{3,7},{4,0},{5,1},{6,2},{7,3},{8,12},{9,13},{10,... | collective-permute-start | bytes 786440 | tf_op jit(solution)/shard_map/ppermute | solution.py:305
  107.0 21.9 %collective-permute-start.25 = (bf16[2048,128]{1,0:T(8,128)(2,1)S(1)}, bf16[2048,128]{1,0:T(8,128)(2,1)S(1)}, u32[]{:S(2)}, u32[]{:S(2)}) collective-permute-start(bf16[2048,128]{1,0:T(8,128)(2,1)S(1)} %get-tuple-element.188), channel_id=1, source_target_pairs={{0,1},{1,0},{2,3},{3,2},{4,5},{5,4},{6,7},{7,6},{8,9},{9,8},{10,11... | collective-permute-start | bytes 1572872 | tf_op jit(solution)/shard_map/ppermute | solution.py:305
  110.0 19.0 %collective-permute-start.24 = (bf16[1024,128]{1,0:T(8,128)(2,1)S(1)}, bf16[1024,128]{1,0:T(8,128)(2,1)S(1)}, u32[]{:S(2)}, u32[]{:S(2)}) collective-permute-start(bf16[1024,128]{1,0:T(8,128)(2,1)S(1)} %add_convert_fusion.4), channel_id=1, source_target_pairs={{0,1},{1,0},{2,3},{3,2},{4,5},{5,4},{6,7},{7,6},{8,9},{9,8},{10,11... | collective-permute-start | bytes 786440 | tf_op jit(solution)/shard_map/ppermute | solution.py:305
  110.8 20.2 %collective-permute-start.23 = (bf16[1024,128]{1,0:T(8,128)(2,1)S(1)}, bf16[1024,128]{1,0:T(8,128)(2,1)S(1)}, u32[]{:S(2)}, u32[]{:S(2)}) collective-permute-start(bf16[1024,128]{1,0:T(8,128)(2,1)S(1)} %slice.293), channel_id=1, source_target_pairs={{0,4},{1,5},{2,6},{3,7},{4,0},{5,1},{6,2},{7,3},{8,12},{9,13},{10,... | collective-permute-start | bytes 786440 | tf_op jit(solution)/shard_map/ppermute | solution.py:305
  127.3 9.9 %collective-permute-start.22 = (bf16[1600,128]{1,0:T(8,128)(2,1)S(1)}, bf16[1600,128]{1,0:T(8,128)(2,1)S(1)}, u32[]{:S(2)}, u32[]{:S(2)}) collective-permute-start(bf16[1600,128]{1,0:T(8,128)(2,1)S(1)} %get-tuple-element.184), channel_id=1, source_target_pairs={{0,1},{1,0},{2,3},{3,2},{4,5},{5,4},{6,7},{7,6},{8,9},{9,8},{10,11... | collective-permute-start | bytes 1228808 | tf_op jit(solution)/shard_map/ppermute | solution.py:305
  128.9 11.2 %collective-permute-start.29 = (bf16[4,256,1024]{2,1,0:T(8,128)(2,1)S(1)}, bf16[4,256,1024]{2,1,0:T(8,128)(2,1)S(1)}, u32[]{:S(2)}, u32[]{:S(2)}) collective-permute-start(bf16[4,256,1024]{2,1,0:T(8,128)(2,1)S(1)} %shard_map.275), channel_id=1, source_target_pairs={{0,8},{1,9},{2,10},{3,11},{4,12},{5,13},{6,14},{7,15},{8,0},{9,1},... | collective-permute-start | bytes 6291464 | tf_op jit(solution)/shard_map/ppermute | solution.py:305
  129.0 24.3 %collective-permute-start.31 = (bf16[1024,128]{1,0:T(8,128)(2,1)S(1)}, bf16[1024,128]{1,0:T(8,128)(2,1)S(1)}, u32[]{:S(2)}, u32[]{:S(2)}) collective-permute-start(bf16[1024,128]{1,0:T(8,128)(2,1)S(1)} %slice.292), channel_id=1, source_target_pairs={{0,4},{1,5},{2,6},{3,7},{4,0},{5,1},{6,2},{7,3},{8,12},{9,13},{10,... | collective-permute-start | bytes 786440 | tf_op jit(solution)/shard_map/ppermute | solution.py:305
  131.1 12.0 %collective-permute-start.27 = (bf16[512,128]{1,0:T(8,128)(2,1)S(1)}, bf16[512,128]{1,0:T(8,128)(2,1)S(1)}, u32[]{:S(2)}, u32[]{:S(2)}) collective-permute-start(bf16[512,128]{1,0:T(8,128)(2,1)S(1)} %get-tuple-element.234), channel_id=1, source_target_pairs={{0,2},{1,3},{2,0},{3,1},{4,6},{5,7},{6,4},{7,5},{8,10},{9,11},{10,... | collective-permute-start | bytes 393224 | tf_op jit(solution)/shard_map/ppermute | solution.py:305
  131.2 8.8 %collective-permute-start.28 = (bf16[1024,128]{1,0:T(8,128)(2,1)S(1)}, bf16[1024,128]{1,0:T(8,128)(2,1)S(1)}, u32[]{:S(2)}, u32[]{:S(2)}) collective-permute-start(bf16[1024,128]{1,0:T(8,128)(2,1)S(1)} %get-tuple-element.243), channel_id=1, source_target_pairs={{0,16},{1,17},{2,18},{3,19},{4,20},{5,21},{6,22},{7,23},{8,24},{9,... | collective-permute-start | bytes 786440 | tf_op jit(solution)/shard_map/ppermute | solution.py:305
  137.3 15.9 %collective-permute-start.26 = (bf16[800,128]{1,0:T(8,128)(2,1)S(1)}, bf16[800,128]{1,0:T(8,128)(2,1)S(1)}, u32[]{:S(2)}, u32[]{:S(2)}) collective-permute-start(bf16[800,128]{1,0:T(8,128)(2,1)S(1)} %slice.294), channel_id=1, source_target_pairs={{0,4},{1,5},{2,6},{3,7},{4,0},{5,1},{6,2},{7,3},{8,12},{9,13},{10,... | collective-permute-start | bytes 614408 | tf_op jit(solution)/shard_map/ppermute | solution.py:305
  141.2 20.7 %collective-permute-start.33 = (bf16[2,128,1024]{2,1,0:T(8,128)(2,1)S(1)}, bf16[2,128,1024]{2,1,0:T(8,128)(2,1)S(1)}, u32[]{:S(2)}, u32[]{:S(2)}) collective-permute-start(bf16[2,128,1024]{2,1,0:T(8,128)(2,1)S(1)} %get-tuple-element.218), channel_id=1, source_target_pairs={{0,2},{1,3},{2,0},{3,1},{4,6},{5,7},{6,4},{7,5},{8,10},{9,11},{10,... | collective-permute-start | bytes 1572872 | tf_op jit(solution)/shard_map/ppermute | solution.py:305
  142.6 19.4 %collective-permute-start.32 = (bf16[2,128,1024]{2,1,0:T(8,128)(2,1)S(1)}, bf16[2,128,1024]{2,1,0:T(8,128)(2,1)S(1)}, u32[]{:S(2)}, u32[]{:S(2)}) collective-permute-start(bf16[2,128,1024]{2,1,0:T(8,128)(2,1)S(1)} %get-tuple-element.219), channel_id=1, source_target_pairs={{0,16},{1,17},{2,18},{3,19},{4,20},{5,21},{6,22},{7,23},{8,24},{9,... | collective-permute-start | bytes 1572872 | tf_op jit(solution)/shard_map/ppermute | solution.py:305
  143.1 17.7 %collective-permute-start.34 = (bf16[1024,128]{1,0:T(8,128)(2,1)S(1)}, bf16[1024,128]{1,0:T(8,128)(2,1)S(1)}, u32[]{:S(2)}, u32[]{:S(2)}) collective-permute-start(bf16[1024,128]{1,0:T(8,128)(2,1)S(1)} %pad_maximum_fusion.8), channel_id=1, source_target_pairs={{0,16},{1,17},{2,18},{3,19},{4,20},{5,21},{6,22},{7,23},{8,24},{9,... | collective-permute-start | bytes 786440 | tf_op jit(solution)/shard_map/ppermute | solution.py:305
  153.3 10.8 %collective-permute-start.30 = (bf16[400,128]{1,0:T(8,128)(2,1)S(1)}, bf16[400,128]{1,0:T(8,128)(2,1)S(1)}, u32[]{:S(2)}, u32[]{:S(2)}) collective-permute-start(bf16[400,128]{1,0:T(8,128)(2,1)S(1)} %get-tuple-element.236), channel_id=1, source_target_pairs={{0,2},{1,3},{2,0},{3,1},{4,6},{5,7},{6,4},{7,5},{8,10},{9,11},{10,... | collective-permute-start | bytes 307208 | tf_op jit(solution)/shard_map/ppermute | solution.py:305
  153.5 14.8 %collective-permute-start.36 = (bf16[512,128]{1,0:T(8,128)(2,1)S(1)}, bf16[512,128]{1,0:T(8,128)(2,1)S(1)}, u32[]{:S(2)}, u32[]{:S(2)}) collective-permute-start(bf16[512,128]{1,0:T(8,128)(2,1)S(1)} %get-tuple-element.232), channel_id=1, source_target_pairs={{0,2},{1,3},{2,0},{3,1},{4,6},{5,7},{6,4},{7,5},{8,10},{9,11},{10,... | collective-permute-start | bytes 393224 | tf_op jit(solution)/shard_map/ppermute | solution.py:305
  162.3 11.3 %copy-start.1 = (bf16[256,1024]{1,0:T(8,128)(2,1)S(1)}, bf16[256,1024]{1,0:T(8,128)(2,1)}, u32[]{:S(2)}) copy-start(bf16[256,1024]{1,0:T(8,128)(2,1)} %block.1) | copy-start | bytes 1572868
  162.3 11.3 %copy-start.3 = (bf16[256,1024]{1,0:T(8,128)(2,1)S(1)}, bf16[256,1024]{1,0:T(8,128)(2,1)}, u32[]{:S(2)}) copy-start(bf16[256,1024]{1,0:T(8,128)(2,1)} %cot.3) | copy-start | bytes 1572868
  164.1 9.3 %collective-permute-start.39 = (bf16[128,1024]{1,0:T(8,128)(2,1)S(1)}, bf16[128,1024]{1,0:T(8,128)(2,1)S(1)}, u32[]{:S(2)}, u32[]{:S(2)}) collective-permute-start(bf16[128,1024]{1,0:T(8,128)(2,1)S(1)} %fusion.5), channel_id=1, source_target_pairs={{0,2},{1,3},{2,0},{3,1},{4,6},{5,7},{6,4},{7,5},{8,10},{9,11},{10,... | collective-permute-start | bytes 786440 | tf_op jit(solution)/shard_map/ppermute | solution.py:305
  164.2 9.3 %collective-permute-start.40 = (bf16[128,1024]{1,0:T(8,128)(2,1)S(1)}, bf16[128,1024]{1,0:T(8,128)(2,1)S(1)}, u32[]{:S(2)}, u32[]{:S(2)}) collective-permute-start(bf16[128,1024]{1,0:T(8,128)(2,1)S(1)} %fusion.6), channel_id=1, source_target_pairs={{0,16},{1,17},{2,18},{3,19},{4,20},{5,21},{6,22},{7,23},{8,24},{9,... | collective-permute-start | bytes 786440 | tf_op jit(solution)/shard_map/ppermute | solution.py:305
  164.6 14.6 %collective-permute-start.41 = (bf16[800,128]{1,0:T(8,128)(2,1)S(1)}, bf16[800,128]{1,0:T(8,128)(2,1)S(1)}, u32[]{:S(2)}, u32[]{:S(2)}) collective-permute-start(bf16[800,128]{1,0:T(8,128)(2,1)S(1)} %pad_maximum_fusion.10), channel_id=1, source_target_pairs={{0,16},{1,17},{2,18},{3,19},{4,20},{5,21},{6,22},{7,23},{8,24},{9,... | collective-permute-start | bytes 614408 | tf_op jit(solution)/shard_map/ppermute | solution.py:305
  166.3 15.7 %collective-permute-start.35 = (bf16[256,1024]{1,0:T(8,128)(2,1)S(1)}, bf16[256,1024]{1,0:T(8,128)(2,1)S(1)}, u32[]{:S(2)}, u32[]{:S(2)}) collective-permute-start(bf16[256,1024]{1,0:T(8,128)(2,1)S(1)} %slice_bitcast_fusion.2), channel_id=1, source_target_pairs={{0,2},{1,3},{2,0},{3,1},{4,6},{5,7},{6,4},{7,5},{8,10},{9,11},{10,... | collective-permute-start | bytes 1572872 | tf_op jit(solution)/shard_map/ppermute | solution.py:305
  168.3 10.8 %collective-permute-start.37 = (bf16[1024,128]{1,0:T(8,128)(2,1)S(1)}, bf16[1024,128]{1,0:T(8,128)(2,1)S(1)}, u32[]{:S(2)}, u32[]{:S(2)}) collective-permute-start(bf16[1024,128]{1,0:T(8,128)(2,1)S(1)} %pad_maximum_fusion.9), channel_id=1, source_target_pairs={{0,16},{1,17},{2,18},{3,19},{4,20},{5,21},{6,22},{7,23},{8,24},{9,... | collective-permute-start | bytes 786440 | tf_op jit(solution)/shard_map/ppermute | solution.py:305
  173.4 2.3 %collective-permute-start.38 = (bf16[3072,128]{1,0:T(8,128)(2,1)S(1)}, bf16[3072,128]{1,0:T(8,128)(2,1)S(1)}, u32[]{:S(2)}, u32[]{:S(2)}) collective-permute-start(bf16[3072,128]{1,0:T(8,128)(2,1)S(1)} %pad_maximum_fusion.near), channel_id=1, source_target_pairs={{0,8},{1,9},{2,10},{3,11},{4,12},{5,13},{6,14},{7,15},{8,0},{9,1},... | collective-permute-start | bytes 2359304 | tf_op jit(solution)/shard_map/ppermute | solution.py:305
  179.3 3.9 %collective-permute-start.42 = (bf16[1616,128]{1,0:T(8,128)(2,1)S(1)}, bf16[1616,128]{1,0:T(8,128)(2,1)S(1)}, u32[]{:S(2)}, u32[]{:S(2)}) collective-permute-start(bf16[1616,128]{1,0:T(8,128)(2,1)S(1)} %pad_maximum_fusion.7.near), channel_id=1, source_target_pairs={{0,8},{1,9},{2,10},{3,11},{4,12},{5,13},{6,14},{7,15},{8,0},{9,1},... | collective-permute-start | bytes 1241096 | tf_op jit(solution)/shard_map/ppermute | solution.py:305
  179.4 8.4 %collective-permute-start.43 = (bf16[2048,128]{1,0:T(8,128)(2,1)S(1)}, bf16[2048,128]{1,0:T(8,128)(2,1)S(1)}, u32[]{:S(2)}, u32[]{:S(2)}) collective-permute-start(bf16[2048,128]{1,0:T(8,128)(2,1)S(1)} %pad_maximum_fusion.6.near), channel_id=1, source_target_pairs={{0,8},{1,9},{2,10},{3,11},{4,12},{5,13},{6,14},{7,15},{8,0},{9,1},... | collective-permute-start | bytes 1572872 | tf_op jit(solution)/shard_map/ppermute | solution.py:305
  (8 other events, 24.3 us)
